TPU v7x, 32 devices: a whole 2x2x4 slice. The times are simulated.
32 devices in a mesh: wide: 8 (over y, x, core), narrow: 4 (over z).
Axes of the slice: x: 2, y: 2, z: 4, core: 2. Of those that a mesh axis runs over, the one named last changes fastest.
Arguments:
- blocks: float32 [8, 4, 2, 64, 4096], P('wide', 'narrow'), may hold values from -786432 to 786432
- block_coords: int32 [8, 4, 2, 3], P('wide', 'narrow'), may hold values from 0 to 63, as said below
- block_count: int32 [8, 4], P('wide', 'narrow'), may hold values from 0 to 2, as said below
- orbital_factor: float32 [4096, 128], P('narrow'), may hold values from -8 to 8
Outputs:
- aux_new: float32 [4, 4096, 128], P('narrow', 'wide')
- orbital_new: float32 [4096, 128], P('narrow')
Inputs may be any that keep to these rules, and one draw needn't show every extreme that they name: `block_coords`: entries are (auxiliary block 0 to 63, orbital block 0 to 63, orbital block 0 to 63); no triple repeats within a column. `block_count`: slot s of a device is live when s < its count; some device holds 2 live blocks in every draw.
All inputs are finite; a program needn't handle non-finite values.
Results may differ from a plain program's by a relative error of at most 0.0003.
Values sent between devices are 32-bit elements; how exact they have to be, the bound alone decides.
No kernel may reach another device: no remote copies, remote signals or barrier semaphores. Data moves between devices by JAX's collectives and lax.ppermute only.
A program may use at most 64 MiB of HBM per device.

v0:
```python
import jax
import jax.numpy as jnp
from jax import lax
from jax.sharding import PartitionSpec as P

NP = 16384


precise_level = lax.Precision.HIGHEST


def product(left, right):
    return jnp.dot(left, right, precision=precise_level, preferred_element_type=jnp.float32)


def inverse_of(gram):
    lower = jnp.linalg.cholesky(gram)
    return jax.scipy.linalg.cho_solve((lower, True), jnp.eye(gram.shape[0], dtype=gram.dtype))


def digits_of(size):
    digits = []
    stride = 1
    while stride < size:
        left = size // stride
        radix = 2 if left.bit_length() % 2 == 0 else 4
        digits.append((stride, radix))
        stride *= radix
    return digits


def swap_with(value, axis, mask):
    size = lax.axis_size(axis)
    return lax.ppermute(value, axis, [(index, index ^ mask) for index in range(size)])


def gather_from(value, axis):
    size = lax.axis_size(axis)
    held = {0: value}
    for stride, radix in reversed(digits_of(size)):
        fresh = {}
        sent = sorted(held)
        packed = jnp.stack([held[key] for key in sent])
        for digit in range(1, radix):
            arrived = swap_with(packed, axis, digit * stride)
            for place, key in enumerate(sent):
                fresh[key + digit * stride] = arrived[place]
        held.update(fresh)
    return jnp.stack([held[key] for key in range(size)])


def exchange(value, axis):
    size = lax.axis_size(axis)
    for stride, radix in digits_of(size):
        view = value.reshape((size // (stride * radix), radix, stride) + value.shape[1:])
        parts = [view[:, 0]]
        for digit in range(1, radix):
            parts.append(swap_with(view[:, digit], axis, digit * stride))
        value = jnp.stack(parts, axis=1).reshape(value.shape)
    return value


def on_device(blocks, block_coords, block_count, orbital_factor):
    slots = blocks.shape[2]
    edge = blocks.shape[3]
    rank = orbital_factor.shape[1]
    wide_size = lax.axis_size("wide")
    narrow_size = lax.axis_size("narrow")
    wide_at = lax.axis_index("wide")
    narrow_at = lax.axis_index("narrow")
    others = wide_at ^ jnp.arange(wide_size, dtype=jnp.int32)
    columns = narrow_at ^ jnp.arange(narrow_size, dtype=jnp.int32)
    slice_rows = edge // wide_size
    own_blocks = orbital_factor.shape[0] // edge
    column_rows = NP // narrow_size
    own_rows = column_rows // wide_size
    coords = block_coords[0, 0]
    live = (jnp.arange(slots, dtype=jnp.int32) < block_count[0, 0]).astype(jnp.int32)
    tags = jnp.concatenate([coords, live[:, None]], axis=1)

    by_slice = orbital_factor.reshape(own_blocks, wide_size, slice_rows, rank)
    own_slice = lax.dynamic_index_in_dim(by_slice, wide_at, 1, keepdims=False)
    slices = gather_from(own_slice, "narrow").reshape(-1, slice_rows, rank)
    all_tags = gather_from(tags, "wide")
    pair = all_tags[:, :, 1:3].reshape(wide_size, slots * 2)
    place = ((pair // own_blocks) ^ narrow_at) * own_blocks + pair % own_blocks
    wanted = jnp.take(slices, place.reshape(-1), axis=0).reshape(
        wide_size, slots * 2, slice_rows, rank
    )
    pieces = jnp.take(exchange(wanted, "wide"), others, axis=0)
    rows = jnp.transpose(pieces, (1, 0, 2, 3)).reshape(slots, 2, edge, rank)

    gram_b = jnp.sum(gather_from(product(orbital_factor.T, orbital_factor), "narrow"), axis=0)
    inverse_b = inverse_of(gram_b * gram_b)

    terms = []
    for slot in range(slots):
        pairs = (rows[slot, 0][:, None, :] * rows[slot, 1][None, :, :]).reshape(edge * edge, rank)
        terms.append(product(blocks[0, 0, slot], pairs) * live[slot].astype(jnp.float32))
    column_terms = jnp.take(gather_from(jnp.stack(terms), "wide"), others, axis=0)
    column_terms = column_terms.reshape(wide_size * slots, edge, rank)
    column_tags = jnp.take(all_tags, others, axis=0).reshape(wide_size * slots, 4)
    same = column_tags[:, None, 0] == column_tags[None, :, 0]
    order = jnp.arange(wide_size * slots, dtype=jnp.int32)
    first = jnp.argmax(same, axis=1).astype(jnp.int32)
    member = (first[None, :] == order[:, None]).astype(jnp.float32)
    sums = jnp.einsum("st,ter->ser", member, column_terms, precision=precise_level)
    aux = product(sums.reshape(-1, rank), inverse_b)
    gram_a = jnp.sum(gather_from(product(aux.T, aux), "narrow"), axis=0)
    aux = aux.reshape(wide_size * slots, edge, rank)
    target = (
        jnp.arange(own_rows, dtype=jnp.int32) + wide_at * own_rows
    )
    grain = min(own_rows, edge)
    aux_grains = aux.reshape(-1, grain, rank)
    grain_ids = (
        column_tags[:, 0, None] * (edge // grain)
        + jnp.arange(edge // grain, dtype=jnp.int32)[None, :]
    ).reshape(-1)
    wanted_ids = wide_at * (own_rows // grain) + jnp.arange(own_rows // grain, dtype=jnp.int32)
    pick = (wanted_ids[:, None] == grain_ids[None, :]).astype(jnp.float32)
    aux_owned = jnp.einsum("og,ger->oer", pick, aux_grains, precision=precise_level)
    aux_owned = aux_owned.reshape(own_rows, rank)

    orbital_terms = []
    for slot in range(slots):
        mine = jnp.take(first, wide_at * slots + slot)
        aux_rows = jnp.take(aux, mine, axis=0)
        spread = lax.dot_general(
            blocks[0, 0, slot],
            aux_rows,
            (((0,), (0,)), ((), ())),
            precision=precise_level,
            preferred_element_type=jnp.float32,
        ).reshape(edge, edge, rank)
        weight = live[slot].astype(jnp.float32)
        orbital_terms.append(jnp.sum(spread * rows[slot, 1][None], axis=1) * weight)
        orbital_terms.append(jnp.sum(spread * rows[slot, 0][:, None, :], axis=0) * weight)
    by_slice = jnp.stack(orbital_terms).reshape(slots * 2, wide_size, slice_rows, rank)
    outgoing = jnp.transpose(jnp.take(by_slice, others, axis=1), (1, 0, 2, 3))
    arrived = exchange(outgoing, "wide").reshape(wide_size * slots * 2, slice_rows, rank)
    total_blocks = own_blocks * narrow_size
    onehot = (
        jnp.arange(total_blocks, dtype=jnp.int32)[:, None] == pair.reshape(-1)[None, :]
    ).astype(jnp.float32)
    dense = jnp.einsum("bt,ter->ber", onehot, arrived, precision=precise_level)
    dense = dense.reshape(narrow_size, own_blocks, slice_rows, rank)
    owned = jnp.sum(exchange(jnp.take(dense, columns, axis=0), "narrow"), axis=0)
    orbital_sum = jnp.take(gather_from(owned, "wide"), others, axis=0)
    orbital_sum = jnp.transpose(orbital_sum, (1, 0, 2, 3)).reshape(own_blocks * edge, rank)
    orbital_new = product(orbital_sum, inverse_of(2.0 * gram_a * gram_b))
    return (aux_owned[None], orbital_new)


def solution(mesh):
    return jax.shard_map(
        on_device,
        mesh=mesh,
        in_specs=(
            P("wide", "narrow", None, None, None),
            P("wide", "narrow", None, None),
            P("wide", "narrow"),
            P("narrow", None),
        ),
        out_specs=(P("narrow", "wide", None), P("narrow", None)),
        check_vma=False,
    )
```

profile of v0, /device:TPU:0, one launch (start us, length us, event | category | flops | bytes accessed | tf_op | source)
XLA Modules:
  0.0 147.9 jit_solution(14211379098285154280)
XLA Ops:
  1.4 0.8 constant_dynamic-update-slice_fusion.7
  2.1 2.9 %collective-permute-start = (s32[1,2,4]{2,1,0:T(2,128)S(1)}, s32[1,2,4]{2,1,0:T(2,128)S(1)}, u32[]{:S(2)}, u32[]{:S(2)}) collective-permute-start(s32[1,2,4]{2,1,0:T(2,128)S(1)} %get-tuple-element.45), channel_id=1, source_target_pairs={{0,8},{4,12},{8,0},{12,4},{16,24},{20,28},{24,16},{28,20},{1,9},{5... | collective-permute-start | bytes 104 | tf_op jit(solution)/shard_map/ppermute | solution.py:34
  5.1 1.5 %collective-permute-start.1 = (s32[1,2,4]{2,1,0:T(2,128)S(1)}, s32[1,2,4]{2,1,0:T(2,128)S(1)}, u32[]{:S(2)}, u32[]{:S(2)}) collective-permute-start(s32[1,2,4]{2,1,0:T(2,128)S(1)} %get-tuple-element.45), channel_id=1, source_target_pairs={{0,16},{4,20},{8,24},{12,28},{16,0},{20,4},{24,8},{28,12},{1,17},{... | collective-permute-start | bytes 104 | tf_op jit(solution)/shard_map/ppermute | solution.py:34
  6.6 2.1 %collective-permute-start.4 = (f32[1,16,8,128]{3,2,1,0:T(8,128)S(1)}, f32[1,16,8,128]{3,2,1,0:T(8,128)S(1)}, u32[]{:S(2)}, u32[]{:S(2)}) collective-permute-start(f32[1,16,8,128]{3,2,1,0:T(8,128)S(1)} %dynamic-slice_bitcast_fusion), channel_id=1, source_target_pairs={{0,1},{1,0},{2,3},{3,2},{4,5},{5,4},{6,7},{7,6},{8,9},{9,8},{10,11... | collective-permute-start | bytes 196616 | tf_op jit(solution)/shard_map/ppermute | solution.py:34
  8.7 2.6 %collective-permute-start.5 = (f32[1,16,8,128]{3,2,1,0:T(8,128)S(1)}, f32[1,16,8,128]{3,2,1,0:T(8,128)S(1)}, u32[]{:S(2)}, u32[]{:S(2)}) collective-permute-start(f32[1,16,8,128]{3,2,1,0:T(8,128)S(1)} %dynamic-slice_bitcast_fusion), channel_id=1, source_target_pairs={{0,2},{1,3},{2,0},{3,1},{4,6},{5,7},{6,4},{7,5},{8,10},{9,11},{10,... | collective-permute-start | bytes 196616 | tf_op jit(solution)/shard_map/ppermute | solution.py:34
  11.3 1.0 fusion.76
  15.5 0.9 collective-permute-start.15
  16.5 1.1 collective-permute-done.3
  17.7 3.5 %collective-permute-start.16 = (f32[1,128,128]{1,2,0:T(8,128)S(1)}, f32[1,128,128]{1,2,0:T(8,128)S(1)}, u32[]{:S(2)}, u32[]{:S(2)}) collective-permute-start(f32[1,128,128]{1,2,0:T(8,128)S(1)} %bitcast.258), channel_id=1, source_target_pairs={{0,2},{1,3},{2,0},{3,1},{4,6},{5,7},{6,4},{7,5},{8,10},{9,11},{10,... | collective-permute-start | bytes 196616 | tf_op jit(solution)/shard_map/ppermute | solution.py:34
  22.2 0.7 iota_reduce_fusion
  22.9 0.6 fusion.74
  24.9 0.6 reshape.423
  26.6 5.1 %collective-permute-done.17 = f32[1,128,128]{1,2,0:T(8,128)S(1)} collective-permute-done((f32[1,128,128]{1,2,0:T(8,128)S(1)}, f32[1,128,128]{1,2,0:T(8,128)S(1)}, u32[]{:S(2)}, u32[]{:S(2)}) %collective-permute-start.17) | collective-permute-done | bytes 65568 | tf_op jit(solution)/shard_map/ppermute | solution.py:34
  31.9 11.7 %cholesky.44 = f32[128,128]{1,0:T(8,128)S(1)} custom-call(f32[128,128]{1,0:T(8,128)S(1)} %fusion.33), custom_call_target="Cholesky" | custom-call | tf_op jit(solution)/shard_map/jit(cholesky)/cholesky | solution.py:17
  43.6 0.6 compare_reduce_fusion.1
  44.3 1.6 %collective-permute-start.8 = (f32[1,2,4,8,128]{4,3,2,1,0:T(8,128)S(1)}, f32[1,2,4,8,128]{4,3,2,1,0:T(8,128)S(1)}, u32[]{:S(2)}, u32[]{:S(2)}) collective-permute-start(f32[1,2,4,8,128]{4,3,2,1,0:T(8,128)S(1)} %get-tuple-element.61), channel_id=1, source_target_pairs={{0,8},{4,12},{8,0},{12,4},{16,24},{20,28},{24,16},{28,20},{1,9},{5... | collective-permute-start | bytes 98312 | tf_op jit(solution)/shard_map/ppermute | solution.py:34
  45.8 1.5 %collective-permute-start.9 = (f32[1,2,4,8,128]{4,3,2,1,0:T(8,128)S(1)}, f32[1,2,4,8,128]{4,3,2,1,0:T(8,128)S(1)}, u32[]{:S(2)}, u32[]{:S(2)}) collective-permute-start(f32[1,2,4,8,128]{4,3,2,1,0:T(8,128)S(1)} %get-tuple-element.60), channel_id=1, source_target_pairs={{0,16},{4,20},{8,24},{12,28},{16,0},{20,4},{24,8},{28,12},{1,17},{... | collective-permute-start | bytes 98312 | tf_op jit(solution)/shard_map/ppermute | solution.py:34
  47.8 0.7 fusion.19
  48.5 9.8 %custom-call.8 = f32[1,128,128]{1,2,0:T(8,128)S(1)} custom-call(f32[1,128,128]{2,1,0:T(8,128)S(1)} %fusion.19), custom_call_target="InvertDiagBlocksLowerTriangular" | custom-call | tf_op jit(solution)/shard_map/jit(_cho_solve)/triangular_solve | solution.py:18
  59.6 1.1 copy-done.1
  60.6 1.5 fusion.1
  62.1 1.5 fusion
  63.6 1.6 %collective-permute-start.11 = (f32[1,2,64,128]{3,2,1,0:T(8,128)S(1)}, f32[1,2,64,128]{3,2,1,0:T(8,128)S(1)}, u32[]{:S(2)}, u32[]{:S(2)}) collective-permute-start(f32[1,2,64,128]{3,2,1,0:T(8,128)S(1)} %maximum_bitcast_fusion.1), channel_id=1, source_target_pairs={{0,8},{4,12},{8,0},{12,4},{16,24},{20,28},{24,16},{28,20},{1,9},{5... | collective-permute-start | bytes 196616 | tf_op jit(solution)/shard_map/ppermute | solution.py:34
  65.2 1.5 %collective-permute-start.12 = (f32[1,2,64,128]{3,2,1,0:T(8,128)S(1)}, f32[1,2,64,128]{3,2,1,0:T(8,128)S(1)}, u32[]{:S(2)}, u32[]{:S(2)}) collective-permute-start(f32[1,2,64,128]{3,2,1,0:T(8,128)S(1)} %maximum_bitcast_fusion.1), channel_id=1, source_target_pairs={{0,16},{4,20},{8,24},{12,28},{16,0},{20,4},{24,8},{28,12},{1,17},{... | collective-permute-start | bytes 196616 | tf_op jit(solution)/shard_map/ppermute | solution.py:34
  68.0 1.5 collective-permute-done.12
  69.4 2.4 %collective-permute-done.13 = f32[1,2,64,128]{3,2,1,0:T(8,128)S(1)} collective-permute-done((f32[1,2,64,128]{3,2,1,0:T(8,128)S(1)}, f32[1,2,64,128]{3,2,1,0:T(8,128)S(1)}, u32[]{:S(2)}, u32[]{:S(2)}) %collective-permute-start.13) | collective-permute-done | bytes 65568 | tf_op jit(solution)/shard_map/ppermute | solution.py:34
  72.2 0.6 constant_dynamic-update-slice_fusion.11
  72.8 0.7 collective-permute-done.14
  73.5 0.6 slice_dynamic-update-slice_fusion.7
  74.1 0.6 constant_dynamic-update-slice_fusion.10
  74.8 0.6 slice_dynamic-update-slice_fusion.6
  75.4 0.6 constant_dynamic-update-slice_fusion.9
  76.0 0.6 slice_dynamic-update-slice_fusion.5
  76.7 0.6 constant_dynamic-update-slice_fusion.8
  77.3 0.6 slice_dynamic-update-slice_fusion.4
  77.9 1.6 %gather_fusion.3 = f32[8,2,64,128]{3,2,1,0:T(8,128)S(1)} fusion(f32[8,2,64,128]{3,2,1,0:T(8,128)} %slice_dynamic-update-slice_fusion.4, s32[1024]{0:T(1024)S(1)} %pad_clamp_fusion.2), kind=kCustom, calls=%fused_computation.3 | custom fusion | bytes 1048608 | tf_op jit(solution)/shard_map/jit(_take)/gather | solution.py:100
  79.6 0.7 fusion.12
  81.2 1.0 fusion.78
  82.3 0.8 collective-permute-start.30
  83.1 3.5 %collective-permute-start.31 = (f32[1,128,128]{1,2,0:T(8,128)S(1)}, f32[1,128,128]{1,2,0:T(8,128)}, u32[]{:S(2)}, u32[]{:S(2)}) collective-permute-start(f32[1,128,128]{1,2,0:T(8,128)S(1)} %bitcast.262), channel_id=1, source_target_pairs={{0,3},{1,2},{2,1},{3,0},{4,7},{5,6},{6,5},{7,4},{8,11},{9,10},{10,... | collective-permute-start | bytes 196616 | tf_op jit(solution)/shard_map/ppermute | solution.py:34
  86.6 3.2 %convolution_bitcast_fusion.1 = f32[4096,128]{0,1:T(8,128)} fusion(f32[1,1,2,64,4096]{4,3,2,1,0:T(8,128)S(1)} %copy-done.1, f32[16,64,128]{2,1,0:T(8,128)S(1)} %bitcast.242, s32[]{:T(128)S(6)} %select_n.216, pred[]{:T(512)S(6)} %and.109), kind=kOutput, calls=%fused_computation.8 | convolution fusion | flops 402661376 | bytes 3178501 | tf_op jit(solution)/shard_map/dot_general | solution.py:129
  89.8 1.9 %copy.93 = f32[4096,128]{1,0:T(8,128)S(1)} copy(f32[4096,128]{0,1:T(8,128)} %convolution_bitcast_fusion.1) | data formatting | bytes 4194304 | tf_op jit(solution)/shard_map/dot_general | solution.py:129
  92.3 1.0 copy-done.2
  93.3 3.2 %convolution_bitcast_fusion = f32[4096,128]{0,1:T(8,128)} fusion(f32[1,1,2,64,4096]{4,3,2,1,0:T(8,128)S(1)} %copy-done.2, f32[16,64,128]{2,1,0:T(8,128)S(1)} %bitcast.243, s32[]{:T(128)S(6)} %select_n.218, pred[]{:T(512)S(6)} %and.110), kind=kOutput, calls=%fused_computation.7 | convolution fusion | flops 402661376 | bytes 3178501 | tf_op jit(solution)/shard_map/dot_general | solution.py:129
  96.5 1.9 %copy.94 = f32[4096,128]{1,0:T(8,128)S(1)} copy(f32[4096,128]{0,1:T(8,128)} %convolution_bitcast_fusion) | data formatting | bytes 4194304 | tf_op jit(solution)/shard_map/dot_general | solution.py:129
  99.6 0.7 broadcast_select_fusion
  100.4 1.2 fusion.10
  101.7 0.8 copy.92
  102.4 0.9 fusion.29
  103.5 11.7 %cholesky.55 = f32[128,128]{1,0:T(8,128)S(1)} custom-call(f32[128,128]{1,0:T(8,128)S(1)} %fusion.27), custom_call_target="Cholesky" | custom-call | tf_op jit(solution)/shard_map/jit(cholesky)/cholesky | solution.py:17
  115.2 0.6 collective-permute-start.19
  116.3 2.4 %collective-permute-start.21 = (f32[1,2,4,8,128]{4,3,2,1,0:T(8,128)S(1)}, f32[1,2,4,8,128]{4,3,2,1,0:T(8,128)S(1)}, u32[]{:S(2)}, u32[]{:S(2)}) collective-permute-start(f32[1,2,4,8,128]{4,3,2,1,0:T(8,128)S(1)} %get-tuple-element.50), channel_id=1, source_target_pairs={{0,24},{4,28},{8,16},{12,20},{16,8},{20,12},{24,0},{28,4},{1,25},{... | collective-permute-start | bytes 98312 | tf_op jit(solution)/shard_map/ppermute | solution.py:34
  119.7 1.4 collective-permute-done.21
  122.4 0.7 collective-permute-start.23
  123.1 3.7 %collective-permute-start.24 = (f32[1,1,16,8,128]{4,2,3,1,0:T(8,128)S(1)}, f32[1,1,16,8,128]{4,2,3,1,0:T(8,128)S(1)}, u32[]{:S(2)}, u32[]{:S(2)}) collective-permute-start(f32[1,1,16,8,128]{4,2,3,1,0:T(8,128)S(1)} %slice_bitcast_fusion), channel_id=1, source_target_pairs={{0,3},{1,2},{2,1},{3,0},{4,7},{5,6},{6,5},{7,4},{8,11},{9,10},{10,... | collective-permute-start | bytes 196616 | tf_op jit(solution)/shard_map/ppermute | solution.py:34
  126.8 0.6 compare_reduce_fusion
  127.4 0.8 collective-permute-done.23
  128.3 1.6 %collective-permute-done.24 = f32[1,1,16,8,128]{4,2,3,1,0:T(8,128)S(1)} collective-permute-done((f32[1,1,16,8,128]{4,2,3,1,0:T(8,128)S(1)}, f32[1,1,16,8,128]{4,2,3,1,0:T(8,128)S(1)}, u32[]{:S(2)}, u32[]{:S(2)}) %collective-permute-start.24) | collective-permute-done | bytes 65568 | tf_op jit(solution)/shard_map/ppermute | solution.py:34
  129.8 1.6 %collective-permute-start.25 = (f32[1,16,8,128]{3,1,2,0:T(8,128)S(1)}, f32[1,16,8,128]{3,1,2,0:T(8,128)S(1)}, u32[]{:S(2)}, u32[]{:S(2)}) collective-permute-start(f32[1,16,8,128]{3,1,2,0:T(8,128)S(1)} %get-tuple-element.41), channel_id=1, source_target_pairs={{0,8},{4,12},{8,0},{12,4},{16,24},{20,28},{24,16},{28,20},{1,9},{5... | collective-permute-start | bytes 196616 | tf_op jit(solution)/shard_map/ppermute | solution.py:34
  131.4 1.5 %collective-permute-start.26 = (f32[1,16,8,128]{3,1,2,0:T(8,128)S(1)}, f32[1,16,8,128]{3,1,2,0:T(8,128)S(1)}, u32[]{:S(2)}, u32[]{:S(2)}) collective-permute-start(f32[1,16,8,128]{3,1,2,0:T(8,128)S(1)} %get-tuple-element.41), channel_id=1, source_target_pairs={{0,16},{4,20},{8,24},{12,28},{16,0},{20,4},{24,8},{28,12},{1,17},{... | collective-permute-start | bytes 196616 | tf_op jit(solution)/shard_map/ppermute | solution.py:34
  133.4 0.7 fusion.20
  134.1 9.8 %custom-call.9 = f32[1,128,128]{1,2,0:T(8,128)S(1)} custom-call(f32[1,128,128]{2,1,0:T(8,128)S(1)} %fusion.20), custom_call_target="InvertDiagBlocksLowerTriangular" | custom-call | tf_op jit(solution)/shard_map/jit(_cho_solve)/triangular_solve | solution.py:18
  144.5 1.0 collective-permute-done.28
  146.5 1.4 fusion.79
  (140 shorter events, 15.0 us)
Async XLA Ops:
  0.6 6.0 %copy-start = (f32[1024,128]{1,0:T(8,128)S(1)}, f32[1024,128]{1,0:T(8,128)}, u32[]{:S(2)}) copy-start(f32[1024,128]{1,0:T(8,128)} %param.12) | copy-start | bytes 1572868
  2.1 13.4 %collective-permute-start = (s32[1,2,4]{2,1,0:T(2,128)S(1)}, s32[1,2,4]{2,1,0:T(2,128)S(1)}, u32[]{:S(2)}, u32[]{:S(2)}) collective-permute-start(s32[1,2,4]{2,1,0:T(2,128)S(1)} %get-tuple-element.45), channel_id=1, source_target_pairs={{0,8},{4,12},{8,0},{12,4},{16,24},{20,28},{24,16},{28,20},{1,9},{5... | collective-permute-start | bytes 104 | tf_op jit(solution)/shard_map/ppermute | solution.py:34
  5.1 10.5 %collective-permute-start.1 = (s32[1,2,4]{2,1,0:T(2,128)S(1)}, s32[1,2,4]{2,1,0:T(2,128)S(1)}, u32[]{:S(2)}, u32[]{:S(2)}) collective-permute-start(s32[1,2,4]{2,1,0:T(2,128)S(1)} %get-tuple-element.45), channel_id=1, source_target_pairs={{0,16},{4,20},{8,24},{12,28},{16,0},{20,4},{24,8},{28,12},{1,17},{... | collective-permute-start | bytes 104 | tf_op jit(solution)/shard_map/ppermute | solution.py:34
  6.6 9.9 %collective-permute-start.2 = (s32[1,2,4]{2,1,0:T(2,128)S(1)}, s32[1,2,4]{2,1,0:T(2,128)S(1)}, u32[]{:S(2)}, u32[]{:S(2)}) collective-permute-start(s32[1,2,4]{2,1,0:T(2,128)S(1)} %get-tuple-element.45), channel_id=1, source_target_pairs={{0,24},{4,28},{8,16},{12,20},{16,8},{20,12},{24,0},{28,4},{1,25},{... | collective-permute-start | bytes 104 | tf_op jit(solution)/shard_map/ppermute | solution.py:34
  6.6 19.0 %collective-permute-start.4 = (f32[1,16,8,128]{3,2,1,0:T(8,128)S(1)}, f32[1,16,8,128]{3,2,1,0:T(8,128)S(1)}, u32[]{:S(2)}, u32[]{:S(2)}) collective-permute-start(f32[1,16,8,128]{3,2,1,0:T(8,128)S(1)} %dynamic-slice_bitcast_fusion), channel_id=1, source_target_pairs={{0,1},{1,0},{2,3},{3,2},{4,5},{5,4},{6,7},{7,6},{8,9},{9,8},{10,11... | collective-permute-start | bytes 196616 | tf_op jit(solution)/shard_map/ppermute | solution.py:34
  8.7 17.0 %collective-permute-start.5 = (f32[1,16,8,128]{3,2,1,0:T(8,128)S(1)}, f32[1,16,8,128]{3,2,1,0:T(8,128)S(1)}, u32[]{:S(2)}, u32[]{:S(2)}) collective-permute-start(f32[1,16,8,128]{3,2,1,0:T(8,128)S(1)} %dynamic-slice_bitcast_fusion), channel_id=1, source_target_pairs={{0,2},{1,3},{2,0},{3,1},{4,6},{5,7},{6,4},{7,5},{8,10},{9,11},{10,... | collective-permute-start | bytes 196616 | tf_op jit(solution)/shard_map/ppermute | solution.py:34
  11.3 50.8 %copy-start.3 = (pred[8]{0:T(512)(128)(4,1)}, pred[8]{0:T(512)(128)(4,1)S(1)}, u32[]{:S(2)}) copy-start(pred[8]{0:T(512)(128)(4,1)S(1)} %compare_and_fusion.2) | copy-start | bytes 28
  15.5 10.2 %collective-permute-start.6 = (f32[1,16,8,128]{3,2,1,0:T(8,128)S(1)}, f32[1,16,8,128]{3,2,1,0:T(8,128)S(1)}, u32[]{:S(2)}, u32[]{:S(2)}) collective-permute-start(f32[1,16,8,128]{3,2,1,0:T(8,128)S(1)} %dynamic-slice_bitcast_fusion), channel_id=1, source_target_pairs={{0,3},{1,2},{2,1},{3,0},{4,7},{5,6},{6,5},{7,4},{8,11},{9,10},{10,... | collective-permute-start | bytes 196616 | tf_op jit(solution)/shard_map/ppermute | solution.py:34
  15.5 11.0 %collective-permute-start.15 = (f32[1,128,128]{1,2,0:T(8,128)S(1)}, f32[1,128,128]{1,2,0:T(8,128)S(1)}, u32[]{:S(2)}, u32[]{:S(2)}) collective-permute-start(f32[1,128,128]{1,2,0:T(8,128)S(1)} %bitcast.257), channel_id=1, source_target_pairs={{0,1},{1,0},{2,3},{3,2},{4,5},{5,4},{6,7},{7,6},{8,9},{9,8},{10,11... | collective-permute-start | bytes 196616 | tf_op jit(solution)/shard_map/ppermute | solution.py:34
  16.4 1.2 collective-permute-start.3
  17.7 8.9 %collective-permute-start.16 = (f32[1,128,128]{1,2,0:T(8,128)S(1)}, f32[1,128,128]{1,2,0:T(8,128)S(1)}, u32[]{:S(2)}, u32[]{:S(2)}) collective-permute-start(f32[1,128,128]{1,2,0:T(8,128)S(1)} %bitcast.258), channel_id=1, source_target_pairs={{0,2},{1,3},{2,0},{3,1},{4,6},{5,7},{6,4},{7,5},{8,10},{9,11},{10,... | collective-permute-start | bytes 196616 | tf_op jit(solution)/shard_map/ppermute | solution.py:34
  25.6 6.1 %collective-permute-start.17 = (f32[1,128,128]{1,2,0:T(8,128)S(1)}, f32[1,128,128]{1,2,0:T(8,128)S(1)}, u32[]{:S(2)}, u32[]{:S(2)}) collective-permute-start(f32[1,128,128]{1,2,0:T(8,128)S(1)} %bitcast.259), channel_id=1, source_target_pairs={{0,3},{1,2},{2,1},{3,0},{4,7},{5,6},{6,5},{7,4},{8,11},{9,10},{10,... | collective-permute-start | bytes 196616 | tf_op jit(solution)/shard_map/ppermute | solution.py:34
  26.5 17.8 %collective-permute-start.7 = (f32[4,1,4,8,128]{4,3,2,0,1:T(8,128)S(1)}, f32[4,1,4,8,128]{4,3,2,0,1:T(8,128)S(1)}, u32[]{:S(2)}, u32[]{:S(2)}) collective-permute-start(f32[4,1,4,8,128]{4,3,2,0,1:T(8,128)S(1)} %get-tuple-element.63), channel_id=1, source_target_pairs={{0,4},{4,0},{8,12},{12,8},{16,20},{20,16},{24,28},{28,24},{1,5},{5... | collective-permute-start | bytes 196616 | tf_op jit(solution)/shard_map/ppermute | solution.py:34
  44.3 14.0 %collective-permute-start.8 = (f32[1,2,4,8,128]{4,3,2,1,0:T(8,128)S(1)}, f32[1,2,4,8,128]{4,3,2,1,0:T(8,128)S(1)}, u32[]{:S(2)}, u32[]{:S(2)}) collective-permute-start(f32[1,2,4,8,128]{4,3,2,1,0:T(8,128)S(1)} %get-tuple-element.61), channel_id=1, source_target_pairs={{0,8},{4,12},{8,0},{12,4},{16,24},{20,28},{24,16},{28,20},{1,9},{5... | collective-permute-start | bytes 98312 | tf_op jit(solution)/shard_map/ppermute | solution.py:34
  45.8 12.5 %collective-permute-start.9 = (f32[1,2,4,8,128]{4,3,2,1,0:T(8,128)S(1)}, f32[1,2,4,8,128]{4,3,2,1,0:T(8,128)S(1)}, u32[]{:S(2)}, u32[]{:S(2)}) collective-permute-start(f32[1,2,4,8,128]{4,3,2,1,0:T(8,128)S(1)} %get-tuple-element.60), channel_id=1, source_target_pairs={{0,16},{4,20},{8,24},{12,28},{16,0},{20,4},{24,8},{28,12},{1,17},{... | collective-permute-start | bytes 98312 | tf_op jit(solution)/shard_map/ppermute | solution.py:34
  47.4 11.0 %collective-permute-start.10 = (f32[1,2,4,8,128]{4,3,2,1,0:T(8,128)S(1)}, f32[1,2,4,8,128]{4,3,2,1,0:T(8,128)S(1)}, u32[]{:S(2)}, u32[]{:S(2)}) collective-permute-start(f32[1,2,4,8,128]{4,3,2,1,0:T(8,128)S(1)} %get-tuple-element.59), channel_id=1, source_target_pairs={{0,24},{4,28},{8,16},{12,20},{16,8},{20,12},{24,0},{28,4},{1,25},{... | collective-permute-start | bytes 98312 | tf_op jit(solution)/shard_map/ppermute | solution.py:34
  59.1 1.6 %copy-start.1 = (f32[1,1,2,64,4096]{4,3,2,1,0:T(8,128)S(1)}, f32[1,1,2,64,4096]{4,3,2,1,0:T(8,128)}, u32[]{:S(2)}) copy-start(f32[1,1,2,64,4096]{4,3,2,1,0:T(8,128)} %param.9) | copy-start | bytes 6291460
  63.6 4.4 %collective-permute-start.11 = (f32[1,2,64,128]{3,2,1,0:T(8,128)S(1)}, f32[1,2,64,128]{3,2,1,0:T(8,128)S(1)}, u32[]{:S(2)}, u32[]{:S(2)}) collective-permute-start(f32[1,2,64,128]{3,2,1,0:T(8,128)S(1)} %maximum_bitcast_fusion.1), channel_id=1, source_target_pairs={{0,8},{4,12},{8,0},{12,4},{16,24},{20,28},{24,16},{28,20},{1,9},{5... | collective-permute-start | bytes 196616 | tf_op jit(solution)/shard_map/ppermute | solution.py:34
  65.2 4.3 %collective-permute-start.12 = (f32[1,2,64,128]{3,2,1,0:T(8,128)S(1)}, f32[1,2,64,128]{3,2,1,0:T(8,128)S(1)}, u32[]{:S(2)}, u32[]{:S(2)}) collective-permute-start(f32[1,2,64,128]{3,2,1,0:T(8,128)S(1)} %maximum_bitcast_fusion.1), channel_id=1, source_target_pairs={{0,16},{4,20},{8,24},{12,28},{16,0},{20,4},{24,8},{28,12},{1,17},{... | collective-permute-start | bytes 196616 | tf_op jit(solution)/shard_map/ppermute | solution.py:34
  66.7 5.2 %collective-permute-start.13 = (f32[1,2,64,128]{3,2,1,0:T(8,128)S(1)}, f32[1,2,64,128]{3,2,1,0:T(8,128)S(1)}, u32[]{:S(2)}, u32[]{:S(2)}) collective-permute-start(f32[1,2,64,128]{3,2,1,0:T(8,128)S(1)} %maximum_bitcast_fusion.1), channel_id=1, source_target_pairs={{0,24},{4,28},{8,16},{12,20},{16,8},{20,12},{24,0},{28,4},{1,25},{... | collective-permute-start | bytes 196616 | tf_op jit(solution)/shard_map/ppermute | solution.py:34
  71.9 1.6 %collective-permute-start.14 = (f32[4,2,64,128]{3,2,1,0:T(8,128)S(1)}, f32[4,2,64,128]{3,2,1,0:T(8,128)S(1)}, u32[]{:S(2)}, u32[]{:S(2)}) collective-permute-start(f32[4,2,64,128]{3,2,1,0:T(8,128)S(1)} %pad_maximum_fusion.1), channel_id=1, source_target_pairs={{0,4},{4,0},{8,12},{12,8},{16,20},{20,16},{24,28},{28,24},{1,5},{5... | collective-permute-start | bytes 786440 | tf_op jit(solution)/shard_map/ppermute | solution.py:34
  82.2 20.3 %collective-permute-start.29 = (f32[1,128,128]{1,2,0:T(8,128)S(1)}, f32[1,128,128]{1,2,0:T(8,128)S(1)}, u32[]{:S(2)}, u32[]{:S(2)}) collective-permute-start(f32[1,128,128]{1,2,0:T(8,128)S(1)} %bitcast.260), channel_id=1, source_target_pairs={{0,1},{1,0},{2,3},{3,2},{4,5},{5,4},{6,7},{7,6},{8,9},{9,8},{10,11... | collective-permute-start | bytes 196616 | tf_op jit(solution)/shard_map/ppermute | solution.py:34
  82.3 20.2 %collective-permute-start.30 = (f32[1,128,128]{1,2,0:T(8,128)S(1)}, f32[1,128,128]{1,2,0:T(8,128)}, u32[]{:S(2)}, u32[]{:S(2)}) collective-permute-start(f32[1,128,128]{1,2,0:T(8,128)S(1)} %bitcast.261), channel_id=1, source_target_pairs={{0,2},{1,3},{2,0},{3,1},{4,6},{5,7},{6,4},{7,5},{8,10},{9,11},{10,... | collective-permute-start | bytes 196616 | tf_op jit(solution)/shard_map/ppermute | solution.py:34
  83.1 19.4 %collective-permute-start.31 = (f32[1,128,128]{1,2,0:T(8,128)S(1)}, f32[1,128,128]{1,2,0:T(8,128)}, u32[]{:S(2)}, u32[]{:S(2)}) collective-permute-start(f32[1,128,128]{1,2,0:T(8,128)S(1)} %bitcast.262), channel_id=1, source_target_pairs={{0,3},{1,2},{2,1},{3,0},{4,7},{5,6},{6,5},{7,4},{8,11},{9,10},{10,... | collective-permute-start | bytes 196616 | tf_op jit(solution)/shard_map/ppermute | solution.py:34
  91.7 1.6 %copy-start.2 = (f32[1,1,2,64,4096]{4,3,2,1,0:T(8,128)S(1)}, f32[1,1,2,64,4096]{4,3,2,1,0:T(8,128)}, u32[]{:S(2)}) copy-start(f32[1,1,2,64,4096]{4,3,2,1,0:T(8,128)} %param.9) | copy-start | bytes 6291460
  99.0 22.2 %copy-start.6 = (s32[32]{0:T(128)S(1)}, s32[32]{0:T(128)}, u32[]{:S(2)}) copy-start(s32[32]{0:T(128)} %reshape.423) | copy-start | bytes 388
  100.3 21.8 %copy-start.5 = (pred[4]{0:T(512)(128)(4,1)S(1)}, pred[4]{0:T(512)(128)(4,1)}, u32[]{:S(2)}) copy-start(pred[4]{0:T(512)(128)(4,1)} %compare_and_fusion.1) | copy-start | bytes 16
  100.4 14.8 %collective-permute-start.18 = (f32[4,1,4,8,128]{4,3,2,0,1:T(8,128)S(1)}, f32[4,1,4,8,128]{4,3,2,0,1:T(8,128)S(1)}, u32[]{:S(2)}, u32[]{:S(2)}) collective-permute-start(f32[4,1,4,8,128]{4,3,2,0,1:T(8,128)S(1)} %get-tuple-element.53), channel_id=1, source_target_pairs={{0,4},{4,0},{8,12},{12,8},{16,20},{20,16},{24,28},{28,24},{1,5},{5... | collective-permute-start | bytes 196616 | tf_op jit(solution)/shard_map/ppermute | solution.py:34
  115.2 4.0 %collective-permute-start.19 = (f32[1,2,4,8,128]{4,3,2,1,0:T(8,128)S(1)}, f32[1,2,4,8,128]{4,3,2,1,0:T(8,128)S(1)}, u32[]{:S(2)}, u32[]{:S(2)}) collective-permute-start(f32[1,2,4,8,128]{4,3,2,1,0:T(8,128)S(1)} %get-tuple-element.49), channel_id=1, source_target_pairs={{0,8},{4,12},{8,0},{12,4},{16,24},{20,28},{24,16},{28,20},{1,9},{5... | collective-permute-start | bytes 98312 | tf_op jit(solution)/shard_map/ppermute | solution.py:34
  115.8 3.9 %collective-permute-start.20 = (f32[1,2,4,8,128]{4,3,2,1,0:T(8,128)S(1)}, f32[1,2,4,8,128]{4,3,2,1,0:T(8,128)S(1)}, u32[]{:S(2)}, u32[]{:S(2)}) collective-permute-start(f32[1,2,4,8,128]{4,3,2,1,0:T(8,128)S(1)} %get-tuple-element.51), channel_id=1, source_target_pairs={{0,16},{4,20},{8,24},{12,28},{16,0},{20,4},{24,8},{28,12},{1,17},{... | collective-permute-start | bytes 98312 | tf_op jit(solution)/shard_map/ppermute | solution.py:34
  116.3 4.8 %collective-permute-start.21 = (f32[1,2,4,8,128]{4,3,2,1,0:T(8,128)S(1)}, f32[1,2,4,8,128]{4,3,2,1,0:T(8,128)S(1)}, u32[]{:S(2)}, u32[]{:S(2)}) collective-permute-start(f32[1,2,4,8,128]{4,3,2,1,0:T(8,128)S(1)} %get-tuple-element.50), channel_id=1, source_target_pairs={{0,24},{4,28},{8,16},{12,20},{16,8},{20,12},{24,0},{28,4},{1,25},{... | collective-permute-start | bytes 98312 | tf_op jit(solution)/shard_map/ppermute | solution.py:34
  122.2 24.0 %copy-start.4 = (pred[8]{0:T(512)(128)(4,1)S(1)}, pred[8]{0:T(512)(128)(4,1)}, u32[]{:S(2)}) copy-start(pred[8]{0:T(512)(128)(4,1)} %copy-done.3) | copy-start | bytes 28
  122.3 5.1 %collective-permute-start.22 = (f32[1,1,16,8,128]{4,2,3,1,0:T(8,128)S(1)}, f32[1,1,16,8,128]{4,2,3,1,0:T(8,128)S(1)}, u32[]{:S(2)}, u32[]{:S(2)}) collective-permute-start(f32[1,1,16,8,128]{4,2,3,1,0:T(8,128)S(1)} %get-tuple-element.46), channel_id=1, source_target_pairs={{0,1},{1,0},{2,3},{3,2},{4,5},{5,4},{6,7},{7,6},{8,9},{9,8},{10,11... | collective-permute-start | bytes 196616 | tf_op jit(solution)/shard_map/ppermute | solution.py:34
  122.4 5.9 %collective-permute-start.23 = (f32[1,1,16,8,128]{4,2,3,1,0:T(8,128)S(1)}, f32[1,1,16,8,128]{4,2,3,1,0:T(8,128)S(1)}, u32[]{:S(2)}, u32[]{:S(2)}) collective-permute-start(f32[1,1,16,8,128]{4,2,3,1,0:T(8,128)S(1)} %get-tuple-element.47), channel_id=1, source_target_pairs={{0,2},{1,3},{2,0},{3,1},{4,6},{5,7},{6,4},{7,5},{8,10},{9,11},{10,... | collective-permute-start | bytes 196616 | tf_op jit(solution)/shard_map/ppermute | solution.py:34
  123.1 6.7 %collective-permute-start.24 = (f32[1,1,16,8,128]{4,2,3,1,0:T(8,128)S(1)}, f32[1,1,16,8,128]{4,2,3,1,0:T(8,128)S(1)}, u32[]{:S(2)}, u32[]{:S(2)}) collective-permute-start(f32[1,1,16,8,128]{4,2,3,1,0:T(8,128)S(1)} %slice_bitcast_fusion), channel_id=1, source_target_pairs={{0,3},{1,2},{2,1},{3,0},{4,7},{5,6},{6,5},{7,4},{8,11},{9,10},{10,... | collective-permute-start | bytes 196616 | tf_op jit(solution)/shard_map/ppermute | solution.py:34
  129.8 14.0 %collective-permute-start.25 = (f32[1,16,8,128]{3,1,2,0:T(8,128)S(1)}, f32[1,16,8,128]{3,1,2,0:T(8,128)S(1)}, u32[]{:S(2)}, u32[]{:S(2)}) collective-permute-start(f32[1,16,8,128]{3,1,2,0:T(8,128)S(1)} %get-tuple-element.41), channel_id=1, source_target_pairs={{0,8},{4,12},{8,0},{12,4},{16,24},{20,28},{24,16},{28,20},{1,9},{5... | collective-permute-start | bytes 196616 | tf_op jit(solution)/shard_map/ppermute | solution.py:34
  131.4 12.5 %collective-permute-start.26 = (f32[1,16,8,128]{3,1,2,0:T(8,128)S(1)}, f32[1,16,8,128]{3,1,2,0:T(8,128)S(1)}, u32[]{:S(2)}, u32[]{:S(2)}) collective-permute-start(f32[1,16,8,128]{3,1,2,0:T(8,128)S(1)} %get-tuple-element.41), channel_id=1, source_target_pairs={{0,16},{4,20},{8,24},{12,28},{16,0},{20,4},{24,8},{28,12},{1,17},{... | collective-permute-start | bytes 196616 | tf_op jit(solution)/shard_map/ppermute | solution.py:34
  132.9 11.0 %collective-permute-start.27 = (f32[1,16,8,128]{3,1,2,0:T(8,128)S(1)}, f32[1,16,8,128]{3,1,2,0:T(8,128)S(1)}, u32[]{:S(2)}, u32[]{:S(2)}) collective-permute-start(f32[1,16,8,128]{3,1,2,0:T(8,128)S(1)} %get-tuple-element.41), channel_id=1, source_target_pairs={{0,24},{4,28},{8,16},{12,20},{16,8},{20,12},{24,0},{28,4},{1,25},{... | collective-permute-start | bytes 196616 | tf_op jit(solution)/shard_map/ppermute | solution.py:34
  143.9 1.6 %collective-permute-start.28 = (f32[4,16,8,128]{3,1,2,0:T(8,128)S(1)}, f32[4,16,8,128]{3,1,2,0:T(8,128)S(1)}, u32[]{:S(2)}, u32[]{:S(2)}) collective-permute-start(f32[4,16,8,128]{3,1,2,0:T(8,128)S(1)} %pad_maximum_fusion.2), channel_id=1, source_target_pairs={{0,4},{4,0},{8,12},{12,8},{16,20},{20,16},{24,28},{28,24},{1,5},{5... | collective-permute-start | bytes 786440 | tf_op jit(solution)/shard_map/ppermute | solution.py:34
where the time goes:
time: 148 us
  other arithmetic  53.1 us (36%)
  starting transfers between devices  37.1 us (25%)
  local copies, waits for them, and re-layouts  19.3 us (13%)
  waiting for transfers between devices  17.2 us (12%)
  matrix products  16.4 us (11%)
  between operations  4.76 us (3%)
    ppermute x32, starting transfers between devices, swap_with(): lax.ppermute(value, axis, [(index, index ^ mask) for index in range(size)])  37.1 us
    another operation x6, other arithmetic, inverse_of(): lower = jnp.linalg.cholesky(gram)  24.8 us
    another operation x4, other arithmetic, inverse_of(): jax.scipy.linalg.cho_solve((lower, True), jnp.eye(gram.shape[0], dtype=gr...  20.9 us
    ppermute x32, waiting for transfers between devices, swap_with(): lax.ppermute(value, axis, [(index, index ^ mask) for index in range(size)])  17.2 us
    dot_general x6, matrix products, product(): jnp.dot(left, right, precision=precise_level, preferred_element_type=jnp....  6.86 us
    dot_general x2, matrix products, on_device(): lax.dot_general(blocks[0, 0, slot], aux_rows, (((0,), (0,)), ((), ())), p...  6.34 us
    unnamed x35, local copies, waits for them, and re-layouts  6.01 us
    dot_general x2, local copies, waits for them, and re-layouts, on_device(): lax.dot_general(blocks[0, 0, slot], aux_rows, (((0,), (0,)), ((), ())), p...  3.81 us
  transfers between devices with their start and end apart: 32, of which 12 were waited for; matrix products, arithmetic and copies ran while one was open for 47% of the time, Pallas kernels for 0%

commit v1 on v0

v1 whole, which is shorter than its diff:
```python
import functools

import jax
import jax.numpy as jnp
from jax import lax
from jax.experimental import pallas as pl
from jax.experimental.pallas import tpu as pltpu
from jax.sharding import PartitionSpec as P

NP = 16384


precise_level = lax.Precision.HIGHEST
in_vmem = pl.BlockSpec(memory_space=pltpu.VMEM)
in_smem = pl.BlockSpec(memory_space=pltpu.SMEM)


def product(left, right):
    return jnp.dot(left, right, precision=precise_level, preferred_element_type=jnp.float32)


def kernel_call(body, outputs, operands, scalars=0, scratch=(), flops=0):
    moved = sum(int(item.size) * item.dtype.itemsize for item in operands[scalars:])
    moved += sum(int(item.size) * item.dtype.itemsize for item in outputs)
    return pl.pallas_call(
        body,
        out_shape=outputs,
        in_specs=[in_smem] * scalars + [in_vmem] * (len(operands) - scalars),
        out_specs=[in_vmem] * len(outputs),
        scratch_shapes=list(scratch),
        compiler_params=pltpu.CompilerParams(vmem_limit_bytes=48 * 1024 * 1024),
        cost_estimate=pl.CostEstimate(flops=flops, bytes_accessed=moved, transcendentals=0),
    )(*operands)


def shaped(*shape, dtype=jnp.float32):
    return jax.ShapeDtypeStruct(shape, dtype)


def digits_of(size):
    digits = []
    stride = 1
    while stride < size:
        left = size // stride
        radix = 2 if left.bit_length() % 2 == 0 else 4
        digits.append((stride, radix))
        stride *= radix
    return digits


def swap_with(value, axis, mask):
    size = lax.axis_size(axis)
    return lax.ppermute(value, axis, [(index, index ^ mask) for index in range(size)])


def gather_from(value, axis, skip=0):
    digits = digits_of(lax.axis_size(axis))
    held = {0: value}
    for stride, radix in reversed(digits[skip:]):
        fresh = {}
        for digit in range(1, radix):
            for key, item in held.items():
                fresh[key + digit * stride] = swap_with(item, axis, digit * stride)
        held.update(fresh)
    return [held[key] for key in sorted(held)]


def exchange(items, axis, skip=0):
    digits = digits_of(lax.axis_size(axis))
    unit = digits[skip][0] if skip < len(digits) else 1
    items = list(items)
    for stride, radix in digits[skip:]:
        step = stride // unit
        for digit in range(1, radix):
            at = [key for key in range(len(items)) if key // step % radix == digit]
            if len(at) == 1:
                items[at[0]] = swap_with(items[at[0]], axis, digit * stride)
            else:
                packed = swap_with(jnp.stack([items[key] for key in at]), axis, digit * stride)
                for place, key in enumerate(at):
                    items[key] = packed[place]
    return items


def inverse_of(grams, other, scale):
    size = grams[0].shape[0]
    step = 8
    count = size // step
    own = other is None
    operands = list(grams) + ([] if own else [other])
    outputs = [shaped(size, size)] + ([shaped(size, size)] if own else [])

    def body(*refs):
        parts = refs[: len(grams)]
        out_ref = refs[len(operands)]
        sub = lax.broadcasted_iota(jnp.int32, (step, size), 0)
        lane = lax.broadcasted_iota(jnp.int32, (step, size), 1)
        held = []
        for block in range(count):
            at = slice(step * block, step * block + step)
            total = parts[0][at, :]
            for part in parts[1:]:
                total = total + part[at, :]
            if own:
                refs[len(operands) + 1][at, :] = total
                held.append(total * total)
            else:
                held.append(scale * total * refs[len(grams)][at, :])

        def splat_lane(value, index):
            return jnp.broadcast_to(value[:, index : index + 1], (step, size))

        def splat_row(value, index):
            return jnp.broadcast_to(value[index : index + 1, :], (step, size))

        for block in range(count):
            inside = (lane >= step * block) & (lane < step * block + step)
            unit = (lane - step * block == sub).astype(jnp.float32)
            left = [[splat_lane(row, step * block + t) for t in range(step)] for row in held]
            pivots = list(left[block])
            panel = jnp.where(inside, unit, held[block])
            for p in range(step):
                here = sub == p
                inverse = 1.0 / splat_row(pivots[p], p)
                factor = jnp.where(here, -inverse, pivots[p] * inverse)
                for t in range(p + 1, step):
                    pivots[t] = jnp.where(here, 0.0, pivots[t]) - factor * splat_row(pivots[t], p)
                panel = jnp.where(here, 0.0, panel) - factor * splat_row(panel, p)
            rows = [splat_row(panel, t) for t in range(step)]
            fresh = []
            for index in range(count):
                if index == block:
                    fresh.append(panel)
                    continue
                pairs = [left[index][t] * rows[t] for t in range(step)]
                while len(pairs) > 1:
                    pairs = [pairs[t] + pairs[t + 1] for t in range(0, len(pairs), 2)]
                fresh.append(jnp.where(inside, 0.0, held[index]) - pairs[0])
            held = fresh
        for block in range(count):
            out_ref[step * block : step * block + step, :] = held[block]

    return kernel_call(body, outputs, operands, flops=4 * size**3)


def pick_pieces(tags, slices, narrow_at, own_blocks):
    narrow_size, low = len(slices), len(slices[0])
    _, rows, rank = slices[0][0].shape
    slots = tags[0].shape[0]

    def body(at_ref, *refs):
        tag_refs = refs[: len(tags)]
        slice_refs = refs[len(tags) : len(tags) + narrow_size * low]
        out_refs = refs[len(tags) + narrow_size * low :]
        for tag_ref, out_ref in zip(tag_refs, out_refs):
            for pair in range(slots * 2):
                block = tag_ref[pair // 2, 1 + pair % 2]
                owner = (block // own_blocks) ^ at_ref[0]
                local = block % own_blocks
                for j in range(low):
                    value = slice_refs[j][local]
                    for m in range(1, narrow_size):
                        value = jnp.where(owner == m, slice_refs[m * low + j][local], value)
                    out_ref[pair, j] = value

    return kernel_call(
        body,
        [shaped(slots * 2, low, rows, rank)] * len(tags),
        [narrow_at] + list(tags) + [item for group in slices for item in group],
        scalars=1 + len(tags),
    )


def lay_rows(wide_at, pieces, wide_size):
    pairs, low, rows, rank = pieces[0].shape

    def body(at_ref, *refs):
        out_ref = refs[-1]
        for d, piece_ref in enumerate(refs[:-1]):
            for j in range(low):
                place = at_ref[0] ^ (d * low + j)
                for pair in range(pairs):
                    out_ref[pair, place] = piece_ref[pair, j]

    return kernel_call(
        body, [shaped(pairs, wide_size, rows, rank)], [wide_at] + list(pieces), scalars=1
    )[0]


def split_blocks(blocks):
    slots, edge, pairs = blocks.shape
    chunk = min(pairs, 512)

    def body(in_ref, out_ref):
        value = in_ref[0]
        high = value.astype(jnp.bfloat16).astype(jnp.float32)
        rest = value - high
        middle = rest.astype(jnp.bfloat16).astype(jnp.float32)
        low = rest - middle
        stacked = jnp.concatenate([high, middle, low, high], axis=0)
        out_ref[0] = stacked.T.astype(jnp.bfloat16)

    return pl.pallas_call(
        body,
        out_shape=shaped(slots, pairs, 4 * edge, dtype=jnp.bfloat16),
        grid=(slots, pairs // chunk),
        in_specs=[pl.BlockSpec((1, edge, chunk), lambda s, c: (s, 0, c))],
        out_specs=pl.BlockSpec((1, chunk, 4 * edge), lambda s, c: (s, c, 0)),
        compiler_params=pltpu.CompilerParams(vmem_limit_bytes=48 * 1024 * 1024),
        cost_estimate=pl.CostEstimate(
            flops=0, bytes_accessed=slots * edge * pairs * 12, transcendentals=0
        ),
    )(blocks)


def split3(value):
    high = value.astype(jnp.bfloat16)
    rest = value - high.astype(jnp.float32)
    middle = rest.astype(jnp.bfloat16)
    low = (rest - middle.astype(jnp.float32)).astype(jnp.bfloat16)
    return high, middle, low


def second_mode(wide_at, tags, terms, inverse, spread_blocks, rows, wide_size, low):
    slots, edge, rank = terms[0].shape
    pairs = spread_blocks.shape[1]
    slice_rows = edge // wide_size
    chunk = 4

    def body(at_ref, tag_ref, *refs):
        term_refs = refs[: len(terms)]
        inverse_ref, spread_ref, rows_ref = refs[len(terms) : len(terms) + 3]
        out_refs = refs[len(terms) + 3 : len(terms) + 3 + low]
        held_ref = refs[-1]
        sums = []
        for slot in range(slots):
            total = None
            for m, term_ref in enumerate(term_refs):
                for other in range(slots):
                    same = (tag_ref[m, other, 0] == tag_ref[0, slot, 0]).astype(jnp.float32)
                    part = term_ref[other] * same
                    total = part if total is None else total + part
            sums.append(total)
        aux = product(jnp.concatenate(sums, axis=0), inverse_ref[...])
        for slot in range(slots):
            weight = tag_ref[0, slot, 3].astype(jnp.float32)
            high, middle, least = split3(aux[slot * edge : (slot + 1) * edge] * weight)
            none = jnp.zeros_like(high)
            stacked = jnp.concatenate(
                [
                    jnp.concatenate([high, high, high, none], axis=0),
                    jnp.concatenate([middle, middle, none, least], axis=0),
                ],
                axis=1,
            )
            rows_i, rows_j = rows_ref[2 * slot], rows_ref[2 * slot + 1]

            def step(index, total_j):
                at = pl.multiple_of(index * (chunk * edge), chunk * edge)
                spread = jnp.dot(
                    spread_ref[slot, pl.ds(at, chunk * edge), :],
                    stacked,
                    preferred_element_type=jnp.float32,
                )
                spread = spread[:, :rank] + spread[:, rank:]
                for inner in range(chunk):
                    part = spread[inner * edge : (inner + 1) * edge]
                    here = index * chunk + inner
                    held_ref[2 * slot, pl.ds(here, 1), :] = jnp.sum(
                        part * rows_j, axis=0, keepdims=True
                    )
                    total_j = total_j + part * rows_ref[2 * slot, pl.ds(here, 1), :]
                return total_j

            held_ref[2 * slot + 1] = lax.fori_loop(
                0, edge // chunk, step, jnp.zeros((edge, rank), jnp.float32), unroll=True
            )
        for place in range(wide_size):
            source = (at_ref[0] ^ place) * slice_rows
            for pair in range(2 * slots):
                out_refs[place % low][place // low, pair] = held_ref[
                    pair, pl.ds(pl.multiple_of(source, slice_rows), slice_rows), :
                ]

    return kernel_call(
        body,
        [shaped(wide_size // low, 2 * slots, slice_rows, rank)] * low,
        [wide_at, tags] + list(terms) + [inverse, spread_blocks, rows],
        scalars=2,
        scratch=[pltpu.VMEM((2 * slots, edge, rank), jnp.float32)],
        flops=slots * 2 * pairs * 4 * edge * 2 * rank,
    )


def column_rows(wide_at, tags, first, terms, inverse, own_rows):
    slots, edge, rank = terms[0].shape
    count = slots * len(terms)
    grain = min(own_rows, edge)

    def body(at_ref, tag_ref, first_ref, *refs):
        term_refs = refs[: len(terms)]
        inverse_ref, gram_ref, out_ref, held_ref = refs[len(terms) :]
        held_ref[...] = jnp.zeros_like(held_ref)
        for index in range(count):
            to = first_ref[index]
            held_ref[to] += term_refs[index // slots][index % slots]
        aux = product(held_ref[...].reshape(count * edge, rank), inverse_ref[...])
        held_ref[...] = aux.reshape(count, edge, rank)
        gram_ref[...] = lax.dot_general(
            aux,
            aux,
            (((0,), (0,)), ((), ())),
            precision=precise_level,
            preferred_element_type=jnp.float32,
        )
        out_ref[...] = jnp.zeros_like(out_ref)
        per_block = edge // grain
        per_device = own_rows // grain
        for index in range(count):
            for part in range(per_block):
                grain_at = tag_ref[index // slots, index % slots, 0] * per_block + part

                @pl.when((first_ref[index] == index) & (grain_at // per_device == at_ref[0]))
                def _():
                    out_ref[grain_at % per_device] = held_ref[
                        index, part * grain : (part + 1) * grain, :
                    ]

    gram, owned = kernel_call(
        body,
        [shaped(rank, rank), shaped(own_rows // grain, grain, rank)],
        [wide_at, tags, first] + list(terms) + [inverse],
        scalars=3,
        scratch=[pltpu.VMEM((count, edge, rank), jnp.float32)],
        flops=4 * count * edge * rank * rank,
    )
    return gram, owned.reshape(own_rows, rank)


def pack_pieces(groups):
    low = len(groups)
    partners = groups[0].shape[0]

    def body(*refs):
        for d in range(partners):
            for j in range(low):
                refs[low + d][j] = refs[j][d]

    return kernel_call(body, [shaped(low, *groups[0].shape[1:])] * partners, list(groups))


def add_pieces(narrow_at, tags, pieces, narrow_size, own_blocks):
    low, pairs, rows, rank = pieces[0].shape

    def body(at_ref, tag_ref, *refs):
        piece_refs = refs[: len(pieces)]
        out_refs = refs[len(pieces) : len(pieces) + narrow_size]
        held_ref = refs[-1]
        held_ref[...] = jnp.zeros_like(held_ref)
        for d, piece_ref in enumerate(piece_refs):
            for j in range(low):
                for pair in range(pairs):
                    block = tag_ref[d * low + j, pair // 2, 1 + pair % 2]
                    held_ref[block] += piece_ref[j, pair]
        for m, out_ref in enumerate(out_refs):
            owner = at_ref[0] ^ m
            out_ref[...] = held_ref[pl.ds(owner * own_blocks, own_blocks)]

    return kernel_call(
        body,
        [shaped(own_blocks, rows, rank)] * narrow_size,
        [narrow_at, tags] + list(pieces),
        scalars=2,
        scratch=[pltpu.VMEM((narrow_size * own_blocks, rows, rank), jnp.float32)],
    )


def solve_rows(parts, inverse):
    own_blocks, rows, rank = parts[0].shape

    def body(*refs):
        total = refs[0][...]
        for ref in refs[1 : len(parts)]:
            total = total + ref[...]
        solved = product(total.reshape(own_blocks * rows, rank), refs[len(parts)][...])
        refs[-1][...] = solved.reshape(own_blocks, rows, rank)

    return kernel_call(
        body,
        [shaped(own_blocks, rows, rank)],
        list(parts) + [inverse],
        flops=2 * own_blocks * rows * rank * rank,
    )[0]


def lay_result(wide_at, parts):
    own_blocks, rows, rank = parts[0].shape

    def body(at_ref, *refs):
        for m, ref in enumerate(refs[:-1]):
            place = at_ref[0] ^ m
            for block in range(own_blocks):
                refs[-1][block, place] = ref[block]

    return kernel_call(
        body,
        [shaped(own_blocks, len(parts), rows, rank)],
        [wide_at] + list(parts),
        scalars=1,
    )[0]


def on_device(blocks, block_coords, block_count, orbital_factor):
    slots, edge = blocks.shape[2:4]
    rank = orbital_factor.shape[1]
    wide_size = lax.axis_size("wide")
    narrow_size = lax.axis_size("narrow")
    low = digits_of(wide_size)[0][1]
    wide_index = lax.axis_index("wide")
    wide_at = wide_index.reshape(1)
    narrow_at = lax.axis_index("narrow").reshape(1)
    slice_rows = edge // wide_size
    own_blocks = orbital_factor.shape[0] // edge
    own_rows = NP // narrow_size // wide_size
    live = (jnp.arange(slots, dtype=jnp.int32) < block_count[0, 0]).astype(jnp.int32)
    tags = jnp.concatenate([block_coords[0, 0], live[:, None]], axis=1)

    by_slice = orbital_factor.reshape(own_blocks, wide_size, slice_rows, rank)
    own_slices = [
        lax.dynamic_index_in_dim(by_slice, wide_index ^ j, 1, keepdims=False) for j in range(low)
    ]
    slices = [[item] for item in gather_from(own_slices[0], "narrow")]
    slices[0] = own_slices
    for group in slices[1:]:
        group.extend(swap_with(group[0], "wide", j) for j in range(1, low))
    partner_tags = gather_from(tags, "wide", skip=1)
    wanted = pick_pieces(partner_tags, slices, narrow_at, own_blocks)
    rows = lay_rows(wide_at, exchange(wanted, "wide", skip=1), wide_size)
    rows = rows.reshape(slots * 2, edge, rank)
    near = jnp.stack(partner_tags)
    all_tags = jnp.stack([near] + [swap_with(near, "wide", j) for j in range(1, low)], axis=1)
    all_tags = all_tags.reshape(wide_size, slots, 4)

    grams = gather_from(product(orbital_factor.T, orbital_factor), "narrow")
    inverse_b, gram_b = inverse_of(grams, None, 1.0)

    spread_blocks = split_blocks(blocks[0, 0])
    terms = []
    for slot in range(slots):
        pairs = rows[2 * slot][:, None, :] * rows[2 * slot + 1][None, :, :]
        term = product(blocks[0, 0, slot], pairs.reshape(edge * edge, rank))
        terms.append(term * live[slot].astype(jnp.float32))
    column_terms = gather_from(jnp.stack(terms), "wide")

    groups = second_mode(
        wide_at, all_tags, column_terms, inverse_b, spread_blocks, rows, wide_size, low
    )

    blocks_at = all_tags[:, :, 0].reshape(-1)
    first = jnp.argmax(blocks_at[:, None] == blocks_at[None, :], axis=1).astype(jnp.int32)
    gram_part, aux_owned = column_rows(
        wide_at, all_tags, first, column_terms, inverse_b, own_rows
    )
    inverse_a, = inverse_of(gather_from(gram_part, "narrow"), gram_b, 2.0)

    groups = [groups[0]] + [swap_with(groups[j], "wide", j) for j in range(1, low)]
    pieces = exchange(pack_pieces(groups), "wide", skip=1)
    sums = add_pieces(narrow_at, all_tags, pieces, narrow_size, own_blocks)
    solved = solve_rows(exchange(sums, "narrow"), inverse_a)
    orbital_new = lay_result(wide_at, gather_from(solved, "wide"))
    return (aux_owned[None], orbital_new.reshape(own_blocks * edge, rank))


def solution(mesh):
    return jax.shard_map(
        on_device,
        mesh=mesh,
        in_specs=(
            P("wide", "narrow", None, None, None),
            P("wide", "narrow", None, None),
            P("wide", "narrow"),
            P("narrow", None),
        ),
        out_specs=(P("narrow", "wide", None), P("narrow", None)),
        check_vma=False,
    )
```

time: 148 us -> 96.7 us (0.65)
  other arithmetic: 53.1 us -> 2.17 us
  Pallas kernels: 0 us -> 28.7 us
  local copies, waits for them, and re-layouts: 19.3 us -> 6.49 us
  matrix products: 16.4 us -> 5.31 us
  waiting for transfers between devices: 17.2 us -> 9.81 us
  starting transfers between devices: 37.1 us -> 41.1 us
  between operations: 4.76 us -> 2.81 us
    another operation x21 -> x6, other arithmetic: 46.5 us -> 0.81 us  [the longest x1 0.71 us: on_device(): jnp.argmax(blocks_at[:, None] == blocks_at[None, :], axis=1)]
    pallas_call x0 -> x11, Pallas kernels: none -> 28.7 us  [the longest x10 21.7 us: kernel_call(): pl.pallas_call(body, out_shape=outputs, in_specs=[in_smem] * scalars + [i...]
    dot_general x5 -> x0, matrix products: 8.58 us -> none  [the longest x2 6.34 us: on_device(): lax.dot_general(blocks[0, 0, slot], aux_rows, (((0,), (0,)), ((), ())), p...]
    ppermute x32 -> x40, waiting for transfers between devices: 17.2 us -> 9.81 us  [swap_with(): lax.ppermute(value, axis, [(index, index ^ mask) for index in range(size)])]
    gather x7 -> x0, local copies, waits for them, and re-layouts: 5.05 us -> none  [the longest x1 1.62 us: on_device(): jnp.take(gather_from(jnp.stack(terms), 'wide'), others, axis=0)]
    dot_general x4 -> x0, local copies, waits for them, and re-layouts: 4.92 us -> none  [the longest x2 3.81 us: on_device(): lax.dot_general(blocks[0, 0, slot], aux_rows, (((0,), (0,)), ((), ())), p...]
    ppermute x32 -> x40, starting transfers between devices: 37.1 us -> 41.1 us  [swap_with(): lax.ppermute(value, axis, [(index, index ^ mask) for index in range(size)])]
    dot_general x6 -> x3, matrix products: 6.86 us -> 5.31 us  [product(): jnp.dot(left, right, precision=precise_level, preferred_element_type=jnp....]
  transfers between devices with their start and end apart: 32 -> 40, of which waited for: 12 -> 11; matrix products, arithmetic and copies ran while one was open for 47% -> 9% of each run, Pallas kernels for 0% -> 26%
where the time goes in v1:
time: 96.7 us; the launch traced here: 96.4 us
  starting transfers between devices  41.1 us (43%)
  Pallas kernels  28.7 us (30%)
  waiting for transfers between devices  9.81 us (10%)
  local copies, waits for them, and re-layouts  6.49 us (7%)
  matrix products  5.31 us (5%)
  between operations  2.81 us (3%)
  other arithmetic  2.17 us (2%)
    ppermute x40, starting transfers between devices, swap_with(): lax.ppermute(value, axis, [(index, index ^ mask) for index in range(size)])  41.1 us
    pallas_call x10, Pallas kernels, kernel_call(): pl.pallas_call(body, out_shape=outputs, in_specs=[in_smem] * scalars + [i...  21.7 us
    ppermute x40, waiting for transfers between devices, swap_with(): lax.ppermute(value, axis, [(index, index ^ mask) for index in range(size)])  9.81 us
    pallas_call x1, Pallas kernels, split_blocks(): pl.pallas_call(body, out_shape=shaped(slots, pairs, 4 * edge, dtype=jnp.b...  7.02 us
    dot_general x3, matrix products, product(): jnp.dot(left, right, precision=precise_level, preferred_element_type=jnp....  5.31 us
    unnamed x8, local copies, waits for them, and re-layouts  4.75 us
  transfers between devices with their start and end apart: 40, of which 11 were waited for; matrix products, arithmetic and copies ran while one was open for 9% of the time, Pallas kernels for 26%

profile of v1, /device:TPU:0, one launch (start us, length us, event | category | flops | bytes accessed | tf_op | source)
XLA Modules:
  0.0 96.4 jit_solution(12675529119429852979)
XLA Ops:
  1.3 0.8 pad_add_fusion.2.refs_0_
  2.0 3.9 %collective-permute-start.2 = (s32[2,4]{1,0:T(2,128)S(1)}, s32[2,4]{1,0:T(2,128)S(1)}, u32[]{:S(2)}, u32[]{:S(2)}) collective-permute-start(s32[2,4]{1,0:T(2,128)S(1)} %pad_add_fusion.2.refs_0_), channel_id=1, source_target_pairs={{0,24},{4,28},{8,16},{12,20},{16,8},{20,12},{24,0},{28,4},{1,25},{... | collective-permute-start | bytes 104 | tf_op jit(solution)/shard_map/ppermute | solution.py:53
  5.9 0.5 collective-permute-start.1
  6.4 0.9 dynamic-slice_bitcast_fusion
  7.3 3.7 %collective-permute-start.8 = (f32[16,8,128]{2,1,0:T(8,128)S(1)}, f32[16,8,128]{2,1,0:T(8,128)S(1)}, u32[]{:S(2)}, u32[]{:S(2)}) collective-permute-start(f32[16,8,128]{2,1,0:T(8,128)S(1)} %get-tuple-element.41.refs_4_), channel_id=1, source_target_pairs={{0,3},{1,2},{2,1},{3,0},{4,7},{5,6},{6,5},{7,4},{8,11},{9,10},{10,... | collective-permute-start | bytes 196616 | tf_op jit(solution)/shard_map/ppermute | solution.py:53
  11.0 0.8 collective-permute-start.4
  11.8 2.2 %fusion.7.refs_0_ = f32[128,128]{1,0:T(8,128)S(1)} fusion(f32[1024,128]{1,0:T(8,128)} %param.7), kind=kOutput, calls=%fused_computation.24 | convolution fusion | flops 201326592 | bytes 589824 | tf_op jit(solution)/shard_map/dot_general | solution.py:19
  14.0 0.6 fusion.6
  15.9 1.6 %copy-done.1 = f32[1,1,2,64,4096]{4,3,2,1,0:T(8,128)S(1)} copy-done((f32[1,1,2,64,4096]{4,3,2,1,0:T(8,128)S(1)}, f32[1,1,2,64,4096]{4,3,2,1,0:T(8,128)}, u32[]{:S(2)}) %copy-start.1) | copy-done | bytes 2097176
  17.5 7.0 %shard_map.63.refs_9_ = bf16[2,4096,256]{2,1,0:T(8,128)(2,1)} custom-call(f32[2,64,4096]{2,1,0:T(8,128)S(1)} %bitcast.61), custom_call_target="tpu_custom_call" | custom-call | bytes 6291456 | tf_op jit(solution)/shard_map/pallas_call | solution.py:203
  24.5 0.5 collective-permute-start.7
  25.1 0.1 collective-permute-start.5
  25.1 0.1 fusion.13
  25.2 0.4 collective-permute-start
  25.6 3.7 %collective-permute-start.22 = (f32[128,128]{1,0:T(8,128)S(1)}, f32[128,128]{1,0:T(8,128)S(1)}, u32[]{:S(2)}, u32[]{:S(2)}) collective-permute-start(f32[128,128]{1,0:T(8,128)S(1)} %fusion.7.refs_0_), channel_id=1, source_target_pairs={{0,3},{1,2},{2,1},{3,0},{4,7},{5,6},{6,5},{7,4},{8,11},{9,10},{10,... | collective-permute-start | bytes 196616 | tf_op jit(solution)/shard_map/ppermute | solution.py:53
  29.4 1.6 %collective-permute-start.21 = (f32[128,128]{1,0:T(8,128)S(1)}, f32[128,128]{1,0:T(8,128)S(1)}, u32[]{:S(2)}, u32[]{:S(2)}) collective-permute-start(f32[128,128]{1,0:T(8,128)S(1)} %fusion.7.refs_0_), channel_id=1, source_target_pairs={{0,2},{1,3},{2,0},{3,1},{4,6},{5,7},{6,4},{7,5},{8,10},{9,11},{10,... | collective-permute-start | bytes 196616 | tf_op jit(solution)/shard_map/ppermute | solution.py:53
  30.9 0.8 shard_map.59
  31.7 0.6 collective-permute-start.10
  32.3 1.5 %collective-permute-start.11 = (f32[4,2,8,128]{3,2,1,0:T(8,128)S(1)}, f32[4,2,8,128]{3,2,1,0:T(8,128)S(1)}, u32[]{:S(2)}, u32[]{:S(2)}) collective-permute-start(f32[4,2,8,128]{3,2,1,0:T(8,128)S(1)} %get-tuple-element.24), channel_id=1, source_target_pairs={{0,16},{4,20},{8,24},{12,28},{16,0},{20,4},{24,8},{28,12},{1,17},{... | collective-permute-start | bytes 98312 | tf_op jit(solution)/shard_map/ppermute | solution.py:53
  33.8 1.4 %collective-permute-start.12 = (f32[4,2,8,128]{3,2,1,0:T(8,128)S(1)}, f32[4,2,8,128]{3,2,1,0:T(8,128)S(1)}, u32[]{:S(2)}, u32[]{:S(2)}) collective-permute-start(f32[4,2,8,128]{3,2,1,0:T(8,128)S(1)} %get-tuple-element.25), channel_id=1, source_target_pairs={{0,24},{4,28},{8,16},{12,20},{16,8},{20,12},{24,0},{28,4},{1,25},{... | collective-permute-start | bytes 98312 | tf_op jit(solution)/shard_map/ppermute | solution.py:53
  35.3 0.5 collective-permute-done.10.refs_1_
  35.8 0.8 collective-permute-done.11.refs_2_
  36.6 2.1 %collective-permute-done.12.refs_3_ = f32[4,2,8,128]{3,2,1,0:T(8,128)S(1)} collective-permute-done((f32[4,2,8,128]{3,2,1,0:T(8,128)S(1)}, f32[4,2,8,128]{3,2,1,0:T(8,128)S(1)}, u32[]{:S(2)}, u32[]{:S(2)}) %collective-permute-start.12) | collective-permute-done | bytes 32800 | tf_op jit(solution)/shard_map/ppermute | solution.py:53
  38.7 0.6 broadcast_multiply_fusion
  39.3 1.0 %copy-done.2 = f32[1,1,2,64,4096]{4,3,2,1,0:T(8,128)S(1)} copy-done((f32[1,1,2,64,4096]{4,3,2,1,0:T(8,128)S(1)}, f32[1,1,2,64,4096]{4,3,2,1,0:T(8,128)}, u32[]{:S(2)}) %copy-start.2) | copy-done | bytes 2097176
  40.3 1.5 %fusion = f32[1,64,128]{2,1,0:T(8,128)S(1)} fusion(f32[4096,128]{1,0:T(8,128)S(1)} %bitcast.70, f32[1,1,2,64,4096]{4,3,2,1,0:T(8,128)S(1)} %copy-done.2, f32[]{:T(128)} %bitcast.25), kind=kOutput, calls=%fused_computation.1 | convolution fusion | flops 402661376 | bytes 3178500 | tf_op jit(solution)/shard_map/dot_general | solution.py:19
  41.8 1.6 %fusion.1 = f32[1,64,128]{2,1,0:T(8,128)S(1)} fusion(f32[4096,128]{1,0:T(8,128)S(1)} %bitcast.69, f32[1,1,2,64,4096]{4,3,2,1,0:T(8,128)S(1)} %copy-done.2, f32[]{:T(128)} %bitcast.18), kind=kOutput, calls=%fused_computation.3 | convolution fusion | flops 402661376 | bytes 3178500 | tf_op jit(solution)/shard_map/dot_general | solution.py:19
  43.4 1.5 %collective-permute-start.18 = (f32[2,64,128]{2,1,0:T(8,128)S(1)}, f32[2,64,128]{2,1,0:T(8,128)S(1)}, u32[]{:S(2)}, u32[]{:S(2)}) collective-permute-start(f32[2,64,128]{2,1,0:T(8,128)S(1)} %pad_maximum_fusion.refs_0_), channel_id=1, source_target_pairs={{0,24},{4,28},{8,16},{12,20},{16,8},{20,12},{24,0},{28,4},{1,25},{... | collective-permute-start | bytes 196616 | tf_op jit(solution)/shard_map/ppermute | solution.py:53
  44.9 1.5 %collective-permute-start.16 = (f32[2,64,128]{2,1,0:T(8,128)S(1)}, f32[2,64,128]{2,1,0:T(8,128)S(1)}, u32[]{:S(2)}, u32[]{:S(2)}) collective-permute-start(f32[2,64,128]{2,1,0:T(8,128)S(1)} %pad_maximum_fusion.refs_0_), channel_id=1, source_target_pairs={{0,16},{4,20},{8,24},{12,28},{16,0},{20,4},{24,8},{28,12},{1,17},{... | collective-permute-start | bytes 196616 | tf_op jit(solution)/shard_map/ppermute | solution.py:53
  46.4 0.5 collective-permute-start.14
  47.0 2.1 %collective-permute-start.20 = (f32[128,128]{1,0:T(8,128)S(1)}, f32[128,128]{1,0:T(8,128)S(1)}, u32[]{:S(2)}, u32[]{:S(2)}) collective-permute-start(f32[128,128]{1,0:T(8,128)S(1)} %fusion.7.refs_0_), channel_id=1, source_target_pairs={{0,1},{1,0},{2,3},{3,2},{4,5},{5,4},{6,7},{7,6},{8,9},{9,8},{10,11... | collective-permute-start | bytes 196616 | tf_op jit(solution)/shard_map/ppermute | solution.py:53
  49.1 0.5 collective-permute-start.19
  49.6 1.0 %collective-permute-done.14.refs_2_ = f32[2,64,128]{2,1,0:T(8,128)S(1)} collective-permute-done((f32[2,64,128]{2,1,0:T(8,128)S(1)}, f32[2,64,128]{2,1,0:T(8,128)S(1)}, u32[]{:S(2)}, u32[]{:S(2)}) %collective-permute-start.14) | collective-permute-done | bytes 65568 | tf_op jit(solution)/shard_map/ppermute | solution.py:53
  50.7 0.1 copy.21
  50.9 0.1 eq.17
  50.9 0.4 collective-permute-done.20.refs_1_
  51.3 6.6 %shard_map.61 = (f32[128,128]{1,0:T(8,128)S(1)}, f32[128,128]{1,0:T(8,128)S(1)}) custom-call(f32[128,128]{1,0:T(8,128)S(1)} %fusion.7.refs_0_, f32[128,128]{1,0:T(8,128)S(1)} %collective-permute-done.20.refs_1_, f32[128,128]{1,0:T(8,128)S(1)} %collective-permute-done.21.refs_2_, f32[128,128]{1,0:T(8,128)S(1)} %collective-permute-done.22.refs_3_), custom_call_target="tpu_custom_call" | custom-call | flops 8388608 | bytes 393216 | tf_op jit(solution)/shard_map/pallas_call | solution.py:25
  57.9 2.2 %copy-done = bf16[2,4096,256]{2,1,0:T(8,128)(2,1)S(1)} copy-done((bf16[2,4096,256]{2,1,0:T(8,128)(2,1)S(1)}, bf16[2,4096,256]{2,1,0:T(8,128)(2,1)}, u32[]{:S(2)}) %copy-start) | copy-done | bytes 4194328
  60.1 2.3 %shard_map.64 = (f32[4,4,8,128]{3,2,1,0:T(8,128)S(1)}, f32[4,4,8,128]{3,2,1,0:T(8,128)S(1)}) custom-call(s32[1]{0:T(128)} %bitcast.at_ref, s32[8,2,4]{2,1,0:T(2,128)S(1)} %copy.24.tag_ref, f32[2,64,128]{2,1,0:T(8,128)S(1)} %pad_maximum_fusion.refs_0_, f32[2,64,128]{2,1,0:T(8,128)S(1)} %collective-permute-done.13.refs_1_, ...), custom_call_target="tpu_custom_call" | custom-call | flops 1073741824 | bytes 5046272 | tf_op jit(solution)/shard_map/pallas_call | solution.py:25
  62.5 0.2 collective-permute-start.23
  62.7 0.7 iota_reduce_fusion
  63.4 3.5 %shard_map.62 = (f32[128,128]{1,0:T(8,128)S(1)}, f32[8,64,128]{2,1,0:T(8,128)}) custom-call(s32[1]{0:T(128)} %bitcast.at_ref, s32[8,2,4]{2,1,0:T(2,128)S(1)} %copy.24.tag_ref, s32[16]{0:T(128)S(1)} %get-tuple-element.21.first_ref, f32[2,64,128]{2,1,0:T(8,128)S(1)} %pad_maximum_fusion.refs_0_, f32[2,64,128]{2,1,0:T(8,128)S(1)} %collective-permute-done.13.refs_1_, ...), custom_call_target="tpu_custom_call" | custom-call | flops 67108864 | bytes 917504 | tf_op jit(solution)/shard_map/pallas_call | solution.py:25
  66.9 1.8 %collective-permute-start.32 = (f32[128,128]{1,0:T(8,128)S(1)}, f32[128,128]{1,0:T(8,128)S(1)}, u32[]{:S(2)}, u32[]{:S(2)}) collective-permute-start(f32[128,128]{1,0:T(8,128)S(1)} %get-tuple-element.38.refs_0_), channel_id=1, source_target_pairs={{0,3},{1,2},{2,1},{3,0},{4,7},{5,6},{6,5},{7,4},{8,11},{9,10},{10,... | collective-permute-start | bytes 196616 | tf_op jit(solution)/shard_map/ppermute | solution.py:53
  68.7 1.3 %collective-permute-start.24 = (f32[2,4,8,128]{3,2,1,0:T(8,128)S(1)}, f32[2,4,8,128]{3,2,1,0:T(8,128)S(1)}, u32[]{:S(2)}, u32[]{:S(2)}) collective-permute-start(f32[2,4,8,128]{3,2,1,0:T(8,128)S(1)} %get-tuple-element.31), channel_id=1, source_target_pairs={{0,8},{4,12},{8,0},{12,4},{16,24},{20,28},{24,16},{28,20},{1,9},{5... | collective-permute-start | bytes 98312 | tf_op jit(solution)/shard_map/ppermute | solution.py:53
  70.0 0.5 collective-permute-start.25
  70.5 1.8 %collective-permute-start.26 = (f32[2,4,8,128]{3,2,1,0:T(8,128)S(1)}, f32[2,4,8,128]{3,2,1,0:T(8,128)S(1)}, u32[]{:S(2)}, u32[]{:S(2)}) collective-permute-start(f32[2,4,8,128]{3,2,1,0:T(8,128)S(1)} %get-tuple-element.33), channel_id=1, source_target_pairs={{0,24},{4,28},{8,16},{12,20},{16,8},{20,12},{24,0},{28,4},{1,25},{... | collective-permute-start | bytes 98312 | tf_op jit(solution)/shard_map/ppermute | solution.py:53
  72.3 1.7 %collective-permute-start.31 = (f32[128,128]{1,0:T(8,128)S(1)}, f32[128,128]{1,0:T(8,128)S(1)}, u32[]{:S(2)}, u32[]{:S(2)}) collective-permute-start(f32[128,128]{1,0:T(8,128)S(1)} %get-tuple-element.38.refs_0_), channel_id=1, source_target_pairs={{0,2},{1,3},{2,0},{3,1},{4,6},{5,7},{6,4},{7,5},{8,10},{9,11},{10,... | collective-permute-start | bytes 196616 | tf_op jit(solution)/shard_map/ppermute | solution.py:53
  74.0 0.9 collective-permute-start.30
  74.9 0.4 collective-permute-done.26.refs_3_
  75.3 0.8 shard_map.66
  76.1 0.8 collective-permute-start.27
  76.9 2.2 %collective-permute-start.28 = (f32[16,8,128]{2,1,0:T(8,128)S(1)}, f32[16,8,128]{2,1,0:T(8,128)S(1)}, u32[]{:S(2)}, u32[]{:S(2)}) collective-permute-start(f32[16,8,128]{2,1,0:T(8,128)S(1)} %get-tuple-element.36), channel_id=1, source_target_pairs={{0,2},{1,3},{2,0},{3,1},{4,6},{5,7},{6,4},{7,5},{8,10},{9,11},{10,... | collective-permute-start | bytes 196616 | tf_op jit(solution)/shard_map/ppermute | solution.py:53
  79.1 1.5 %collective-permute-start.29 = (f32[16,8,128]{2,1,0:T(8,128)S(1)}, f32[16,8,128]{2,1,0:T(8,128)S(1)}, u32[]{:S(2)}, u32[]{:S(2)}) collective-permute-start(f32[16,8,128]{2,1,0:T(8,128)S(1)} %get-tuple-element.37), channel_id=1, source_target_pairs={{0,3},{1,2},{2,1},{3,0},{4,7},{5,6},{6,5},{7,4},{8,11},{9,10},{10,... | collective-permute-start | bytes 196616 | tf_op jit(solution)/shard_map/ppermute | solution.py:53
  80.6 6.6 %shard_map.67.refs_4_ = f32[128,128]{1,0:T(8,128)S(1)} custom-call(f32[128,128]{1,0:T(8,128)S(1)} %get-tuple-element.38.refs_0_, f32[128,128]{1,0:T(8,128)S(1)} %collective-permute-done.30.refs_1_, f32[128,128]{1,0:T(8,128)S(1)} %collective-permute-done.31.refs_2_, f32[128,128]{1,0:T(8,128)S(1)} %collective-permute-done.32.refs_3_, ...), custom_call_target="tpu_custom_call" | custom-call | flops 8388608 | bytes 393216 | tf_op jit(solution)/shard_map/pallas_call | solution.py:25
  87.2 0.2 shard_map.68.refs_0_
  87.4 1.8 %collective-permute-start.38 = (f32[16,8,128]{2,1,0:T(8,128)S(1)}, f32[16,8,128]{2,1,0:T(8,128)S(1)}, u32[]{:S(2)}, u32[]{:S(2)}) collective-permute-start(f32[16,8,128]{2,1,0:T(8,128)S(1)} %shard_map.68.refs_0_), channel_id=1, source_target_pairs={{0,24},{4,28},{8,16},{12,20},{16,8},{20,12},{24,0},{28,4},{1,25},{... | collective-permute-start | bytes 196616 | tf_op jit(solution)/shard_map/ppermute | solution.py:53
  89.2 0.8 collective-permute-start.36
  90.0 0.9 collective-permute-start.34
  91.0 1.7 %collective-permute-done.38.refs_6_ = f32[16,8,128]{2,1,0:T(8,128)S(1)} collective-permute-done((f32[16,8,128]{2,1,0:T(8,128)S(1)}, f32[16,8,128]{2,1,0:T(8,128)S(1)}, u32[]{:S(2)}, u32[]{:S(2)}) %collective-permute-start.38) | collective-permute-done | bytes 65568 | tf_op jit(solution)/shard_map/ppermute | solution.py:53
  92.6 0.9 collective-permute-done.36.refs_4_
  93.5 0.8 collective-permute-done.34.refs_2_
  94.3 0.4 collective-permute-done.37.refs_5_
  94.8 0.8 collective-permute-done.35.refs_3_
  95.6 0.8 shard_map.69
  (55 shorter events, 0.3 us)
Async XLA Ops:
  2.0 23.2 %collective-permute-start.2 = (s32[2,4]{1,0:T(2,128)S(1)}, s32[2,4]{1,0:T(2,128)S(1)}, u32[]{:S(2)}, u32[]{:S(2)}) collective-permute-start(s32[2,4]{1,0:T(2,128)S(1)} %pad_add_fusion.2.refs_0_), channel_id=1, source_target_pairs={{0,24},{4,28},{8,16},{12,20},{16,8},{20,12},{24,0},{28,4},{1,25},{... | collective-permute-start | bytes 104 | tf_op jit(solution)/shard_map/ppermute | solution.py:53
  5.9 19.7 %collective-permute-start.1 = (s32[2,4]{1,0:T(2,128)S(1)}, s32[2,4]{1,0:T(2,128)S(1)}, u32[]{:S(2)}, u32[]{:S(2)}) collective-permute-start(s32[2,4]{1,0:T(2,128)S(1)} %pad_add_fusion.2.refs_0_), channel_id=1, source_target_pairs={{0,16},{4,20},{8,24},{12,28},{16,0},{20,4},{24,8},{28,12},{1,17},{... | collective-permute-start | bytes 104 | tf_op jit(solution)/shard_map/ppermute | solution.py:53
  7.3 17.2 %collective-permute-start.8 = (f32[16,8,128]{2,1,0:T(8,128)S(1)}, f32[16,8,128]{2,1,0:T(8,128)S(1)}, u32[]{:S(2)}, u32[]{:S(2)}) collective-permute-start(f32[16,8,128]{2,1,0:T(8,128)S(1)} %get-tuple-element.41.refs_4_), channel_id=1, source_target_pairs={{0,3},{1,2},{2,1},{3,0},{4,7},{5,6},{6,5},{7,4},{8,11},{9,10},{10,... | collective-permute-start | bytes 196616 | tf_op jit(solution)/shard_map/ppermute | solution.py:53
  11.0 13.5 %collective-permute-start.6 = (f32[16,8,128]{2,1,0:T(8,128)S(1)}, f32[16,8,128]{2,1,0:T(8,128)S(1)}, u32[]{:S(2)}, u32[]{:S(2)}) collective-permute-start(f32[16,8,128]{2,1,0:T(8,128)S(1)} %get-tuple-element.41.refs_4_), channel_id=1, source_target_pairs={{0,2},{1,3},{2,0},{3,1},{4,6},{5,7},{6,4},{7,5},{8,10},{9,11},{10,... | collective-permute-start | bytes 196616 | tf_op jit(solution)/shard_map/ppermute | solution.py:53
  11.0 14.0 %collective-permute-start.4 = (f32[16,8,128]{2,1,0:T(8,128)S(1)}, f32[16,8,128]{2,1,0:T(8,128)S(1)}, u32[]{:S(2)}, u32[]{:S(2)}) collective-permute-start(f32[16,8,128]{2,1,0:T(8,128)S(1)} %get-tuple-element.41.refs_4_), channel_id=1, source_target_pairs={{0,1},{1,0},{2,3},{3,2},{4,5},{5,4},{6,7},{7,6},{8,9},{9,8},{10,11... | collective-permute-start | bytes 196616 | tf_op jit(solution)/shard_map/ppermute | solution.py:53
  15.9 1.6 %copy-start.1 = (f32[1,1,2,64,4096]{4,3,2,1,0:T(8,128)S(1)}, f32[1,1,2,64,4096]{4,3,2,1,0:T(8,128)}, u32[]{:S(2)}) copy-start(f32[1,1,2,64,4096]{4,3,2,1,0:T(8,128)} %param.4) | copy-start | bytes 6291460
  17.5 7.6 %copy-start.3 = (s32[1,1,2,3]{3,2,1,0:T(2,128)S(1)}, s32[1,1,2,3]{3,2,1,0:T(2,128)}, u32[]{:S(2)}) copy-start(s32[1,1,2,3]{3,2,1,0:T(2,128)} %param.5) | copy-start | bytes 76
  24.5 6.4 %collective-permute-start.9 = (f32[16,8,128]{2,1,0:T(8,128)S(1)}, f32[16,8,128]{2,1,0:T(8,128)S(1)}, u32[]{:S(2)}, u32[]{:S(2)}) collective-permute-start(f32[16,8,128]{2,1,0:T(8,128)S(1)} %collective-permute-done.8.refs_10_), channel_id=1, source_target_pairs={{0,4},{4,0},{8,12},{12,8},{16,20},{20,16},{24,28},{28,24},{1,5},{5... | collective-permute-start | bytes 196616 | tf_op jit(solution)/shard_map/ppermute | solution.py:53
  24.5 6.4 %collective-permute-start.7 = (f32[16,8,128]{2,1,0:T(8,128)S(1)}, f32[16,8,128]{2,1,0:T(8,128)S(1)}, u32[]{:S(2)}, u32[]{:S(2)}) collective-permute-start(f32[16,8,128]{2,1,0:T(8,128)S(1)} %collective-permute-done.6.refs_8_), channel_id=1, source_target_pairs={{0,4},{4,0},{8,12},{12,8},{16,20},{20,16},{24,28},{28,24},{1,5},{5... | collective-permute-start | bytes 196616 | tf_op jit(solution)/shard_map/ppermute | solution.py:53
  25.1 5.9 %collective-permute-start.5 = (f32[16,8,128]{2,1,0:T(8,128)S(1)}, f32[16,8,128]{2,1,0:T(8,128)S(1)}, u32[]{:S(2)}, u32[]{:S(2)}) collective-permute-start(f32[16,8,128]{2,1,0:T(8,128)S(1)} %collective-permute-done.4.refs_6_), channel_id=1, source_target_pairs={{0,4},{4,0},{8,12},{12,8},{16,20},{20,16},{24,28},{28,24},{1,5},{5... | collective-permute-start | bytes 196616 | tf_op jit(solution)/shard_map/ppermute | solution.py:53
  25.2 4.2 %collective-permute-start = (s32[2,4]{1,0:T(2,128)S(1)}, s32[2,4]{1,0:T(2,128)S(1)}, u32[]{:S(2)}, u32[]{:S(2)}) collective-permute-start(s32[2,4]{1,0:T(2,128)S(1)} %pad_add_fusion.2.refs_0_), channel_id=1, source_target_pairs={{0,8},{4,12},{8,0},{12,4},{16,24},{20,28},{24,16},{28,20},{1,9},{5... | collective-permute-start | bytes 104 | tf_op jit(solution)/shard_map/ppermute | solution.py:53
  25.6 21.4 %collective-permute-start.22 = (f32[128,128]{1,0:T(8,128)S(1)}, f32[128,128]{1,0:T(8,128)S(1)}, u32[]{:S(2)}, u32[]{:S(2)}) collective-permute-start(f32[128,128]{1,0:T(8,128)S(1)} %fusion.7.refs_0_), channel_id=1, source_target_pairs={{0,3},{1,2},{2,1},{3,0},{4,7},{5,6},{6,5},{7,4},{8,11},{9,10},{10,... | collective-permute-start | bytes 196616 | tf_op jit(solution)/shard_map/ppermute | solution.py:53
  29.4 19.7 %collective-permute-start.21 = (f32[128,128]{1,0:T(8,128)S(1)}, f32[128,128]{1,0:T(8,128)S(1)}, u32[]{:S(2)}, u32[]{:S(2)}) collective-permute-start(f32[128,128]{1,0:T(8,128)S(1)} %fusion.7.refs_0_), channel_id=1, source_target_pairs={{0,2},{1,3},{2,0},{3,1},{4,6},{5,7},{6,4},{7,5},{8,10},{9,11},{10,... | collective-permute-start | bytes 196616 | tf_op jit(solution)/shard_map/ppermute | solution.py:53
  31.7 4.1 %collective-permute-start.10 = (f32[4,2,8,128]{3,2,1,0:T(8,128)S(1)}, f32[4,2,8,128]{3,2,1,0:T(8,128)S(1)}, u32[]{:S(2)}, u32[]{:S(2)}) collective-permute-start(f32[4,2,8,128]{3,2,1,0:T(8,128)S(1)} %get-tuple-element.23), channel_id=1, source_target_pairs={{0,8},{4,12},{8,0},{12,4},{16,24},{20,28},{24,16},{28,20},{1,9},{5... | collective-permute-start | bytes 98312 | tf_op jit(solution)/shard_map/ppermute | solution.py:53
  32.3 4.3 %collective-permute-start.11 = (f32[4,2,8,128]{3,2,1,0:T(8,128)S(1)}, f32[4,2,8,128]{3,2,1,0:T(8,128)S(1)}, u32[]{:S(2)}, u32[]{:S(2)}) collective-permute-start(f32[4,2,8,128]{3,2,1,0:T(8,128)S(1)} %get-tuple-element.24), channel_id=1, source_target_pairs={{0,16},{4,20},{8,24},{12,28},{16,0},{20,4},{24,8},{28,12},{1,17},{... | collective-permute-start | bytes 98312 | tf_op jit(solution)/shard_map/ppermute | solution.py:53
  33.8 4.8 %collective-permute-start.12 = (f32[4,2,8,128]{3,2,1,0:T(8,128)S(1)}, f32[4,2,8,128]{3,2,1,0:T(8,128)S(1)}, u32[]{:S(2)}, u32[]{:S(2)}) collective-permute-start(f32[4,2,8,128]{3,2,1,0:T(8,128)S(1)} %get-tuple-element.25), channel_id=1, source_target_pairs={{0,24},{4,28},{8,16},{12,20},{16,8},{20,12},{24,0},{28,4},{1,25},{... | collective-permute-start | bytes 98312 | tf_op jit(solution)/shard_map/ppermute | solution.py:53
  35.8 10.6 %collective-permute-start.3 = (s32[4,2,4]{2,1,0:T(2,128)S(1)}, s32[4,2,4]{2,1,0:T(2,128)S(1)}, u32[]{:S(2)}, u32[]{:S(2)}) collective-permute-start(s32[4,2,4]{2,1,0:T(2,128)S(1)} %pad_add_fusion.1), channel_id=1, source_target_pairs={{0,4},{4,0},{8,12},{12,8},{16,20},{20,16},{24,28},{28,24},{1,5},{5... | collective-permute-start | bytes 392 | tf_op jit(solution)/shard_map/ppermute | solution.py:53
  38.7 1.6 %copy-start.2 = (f32[1,1,2,64,4096]{4,3,2,1,0:T(8,128)S(1)}, f32[1,1,2,64,4096]{4,3,2,1,0:T(8,128)}, u32[]{:S(2)}) copy-start(f32[1,1,2,64,4096]{4,3,2,1,0:T(8,128)} %param.4) | copy-start | bytes 6291460
  43.4 5.7 %collective-permute-start.18 = (f32[2,64,128]{2,1,0:T(8,128)S(1)}, f32[2,64,128]{2,1,0:T(8,128)S(1)}, u32[]{:S(2)}, u32[]{:S(2)}) collective-permute-start(f32[2,64,128]{2,1,0:T(8,128)S(1)} %pad_maximum_fusion.refs_0_), channel_id=1, source_target_pairs={{0,24},{4,28},{8,16},{12,20},{16,8},{20,12},{24,0},{28,4},{1,25},{... | collective-permute-start | bytes 196616 | tf_op jit(solution)/shard_map/ppermute | solution.py:53
  44.9 4.7 %collective-permute-start.16 = (f32[2,64,128]{2,1,0:T(8,128)S(1)}, f32[2,64,128]{2,1,0:T(8,128)S(1)}, u32[]{:S(2)}, u32[]{:S(2)}) collective-permute-start(f32[2,64,128]{2,1,0:T(8,128)S(1)} %pad_maximum_fusion.refs_0_), channel_id=1, source_target_pairs={{0,16},{4,20},{8,24},{12,28},{16,0},{20,4},{24,8},{28,12},{1,17},{... | collective-permute-start | bytes 196616 | tf_op jit(solution)/shard_map/ppermute | solution.py:53
  46.4 4.3 %collective-permute-start.14 = (f32[2,64,128]{2,1,0:T(8,128)S(1)}, f32[2,64,128]{2,1,0:T(8,128)S(1)}, u32[]{:S(2)}, u32[]{:S(2)}) collective-permute-start(f32[2,64,128]{2,1,0:T(8,128)S(1)} %pad_maximum_fusion.refs_0_), channel_id=1, source_target_pairs={{0,8},{4,12},{8,0},{12,4},{16,24},{20,28},{24,16},{28,20},{1,9},{5... | collective-permute-start | bytes 196616 | tf_op jit(solution)/shard_map/ppermute | solution.py:53
  47.0 4.3 %collective-permute-start.20 = (f32[128,128]{1,0:T(8,128)S(1)}, f32[128,128]{1,0:T(8,128)S(1)}, u32[]{:S(2)}, u32[]{:S(2)}) collective-permute-start(f32[128,128]{1,0:T(8,128)S(1)} %fusion.7.refs_0_), channel_id=1, source_target_pairs={{0,1},{1,0},{2,3},{3,2},{4,5},{5,4},{6,7},{7,6},{8,9},{9,8},{10,11... | collective-permute-start | bytes 196616 | tf_op jit(solution)/shard_map/ppermute | solution.py:53
  49.1 8.8 %collective-permute-start.13 = (f32[2,64,128]{2,1,0:T(8,128)S(1)}, f32[2,64,128]{2,1,0:T(8,128)S(1)}, u32[]{:S(2)}, u32[]{:S(2)}) collective-permute-start(f32[2,64,128]{2,1,0:T(8,128)S(1)} %pad_maximum_fusion.refs_0_), channel_id=1, source_target_pairs={{0,4},{4,0},{8,12},{12,8},{16,20},{20,16},{24,28},{28,24},{1,5},{5... | collective-permute-start | bytes 196616 | tf_op jit(solution)/shard_map/ppermute | solution.py:53
  49.1 8.8 %collective-permute-start.19 = (f32[2,64,128]{2,1,0:T(8,128)S(1)}, f32[2,64,128]{2,1,0:T(8,128)S(1)}, u32[]{:S(2)}, u32[]{:S(2)}) collective-permute-start(f32[2,64,128]{2,1,0:T(8,128)S(1)} %collective-permute-done.18.refs_6_), channel_id=1, source_target_pairs={{0,4},{4,0},{8,12},{12,8},{16,20},{20,16},{24,28},{28,24},{1,5},{5... | collective-permute-start | bytes 196616 | tf_op jit(solution)/shard_map/ppermute | solution.py:53
  49.6 8.3 %collective-permute-start.17 = (f32[2,64,128]{2,1,0:T(8,128)S(1)}, f32[2,64,128]{2,1,0:T(8,128)S(1)}, u32[]{:S(2)}, u32[]{:S(2)}) collective-permute-start(f32[2,64,128]{2,1,0:T(8,128)S(1)} %collective-permute-done.16.refs_4_), channel_id=1, source_target_pairs={{0,4},{4,0},{8,12},{12,8},{16,20},{20,16},{24,28},{28,24},{1,5},{5... | collective-permute-start | bytes 196616 | tf_op jit(solution)/shard_map/ppermute | solution.py:53
  50.7 7.2 %collective-permute-start.15 = (f32[2,64,128]{2,1,0:T(8,128)S(1)}, f32[2,64,128]{2,1,0:T(8,128)S(1)}, u32[]{:S(2)}, u32[]{:S(2)}) collective-permute-start(f32[2,64,128]{2,1,0:T(8,128)S(1)} %collective-permute-done.14.refs_2_), channel_id=1, source_target_pairs={{0,4},{4,0},{8,12},{12,8},{16,20},{20,16},{24,28},{28,24},{1,5},{5... | collective-permute-start | bytes 196616 | tf_op jit(solution)/shard_map/ppermute | solution.py:53
  57.9 2.2 %copy-start = (bf16[2,4096,256]{2,1,0:T(8,128)(2,1)S(1)}, bf16[2,4096,256]{2,1,0:T(8,128)(2,1)}, u32[]{:S(2)}) copy-start(bf16[2,4096,256]{2,1,0:T(8,128)(2,1)} %shard_map.63.refs_9_) | copy-start | bytes 12582916
  62.5 6.2 %collective-permute-start.23 = (f32[4,4,8,128]{3,2,1,0:T(8,128)S(1)}, f32[4,4,8,128]{3,2,1,0:T(8,128)S(1)}, u32[]{:S(2)}, u32[]{:S(2)}) collective-permute-start(f32[4,4,8,128]{3,2,1,0:T(8,128)S(1)} %get-tuple-element.29), channel_id=1, source_target_pairs={{0,4},{4,0},{8,12},{12,8},{16,20},{20,16},{24,28},{28,24},{1,5},{5... | collective-permute-start | bytes 196616 | tf_op jit(solution)/shard_map/ppermute | solution.py:53
  66.9 12.2 %collective-permute-start.32 = (f32[128,128]{1,0:T(8,128)S(1)}, f32[128,128]{1,0:T(8,128)S(1)}, u32[]{:S(2)}, u32[]{:S(2)}) collective-permute-start(f32[128,128]{1,0:T(8,128)S(1)} %get-tuple-element.38.refs_0_), channel_id=1, source_target_pairs={{0,3},{1,2},{2,1},{3,0},{4,7},{5,6},{6,5},{7,4},{8,11},{9,10},{10,... | collective-permute-start | bytes 196616 | tf_op jit(solution)/shard_map/ppermute | solution.py:53
  68.7 5.3 %collective-permute-start.24 = (f32[2,4,8,128]{3,2,1,0:T(8,128)S(1)}, f32[2,4,8,128]{3,2,1,0:T(8,128)S(1)}, u32[]{:S(2)}, u32[]{:S(2)}) collective-permute-start(f32[2,4,8,128]{3,2,1,0:T(8,128)S(1)} %get-tuple-element.31), channel_id=1, source_target_pairs={{0,8},{4,12},{8,0},{12,4},{16,24},{20,28},{24,16},{28,20},{1,9},{5... | collective-permute-start | bytes 98312 | tf_op jit(solution)/shard_map/ppermute | solution.py:53
  70.0 4.9 %collective-permute-start.25 = (f32[2,4,8,128]{3,2,1,0:T(8,128)S(1)}, f32[2,4,8,128]{3,2,1,0:T(8,128)S(1)}, u32[]{:S(2)}, u32[]{:S(2)}) collective-permute-start(f32[2,4,8,128]{3,2,1,0:T(8,128)S(1)} %get-tuple-element.32), channel_id=1, source_target_pairs={{0,16},{4,20},{8,24},{12,28},{16,0},{20,4},{24,8},{28,12},{1,17},{... | collective-permute-start | bytes 98312 | tf_op jit(solution)/shard_map/ppermute | solution.py:53
  70.5 4.8 %collective-permute-start.26 = (f32[2,4,8,128]{3,2,1,0:T(8,128)S(1)}, f32[2,4,8,128]{3,2,1,0:T(8,128)S(1)}, u32[]{:S(2)}, u32[]{:S(2)}) collective-permute-start(f32[2,4,8,128]{3,2,1,0:T(8,128)S(1)} %get-tuple-element.33), channel_id=1, source_target_pairs={{0,24},{4,28},{8,16},{12,20},{16,8},{20,12},{24,0},{28,4},{1,25},{... | collective-permute-start | bytes 98312 | tf_op jit(solution)/shard_map/ppermute | solution.py:53
  72.3 8.3 %collective-permute-start.31 = (f32[128,128]{1,0:T(8,128)S(1)}, f32[128,128]{1,0:T(8,128)S(1)}, u32[]{:S(2)}, u32[]{:S(2)}) collective-permute-start(f32[128,128]{1,0:T(8,128)S(1)} %get-tuple-element.38.refs_0_), channel_id=1, source_target_pairs={{0,2},{1,3},{2,0},{3,1},{4,6},{5,7},{6,4},{7,5},{8,10},{9,11},{10,... | collective-permute-start | bytes 196616 | tf_op jit(solution)/shard_map/ppermute | solution.py:53
  74.0 6.6 %collective-permute-start.30 = (f32[128,128]{1,0:T(8,128)S(1)}, f32[128,128]{1,0:T(8,128)S(1)}, u32[]{:S(2)}, u32[]{:S(2)}) collective-permute-start(f32[128,128]{1,0:T(8,128)S(1)} %get-tuple-element.38.refs_0_), channel_id=1, source_target_pairs={{0,1},{1,0},{2,3},{3,2},{4,5},{5,4},{6,7},{7,6},{8,9},{9,8},{10,11... | collective-permute-start | bytes 196616 | tf_op jit(solution)/shard_map/ppermute | solution.py:53
  76.1 11.1 %collective-permute-start.27 = (f32[16,8,128]{2,1,0:T(8,128)S(1)}, f32[16,8,128]{2,1,0:T(8,128)S(1)}, u32[]{:S(2)}, u32[]{:S(2)}) collective-permute-start(f32[16,8,128]{2,1,0:T(8,128)S(1)} %get-tuple-element.35), channel_id=1, source_target_pairs={{0,1},{1,0},{2,3},{3,2},{4,5},{5,4},{6,7},{7,6},{8,9},{9,8},{10,11... | collective-permute-start | bytes 196616 | tf_op jit(solution)/shard_map/ppermute | solution.py:53
  76.9 10.3 %collective-permute-start.28 = (f32[16,8,128]{2,1,0:T(8,128)S(1)}, f32[16,8,128]{2,1,0:T(8,128)S(1)}, u32[]{:S(2)}, u32[]{:S(2)}) collective-permute-start(f32[16,8,128]{2,1,0:T(8,128)S(1)} %get-tuple-element.36), channel_id=1, source_target_pairs={{0,2},{1,3},{2,0},{3,1},{4,6},{5,7},{6,4},{7,5},{8,10},{9,11},{10,... | collective-permute-start | bytes 196616 | tf_op jit(solution)/shard_map/ppermute | solution.py:53
  79.1 8.1 %collective-permute-start.29 = (f32[16,8,128]{2,1,0:T(8,128)S(1)}, f32[16,8,128]{2,1,0:T(8,128)S(1)}, u32[]{:S(2)}, u32[]{:S(2)}) collective-permute-start(f32[16,8,128]{2,1,0:T(8,128)S(1)} %get-tuple-element.37), channel_id=1, source_target_pairs={{0,3},{1,2},{2,1},{3,0},{4,7},{5,6},{6,5},{7,4},{8,11},{9,10},{10,... | collective-permute-start | bytes 196616 | tf_op jit(solution)/shard_map/ppermute | solution.py:53
  87.4 5.2 %collective-permute-start.38 = (f32[16,8,128]{2,1,0:T(8,128)S(1)}, f32[16,8,128]{2,1,0:T(8,128)S(1)}, u32[]{:S(2)}, u32[]{:S(2)}) collective-permute-start(f32[16,8,128]{2,1,0:T(8,128)S(1)} %shard_map.68.refs_0_), channel_id=1, source_target_pairs={{0,24},{4,28},{8,16},{12,20},{16,8},{20,12},{24,0},{28,4},{1,25},{... | collective-permute-start | bytes 196616 | tf_op jit(solution)/shard_map/ppermute | solution.py:53
  89.2 4.3 %collective-permute-start.36 = (f32[16,8,128]{2,1,0:T(8,128)S(1)}, f32[16,8,128]{2,1,0:T(8,128)S(1)}, u32[]{:S(2)}, u32[]{:S(2)}) collective-permute-start(f32[16,8,128]{2,1,0:T(8,128)S(1)} %shard_map.68.refs_0_), channel_id=1, source_target_pairs={{0,16},{4,20},{8,24},{12,28},{16,0},{20,4},{24,8},{28,12},{1,17},{... | collective-permute-start | bytes 196616 | tf_op jit(solution)/shard_map/ppermute | solution.py:53
  90.0 4.3 %collective-permute-start.34 = (f32[16,8,128]{2,1,0:T(8,128)S(1)}, f32[16,8,128]{2,1,0:T(8,128)S(1)}, u32[]{:S(2)}, u32[]{:S(2)}) collective-permute-start(f32[16,8,128]{2,1,0:T(8,128)S(1)} %shard_map.68.refs_0_), channel_id=1, source_target_pairs={{0,8},{4,12},{8,0},{12,4},{16,24},{20,28},{24,16},{28,20},{1,9},{5... | collective-permute-start | bytes 196616 | tf_op jit(solution)/shard_map/ppermute | solution.py:53
  91.0 3.4 %collective-permute-start.33 = (f32[16,8,128]{2,1,0:T(8,128)S(1)}, f32[16,8,128]{2,1,0:T(8,128)S(1)}, u32[]{:S(2)}, u32[]{:S(2)}) collective-permute-start(f32[16,8,128]{2,1,0:T(8,128)S(1)} %shard_map.68.refs_0_), channel_id=1, source_target_pairs={{0,4},{4,0},{8,12},{12,8},{16,20},{20,16},{24,28},{28,24},{1,5},{5... | collective-permute-start | bytes 196616 | tf_op jit(solution)/shard_map/ppermute | solution.py:53
  92.6 1.7 %collective-permute-start.39 = (f32[16,8,128]{2,1,0:T(8,128)S(1)}, f32[16,8,128]{2,1,0:T(8,128)S(1)}, u32[]{:S(2)}, u32[]{:S(2)}) collective-permute-start(f32[16,8,128]{2,1,0:T(8,128)S(1)} %collective-permute-done.38.refs_6_), channel_id=1, source_target_pairs={{0,4},{4,0},{8,12},{12,8},{16,20},{20,16},{24,28},{28,24},{1,5},{5... | collective-permute-start | bytes 196616 | tf_op jit(solution)/shard_map/ppermute | solution.py:53
  93.5 1.3 %collective-permute-start.37 = (f32[16,8,128]{2,1,0:T(8,128)S(1)}, f32[16,8,128]{2,1,0:T(8,128)S(1)}, u32[]{:S(2)}, u32[]{:S(2)}) collective-permute-start(f32[16,8,128]{2,1,0:T(8,128)S(1)} %collective-permute-done.36.refs_4_), channel_id=1, source_target_pairs={{0,4},{4,0},{8,12},{12,8},{16,20},{20,16},{24,28},{28,24},{1,5},{5... | collective-permute-start | bytes 196616 | tf_op jit(solution)/shard_map/ppermute | solution.py:53
  94.3 1.3 %collective-permute-start.35 = (f32[16,8,128]{2,1,0:T(8,128)S(1)}, f32[16,8,128]{2,1,0:T(8,128)S(1)}, u32[]{:S(2)}, u32[]{:S(2)}) collective-permute-start(f32[16,8,128]{2,1,0:T(8,128)S(1)} %collective-permute-done.34.refs_2_), channel_id=1, source_target_pairs={{0,4},{4,0},{8,12},{12,8},{16,20},{20,16},{24,28},{28,24},{1,5},{5... | collective-permute-start | bytes 196616 | tf_op jit(solution)/shard_map/ppermute | solution.py:53

commit v2 on v1

v2 whole, which is shorter than its diff:
```python
import functools

import jax
import jax.numpy as jnp
from jax import lax
from jax.experimental import pallas as pl
from jax.experimental.pallas import tpu as pltpu
from jax.sharding import PartitionSpec as P

NP = 16384


precise_level = lax.Precision.HIGHEST
in_vmem = pl.BlockSpec(memory_space=pltpu.VMEM)
in_smem = pl.BlockSpec(memory_space=pltpu.SMEM)
live_at = 3
in_hbm = pl.BlockSpec(memory_space=pltpu.HBM)


def product(left, right):
    return jnp.dot(left, right, precision=precise_level, preferred_element_type=jnp.float32)


def kernel_call(body, outputs, operands, scalars=0, scratch=(), about_us=0.3, after=(), far=False):
    after = list(after)

    def whole(*refs):
        body(*refs[: len(operands)], *refs[len(operands) + len(after) :])

    return pl.pallas_call(
        whole,
        out_shape=outputs,
        in_specs=[in_smem] * scalars
        + [in_hbm if far else in_vmem] * (len(operands) - scalars)
        + [pl.BlockSpec(memory_space=pl.ANY)] * len(after),
        out_specs=[in_vmem] * len(outputs),
        scratch_shapes=list(scratch),
        compiler_params=pltpu.CompilerParams(vmem_limit_bytes=24 * 1024 * 1024),
        cost_estimate=pl.CostEstimate(
            flops=int(about_us * 1e6), bytes_accessed=0, transcendentals=0
        ),
    )(*operands, *after)


def shaped(*shape, dtype=jnp.float32):
    return jax.ShapeDtypeStruct(shape, dtype)


def add_tree(items):
    while len(items) > 1:
        items = [items[t] + items[t + 1] for t in range(0, len(items), 2)]
    return items[0]


def digits_of(size):
    digits = []
    stride = 1
    while stride < size:
        left = size // stride
        radix = 2 if left.bit_length() % 2 == 0 else 4
        digits.append((stride, radix))
        stride *= radix
    return digits


def swap_with(value, axis, mask):
    size = lax.axis_size(axis)
    return lax.ppermute(value, axis, [(index, index ^ mask) for index in range(size)])


def send_by_core(value, masks):
    wide_size, narrow_size = lax.axis_size("wide"), lax.axis_size("narrow")
    pairs = [
        (w * narrow_size + n, w * narrow_size + (n ^ masks[w % len(masks)]))
        for w in range(wide_size)
        for n in range(narrow_size)
    ]
    return lax.ppermute(value, ("wide", "narrow"), pairs)


def gather_from(value, axis, skip=0):
    digits = digits_of(lax.axis_size(axis))
    held = {0: value}
    for stride, radix in reversed(digits[skip:]):
        fresh = {}
        for digit in range(1, radix):
            for key, item in held.items():
                fresh[key + digit * stride] = swap_with(item, axis, digit * stride)
        held.update(fresh)
    return [held[key] for key in sorted(held)]


def exchange(items, axis, skip=0):
    digits = digits_of(lax.axis_size(axis))
    unit = digits[skip][0] if skip < len(digits) else 1
    items = list(items)
    for stride, radix in digits[skip:]:
        step = stride // unit
        for digit in range(1, radix):
            at = [key for key in range(len(items)) if key // step % radix == digit]
            if len(at) == 1:
                items[at[0]] = swap_with(items[at[0]], axis, digit * stride)
            else:
                packed = swap_with(jnp.stack([items[key] for key in at]), axis, digit * stride)
                for place, key in enumerate(at):
                    items[key] = packed[place]
    return items


def inverse_of(grams, other, scale, after=()):
    size = grams[0].shape[-1]
    step = 16
    count = size // step
    own = other is None
    operands = list(grams) + ([] if own else [other])
    outputs = [shaped(size, size)] + ([shaped(size, size)] if own else [])

    def body(*refs):
        parts = refs[: len(grams)]
        out_ref = refs[len(operands)]
        left_ref, right_ref = refs[-2:]
        sub = lax.broadcasted_iota(jnp.int32, (step, size), 0)
        lane = lax.broadcasted_iota(jnp.int32, (step, size), 1)
        held = []
        for block in range(count):
            at = slice(step * block, step * block + step)
            total = add_tree([part[pl.ds(part.shape[0] - size + step * block, step), :] for part in parts])
            if own:
                refs[len(operands) + 1][at, :] = total
                held.append(total * total)
            else:
                held.append(scale * total * refs[len(grams)][at, :])

        def splat_lane(value, index):
            return jnp.broadcast_to(value[:, index : index + 1], (step, size))

        def splat_row(value, index):
            return jnp.broadcast_to(value[index : index + 1, :], (step, size))

        for block in range(count):
            at = slice(step * block, step * block + step)
            inside = (lane >= step * block) & (lane < step * block + step)
            upto = lane < step * block + step
            unit = (lane - step * block == sub).astype(jnp.float32)
            pivots = [splat_lane(held[block], step * block + t) for t in range(step)]
            panel = jnp.where(inside, unit, held[block])
            left_ref[at, :] = jnp.where(upto, panel, 0.0)
            for p in range(0, step, 2):
                first, second = sub == p, sub == p + 1
                corner = splat_row(pivots[p], p)
                above, below = splat_row(pivots[p + 1], p), splat_row(pivots[p], p + 1)
                last = splat_row(pivots[p + 1], p + 1)
                scaled = 1.0 / (corner * last - above * below)
                i11, i12, i21, i22 = last * scaled, -above * scaled, -below * scaled, corner * scaled
                one = jnp.where(
                    first, -i11, jnp.where(second, -i21, pivots[p] * i11 + pivots[p + 1] * i21)
                )
                two = jnp.where(
                    first, -i12, jnp.where(second, -i22, pivots[p] * i12 + pivots[p + 1] * i22)
                )

                def clear(value):
                    kept = jnp.where(first | second, 0.0, value)
                    return kept - (one * splat_row(value, p) + two * splat_row(value, p + 1))

                for t in range(p + 2, step):
                    pivots[t] = clear(pivots[t])
                panel = clear(panel)
            right_ref[at, :] = jnp.where(upto, panel, 0.0)
            rows = [splat_row(panel, t) for t in range(step)]
            for index in range(block + 1, count):
                pairs = [splat_lane(held[index], step * block + t) * rows[t] for t in range(step)]
                held[index] = jnp.where(inside, 0.0, held[index]) - add_tree(pairs)
        out_ref[...] = lax.dot_general(
            left_ref[...],
            right_ref[...],
            (((0,), (0,)), ((), ())),
            precision=precise_level,
            preferred_element_type=jnp.float32,
        )

    return kernel_call(
        body,
        outputs,
        operands,
        scratch=[pltpu.VMEM((size, size), jnp.float32)] * 2,
        about_us=3.5,
        after=after,
    )


def own_part(chip_slice):
    own_blocks, low, rows, rank = chip_slice.shape

    def body(in_ref, out_ref):
        core = lax.axis_index("wide") % low
        for block in range(own_blocks):
            out_ref[block] = in_ref[block, core]

    return kernel_call(body, [shaped(own_blocks, rows, rank)], [chip_slice])[0]


def open_tags(coords, count, after):
    slots, axes = coords.shape
    rank = after[0].shape[-1]

    def body(coords_ref, count_ref, tag_ref, out_ref):
        slot_at = lax.broadcasted_iota(jnp.int32, (slots, 1), 0)
        tag_ref[...] = jnp.zeros_like(tag_ref)
        tag_ref[:slots, :axes] = coords_ref[...].astype(jnp.float32)
        tag_ref[:slots, axes : axes + 1] = (slot_at < count_ref[...]).astype(jnp.float32)
        out_ref[...] = coords_ref[...]

    return kernel_call(
        body,
        [shaped(8, rank), shaped(slots, axes, dtype=jnp.int32)],
        [coords, count],
        after=after,
    )


def stage(value, after):
    def body(in_ref, out_ref, sem):
        copy = pltpu.make_async_copy(in_ref, out_ref, sem)
        copy.start()
        copy.wait()

    return kernel_call(
        body,
        [shaped(*value.shape)],
        [value],
        scratch=[pltpu.SemaphoreType.DMA],
        after=after,
        far=True,
    )[0]


def pack_slices(pairs, single, after):
    own_blocks, low, rows, rank = pairs[0].shape if pairs else (single.shape[0], 0, 0, 0)
    _, rows, rank = single.shape
    total = own_blocks * (low * len(pairs) + 1)

    def body(*refs):
        out_ref = refs[-1]
        for index, ref in enumerate(refs[: len(pairs)]):
            at = index * own_blocks * low
            out_ref[at : at + own_blocks * low] = ref[...].reshape(own_blocks * low, rows, rank)
        out_ref[total - own_blocks :] = refs[len(pairs)][...]

    return kernel_call(
        body, [shaped(total, rows, rank)], list(pairs) + [single], after=after
    )[0]


def pick_pieces(coords, own, mine, theirs, narrow_size, after):
    own_blocks, low, rows, rank = own.shape
    partners, slots, _ = coords.shape
    piece_rows = slots * 2 * low * rows

    def body(coord_ref, own_ref, mine_ref, theirs_ref, *out_refs):
        narrow_at = lax.axis_index("narrow")
        core = lax.axis_index("wide") % low
        for d, out_ref in enumerate(out_refs):
            for pair in range(slots * 2):
                block = coord_ref[d, pair // 2, 1 + pair % 2]
                owner = (block // own_blocks) ^ narrow_at
                local = block % own_blocks
                before = jnp.maximum(owner, 1) - 1
                last = before == narrow_size - 2
                for j in range(low):
                    slice_at = core ^ j
                    holder = jnp.where(last, slice_at, before % low)
                    at = jnp.where(
                        last,
                        (narrow_size - 2) * own_blocks + local,
                        (before // low * own_blocks + local) * low + slice_at,
                    )
                    away = jnp.where(holder == core, mine_ref[at], theirs_ref[at])
                    to = (pair * low + j) * rows
                    out_ref[to : to + rows, :] = jnp.where(
                        owner == 0, own_ref[local, slice_at], away
                    )
        here, there = mine_ref[...].reshape(-1, rank), theirs_ref[...].reshape(-1, rank)
        rows_of = [jnp.where(core == j, here, there) for j in range(low)]
        gram = join_gram(
            gram_parts(jnp.concatenate([own_ref[...].reshape(-1, rank)] + rows_of, axis=0))
        )
        for out_ref in out_refs:
            out_ref[piece_rows:, :] = gram

    return kernel_call(
        body,
        [shaped(piece_rows + rank, rank)] * partners,
        [coords, own, mine, theirs],
        scalars=1,
        after=after,
    )


def first_mode(tags, pieces, blocks, wide_size, low, after):
    rank = pieces[0].shape[1]
    slots, edge, _ = blocks.shape
    pairs = 2 * slots
    slice_rows = edge // wide_size
    chunk = max(1, 256 // edge)

    def body(tag_ref, *refs):
        piece_refs = refs[: len(pieces)]
        blocks_ref, rows_ref, term_ref, held_ref = refs[len(pieces) :]
        term_ref[slots * edge :, :] = tag_ref[...]
        wide_at = lax.axis_index("wide")
        for d, piece_ref in enumerate(piece_refs):
            for j in range(low):
                place = wide_at ^ (d * low + j)
                for pair in range(pairs):
                    at = (pair * low + j) * slice_rows
                    held_ref[pair, place] = piece_ref[at : at + slice_rows, :]
        rows_ref[...] = held_ref[...].reshape(pairs, edge, rank)
        for slot in range(slots):
            rows_j = rows_ref[2 * slot + 1]

            def step(index, totals):
                wide_total, thin_total = totals
                products = jnp.concatenate(
                    [
                        rows_ref[2 * slot, pl.ds(index * chunk + inner, 1), :] * rows_j
                        for inner in range(chunk)
                    ],
                    axis=0,
                )
                high, middle, least = split3(products)
                at = pl.ds(pl.multiple_of(index * (chunk * edge), chunk * edge), chunk * edge)
                left = jnp.concatenate(split3(blocks_ref[slot, :, at]), axis=0)
                wide_total = wide_total + jnp.dot(
                    left,
                    jnp.concatenate([high, middle], axis=1),
                    preferred_element_type=jnp.float32,
                )
                thin_total = thin_total + jnp.dot(
                    left[:edge], least, preferred_element_type=jnp.float32
                )
                return wide_total, thin_total

            wide_total, thin_total = lax.fori_loop(
                0,
                edge // chunk,
                step,
                (
                    jnp.zeros((3 * edge, 2 * rank), jnp.float32),
                    jnp.zeros((edge, rank), jnp.float32),
                ),
                unroll=True,
            )
            total = wide_total[:, :rank] + wide_total[:, rank:]
            total = thin_total + total[2 * edge :] + total[edge : 2 * edge] + total[:edge]
            live = tag_ref[slot : slot + 1, live_at : live_at + 1]
            term_ref[slot * edge : (slot + 1) * edge, :] = total * live

    return kernel_call(
        body,
        [shaped(pairs, edge, rank), shaped(slots * edge + tags.shape[0], rank)],
        [tags] + list(pieces) + [blocks],
        scratch=[pltpu.VMEM((pairs, wide_size, slice_rows, rank), jnp.float32)],
        about_us=3.0,
        after=after,
    )


def turn_blocks(blocks, after):
    slots, edge, pairs = blocks.shape
    chunk = min(pairs, 512)

    def body(in_ref, turned_ref):
        for slot in range(slots):

            @pl.loop(0, pairs // chunk)
            def _(index):
                at = pl.ds(pl.multiple_of(index * chunk, chunk), chunk)
                high, middle, low = split3(in_ref[slot, :, at])
                turned_ref[slot, at, : 2 * edge] = jnp.concatenate([high, middle], axis=0).T
                turned_ref[slot, at, 2 * edge :] = jnp.concatenate([low, high], axis=0).T

    return kernel_call(
        body, [shaped(slots, pairs, 4 * edge, dtype=jnp.bfloat16)], [blocks], after=after
    )[0]


def dot32(left, right):
    return jnp.dot(left, right, preferred_element_type=jnp.float32)


def gram_parts(rows):
    rank = rows.shape[1]
    high, middle, least = split3(rows)
    both = jnp.concatenate([high, middle], axis=1)
    turned = both.T
    return dot32(turned, both), dot32(turned[:rank], least)


def join_gram(parts):
    square, rest = parts
    rank = rest.shape[0]
    rest = rest + square[:rank, rank:]
    return (square[rank:, rank:] + (rest + rest.T)) + square[:rank, :rank]


def split3(value):
    high = value.astype(jnp.bfloat16)
    rest = value - high.astype(jnp.float32)
    middle = rest.astype(jnp.bfloat16)
    low = (rest - middle.astype(jnp.float32)).astype(jnp.bfloat16)
    return high, middle, low


def second_mode(terms, inverse, spread_blocks, rows, wide_size):
    low = len(terms)
    pairs, edge, rank = rows.shape
    slots = pairs // 2
    slice_rows = edge // wide_size
    chunk = 4

    def tag_of(ref, d, slot, at):
        return ref[d, slots * edge + slot : slots * edge + slot + 1, at : at + 1]

    def body(*refs):
        term_refs = refs[: len(terms)]
        inverse_ref, spread_ref, rows_ref = refs[len(terms) : len(terms) + 3]
        out_refs = refs[len(terms) + 3 : len(terms) + 3 + low]
        held_ref = refs[-1]
        sums = []
        for slot in range(slots):
            total = None
            for m in range(wide_size):
                for other in range(slots):
                    there = tag_of(term_refs[m % low], m // low, other, 0)
                    same = (there == tag_of(term_refs[0], 0, slot, 0)).astype(jnp.float32)
                    here = slice(other * edge, (other + 1) * edge)
                    part = term_refs[m % low][m // low, here, :] * same
                    total = part if total is None else total + part
            sums.append(total)
        aux = product(jnp.concatenate(sums, axis=0), inverse_ref[...])
        for slot in range(slots):
            weight = tag_of(term_refs[0], 0, slot, live_at)
            high, middle, least = split3(aux[slot * edge : (slot + 1) * edge] * weight)
            none = jnp.zeros_like(high)
            stacked = jnp.concatenate(
                [
                    jnp.concatenate([high, high, high, none], axis=0),
                    jnp.concatenate([middle, middle, none, least], axis=0),
                ],
                axis=1,
            )
            rows_i, rows_j = rows_ref[2 * slot], rows_ref[2 * slot + 1]

            def step(index, total_j):
                at = pl.multiple_of(index * (chunk * edge), chunk * edge)
                spread = jnp.dot(
                    spread_ref[slot, pl.ds(at, chunk * edge), :],
                    stacked,
                    preferred_element_type=jnp.float32,
                )
                spread = spread[:, :rank] + spread[:, rank:]
                for inner in range(chunk):
                    part = spread[inner * edge : (inner + 1) * edge]
                    here = index * chunk + inner
                    held_ref[2 * slot, pl.ds(here, 1), :] = jnp.sum(
                        part * rows_j, axis=0, keepdims=True
                    )
                    total_j = total_j + part * rows_ref[2 * slot, pl.ds(here, 1), :]
                return total_j

            held_ref[2 * slot + 1] = lax.fori_loop(
                0, edge // chunk, step, jnp.zeros((edge, rank), jnp.float32), unroll=True
            )
        wide_at = lax.axis_index("wide")
        for place in range(wide_size):
            source = (wide_at ^ place) * slice_rows
            for pair in range(2 * slots):
                out_refs[place % low][place // low, pair] = held_ref[
                    pair, pl.ds(pl.multiple_of(source, slice_rows), slice_rows), :
                ]

    return kernel_call(
        body,
        [shaped(wide_size // low, 2 * slots, slice_rows, rank)] * low,
        list(terms) + [inverse, spread_blocks, rows],
        scratch=[pltpu.VMEM((2 * slots, edge, rank), jnp.float32)],
        about_us=2.5,
    )


def read_coords(terms, slots, edge, axes):
    low = len(terms)
    partners = terms[0].shape[0]

    def body(*refs):
        for j in range(low):
            for d in range(partners):
                tags = refs[j][d, slots * edge : slots * (edge + 1), :axes]
                refs[-1][d * low + j] = tags.astype(jnp.int32)

    return kernel_call(
        body, [shaped(partners * low, slots, axes, dtype=jnp.int32)], list(terms)
    )[0]


def column_gram(coords, terms, inverse, edge, after):
    low = len(terms)
    devices, slots, _ = coords.shape
    rank = inverse.shape[0]
    count = devices * slots

    def body(coord_ref, *refs):
        term_refs = refs[:low]
        inverse_ref, gram_ref, aux_ref = refs[low:]
        wide_at = lax.axis_index("wide")
        aux_ref[...] = jnp.zeros_like(aux_ref)
        blocks_at = [
            coord_ref[wide_at ^ (index // slots), index % slots, 0] for index in range(count)
        ]
        for index in range(count):
            to = jnp.int32(index)
            for earlier in reversed(range(index)):
                to = jnp.where(blocks_at[earlier] == blocks_at[index], earlier, to)
            here = slice(index % slots * edge, (index % slots + 1) * edge)
            place = wide_at ^ (index // slots)
            term = term_refs[0][place // low, here, :]
            for j in range(1, low):
                term = jnp.where(place % low == j, term_refs[j][place // low, here, :], term)
            aux_ref[to] += term
        high, middle, least = split3(inverse_ref[...])
        left_high, left_middle, left_least = split3(aux_ref[...].reshape(count * edge, rank))
        one = jnp.concatenate([high, middle], axis=1)
        aux = dot32(
            jnp.concatenate([left_high, left_middle], axis=1),
            jnp.concatenate([one, one], axis=0),
        )
        aux = (aux[:, :rank] + aux[:, rank:]) + dot32(
            jnp.concatenate([left_least, left_high], axis=1),
            jnp.concatenate([high, least], axis=0),
        )
        aux_ref[...] = aux.reshape(count, edge, rank)
        gram_ref[...] = join_gram(gram_parts(aux))

    return kernel_call(
        body,
        [shaped(rank, rank), shaped(count, edge, rank)],
        [coords] + list(terms) + [inverse],
        scalars=1,
        about_us=0.1,
        after=after,
    )


def own_aux(coords, aux, own_rows, after):
    devices, slots, _ = coords.shape
    count, edge, rank = aux.shape
    grain = min(own_rows, edge)
    per_block = edge // grain
    per_device = own_rows // grain

    def body(coord_ref, aux_ref, out_ref, done_ref):
        done_ref[...] = jnp.zeros_like(done_ref)
        out_ref[...] = jnp.zeros_like(out_ref)
        wide_at = lax.axis_index("wide")
        blocks_at = [
            coord_ref[wide_at ^ (index // slots), index % slots, 0] for index in range(count)
        ]
        for index in range(count):
            first = jnp.bool_(True)
            for earlier in range(index):
                first = first & (blocks_at[earlier] != blocks_at[index])
            for part in range(per_block):
                grain_at = blocks_at[index] * per_block + part

                @pl.when(first & (grain_at // per_device == wide_at))
                def _():
                    out_ref[grain_at % per_device] = aux_ref[
                        index, part * grain : (part + 1) * grain, :
                    ]

    owned, done = kernel_call(
        body,
        [shaped(per_device, grain, rank), shaped(8, rank)],
        [coords, aux],
        scalars=1,
        about_us=0.1,
        after=after,
    )
    return owned.reshape(own_rows, rank), done


def pack_pieces(groups):
    low = len(groups)
    partners = groups[0].shape[0]

    def body(*refs):
        for d in range(partners):
            for j in range(low):
                refs[low + d][j] = refs[j][d]

    return kernel_call(body, [shaped(low, *groups[0].shape[1:])] * partners, list(groups))


def pack_whole(items, after=(), rows=None):
    rows = rows or items[0].shape[0]
    kind = shaped(len(items), rows, *items[0].shape[1:], dtype=items[0].dtype)

    def body(*refs):
        for index, ref in enumerate(refs[:-1]):
            refs[-1][index] = ref[:rows]

    return kernel_call(body, [kind], list(items), after=after)[0]


def with_partners(value, low):
    return [value] + [swap_with(value, "wide", j) for j in range(1, low)]


def add_pieces(coords, pieces, narrow_size, own_blocks, after):
    low, pairs, rows, rank = pieces[0].shape
    part_rows = own_blocks * rows

    def body(coord_ref, *refs):
        narrow_at = lax.axis_index("narrow")
        piece_refs = refs[: len(pieces)]
        out_refs = refs[len(pieces) : len(pieces) + narrow_size]
        held_ref = refs[-1]
        held_ref[...] = jnp.zeros_like(held_ref)
        for d, piece_ref in enumerate(piece_refs):
            for j in range(low):
                for pair in range(pairs):
                    block = coord_ref[d * low + j, pair // 2, 1 + pair % 2]
                    held_ref[block] += piece_ref[j, pair]
        for m, out_ref in enumerate(out_refs):
            owner = narrow_at ^ m
            part = held_ref[pl.ds(owner * own_blocks, own_blocks)]
            out_ref[...] = part.reshape(part_rows, rank)

    return kernel_call(
        body,
        [shaped(part_rows, rank)] * narrow_size,
        [coords] + list(pieces),
        scalars=1,
        after=after,
        scratch=[pltpu.VMEM((narrow_size * own_blocks, rows, rank), jnp.float32)],
    )


def add_parts(parts, after=()):
    def body(*refs):
        total = refs[0][...]
        for ref in refs[1:-1]:
            total = total + ref[...]
        refs[-1][...] = total

    return kernel_call(body, [shaped(*parts[0].shape)], list(parts), after=after)[0]


def solve_rows(parts, inverse, own_blocks):
    low = len(parts)
    partners, part_rows, rank = parts[0].shape
    rows = part_rows // own_blocks

    def body(*refs):
        wide_at = lax.axis_index("wide")
        out_ref = refs[-1]
        for d in range(partners):
            for j in range(low):
                solved = product(refs[j][d], refs[low][...]).reshape(own_blocks, rows, rank)
                place = wide_at ^ (d * low + j)
                for block in range(own_blocks):
                    out_ref[block, place] = solved[block]

    return kernel_call(
        body,
        [shaped(own_blocks, partners * low, rows, rank)],
        list(parts) + [inverse],
        about_us=1.5,
    )[0]


def on_device(blocks, block_coords, block_count, orbital_factor):
    slots, edge = blocks.shape[2:4]
    rank = orbital_factor.shape[1]
    wide_size = lax.axis_size("wide")
    narrow_size = lax.axis_size("narrow")
    low = digits_of(wide_size)[0][1]
    slice_rows = edge // wide_size
    own_blocks = orbital_factor.shape[0] // edge
    own_rows = NP // narrow_size // wide_size

    by_slice = orbital_factor.reshape(own_blocks, wide_size // low, low, slice_rows, rank)
    chip_at = lax.axis_index("wide") // low
    chip_slice = lax.dynamic_index_in_dim(by_slice, chip_at, 1, keepdims=False)
    own_slice = own_part(chip_slice)
    pairs = [send_by_core(chip_slice, [m, m + 1]) for m in range(1, narrow_size - 1, low)]
    single = swap_with(own_slice, "narrow", narrow_size - 1)
    arrived = gather_from(block_coords[0, 0], "wide", skip=1)[1:]
    tags, coords = open_tags(block_coords[0, 0], block_count, [own_slice])
    blocks = stage(blocks[0, 0], [tags])
    coords = pack_whole([coords] + arrived, after=[blocks])
    mine = pack_slices(pairs, single, [coords])
    theirs = swap_with(mine, "wide", 1)
    wanted = pick_pieces(coords, chip_slice, mine, theirs, narrow_size, [])
    pieces = exchange(wanted, "wide", skip=1)

    turned = turn_blocks(blocks, wanted[:1])
    rows, terms = first_mode(tags, pieces, blocks, wide_size, low, [turned])
    inverse_b, gram_b = inverse_of(pieces, None, 1.0, after=[terms])
    terms = pack_whole(gather_from(terms, "wide", skip=1), after=[inverse_b])
    column_terms = with_partners(terms, low)
    all_coords = read_coords(column_terms, slots, edge, block_coords.shape[3])

    groups = second_mode(column_terms, inverse_b, turned, rows, wide_size)
    groups = [groups[0]] + [swap_with(groups[j], "wide", j) for j in range(1, low)]
    packed = pack_pieces(groups)
    pieces = exchange(packed, "wide", skip=1)

    gram, aux = column_gram(all_coords, column_terms, inverse_b, edge, packed[:1])

    sums = add_pieces(all_coords, pieces, narrow_size, own_blocks, [gram])
    parts = exchange(sums, "narrow")
    step = narrow_size // 2
    while step > 1:
        gram = add_parts([gram, swap_with(gram, "narrow", step)], sums[:1])
        step //= 2
    aux_owned, done = own_aux(all_coords, aux, own_rows, sums[:1])
    total = add_parts(parts, [gram, done])
    (inverse_a,) = inverse_of([gram, swap_with(gram, "narrow", step)], gram_b, 2.0, [total])
    totals = pack_whole(gather_from(total, "wide", skip=1), after=[inverse_a])
    orbital_new = solve_rows(with_partners(totals, low), inverse_a, own_blocks)
    return (aux_owned[None], orbital_new.reshape(own_blocks * edge, rank))


def solution(mesh):
    return jax.shard_map(
        on_device,
        mesh=mesh,
        in_specs=(
            P("wide", "narrow", None, None, None),
            P("wide", "narrow", None, None),
            P("wide", "narrow"),
            P("narrow", None),
        ),
        out_specs=(P("narrow", "wide", None), P("narrow", None)),
        check_vma=False,
    )
```

time: 96.7 us -> 65.6 us (0.68)
  starting transfers between devices: 41.1 us -> 28.5 us
  Pallas kernels: 28.7 us -> 19.6 us
  matrix products: 5.31 us -> 0 us
  local copies, waits for them, and re-layouts: 6.49 us -> 3.34 us
  waiting for transfers between devices: 9.81 us -> 12.3 us
  other arithmetic: 2.17 us -> 0 us
  between operations: 2.81 us -> 1.53 us
    ppermute x40 -> x25, starting transfers between devices: 41.1 us -> 25.5 us  [swap_with(): lax.ppermute(value, axis, [(index, index ^ mask) for index in range(size)])]
    pallas_call x11 -> x21, Pallas kernels: 28.7 us -> 19.6 us  [kernel_call(): pl.pallas_call(whole, out_shape=outputs, in_specs=[in_smem] * scalars + [...]
    dot_general x3 -> x0, matrix products: 5.31 us -> none  [product(): jnp.dot(left, right, precision=precise_level, preferred_element_type=jnp....]
    ppermute x0 -> x1, starting transfers between devices: none -> 3.09 us  [send_by_core(): return lax.ppermute(value, ('wide', 'narrow'), pairs)]
    ppermute x40 -> x25, waiting for transfers between devices: 9.81 us -> 12.3 us  [swap_with(): lax.ppermute(value, axis, [(index, index ^ mask) for index in range(size)])]
    unnamed x8 -> x6, local copies, waits for them, and re-layouts: 4.75 us -> 3.33 us
  transfers between devices with their start and end apart: 40 -> 26, of which waited for: 11 -> 10; matrix products, arithmetic and copies ran while one was open for 9% -> 0% of each run, Pallas kernels for 26% -> 20%
where the time goes in v2:
time: 65.6 us; the launch traced here: 65.4 us
  starting transfers between devices  28.5 us (43%)
  Pallas kernels  19.6 us (30%)
  waiting for transfers between devices  12.3 us (19%)
  local copies, waits for them, and re-layouts  3.34 us (5%)
  between operations  1.53 us (2%)
    ppermute x25, starting transfers between devices, swap_with(): lax.ppermute(value, axis, [(index, index ^ mask) for index in range(size)])  25.5 us
    pallas_call x21, Pallas kernels, kernel_call(): pl.pallas_call(whole, out_shape=outputs, in_specs=[in_smem] * scalars + [...  19.6 us
    ppermute x25, waiting for transfers between devices, swap_with(): lax.ppermute(value, axis, [(index, index ^ mask) for index in range(size)])  12.3 us
    unnamed x6, local copies, waits for them, and re-layouts  3.33 us
    ppermute x1, starting transfers between devices, send_by_core(): return lax.ppermute(value, ('wide', 'narrow'), pairs)  3.09 us
  transfers between devices with their start and end apart: 26, of which 10 were waited for; matrix products, arithmetic and copies ran while one was open for 0% of the time, Pallas kernels for 20%

profile of v2, /device:TPU:0, one launch (start us, length us, event | category | flops | bytes accessed | tf_op | source)
XLA Modules:
  0.0 65.4 jit_solution(3225187646410889790)
XLA Ops:
  0.6 0.0 copy-start
  0.7 1.0 %copy-done = f32[1024,128]{1,0:T(8,128)S(1)} copy-done((f32[1024,128]{1,0:T(8,128)S(1)}, f32[1024,128]{1,0:T(8,128)}, u32[]{:S(2)}) %copy-start) | copy-done | bytes 524312
  1.7 3.1 %collective-permute-start.3 = (f32[16,2,8,128]{3,2,1,0:T(8,128)S(1)}, f32[16,2,8,128]{3,2,1,0:T(8,128)S(1)}, u32[]{:S(2)}, u32[]{:S(2)}) collective-permute-start(f32[16,2,8,128]{3,2,1,0:T(8,128)S(1)} %dynamic-slice_bitcast_fusion.refs_0_.refs_1_), channel_id=1, source_target_pairs={{0,1},{1,0},{2,3},{3,2},{4,6},{5,7},{6,4},{7,5},{8,9},{9,8},{10,11... | collective-permute-start | bytes 393224 | tf_op jit(solution)/shard_map/ppermute | solution.py:78
  4.8 2.5 %collective-permute-start.4 = (f32[16,8,128]{2,1,0:T(8,128)S(1)}, f32[16,8,128]{2,1,0:T(8,128)S(1)}, u32[]{:S(2)}, u32[]{:S(2)}) collective-permute-start(f32[16,8,128]{2,1,0:T(8,128)S(1)} %shard_map.59.refs_2_), channel_id=1, source_target_pairs={{0,3},{1,2},{2,1},{3,0},{4,7},{5,6},{6,5},{7,4},{8,11},{9,10},{10,... | collective-permute-start | bytes 196616 | tf_op jit(solution)/shard_map/ppermute | solution.py:68
  7.3 2.4 %collective-permute-start.2 = (s32[2,3]{1,0:T(2,128)}, s32[2,3]{1,0:T(2,128)S(1)}, u32[]{:S(2)}, u32[]{:S(2)}) collective-permute-start(s32[2,3]{1,0:T(2,128)} %bitcast.11), channel_id=1, source_target_pairs={{0,24},{4,28},{8,16},{12,20},{16,8},{20,12},{24,0},{28,4},{1,25},{... | collective-permute-start | bytes 80 | tf_op jit(solution)/shard_map/ppermute | solution.py:68
  9.7 0.5 collective-permute-start.1
  10.9 0.6 collective-permute-start
  11.5 0.7 %copy-done.2 = s32[1,1,2,3]{3,2,1,0:T(2,128)S(1)} copy-done((s32[1,1,2,3]{3,2,1,0:T(2,128)S(1)}, s32[1,1,2,3]{3,2,1,0:T(2,128)}, u32[]{:S(2)}) %copy-start.2) | copy-done | bytes 48
  12.2 0.1 shard_map.60
  12.3 1.6 %copy-done.1 = f32[1,1,2,64,4096]{4,3,2,1,0:T(8,128)S(1)} copy-done((f32[1,1,2,64,4096]{4,3,2,1,0:T(8,128)S(1)}, f32[1,1,2,64,4096]{4,3,2,1,0:T(8,128)}, u32[]{:S(2)}) %copy-start.1) | copy-done | bytes 2097176
  13.8 0.1 shard_map.61.refs_4_.refs_0_.refs_5_
  14.0 0.0 collective-permute-done.2.refs_3_
  14.0 0.0 collective-permute-done.1.refs_2_
  14.0 0.7 %collective-permute-done.refs_1_ = s32[2,3]{1,0:T(2,128)S(1)} collective-permute-done((s32[2,3]{1,0:T(2,128)}, s32[2,3]{1,0:T(2,128)S(1)}, u32[]{:S(2)}, u32[]{:S(2)}) %collective-permute-start) | collective-permute-done | bytes 56 | tf_op jit(solution)/shard_map/ppermute | solution.py:68
  14.7 0.0 collective-permute-done.4.refs_1_
  14.7 0.0 collective-permute-done.3.refs_0_
  14.7 0.1 collective-permute-start.5
  14.8 1.4 %collective-permute-done.5.refs_3_ = f32[48,8,128]{2,1,0:T(8,128)S(1)} collective-permute-done((f32[48,8,128]{2,1,0:T(8,128)S(1)}, f32[48,8,128]{2,1,0:T(8,128)S(1)}, u32[]{:S(2)}, u32[]{:S(2)}) %collective-permute-start.5) | collective-permute-done | bytes 196640 | tf_op jit(solution)/shard_map/ppermute | solution.py:68
  16.3 1.3 %shard_map.64 = (f32[192,128]{1,0:T(8,128)S(1)}, f32[192,128]{1,0:T(8,128)S(1)}, f32[192,128]{1,0:T(8,128)S(1)}, f32[192,128]{1,0:T(8,128)S(1)}) custom-call(s32[4,2,3]{2,1,0:T(2,128)S(1)} %shard_map.62.refs_2_.refs_0_, f32[16,2,8,128]{3,2,1,0:T(8,128)S(1)} %dynamic-slice_bitcast_fusion.refs_0_.refs_1_, f32[48,8,128]{2,1,0:T(8,128)S(1)} %shard_map.63.refs_2_, ...), custom_call_target="tpu_custom_call" | custom-call | flops 300000 | tf_op jit(solution)/shard_map/pallas_call | solution.py:30
  17.6 0.9 %collective-permute-start.6 = (f32[192,128]{1,0:T(8,128)S(1)}, f32[192,128]{1,0:T(8,128)S(1)}, u32[]{:S(2)}, u32[]{:S(2)}) collective-permute-start(f32[192,128]{1,0:T(8,128)S(1)} %get-tuple-element.29), channel_id=1, source_target_pairs={{0,8},{4,12},{8,0},{12,4},{16,24},{20,28},{24,16},{28,20},{1,9},{5... | collective-permute-start | bytes 294920 | tf_op jit(solution)/shard_map/ppermute | solution.py:68
  18.5 1.5 %collective-permute-start.7 = (f32[192,128]{1,0:T(8,128)S(1)}, f32[192,128]{1,0:T(8,128)S(1)}, u32[]{:S(2)}, u32[]{:S(2)}) collective-permute-start(f32[192,128]{1,0:T(8,128)S(1)} %get-tuple-element.30), channel_id=1, source_target_pairs={{0,16},{4,20},{8,24},{12,28},{16,0},{20,4},{24,8},{28,12},{1,17},{... | collective-permute-start | bytes 294920 | tf_op jit(solution)/shard_map/ppermute | solution.py:68
  20.0 1.1 %collective-permute-start.8 = (f32[192,128]{1,0:T(8,128)S(1)}, f32[192,128]{1,0:T(8,128)S(1)}, u32[]{:S(2)}, u32[]{:S(2)}) collective-permute-start(f32[192,128]{1,0:T(8,128)S(1)} %get-tuple-element.31), channel_id=1, source_target_pairs={{0,24},{4,28},{8,16},{12,20},{16,8},{20,12},{24,0},{28,4},{1,25},{... | collective-permute-start | bytes 294920 | tf_op jit(solution)/shard_map/ppermute | solution.py:68
  21.1 2.0 %shard_map.65.refs_6_.refs_3_ = bf16[2,4096,256]{2,1,0:T(8,128)(2,1)S(1)} custom-call(f32[2,64,4096]{2,1,0:T(8,128)S(1)} %shard_map.61.refs_4_.refs_0_.refs_5_, f32[192,128]{1,0:T(8,128)S(1)} %get-tuple-element.28.refs_1_.refs_0_), custom_call_target="tpu_custom_call" | custom-call | flops 300000 | tf_op jit(solution)/shard_map/pallas_call | solution.py:30
  23.1 0.0 collective-permute-done.6.refs_2_.refs_1_
  23.1 1.2 %collective-permute-done.7.refs_3_.refs_2_ = f32[192,128]{1,0:T(8,128)S(1)} collective-permute-done((f32[192,128]{1,0:T(8,128)S(1)}, f32[192,128]{1,0:T(8,128)S(1)}, u32[]{:S(2)}, u32[]{:S(2)}) %collective-permute-start.7) | collective-permute-done | bytes 98336 | tf_op jit(solution)/shard_map/ppermute | solution.py:68
  24.3 1.3 %collective-permute-done.8.refs_4_.refs_3_ = f32[192,128]{1,0:T(8,128)S(1)} collective-permute-done((f32[192,128]{1,0:T(8,128)S(1)}, f32[192,128]{1,0:T(8,128)S(1)}, u32[]{:S(2)}, u32[]{:S(2)}) %collective-permute-start.8) | collective-permute-done | bytes 98336 | tf_op jit(solution)/shard_map/ppermute | solution.py:68
  25.6 1.7 %shard_map.66 = (f32[4,64,128]{2,1,0:T(8,128)S(1)}, f32[136,128]{1,0:T(8,128)S(1)}) custom-call(f32[8,128]{1,0:T(8,128)S(1)} %get-tuple-element.26.refs_1_.refs_0_, f32[192,128]{1,0:T(8,128)S(1)} %get-tuple-element.28.refs_1_.refs_0_, f32[192,128]{1,0:T(8,128)S(1)} %collective-permute-done.6.refs_2_.refs_1_, ...), custom_call_target="tpu_custom_call" | custom-call | flops 3000000 | tf_op jit(solution)/shard_map/pallas_call | solution.py:30
  27.3 1.9 %collective-permute-start.11 = (f32[136,128]{1,0:T(8,128)S(1)}, f32[136,128]{1,0:T(8,128)S(1)}, u32[]{:S(2)}, u32[]{:S(2)}) collective-permute-start(f32[136,128]{1,0:T(8,128)S(1)} %get-tuple-element.32.refs_4_.refs_0_), channel_id=1, source_target_pairs={{0,24},{4,28},{8,16},{12,20},{16,8},{20,12},{24,0},{28,4},{1,25},{... | collective-permute-start | bytes 208904 | tf_op jit(solution)/shard_map/ppermute | solution.py:68
  29.2 0.8 %collective-permute-start.10 = (f32[136,128]{1,0:T(8,128)S(1)}, f32[136,128]{1,0:T(8,128)S(1)}, u32[]{:S(2)}, u32[]{:S(2)}) collective-permute-start(f32[136,128]{1,0:T(8,128)S(1)} %get-tuple-element.32.refs_4_.refs_0_), channel_id=1, source_target_pairs={{0,16},{4,20},{8,24},{12,28},{16,0},{20,4},{24,8},{28,12},{1,17},{... | collective-permute-start | bytes 208904 | tf_op jit(solution)/shard_map/ppermute | solution.py:68
  30.0 0.9 %collective-permute-start.9 = (f32[136,128]{1,0:T(8,128)S(1)}, f32[136,128]{1,0:T(8,128)S(1)}, u32[]{:S(2)}, u32[]{:S(2)}) collective-permute-start(f32[136,128]{1,0:T(8,128)S(1)} %get-tuple-element.32.refs_4_.refs_0_), channel_id=1, source_target_pairs={{0,8},{4,12},{8,0},{12,4},{16,24},{20,28},{24,16},{28,20},{1,9},{5... | collective-permute-start | bytes 208904 | tf_op jit(solution)/shard_map/ppermute | solution.py:68
  30.8 3.4 %shard_map.67 = (f32[128,128]{1,0:T(8,128)S(1)}, f32[128,128]{1,0:T(8,128)S(1)}) custom-call(f32[192,128]{1,0:T(8,128)S(1)} %get-tuple-element.28.refs_1_.refs_0_, f32[192,128]{1,0:T(8,128)S(1)} %collective-permute-done.6.refs_2_.refs_1_, f32[192,128]{1,0:T(8,128)S(1)} %collective-permute-done.7.refs_3_.refs_2_, ...), custom_call_target="tpu_custom_call" | custom-call | flops 3500000 | tf_op jit(solution)/shard_map/pallas_call | solution.py:30
  34.3 0.0 collective-permute-done.11.refs_3_
  34.3 0.0 collective-permute-done.10.refs_2_
  34.3 0.0 collective-permute-done.9.refs_1_
  34.4 0.1 collective-permute-start.12
  34.4 1.5 %collective-permute-done.12.refs_1_.refs_2_ = f32[4,136,128]{2,1,0:T(8,128)S(1)} collective-permute-done((f32[4,136,128]{2,1,0:T(8,128)S(1)}, f32[4,136,128]{2,1,0:T(8,128)S(1)}, u32[]{:S(2)}, u32[]{:S(2)}) %collective-permute-start.12) | collective-permute-done | bytes 278560 | tf_op jit(solution)/shard_map/ppermute | solution.py:68
  36.0 1.7 %shard_map.70 = (f32[4,4,8,128]{3,2,1,0:T(8,128)S(1)}, f32[4,4,8,128]{3,2,1,0:T(8,128)S(1)}) custom-call(f32[4,136,128]{2,1,0:T(8,128)S(1)} %shard_map.68.refs_0_.refs_1_, f32[4,136,128]{2,1,0:T(8,128)S(1)} %collective-permute-done.12.refs_1_.refs_2_, f32[128,128]{1,0:T(8,128)S(1)} %get-tuple-element.33.refs_4_.refs_2_.refs_3_, ...), custom_call_target="tpu_custom_call" | custom-call | flops 2500000 | tf_op jit(solution)/shard_map/pallas_call | solution.py:30
  37.7 0.2 collective-permute-start.13
  37.9 1.1 %collective-permute-done.13.refs_1_ = f32[4,4,8,128]{3,2,1,0:T(8,128)S(1)} collective-permute-done((f32[4,4,8,128]{3,2,1,0:T(8,128)S(1)}, f32[4,4,8,128]{3,2,1,0:T(8,128)S(1)}, u32[]{:S(2)}, u32[]{:S(2)}) %collective-permute-start.13) | collective-permute-done | bytes 65568 | tf_op jit(solution)/shard_map/ppermute | solution.py:68
  39.1 1.2 %collective-permute-start.14 = (f32[2,4,8,128]{3,2,1,0:T(8,128)S(1)}, f32[2,4,8,128]{3,2,1,0:T(8,128)S(1)}, u32[]{:S(2)}, u32[]{:S(2)}) collective-permute-start(f32[2,4,8,128]{3,2,1,0:T(8,128)S(1)} %get-tuple-element.39), channel_id=1, source_target_pairs={{0,8},{4,12},{8,0},{12,4},{16,24},{20,28},{24,16},{28,20},{1,9},{5... | collective-permute-start | bytes 98312 | tf_op jit(solution)/shard_map/ppermute | solution.py:68
  40.3 1.2 %collective-permute-start.15 = (f32[2,4,8,128]{3,2,1,0:T(8,128)S(1)}, f32[2,4,8,128]{3,2,1,0:T(8,128)S(1)}, u32[]{:S(2)}, u32[]{:S(2)}) collective-permute-start(f32[2,4,8,128]{3,2,1,0:T(8,128)S(1)} %get-tuple-element.40), channel_id=1, source_target_pairs={{0,16},{4,20},{8,24},{12,28},{16,0},{20,4},{24,8},{28,12},{1,17},{... | collective-permute-start | bytes 98312 | tf_op jit(solution)/shard_map/ppermute | solution.py:68
  41.5 1.1 %collective-permute-start.16 = (f32[2,4,8,128]{3,2,1,0:T(8,128)S(1)}, f32[2,4,8,128]{3,2,1,0:T(8,128)S(1)}, u32[]{:S(2)}, u32[]{:S(2)}) collective-permute-start(f32[2,4,8,128]{3,2,1,0:T(8,128)S(1)} %get-tuple-element.41), channel_id=1, source_target_pairs={{0,24},{4,28},{8,16},{12,20},{16,8},{20,12},{24,0},{28,4},{1,25},{... | collective-permute-start | bytes 98312 | tf_op jit(solution)/shard_map/ppermute | solution.py:68
  42.6 1.6 %shard_map.72 = (f32[128,128]{1,0:T(8,128)S(1)}, f32[16,64,128]{2,1,0:T(8,128)S(1)}) custom-call(s32[8,2,3]{2,1,0:T(2,128)S(1)} %shard_map.69.refs_0_, f32[4,136,128]{2,1,0:T(8,128)S(1)} %shard_map.68.refs_0_.refs_1_, f32[4,136,128]{2,1,0:T(8,128)S(1)} %collective-permute-done.12.refs_1_.refs_2_, f32[128,128]{1,0:T(8,128)S(1)} %get-tuple-element.33.refs_4_.refs_2_.refs_3_, ...), custom_call_target="tpu_custom_call" | custom-call | flops 100000 | tf_op jit(solution)/shard_map/pallas_call | solution.py:30
  44.2 0.3 collective-permute-start.20
  44.5 1.8 %collective-permute-done.16.refs_4_ = f32[2,4,8,128]{3,2,1,0:T(8,128)S(1)} collective-permute-done((f32[2,4,8,128]{3,2,1,0:T(8,128)S(1)}, f32[2,4,8,128]{3,2,1,0:T(8,128)S(1)}, u32[]{:S(2)}, u32[]{:S(2)}) %collective-permute-start.16) | collective-permute-done | bytes 32800 | tf_op jit(solution)/shard_map/ppermute | solution.py:68
  46.3 0.8 %shard_map.73 = (f32[128,128]{1,0:T(8,128)S(1)}, f32[128,128]{1,0:T(8,128)S(1)}, f32[128,128]{1,0:T(8,128)S(1)}, f32[128,128]{1,0:T(8,128)S(1)}) custom-call(s32[8,2,3]{2,1,0:T(2,128)S(1)} %shard_map.69.refs_0_, f32[2,4,8,128]{3,2,1,0:T(8,128)S(1)} %get-tuple-element.37.refs_4_.refs_1_, f32[2,4,8,128]{3,2,1,0:T(8,128)S(1)} %collective-permute-done.14.refs_2_, ...), custom_call_target="tpu_custom_call" | custom-call | flops 300000 | tf_op jit(solution)/shard_map/pallas_call | solution.py:30
  47.1 0.7 %collective-permute-start.17 = (f32[128,128]{1,0:T(8,128)S(1)}, f32[128,128]{1,0:T(8,128)S(1)}, u32[]{:S(2)}, u32[]{:S(2)}) collective-permute-start(f32[128,128]{1,0:T(8,128)S(1)} %get-tuple-element.45), channel_id=1, source_target_pairs={{0,1},{1,0},{2,3},{3,2},{4,5},{5,4},{6,7},{7,6},{8,9},{9,8},{10,11... | collective-permute-start | bytes 196616 | tf_op jit(solution)/shard_map/ppermute | solution.py:68
  47.9 1.2 %collective-permute-start.18 = (f32[128,128]{1,0:T(8,128)S(1)}, f32[128,128]{1,0:T(8,128)S(1)}, u32[]{:S(2)}, u32[]{:S(2)}) collective-permute-start(f32[128,128]{1,0:T(8,128)S(1)} %get-tuple-element.46), channel_id=1, source_target_pairs={{0,2},{1,3},{2,0},{3,1},{4,6},{5,7},{6,4},{7,5},{8,10},{9,11},{10,... | collective-permute-start | bytes 196616 | tf_op jit(solution)/shard_map/ppermute | solution.py:68
  49.1 2.5 %collective-permute-start.19 = (f32[128,128]{1,0:T(8,128)S(1)}, f32[128,128]{1,0:T(8,128)S(1)}, u32[]{:S(2)}, u32[]{:S(2)}) collective-permute-start(f32[128,128]{1,0:T(8,128)S(1)} %get-tuple-element.47), channel_id=1, source_target_pairs={{0,3},{1,2},{2,1},{3,0},{4,7},{5,6},{6,5},{7,4},{8,11},{9,10},{10,... | collective-permute-start | bytes 196616 | tf_op jit(solution)/shard_map/ppermute | solution.py:68
  51.6 0.0 collective-permute-done.20.refs_1_
  51.6 0.1 collective-permute-start.24
  51.7 1.9 %shard_map.74 = (f32[8,64,128]{2,1,0:T(8,128)}, f32[8,128]{1,0:T(8,128)S(1)}) custom-call(s32[8,2,3]{2,1,0:T(2,128)S(1)} %shard_map.69.refs_0_, f32[16,64,128]{2,1,0:T(8,128)S(1)} %get-tuple-element.38.refs_1_, f32[128,128]{1,0:T(8,128)S(1)} %get-tuple-element.43.refs_2_.refs_0_), custom_call_target="tpu_custom_call" | custom-call | flops 100000 | tf_op jit(solution)/shard_map/pallas_call | solution.py:30
  53.5 0.0 collective-permute-done.17.refs_1_
  53.5 0.8 %collective-permute-done.18.refs_2_ = f32[128,128]{1,0:T(8,128)S(1)} collective-permute-done((f32[128,128]{1,0:T(8,128)S(1)}, f32[128,128]{1,0:T(8,128)S(1)}, u32[]{:S(2)}, u32[]{:S(2)}) %collective-permute-start.18) | collective-permute-done | bytes 65568 | tf_op jit(solution)/shard_map/ppermute | solution.py:68
  54.3 0.9 %collective-permute-done.19.refs_3_ = f32[128,128]{1,0:T(8,128)S(1)} collective-permute-done((f32[128,128]{1,0:T(8,128)S(1)}, f32[128,128]{1,0:T(8,128)S(1)}, u32[]{:S(2)}, u32[]{:S(2)}) %collective-permute-start.19) | collective-permute-done | bytes 65568 | tf_op jit(solution)/shard_map/ppermute | solution.py:68
  55.3 1.7 %collective-permute-start.23 = (f32[128,128]{1,0:T(8,128)S(1)}, f32[128,128]{1,0:T(8,128)S(1)}, u32[]{:S(2)}, u32[]{:S(2)}) collective-permute-start(f32[128,128]{1,0:T(8,128)S(1)} %shard_map.76.refs_3_.refs_0_), channel_id=1, source_target_pairs={{0,24},{4,28},{8,16},{12,20},{16,8},{20,12},{24,0},{28,4},{1,25},{... | collective-permute-start | bytes 196616 | tf_op jit(solution)/shard_map/ppermute | solution.py:68
  57.0 0.8 %collective-permute-start.22 = (f32[128,128]{1,0:T(8,128)S(1)}, f32[128,128]{1,0:T(8,128)S(1)}, u32[]{:S(2)}, u32[]{:S(2)}) collective-permute-start(f32[128,128]{1,0:T(8,128)S(1)} %shard_map.76.refs_3_.refs_0_), channel_id=1, source_target_pairs={{0,16},{4,20},{8,24},{12,28},{16,0},{20,4},{24,8},{28,12},{1,17},{... | collective-permute-start | bytes 196616 | tf_op jit(solution)/shard_map/ppermute | solution.py:68
  57.8 1.1 %collective-permute-start.21 = (f32[128,128]{1,0:T(8,128)S(1)}, f32[128,128]{1,0:T(8,128)S(1)}, u32[]{:S(2)}, u32[]{:S(2)}) collective-permute-start(f32[128,128]{1,0:T(8,128)S(1)} %shard_map.76.refs_3_.refs_0_), channel_id=1, source_target_pairs={{0,8},{4,12},{8,0},{12,4},{16,24},{20,28},{24,16},{28,20},{1,9},{5... | collective-permute-start | bytes 196616 | tf_op jit(solution)/shard_map/ppermute | solution.py:68
  58.8 0.0 collective-permute-done.24.refs_1_
  58.8 3.4 %shard_map.77.refs_4_.refs_2_ = f32[128,128]{1,0:T(8,128)S(1)} custom-call(f32[128,128]{1,0:T(8,128)S(1)} %shard_map.75.refs_4_.refs_0_, f32[128,128]{1,0:T(8,128)S(1)} %collective-permute-done.24.refs_1_, f32[128,128]{1,0:T(8,128)S(1)} %get-tuple-element.49.refs_2_, f32[128,128]{1,0:T(8,128)S(1)} %shard_map.76.refs_3_.refs_0_), custom_call_target="tpu_custom_call" | custom-call | flops 3500000 | tf_op jit(solution)/shard_map/pallas_call | solution.py:30
  62.3 0.0 collective-permute-done.22.refs_2_
  62.4 0.1 collective-permute-start.25
  62.4 1.5 %collective-permute-done.25.refs_1_ = f32[4,128,128]{2,1,0:T(8,128)S(1)} collective-permute-done((f32[4,128,128]{2,1,0:T(8,128)S(1)}, f32[4,128,128]{2,1,0:T(8,128)S(1)}, u32[]{:S(2)}, u32[]{:S(2)}) %collective-permute-start.25) | collective-permute-done | bytes 262176 | tf_op jit(solution)/shard_map/ppermute | solution.py:68
  64.0 1.4 %shard_map.79 = f32[16,8,8,128]{3,2,1,0:T(8,128)} custom-call(f32[4,128,128]{2,1,0:T(8,128)S(1)} %shard_map.78.refs_0_, f32[4,128,128]{2,1,0:T(8,128)S(1)} %collective-permute-done.25.refs_1_, f32[128,128]{1,0:T(8,128)S(1)} %shard_map.77.refs_4_.refs_2_), custom_call_target="tpu_custom_call" | custom-call | flops 1500000 | tf_op jit(solution)/shard_map/pallas_call | solution.py:30
  (16 shorter events, 0.1 us)
Async XLA Ops:
  0.6 1.0 %copy-start = (f32[1024,128]{1,0:T(8,128)S(1)}, f32[1024,128]{1,0:T(8,128)}, u32[]{:S(2)}) copy-start(f32[1024,128]{1,0:T(8,128)} %param.7) | copy-start | bytes 1572868
  1.7 13.0 %collective-permute-start.3 = (f32[16,2,8,128]{3,2,1,0:T(8,128)S(1)}, f32[16,2,8,128]{3,2,1,0:T(8,128)S(1)}, u32[]{:S(2)}, u32[]{:S(2)}) collective-permute-start(f32[16,2,8,128]{3,2,1,0:T(8,128)S(1)} %dynamic-slice_bitcast_fusion.refs_0_.refs_1_), channel_id=1, source_target_pairs={{0,1},{1,0},{2,3},{3,2},{4,6},{5,7},{6,4},{7,5},{8,9},{9,8},{10,11... | collective-permute-start | bytes 393224 | tf_op jit(solution)/shard_map/ppermute | solution.py:78
  4.8 9.9 %collective-permute-start.4 = (f32[16,8,128]{2,1,0:T(8,128)S(1)}, f32[16,8,128]{2,1,0:T(8,128)S(1)}, u32[]{:S(2)}, u32[]{:S(2)}) collective-permute-start(f32[16,8,128]{2,1,0:T(8,128)S(1)} %shard_map.59.refs_2_), channel_id=1, source_target_pairs={{0,3},{1,2},{2,1},{3,0},{4,7},{5,6},{6,5},{7,4},{8,11},{9,10},{10,... | collective-permute-start | bytes 196616 | tf_op jit(solution)/shard_map/ppermute | solution.py:68
  7.3 6.7 %collective-permute-start.2 = (s32[2,3]{1,0:T(2,128)}, s32[2,3]{1,0:T(2,128)S(1)}, u32[]{:S(2)}, u32[]{:S(2)}) collective-permute-start(s32[2,3]{1,0:T(2,128)} %bitcast.11), channel_id=1, source_target_pairs={{0,24},{4,28},{8,16},{12,20},{16,8},{20,12},{24,0},{28,4},{1,25},{... | collective-permute-start | bytes 80 | tf_op jit(solution)/shard_map/ppermute | solution.py:68
  9.7 4.3 %collective-permute-start.1 = (s32[2,3]{1,0:T(2,128)}, s32[2,3]{1,0:T(2,128)S(1)}, u32[]{:S(2)}, u32[]{:S(2)}) collective-permute-start(s32[2,3]{1,0:T(2,128)} %bitcast.12), channel_id=1, source_target_pairs={{0,16},{4,20},{8,24},{12,28},{16,0},{20,4},{24,8},{28,12},{1,17},{... | collective-permute-start | bytes 80 | tf_op jit(solution)/shard_map/ppermute | solution.py:68
  10.9 3.8 %collective-permute-start = (s32[2,3]{1,0:T(2,128)}, s32[2,3]{1,0:T(2,128)S(1)}, u32[]{:S(2)}, u32[]{:S(2)}) collective-permute-start(s32[2,3]{1,0:T(2,128)} %bitcast.13), channel_id=1, source_target_pairs={{0,8},{4,12},{8,0},{12,4},{16,24},{20,28},{24,16},{28,20},{1,9},{5... | collective-permute-start | bytes 80 | tf_op jit(solution)/shard_map/ppermute | solution.py:68
  11.5 0.7 %copy-start.2 = (s32[1,1,2,3]{3,2,1,0:T(2,128)S(1)}, s32[1,1,2,3]{3,2,1,0:T(2,128)}, u32[]{:S(2)}) copy-start(s32[1,1,2,3]{3,2,1,0:T(2,128)} %param.5) | copy-start | bytes 76
  12.3 1.6 %copy-start.1 = (f32[1,1,2,64,4096]{4,3,2,1,0:T(8,128)S(1)}, f32[1,1,2,64,4096]{4,3,2,1,0:T(8,128)}, u32[]{:S(2)}) copy-start(f32[1,1,2,64,4096]{4,3,2,1,0:T(8,128)} %param.4) | copy-start | bytes 6291460
  14.7 1.5 %collective-permute-start.5 = (f32[48,8,128]{2,1,0:T(8,128)S(1)}, f32[48,8,128]{2,1,0:T(8,128)S(1)}, u32[]{:S(2)}, u32[]{:S(2)}) collective-permute-start(f32[48,8,128]{2,1,0:T(8,128)S(1)} %shard_map.63.refs_2_), channel_id=1, source_target_pairs={{0,4},{4,0},{8,12},{12,8},{16,20},{20,16},{24,28},{28,24},{1,5},{5... | collective-permute-start | bytes 589832 | tf_op jit(solution)/shard_map/ppermute | solution.py:68
  17.6 5.5 %collective-permute-start.6 = (f32[192,128]{1,0:T(8,128)S(1)}, f32[192,128]{1,0:T(8,128)S(1)}, u32[]{:S(2)}, u32[]{:S(2)}) collective-permute-start(f32[192,128]{1,0:T(8,128)S(1)} %get-tuple-element.29), channel_id=1, source_target_pairs={{0,8},{4,12},{8,0},{12,4},{16,24},{20,28},{24,16},{28,20},{1,9},{5... | collective-permute-start | bytes 294920 | tf_op jit(solution)/shard_map/ppermute | solution.py:68
  18.5 5.8 %collective-permute-start.7 = (f32[192,128]{1,0:T(8,128)S(1)}, f32[192,128]{1,0:T(8,128)S(1)}, u32[]{:S(2)}, u32[]{:S(2)}) collective-permute-start(f32[192,128]{1,0:T(8,128)S(1)} %get-tuple-element.30), channel_id=1, source_target_pairs={{0,16},{4,20},{8,24},{12,28},{16,0},{20,4},{24,8},{28,12},{1,17},{... | collective-permute-start | bytes 294920 | tf_op jit(solution)/shard_map/ppermute | solution.py:68
  20.0 5.5 %collective-permute-start.8 = (f32[192,128]{1,0:T(8,128)S(1)}, f32[192,128]{1,0:T(8,128)S(1)}, u32[]{:S(2)}, u32[]{:S(2)}) collective-permute-start(f32[192,128]{1,0:T(8,128)S(1)} %get-tuple-element.31), channel_id=1, source_target_pairs={{0,24},{4,28},{8,16},{12,20},{16,8},{20,12},{24,0},{28,4},{1,25},{... | collective-permute-start | bytes 294920 | tf_op jit(solution)/shard_map/ppermute | solution.py:68
  27.3 7.0 %collective-permute-start.11 = (f32[136,128]{1,0:T(8,128)S(1)}, f32[136,128]{1,0:T(8,128)S(1)}, u32[]{:S(2)}, u32[]{:S(2)}) collective-permute-start(f32[136,128]{1,0:T(8,128)S(1)} %get-tuple-element.32.refs_4_.refs_0_), channel_id=1, source_target_pairs={{0,24},{4,28},{8,16},{12,20},{16,8},{20,12},{24,0},{28,4},{1,25},{... | collective-permute-start | bytes 208904 | tf_op jit(solution)/shard_map/ppermute | solution.py:68
  29.2 5.1 %collective-permute-start.10 = (f32[136,128]{1,0:T(8,128)S(1)}, f32[136,128]{1,0:T(8,128)S(1)}, u32[]{:S(2)}, u32[]{:S(2)}) collective-permute-start(f32[136,128]{1,0:T(8,128)S(1)} %get-tuple-element.32.refs_4_.refs_0_), channel_id=1, source_target_pairs={{0,16},{4,20},{8,24},{12,28},{16,0},{20,4},{24,8},{28,12},{1,17},{... | collective-permute-start | bytes 208904 | tf_op jit(solution)/shard_map/ppermute | solution.py:68
  30.0 4.3 %collective-permute-start.9 = (f32[136,128]{1,0:T(8,128)S(1)}, f32[136,128]{1,0:T(8,128)S(1)}, u32[]{:S(2)}, u32[]{:S(2)}) collective-permute-start(f32[136,128]{1,0:T(8,128)S(1)} %get-tuple-element.32.refs_4_.refs_0_), channel_id=1, source_target_pairs={{0,8},{4,12},{8,0},{12,4},{16,24},{20,28},{24,16},{28,20},{1,9},{5... | collective-permute-start | bytes 208904 | tf_op jit(solution)/shard_map/ppermute | solution.py:68
  34.4 1.6 %collective-permute-start.12 = (f32[4,136,128]{2,1,0:T(8,128)S(1)}, f32[4,136,128]{2,1,0:T(8,128)S(1)}, u32[]{:S(2)}, u32[]{:S(2)}) collective-permute-start(f32[4,136,128]{2,1,0:T(8,128)S(1)} %shard_map.68.refs_0_.refs_1_), channel_id=1, source_target_pairs={{0,4},{4,0},{8,12},{12,8},{16,20},{20,16},{24,28},{28,24},{1,5},{5... | collective-permute-start | bytes 835592 | tf_op jit(solution)/shard_map/ppermute | solution.py:68
  37.7 1.3 %collective-permute-start.13 = (f32[4,4,8,128]{3,2,1,0:T(8,128)S(1)}, f32[4,4,8,128]{3,2,1,0:T(8,128)S(1)}, u32[]{:S(2)}, u32[]{:S(2)}) collective-permute-start(f32[4,4,8,128]{3,2,1,0:T(8,128)S(1)} %get-tuple-element.36), channel_id=1, source_target_pairs={{0,4},{4,0},{8,12},{12,8},{16,20},{20,16},{24,28},{28,24},{1,5},{5... | collective-permute-start | bytes 196616 | tf_op jit(solution)/shard_map/ppermute | solution.py:68
  39.1 5.4 %collective-permute-start.14 = (f32[2,4,8,128]{3,2,1,0:T(8,128)S(1)}, f32[2,4,8,128]{3,2,1,0:T(8,128)S(1)}, u32[]{:S(2)}, u32[]{:S(2)}) collective-permute-start(f32[2,4,8,128]{3,2,1,0:T(8,128)S(1)} %get-tuple-element.39), channel_id=1, source_target_pairs={{0,8},{4,12},{8,0},{12,4},{16,24},{20,28},{24,16},{28,20},{1,9},{5... | collective-permute-start | bytes 98312 | tf_op jit(solution)/shard_map/ppermute | solution.py:68
  40.3 4.2 %collective-permute-start.15 = (f32[2,4,8,128]{3,2,1,0:T(8,128)S(1)}, f32[2,4,8,128]{3,2,1,0:T(8,128)S(1)}, u32[]{:S(2)}, u32[]{:S(2)}) collective-permute-start(f32[2,4,8,128]{3,2,1,0:T(8,128)S(1)} %get-tuple-element.40), channel_id=1, source_target_pairs={{0,16},{4,20},{8,24},{12,28},{16,0},{20,4},{24,8},{28,12},{1,17},{... | collective-permute-start | bytes 98312 | tf_op jit(solution)/shard_map/ppermute | solution.py:68
  41.5 4.8 %collective-permute-start.16 = (f32[2,4,8,128]{3,2,1,0:T(8,128)S(1)}, f32[2,4,8,128]{3,2,1,0:T(8,128)S(1)}, u32[]{:S(2)}, u32[]{:S(2)}) collective-permute-start(f32[2,4,8,128]{3,2,1,0:T(8,128)S(1)} %get-tuple-element.41), channel_id=1, source_target_pairs={{0,24},{4,28},{8,16},{12,20},{16,8},{20,12},{24,0},{28,4},{1,25},{... | collective-permute-start | bytes 98312 | tf_op jit(solution)/shard_map/ppermute | solution.py:68
  44.2 7.4 %collective-permute-start.20 = (f32[128,128]{1,0:T(8,128)S(1)}, f32[128,128]{1,0:T(8,128)S(1)}, u32[]{:S(2)}, u32[]{:S(2)}) collective-permute-start(f32[128,128]{1,0:T(8,128)S(1)} %get-tuple-element.42.refs_5_.refs_0_), channel_id=1, source_target_pairs={{0,2},{1,3},{2,0},{3,1},{4,6},{5,7},{6,4},{7,5},{8,10},{9,11},{10,... | collective-permute-start | bytes 196616 | tf_op jit(solution)/shard_map/ppermute | solution.py:68
  47.1 6.4 %collective-permute-start.17 = (f32[128,128]{1,0:T(8,128)S(1)}, f32[128,128]{1,0:T(8,128)S(1)}, u32[]{:S(2)}, u32[]{:S(2)}) collective-permute-start(f32[128,128]{1,0:T(8,128)S(1)} %get-tuple-element.45), channel_id=1, source_target_pairs={{0,1},{1,0},{2,3},{3,2},{4,5},{5,4},{6,7},{7,6},{8,9},{9,8},{10,11... | collective-permute-start | bytes 196616 | tf_op jit(solution)/shard_map/ppermute | solution.py:68
  47.9 6.5 %collective-permute-start.18 = (f32[128,128]{1,0:T(8,128)S(1)}, f32[128,128]{1,0:T(8,128)S(1)}, u32[]{:S(2)}, u32[]{:S(2)}) collective-permute-start(f32[128,128]{1,0:T(8,128)S(1)} %get-tuple-element.46), channel_id=1, source_target_pairs={{0,2},{1,3},{2,0},{3,1},{4,6},{5,7},{6,4},{7,5},{8,10},{9,11},{10,... | collective-permute-start | bytes 196616 | tf_op jit(solution)/shard_map/ppermute | solution.py:68
  49.1 6.2 %collective-permute-start.19 = (f32[128,128]{1,0:T(8,128)S(1)}, f32[128,128]{1,0:T(8,128)S(1)}, u32[]{:S(2)}, u32[]{:S(2)}) collective-permute-start(f32[128,128]{1,0:T(8,128)S(1)} %get-tuple-element.47), channel_id=1, source_target_pairs={{0,3},{1,2},{2,1},{3,0},{4,7},{5,6},{6,5},{7,4},{8,11},{9,10},{10,... | collective-permute-start | bytes 196616 | tf_op jit(solution)/shard_map/ppermute | solution.py:68
  51.6 7.3 %collective-permute-start.24 = (f32[128,128]{1,0:T(8,128)S(1)}, f32[128,128]{1,0:T(8,128)S(1)}, u32[]{:S(2)}, u32[]{:S(2)}) collective-permute-start(f32[128,128]{1,0:T(8,128)S(1)} %shard_map.75.refs_4_.refs_0_), channel_id=1, source_target_pairs={{0,1},{1,0},{2,3},{3,2},{4,5},{5,4},{6,7},{7,6},{8,9},{9,8},{10,11... | collective-permute-start | bytes 196616 | tf_op jit(solution)/shard_map/ppermute | solution.py:68
  55.3 7.0 %collective-permute-start.23 = (f32[128,128]{1,0:T(8,128)S(1)}, f32[128,128]{1,0:T(8,128)S(1)}, u32[]{:S(2)}, u32[]{:S(2)}) collective-permute-start(f32[128,128]{1,0:T(8,128)S(1)} %shard_map.76.refs_3_.refs_0_), channel_id=1, source_target_pairs={{0,24},{4,28},{8,16},{12,20},{16,8},{20,12},{24,0},{28,4},{1,25},{... | collective-permute-start | bytes 196616 | tf_op jit(solution)/shard_map/ppermute | solution.py:68
  57.0 5.4 %collective-permute-start.22 = (f32[128,128]{1,0:T(8,128)S(1)}, f32[128,128]{1,0:T(8,128)S(1)}, u32[]{:S(2)}, u32[]{:S(2)}) collective-permute-start(f32[128,128]{1,0:T(8,128)S(1)} %shard_map.76.refs_3_.refs_0_), channel_id=1, source_target_pairs={{0,16},{4,20},{8,24},{12,28},{16,0},{20,4},{24,8},{28,12},{1,17},{... | collective-permute-start | bytes 196616 | tf_op jit(solution)/shard_map/ppermute | solution.py:68
  57.8 4.6 %collective-permute-start.21 = (f32[128,128]{1,0:T(8,128)S(1)}, f32[128,128]{1,0:T(8,128)S(1)}, u32[]{:S(2)}, u32[]{:S(2)}) collective-permute-start(f32[128,128]{1,0:T(8,128)S(1)} %shard_map.76.refs_3_.refs_0_), channel_id=1, source_target_pairs={{0,8},{4,12},{8,0},{12,4},{16,24},{20,28},{24,16},{28,20},{1,9},{5... | collective-permute-start | bytes 196616 | tf_op jit(solution)/shard_map/ppermute | solution.py:68
  62.4 1.6 %collective-permute-start.25 = (f32[4,128,128]{2,1,0:T(8,128)S(1)}, f32[4,128,128]{2,1,0:T(8,128)S(1)}, u32[]{:S(2)}, u32[]{:S(2)}) collective-permute-start(f32[4,128,128]{2,1,0:T(8,128)S(1)} %shard_map.78.refs_0_), channel_id=1, source_target_pairs={{0,4},{4,0},{8,12},{12,8},{16,20},{20,16},{24,28},{28,24},{1,5},{5... | collective-permute-start | bytes 786440 | tf_op jit(solution)/shard_map/ppermute | solution.py:68

commit v3 on v2

--- a/solution.py
+++ b/solution.py
@@ -200,9 +200,8 @@
     return kernel_call(body, [shaped(own_blocks, rows, rank)], [chip_slice])[0]
 
 
-def open_tags(coords, count, after):
+def open_tags(coords, count, rank, after):
     slots, axes = coords.shape
-    rank = after[0].shape[-1]
 
     def body(coords_ref, count_ref, tag_ref, out_ref):
         slot_at = lax.broadcasted_iota(jnp.int32, (slots, 1), 0)
@@ -257,9 +256,20 @@
     partners, slots, _ = coords.shape
     piece_rows = slots * 2 * low * rows
 
-    def body(coord_ref, own_ref, mine_ref, theirs_ref, *out_refs):
+    def body(there_ref, own_ref, mine_ref, theirs_ref, *refs):
+        out_refs, coord_ref, sem = refs[:partners], refs[partners], refs[partners + 1]
         narrow_at = lax.axis_index("narrow")
         core = lax.axis_index("wide") % low
+        copy = pltpu.make_async_copy(there_ref, coord_ref, sem)
+        copy.start()
+        here, there = mine_ref[...].reshape(-1, rank), theirs_ref[...].reshape(-1, rank)
+        rows_of = [jnp.where(core == j, here, there) for j in range(low)]
+        gram = join_gram(
+            gram_parts(jnp.concatenate([own_ref[...].reshape(-1, rank)] + rows_of, axis=0))
+        )
+        for out_ref in out_refs:
+            out_ref[piece_rows:, :] = gram
+        copy.wait()
         for d, out_ref in enumerate(out_refs):
             for pair in range(slots * 2):
                 block = coord_ref[d, pair // 2, 1 + pair % 2]
@@ -280,33 +290,27 @@
                     out_ref[to : to + rows, :] = jnp.where(
                         owner == 0, own_ref[local, slice_at], away
                     )
-        here, there = mine_ref[...].reshape(-1, rank), theirs_ref[...].reshape(-1, rank)
-        rows_of = [jnp.where(core == j, here, there) for j in range(low)]
-        gram = join_gram(
-            gram_parts(jnp.concatenate([own_ref[...].reshape(-1, rank)] + rows_of, axis=0))
-        )
-        for out_ref in out_refs:
-            out_ref[piece_rows:, :] = gram
 
     return kernel_call(
         body,
         [shaped(piece_rows + rank, rank)] * partners,
         [coords, own, mine, theirs],
-        scalars=1,
+        scratch=[pltpu.SMEM(coords.shape, jnp.int32), pltpu.SemaphoreType.DMA],
         after=after,
     )
 
 
-def first_mode(tags, pieces, blocks, wide_size, low, after):
+def first_mode(tags, pieces, spread, wide_size, low):
     rank = pieces[0].shape[1]
-    slots, edge, _ = blocks.shape
+    slots, _, width = spread.shape
+    edge = width // 4
     pairs = 2 * slots
     slice_rows = edge // wide_size
-    chunk = max(1, 256 // edge)
+    chunk = 4
 
     def body(tag_ref, *refs):
         piece_refs = refs[: len(pieces)]
-        blocks_ref, rows_ref, term_ref, held_ref = refs[len(pieces) :]
+        spread_ref, rows_ref, term_ref, held_ref = refs[len(pieces) :]
         term_ref[slots * edge :, :] = tag_ref[...]
         wide_at = lax.axis_index("wide")
         for d, piece_ref in enumerate(piece_refs):
@@ -317,76 +321,103 @@
                     held_ref[pair, place] = piece_ref[at : at + slice_rows, :]
         rows_ref[...] = held_ref[...].reshape(pairs, edge, rank)
         for slot in range(slots):
-            rows_j = rows_ref[2 * slot + 1]
-
-            def step(index, totals):
-                wide_total, thin_total = totals
-                products = jnp.concatenate(
-                    [
-                        rows_ref[2 * slot, pl.ds(index * chunk + inner, 1), :] * rows_j
-                        for inner in range(chunk)
-                    ],
-                    axis=0,
-                )
-                high, middle, least = split3(products)
-                at = pl.ds(pl.multiple_of(index * (chunk * edge), chunk * edge), chunk * edge)
-                left = jnp.concatenate(split3(blocks_ref[slot, :, at]), axis=0)
-                wide_total = wide_total + jnp.dot(
-                    left,
-                    jnp.concatenate([high, middle], axis=1),
-                    preferred_element_type=jnp.float32,
-                )
-                thin_total = thin_total + jnp.dot(
-                    left[:edge], least, preferred_element_type=jnp.float32
-                )
-                return wide_total, thin_total
-
-            wide_total, thin_total = lax.fori_loop(
-                0,
-                edge // chunk,
-                step,
-                (
-                    jnp.zeros((3 * edge, 2 * rank), jnp.float32),
-                    jnp.zeros((edge, rank), jnp.float32),
-                ),
-                unroll=True,
+            stacked = stack_parts(rows_ref[2 * slot + 1])
+
+            def step(index, total):
+                at = pl.multiple_of(index * (chunk * edge), chunk * edge)
+                product = dot32(spread_ref[slot, pl.ds(at, chunk * edge), :], stacked)
+                product = product[:, :rank] + product[:, rank:]
+                for inner in range(chunk):
+                    row = rows_ref[2 * slot, pl.ds(index * chunk + inner, 1), :]
+                    total = total + product[inner * edge : (inner + 1) * edge] * row
+                return total
+
+            total = lax.fori_loop(
+                0, edge // chunk, step, jnp.zeros((edge, rank), jnp.float32), unroll=True
             )
-            total = wide_total[:, :rank] + wide_total[:, rank:]
-            total = thin_total + total[2 * edge :] + total[edge : 2 * edge] + total[:edge]
             live = tag_ref[slot : slot + 1, live_at : live_at + 1]
             term_ref[slot * edge : (slot + 1) * edge, :] = total * live
 
     return kernel_call(
         body,
         [shaped(pairs, edge, rank), shaped(slots * edge + tags.shape[0], rank)],
-        [tags] + list(pieces) + [blocks],
+        [tags] + list(pieces) + [spread],
         scratch=[pltpu.VMEM((pairs, wide_size, slice_rows, rank), jnp.float32)],
         about_us=3.0,
-        after=after,
-    )
-
-
-def turn_blocks(blocks, after):
+    )
+
+
+def split_blocks(blocks, after):
     slots, edge, pairs = blocks.shape
-    chunk = min(pairs, 512)
-
-    def body(in_ref, turned_ref):
+    turn = 512
+    lanes = 2 * edge
+
+    def body(in_ref, spread_ref, turned_ref):
+        left = lax.broadcasted_iota(jnp.int32, (edge, lanes), 1) < edge
+
+        def roll(value):
+            return pltpu.roll(value, edge, 1)
+
         for slot in range(slots):
 
-            @pl.loop(0, pairs // chunk)
+            @pl.loop(0, pairs // turn)
             def _(index):
-                at = pl.ds(pl.multiple_of(index * chunk, chunk), chunk)
-                high, middle, low = split3(in_ref[slot, :, at])
-                turned_ref[slot, at, : 2 * edge] = jnp.concatenate([high, middle], axis=0).T
-                turned_ref[slot, at, 2 * edge :] = jnp.concatenate([low, high], axis=0).T
-
-    return kernel_call(
-        body, [shaped(slots, pairs, 4 * edge, dtype=jnp.bfloat16)], [blocks], after=after
-    )[0]
+                at = pl.multiple_of(index * turn, turn)
+                parts = []
+                for inner in range(turn // lanes):
+                    value = in_ref[slot, :, pl.ds(at + inner * lanes, lanes)]
+                    high = value.astype(jnp.bfloat16).astype(jnp.float32)
+                    rest = value - high
+                    middle = rest.astype(jnp.bfloat16).astype(jnp.float32)
+                    low = rest - middle
+                    other_high, other_middle, other_low = roll(high), roll(middle), roll(low)
+                    rows = [
+                        [jnp.where(left, high, other_middle), jnp.where(left, low, other_high)],
+                        [jnp.where(left, other_high, middle), jnp.where(left, other_low, high)],
+                    ]
+                    row_at = pl.multiple_of((at // lanes + inner) * lanes, lanes)
+                    for half in range(2):
+                        spread_ref[slot, pl.ds(row_at + half * edge, edge), :] = jnp.concatenate(
+                            rows[half], axis=1
+                        ).astype(jnp.bfloat16)
+                    parts.append([item.astype(jnp.bfloat16) for item in (high, middle, low)])
+                high, middle, low = [jnp.concatenate(item, axis=1) for item in zip(*parts)]
+                here = pl.ds(at, turn)
+                turned_ref[slot, here, : 2 * edge] = jnp.concatenate([high, middle], axis=0).T
+                turned_ref[slot, here, 2 * edge :] = jnp.concatenate([low, high], axis=0).T
+
+    kind = shaped(slots, pairs, 4 * edge, dtype=jnp.bfloat16)
+    return kernel_call(body, [kind, kind], [blocks], after=after)
 
 
 def dot32(left, right):
     return jnp.dot(left, right, preferred_element_type=jnp.float32)
+
+
+def times(rows, matrix):
+    rank = matrix.shape[1]
+    high, middle, least = split3(matrix)
+    left_high, left_middle, left_least = split3(rows)
+    one = jnp.concatenate([high, middle], axis=1)
+    wide = dot32(
+        jnp.concatenate([left_high, left_middle], axis=1), jnp.concatenate([one, one], axis=0)
+    )
+    thin = dot32(
+        jnp.concatenate([left_least, left_high], axis=1), jnp.concatenate([high, least], axis=0)
+    )
+    return (thin + wide[:, rank:]) + wide[:, :rank]
+
+
+def stack_parts(matrix):
+    high, middle, least = split3(matrix)
+    none = jnp.zeros_like(high)
+    return jnp.concatenate(
+        [
+            jnp.concatenate([high, high, high, none], axis=0),
+            jnp.concatenate([middle, middle, none, least], axis=0),
+        ],
+        axis=1,
+    )
 
 
 def gram_parts(rows):
@@ -438,18 +469,10 @@
                     part = term_refs[m % low][m // low, here, :] * same
                     total = part if total is None else total + part
             sums.append(total)
-        aux = product(jnp.concatenate(sums, axis=0), inverse_ref[...])
+        aux = times(jnp.concatenate(sums, axis=0), inverse_ref[...])
         for slot in range(slots):
             weight = tag_of(term_refs[0], 0, slot, live_at)
-            high, middle, least = split3(aux[slot * edge : (slot + 1) * edge] * weight)
-            none = jnp.zeros_like(high)
-            stacked = jnp.concatenate(
-                [
-                    jnp.concatenate([high, high, high, none], axis=0),
-                    jnp.concatenate([middle, middle, none, least], axis=0),
-                ],
-                axis=1,
-            )
+            stacked = stack_parts(aux[slot * edge : (slot + 1) * edge] * weight)
             rows_i, rows_j = rows_ref[2 * slot], rows_ref[2 * slot + 1]
 
             def step(index, total_j):
@@ -528,17 +551,7 @@
             for j in range(1, low):
                 term = jnp.where(place % low == j, term_refs[j][place // low, here, :], term)
             aux_ref[to] += term
-        high, middle, least = split3(inverse_ref[...])
-        left_high, left_middle, left_least = split3(aux_ref[...].reshape(count * edge, rank))
-        one = jnp.concatenate([high, middle], axis=1)
-        aux = dot32(
-            jnp.concatenate([left_high, left_middle], axis=1),
-            jnp.concatenate([one, one], axis=0),
-        )
-        aux = (aux[:, :rank] + aux[:, rank:]) + dot32(
-            jnp.concatenate([left_least, left_high], axis=1),
-            jnp.concatenate([high, least], axis=0),
-        )
+        aux = times(aux_ref[...].reshape(count * edge, rank), inverse_ref[...])
         aux_ref[...] = aux.reshape(count, edge, rank)
         gram_ref[...] = join_gram(gram_parts(aux))
 
@@ -617,33 +630,52 @@
     return [value] + [swap_with(value, "wide", j) for j in range(1, low)]
 
 
-def add_pieces(coords, pieces, narrow_size, own_blocks, after):
+def plan_sums(coords, rows, narrow_size, own_blocks, after):
+    devices, slots, _ = coords.shape
+    count = devices * slots * 2
+    lanes = min(count * rows, 128)
+
+    def body(coord_ref, out_ref, held_ref):
+        narrow_at = lax.axis_index("narrow")
+        held_ref[...] = jnp.zeros_like(held_ref)
+        ahead = lax.broadcasted_iota(jnp.int32, (rows, lanes), 1) - lax.broadcasted_iota(
+            jnp.int32, (rows, lanes), 0
+        )
+        for index in range(count):
+            pair = index % (2 * slots)
+            block = coord_ref[index // (2 * slots), pair // 2, 1 + pair % 2]
+            to = ((block // own_blocks) ^ narrow_at) * own_blocks + block % own_blocks
+            at = index * rows // lanes * lanes
+            held_ref[to, :, at : at + lanes] += (ahead == index * rows - at).astype(jnp.float32)
+        out_ref[...] = held_ref[...].reshape(out_ref.shape).astype(jnp.bfloat16)
+
+    total = narrow_size * own_blocks
+    return kernel_call(
+        body,
+        [shaped(total * rows, count * rows, dtype=jnp.bfloat16)],
+        [coords],
+        scalars=1,
+        scratch=[pltpu.VMEM((total, rows, count * rows), jnp.float32)],
+        after=after,
+    )[0]
+
+
+def add_pieces(plan, pieces, narrow_size, after):
     low, pairs, rows, rank = pieces[0].shape
-    part_rows = own_blocks * rows
-
-    def body(coord_ref, *refs):
-        narrow_at = lax.axis_index("narrow")
-        piece_refs = refs[: len(pieces)]
-        out_refs = refs[len(pieces) : len(pieces) + narrow_size]
-        held_ref = refs[-1]
-        held_ref[...] = jnp.zeros_like(held_ref)
-        for d, piece_ref in enumerate(piece_refs):
-            for j in range(low):
-                for pair in range(pairs):
-                    block = coord_ref[d * low + j, pair // 2, 1 + pair % 2]
-                    held_ref[block] += piece_ref[j, pair]
-        for m, out_ref in enumerate(out_refs):
-            owner = narrow_at ^ m
-            part = held_ref[pl.ds(owner * own_blocks, own_blocks)]
-            out_ref[...] = part.reshape(part_rows, rank)
-
-    return kernel_call(
-        body,
-        [shaped(part_rows, rank)] * narrow_size,
-        [coords] + list(pieces),
-        scalars=1,
-        after=after,
-        scratch=[pltpu.VMEM((narrow_size * own_blocks, rows, rank), jnp.float32)],
+    part_rows = plan.shape[0] // narrow_size
+
+    def body(plan_ref, *refs):
+        terms = jnp.concatenate(
+            [ref[...].reshape(low * pairs * rows, rank) for ref in refs[: len(pieces)]], axis=0
+        )
+        high, middle, least = split3(terms)
+        wide = dot32(plan_ref[...], jnp.concatenate([high, middle], axis=1))
+        sums = (dot32(plan_ref[...], least) + wide[:, rank:]) + wide[:, :rank]
+        for m, out_ref in enumerate(refs[len(pieces) :]):
+            out_ref[...] = sums[m * part_rows : (m + 1) * part_rows]
+
+    return kernel_call(
+        body, [shaped(part_rows, rank)] * narrow_size, [plan] + list(pieces), after=after
     )
 
 
@@ -657,27 +689,33 @@
     return kernel_call(body, [shaped(*parts[0].shape)], list(parts), after=after)[0]
 
 
-def solve_rows(parts, inverse, own_blocks):
+def solve_rows(parts, inverse):
+    rows, rank = parts[0].shape
+    count = len(parts)
+
+    def body(*refs):
+        solved = times(
+            jnp.concatenate([ref[...] for ref in refs[:count]], axis=0), refs[count][...]
+        )
+        refs[-1][...] = solved.reshape(count, rows, rank)
+
+    return kernel_call(body, [shaped(count, rows, rank)], list(parts) + [inverse])[0]
+
+
+def lay_rows(parts, own_blocks):
     low = len(parts)
     partners, part_rows, rank = parts[0].shape
     rows = part_rows // own_blocks
 
     def body(*refs):
         wide_at = lax.axis_index("wide")
-        out_ref = refs[-1]
         for d in range(partners):
             for j in range(low):
-                solved = product(refs[j][d], refs[low][...]).reshape(own_blocks, rows, rank)
                 place = wide_at ^ (d * low + j)
                 for block in range(own_blocks):
-                    out_ref[block, place] = solved[block]
-
-    return kernel_call(
-        body,
-        [shaped(own_blocks, partners * low, rows, rank)],
-        list(parts) + [inverse],
-        about_us=1.5,
-    )[0]
+                    refs[-1][block, place] = refs[j][d, block * rows : (block + 1) * rows, :]
+
+    return kernel_call(body, [shaped(own_blocks, partners * low, rows, rank)], list(parts))[0]
 
 
 def on_device(blocks, block_coords, block_count, orbital_factor):
@@ -697,16 +735,16 @@
     pairs = [send_by_core(chip_slice, [m, m + 1]) for m in range(1, narrow_size - 1, low)]
     single = swap_with(own_slice, "narrow", narrow_size - 1)
     arrived = gather_from(block_coords[0, 0], "wide", skip=1)[1:]
-    tags, coords = open_tags(block_coords[0, 0], block_count, [own_slice])
-    blocks = stage(blocks[0, 0], [tags])
-    coords = pack_whole([coords] + arrived, after=[blocks])
-    mine = pack_slices(pairs, single, [coords])
+    blocks = stage(blocks[0, 0], [own_slice])
+    mine = pack_slices(pairs, single, arrived + [blocks])
     theirs = swap_with(mine, "wide", 1)
+    tags, coords = open_tags(block_coords[0, 0], block_count, rank, [mine])
+    coords = pack_whole([coords] + arrived)
     wanted = pick_pieces(coords, chip_slice, mine, theirs, narrow_size, [])
     pieces = exchange(wanted, "wide", skip=1)
 
-    turned = turn_blocks(blocks, wanted[:1])
-    rows, terms = first_mode(tags, pieces, blocks, wide_size, low, [turned])
+    spread, turned = split_blocks(blocks, wanted[:1])
+    rows, terms = first_mode(tags, pieces, spread, wide_size, low)
     inverse_b, gram_b = inverse_of(pieces, None, 1.0, after=[terms])
     terms = pack_whole(gather_from(terms, "wide", skip=1), after=[inverse_b])
     column_terms = with_partners(terms, low)
@@ -719,7 +757,8 @@
 
     gram, aux = column_gram(all_coords, column_terms, inverse_b, edge, packed[:1])
 
-    sums = add_pieces(all_coords, pieces, narrow_size, own_blocks, [gram])
+    plan = plan_sums(all_coords, slice_rows, narrow_size, own_blocks, [gram])
+    sums = add_pieces(plan, pieces, narrow_size, [])
     parts = exchange(sums, "narrow")
     step = narrow_size // 2
     while step > 1:
@@ -728,8 +767,8 @@
     aux_owned, done = own_aux(all_coords, aux, own_rows, sums[:1])
     total = add_parts(parts, [gram, done])
     (inverse_a,) = inverse_of([gram, swap_with(gram, "narrow", step)], gram_b, 2.0, [total])
-    totals = pack_whole(gather_from(total, "wide", skip=1), after=[inverse_a])
-    orbital_new = solve_rows(with_partners(totals, low), inverse_a, own_blocks)
+    solved = solve_rows(gather_from(total, "wide", skip=1), inverse_a)
+    orbital_new = lay_rows(with_partners(solved, low), own_blocks)
     return (aux_owned[None], orbital_new.reshape(own_blocks * edge, rank))
 
 

time: 65.6 us -> 63.7 us (0.971)
  waiting for transfers between devices: 12.3 us -> 10.3 us
  local copies, waits for them, and re-layouts: 3.34 us -> 2.62 us
    ppermute x25, waiting for transfers between devices: 12.3 us -> 10.3 us  [swap_with(): lax.ppermute(value, axis, [(index, index ^ mask) for index in range(size)])]
    unnamed x6, local copies, waits for them, and re-layouts: 3.33 us -> 2.61 us
    pallas_call x21 -> x22, Pallas kernels: 19.6 us -> 20 us  [kernel_call(): pl.pallas_call(whole, out_shape=outputs, in_specs=[in_smem] * scalars + [...]
  transfers between devices with their start and end apart: 26 -> 26, of which waited for: 10 -> 11; matrix products, arithmetic and copies ran while one was open for 0% -> 0% of each run, Pallas kernels for 20% -> 24%
where the time goes in v3:
time: 63.7 us; the launch traced here: 63.5 us
  starting transfers between devices  29.1 us (46%)
  Pallas kernels  20 us (31%)
  waiting for transfers between devices  10.3 us (16%)
  local copies, waits for them, and re-layouts  2.62 us (4%)
  between operations  1.56 us (2%)
    ppermute x25, starting transfers between devices, swap_with(): lax.ppermute(value, axis, [(index, index ^ mask) for index in range(size)])  26.1 us
    pallas_call x22, Pallas kernels, kernel_call(): pl.pallas_call(whole, out_shape=outputs, in_specs=[in_smem] * scalars + [...  20 us
    ppermute x25, waiting for transfers between devices, swap_with(): lax.ppermute(value, axis, [(index, index ^ mask) for index in range(size)])  10.3 us
    ppermute x1, starting transfers between devices, send_by_core(): return lax.ppermute(value, ('wide', 'narrow'), pairs)  3.09 us
    unnamed x6, local copies, waits for them, and re-layouts  2.61 us
  transfers between devices with their start and end apart: 26, of which 11 were waited for; matrix products, arithmetic and copies ran while one was open for 0% of the time, Pallas kernels for 24%

profile of v3, /device:TPU:0, one launch (start us, length us, event | category | flops | bytes accessed | tf_op | source)
XLA Modules:
  0.0 63.5 jit_solution(6591913967298609917)
XLA Ops:
  0.6 0.0 copy-start
  0.6 0.0 copy-start.2
  0.7 1.0 %copy-done = f32[1024,128]{1,0:T(8,128)S(1)} copy-done((f32[1024,128]{1,0:T(8,128)S(1)}, f32[1024,128]{1,0:T(8,128)}, u32[]{:S(2)}) %copy-start) | copy-done | bytes 524312
  1.7 3.1 %collective-permute-start = (f32[16,2,8,128]{3,2,1,0:T(8,128)S(1)}, f32[16,2,8,128]{3,2,1,0:T(8,128)S(1)}, u32[]{:S(2)}, u32[]{:S(2)}) collective-permute-start(f32[16,2,8,128]{3,2,1,0:T(8,128)S(1)} %dynamic-slice_bitcast_fusion.refs_0_.refs_1_), channel_id=1, source_target_pairs={{0,1},{1,0},{2,3},{3,2},{4,6},{5,7},{6,4},{7,5},{8,9},{9,8},{10,11... | collective-permute-start | bytes 393224 | tf_op jit(solution)/shard_map/ppermute | solution.py:78
  4.8 2.5 %collective-permute-start.1 = (f32[16,8,128]{2,1,0:T(8,128)S(1)}, f32[16,8,128]{2,1,0:T(8,128)S(1)}, u32[]{:S(2)}, u32[]{:S(2)}) collective-permute-start(f32[16,8,128]{2,1,0:T(8,128)S(1)} %shard_map.59.refs_1_), channel_id=1, source_target_pairs={{0,3},{1,2},{2,1},{3,0},{4,7},{5,6},{6,5},{7,4},{8,11},{9,10},{10,... | collective-permute-start | bytes 196616 | tf_op jit(solution)/shard_map/ppermute | solution.py:68
  7.3 2.4 %collective-permute-start.4 = (s32[2,3]{1,0:T(2,128)}, s32[2,3]{1,0:T(2,128)S(1)}, u32[]{:S(2)}, u32[]{:S(2)}) collective-permute-start(s32[2,3]{1,0:T(2,128)} %bitcast.11), channel_id=1, source_target_pairs={{0,24},{4,28},{8,16},{12,20},{16,8},{20,12},{24,0},{28,4},{1,25},{... | collective-permute-start | bytes 80 | tf_op jit(solution)/shard_map/ppermute | solution.py:68
  9.7 0.5 collective-permute-start.3
  10.2 0.5 collective-permute-start.2
  10.8 1.6 %copy-done.1 = f32[1,1,2,64,4096]{4,3,2,1,0:T(8,128)S(1)} copy-done((f32[1,1,2,64,4096]{4,3,2,1,0:T(8,128)S(1)}, f32[1,1,2,64,4096]{4,3,2,1,0:T(8,128)}, u32[]{:S(2)}) %copy-start.1) | copy-done | bytes 2097176
  12.3 0.1 shard_map.60.refs_5_.refs_0_
  12.5 1.0 %collective-permute-done.3.refs_3_.refs_2_ = s32[2,3]{1,0:T(2,128)S(1)} collective-permute-done((s32[2,3]{1,0:T(2,128)}, s32[2,3]{1,0:T(2,128)S(1)}, u32[]{:S(2)}, u32[]{:S(2)}) %collective-permute-start.3) | collective-permute-done | bytes 56 | tf_op jit(solution)/shard_map/ppermute | solution.py:68
  13.5 0.5 collective-permute-done.2.refs_2_.refs_1_
  14.0 0.0 collective-permute-done.1.refs_1_
  14.0 0.0 collective-permute-done.refs_0_
  14.0 0.1 collective-permute-start.5
  14.8 0.1 shard_map.62
  14.8 0.7 %collective-permute-done.5.refs_3_ = f32[48,8,128]{2,1,0:T(8,128)S(1)} collective-permute-done((f32[48,8,128]{2,1,0:T(8,128)S(1)}, f32[48,8,128]{2,1,0:T(8,128)S(1)}, u32[]{:S(2)}, u32[]{:S(2)}) %collective-permute-start.5) | collective-permute-done | bytes 196640 | tf_op jit(solution)/shard_map/ppermute | solution.py:68
  15.5 1.0 %shard_map.64 = (f32[192,128]{1,0:T(8,128)S(1)}, f32[192,128]{1,0:T(8,128)S(1)}, f32[192,128]{1,0:T(8,128)S(1)}, f32[192,128]{1,0:T(8,128)S(1)}) custom-call(s32[4,2,3]{2,1,0:T(2,128)S(1)} %shard_map.63.refs_0_, f32[16,2,8,128]{3,2,1,0:T(8,128)S(1)} %dynamic-slice_bitcast_fusion.refs_0_.refs_1_, f32[48,8,128]{2,1,0:T(8,128)S(1)} %shard_map.61.refs_2_, ...), custom_call_target="tpu_custom_call" | custom-call | flops 300000 | tf_op jit(solution)/shard_map/pallas_call | solution.py:30
  16.5 0.6 collective-permute-start.6
  17.1 1.5 %collective-permute-start.7 = (f32[192,128]{1,0:T(8,128)S(1)}, f32[192,128]{1,0:T(8,128)S(1)}, u32[]{:S(2)}, u32[]{:S(2)}) collective-permute-start(f32[192,128]{1,0:T(8,128)S(1)} %get-tuple-element.32), channel_id=1, source_target_pairs={{0,16},{4,20},{8,24},{12,28},{16,0},{20,4},{24,8},{28,12},{1,17},{... | collective-permute-start | bytes 294920 | tf_op jit(solution)/shard_map/ppermute | solution.py:68
  18.6 1.4 %collective-permute-start.8 = (f32[192,128]{1,0:T(8,128)S(1)}, f32[192,128]{1,0:T(8,128)S(1)}, u32[]{:S(2)}, u32[]{:S(2)}) collective-permute-start(f32[192,128]{1,0:T(8,128)S(1)} %get-tuple-element.33), channel_id=1, source_target_pairs={{0,24},{4,28},{8,16},{12,20},{16,8},{20,12},{24,0},{28,4},{1,25},{... | collective-permute-start | bytes 294920 | tf_op jit(solution)/shard_map/ppermute | solution.py:68
  20.1 3.1 %shard_map.65 = (bf16[2,4096,256]{2,1,0:T(8,128)(2,1)S(1)}, bf16[2,4096,256]{2,1,0:T(8,128)(2,1)S(1)}) custom-call(f32[2,64,4096]{2,1,0:T(8,128)S(1)} %shard_map.60.refs_5_.refs_0_, f32[192,128]{1,0:T(8,128)S(1)} %get-tuple-element.30.refs_1_.refs_0_), custom_call_target="tpu_custom_call" | custom-call | flops 300000 | tf_op jit(solution)/shard_map/pallas_call | solution.py:30
  23.2 0.0 collective-permute-done.7.refs_3_.refs_2_
  23.2 1.2 %collective-permute-done.8.refs_4_.refs_3_ = f32[192,128]{1,0:T(8,128)S(1)} collective-permute-done((f32[192,128]{1,0:T(8,128)S(1)}, f32[192,128]{1,0:T(8,128)S(1)}, u32[]{:S(2)}, u32[]{:S(2)}) %collective-permute-start.8) | collective-permute-done | bytes 98336 | tf_op jit(solution)/shard_map/ppermute | solution.py:68
  24.5 1.3 %shard_map.66 = (f32[4,64,128]{2,1,0:T(8,128)S(1)}, f32[136,128]{1,0:T(8,128)S(1)}) custom-call(f32[8,128]{1,0:T(8,128)S(1)} %get-tuple-element.28.refs_0_, f32[192,128]{1,0:T(8,128)S(1)} %get-tuple-element.30.refs_1_.refs_0_, f32[192,128]{1,0:T(8,128)S(1)} %collective-permute-done.6.refs_2_.refs_1_, f32[192,128]{1,0:T(8,128)S(1)} %collective-permute-done.7.refs_3_.refs_2_, ...), custom_call_target="tpu_custom_call" | custom-call | flops 3000000 | tf_op jit(solution)/shard_map/pallas_call | solution.py:30
  25.8 1.9 %collective-permute-start.11 = (f32[136,128]{1,0:T(8,128)S(1)}, f32[136,128]{1,0:T(8,128)S(1)}, u32[]{:S(2)}, u32[]{:S(2)}) collective-permute-start(f32[136,128]{1,0:T(8,128)S(1)} %get-tuple-element.35.refs_4_.refs_0_), channel_id=1, source_target_pairs={{0,24},{4,28},{8,16},{12,20},{16,8},{20,12},{24,0},{28,4},{1,25},{... | collective-permute-start | bytes 208904 | tf_op jit(solution)/shard_map/ppermute | solution.py:68
  27.6 0.8 %collective-permute-start.10 = (f32[136,128]{1,0:T(8,128)S(1)}, f32[136,128]{1,0:T(8,128)S(1)}, u32[]{:S(2)}, u32[]{:S(2)}) collective-permute-start(f32[136,128]{1,0:T(8,128)S(1)} %get-tuple-element.35.refs_4_.refs_0_), channel_id=1, source_target_pairs={{0,16},{4,20},{8,24},{12,28},{16,0},{20,4},{24,8},{28,12},{1,17},{... | collective-permute-start | bytes 208904 | tf_op jit(solution)/shard_map/ppermute | solution.py:68
  28.5 0.9 %collective-permute-start.9 = (f32[136,128]{1,0:T(8,128)S(1)}, f32[136,128]{1,0:T(8,128)S(1)}, u32[]{:S(2)}, u32[]{:S(2)}) collective-permute-start(f32[136,128]{1,0:T(8,128)S(1)} %get-tuple-element.35.refs_4_.refs_0_), channel_id=1, source_target_pairs={{0,8},{4,12},{8,0},{12,4},{16,24},{20,28},{24,16},{28,20},{1,9},{5... | collective-permute-start | bytes 208904 | tf_op jit(solution)/shard_map/ppermute | solution.py:68
  29.3 3.5 %shard_map.67 = (f32[128,128]{1,0:T(8,128)S(1)}, f32[128,128]{1,0:T(8,128)S(1)}) custom-call(f32[192,128]{1,0:T(8,128)S(1)} %get-tuple-element.30.refs_1_.refs_0_, f32[192,128]{1,0:T(8,128)S(1)} %collective-permute-done.6.refs_2_.refs_1_, f32[192,128]{1,0:T(8,128)S(1)} %collective-permute-done.7.refs_3_.refs_2_, ...), custom_call_target="tpu_custom_call" | custom-call | flops 3500000 | tf_op jit(solution)/shard_map/pallas_call | solution.py:30
  32.8 0.0 collective-permute-done.11.refs_3_
  32.8 0.0 collective-permute-done.10.refs_2_
  32.8 0.1 collective-permute-start.12
  32.9 1.5 %collective-permute-done.12.refs_1_.refs_2_ = f32[4,136,128]{2,1,0:T(8,128)S(1)} collective-permute-done((f32[4,136,128]{2,1,0:T(8,128)S(1)}, f32[4,136,128]{2,1,0:T(8,128)S(1)}, u32[]{:S(2)}, u32[]{:S(2)}) %collective-permute-start.12) | collective-permute-done | bytes 278560 | tf_op jit(solution)/shard_map/ppermute | solution.py:68
  34.5 1.5 %shard_map.70 = (f32[4,4,8,128]{3,2,1,0:T(8,128)S(1)}, f32[4,4,8,128]{3,2,1,0:T(8,128)S(1)}) custom-call(f32[4,136,128]{2,1,0:T(8,128)S(1)} %shard_map.68.refs_0_.refs_1_, f32[4,136,128]{2,1,0:T(8,128)S(1)} %collective-permute-done.12.refs_1_.refs_2_, f32[128,128]{1,0:T(8,128)S(1)} %get-tuple-element.36.refs_4_.refs_2_.refs_3_, ...), custom_call_target="tpu_custom_call" | custom-call | flops 2500000 | tf_op jit(solution)/shard_map/pallas_call | solution.py:30
  36.0 0.2 collective-permute-start.13
  36.2 1.1 %collective-permute-done.13.refs_1_ = f32[4,4,8,128]{3,2,1,0:T(8,128)S(1)} collective-permute-done((f32[4,4,8,128]{3,2,1,0:T(8,128)S(1)}, f32[4,4,8,128]{3,2,1,0:T(8,128)S(1)}, u32[]{:S(2)}, u32[]{:S(2)}) %collective-permute-start.13) | collective-permute-done | bytes 65568 | tf_op jit(solution)/shard_map/ppermute | solution.py:68
  37.3 1.2 %collective-permute-start.14 = (f32[2,4,8,128]{3,2,1,0:T(8,128)S(1)}, f32[2,4,8,128]{3,2,1,0:T(8,128)S(1)}, u32[]{:S(2)}, u32[]{:S(2)}) collective-permute-start(f32[2,4,8,128]{3,2,1,0:T(8,128)S(1)} %get-tuple-element.44), channel_id=1, source_target_pairs={{0,8},{4,12},{8,0},{12,4},{16,24},{20,28},{24,16},{28,20},{1,9},{5... | collective-permute-start | bytes 98312 | tf_op jit(solution)/shard_map/ppermute | solution.py:68
  38.6 1.2 %collective-permute-start.15 = (f32[2,4,8,128]{3,2,1,0:T(8,128)S(1)}, f32[2,4,8,128]{3,2,1,0:T(8,128)S(1)}, u32[]{:S(2)}, u32[]{:S(2)}) collective-permute-start(f32[2,4,8,128]{3,2,1,0:T(8,128)S(1)} %get-tuple-element.45), channel_id=1, source_target_pairs={{0,16},{4,20},{8,24},{12,28},{16,0},{20,4},{24,8},{28,12},{1,17},{... | collective-permute-start | bytes 98312 | tf_op jit(solution)/shard_map/ppermute | solution.py:68
  39.8 1.1 %collective-permute-start.16 = (f32[2,4,8,128]{3,2,1,0:T(8,128)S(1)}, f32[2,4,8,128]{3,2,1,0:T(8,128)S(1)}, u32[]{:S(2)}, u32[]{:S(2)}) collective-permute-start(f32[2,4,8,128]{3,2,1,0:T(8,128)S(1)} %get-tuple-element.46), channel_id=1, source_target_pairs={{0,24},{4,28},{8,16},{12,20},{16,8},{20,12},{24,0},{28,4},{1,25},{... | collective-permute-start | bytes 98312 | tf_op jit(solution)/shard_map/ppermute | solution.py:68
  40.9 1.6 %shard_map.72 = (f32[128,128]{1,0:T(8,128)S(1)}, f32[16,64,128]{2,1,0:T(8,128)S(1)}) custom-call(s32[8,2,3]{2,1,0:T(2,128)S(1)} %shard_map.69.refs_0_, f32[4,136,128]{2,1,0:T(8,128)S(1)} %shard_map.68.refs_0_.refs_1_, f32[4,136,128]{2,1,0:T(8,128)S(1)} %collective-permute-done.12.refs_1_.refs_2_, f32[128,128]{1,0:T(8,128)S(1)} %get-tuple-element.36.refs_4_.refs_2_.refs_3_, ...), custom_call_target="tpu_custom_call" | custom-call | flops 100000 | tf_op jit(solution)/shard_map/pallas_call | solution.py:30
  42.5 0.9 %collective-permute-start.20 = (f32[128,128]{1,0:T(8,128)S(1)}, f32[128,128]{1,0:T(8,128)S(1)}, u32[]{:S(2)}, u32[]{:S(2)}) collective-permute-start(f32[128,128]{1,0:T(8,128)S(1)} %get-tuple-element.43.refs_1_.refs_0_), channel_id=1, source_target_pairs={{0,2},{1,3},{2,0},{3,1},{4,6},{5,7},{6,4},{7,5},{8,10},{9,11},{10,... | collective-permute-start | bytes 196616 | tf_op jit(solution)/shard_map/ppermute | solution.py:68
  43.4 0.9 %shard_map.73.refs_0_ = bf16[512,256]{1,0:T(8,128)(2,1)S(1)} custom-call(s32[8,2,3]{2,1,0:T(2,128)S(1)} %shard_map.69.refs_0_, f32[128,128]{1,0:T(8,128)S(1)} %get-tuple-element.43.refs_1_.refs_0_), custom_call_target="tpu_custom_call" | custom-call | flops 300000 | tf_op jit(solution)/shard_map/pallas_call | solution.py:30
  44.3 0.0 collective-permute-done.14.refs_2_
  44.4 0.2 collective-permute-done.16.refs_4_
  44.6 0.3 shard_map.74
  44.9 0.9 %collective-permute-start.17 = (f32[128,128]{1,0:T(8,128)S(1)}, f32[128,128]{1,0:T(8,128)S(1)}, u32[]{:S(2)}, u32[]{:S(2)}) collective-permute-start(f32[128,128]{1,0:T(8,128)S(1)} %get-tuple-element.49), channel_id=1, source_target_pairs={{0,1},{1,0},{2,3},{3,2},{4,5},{5,4},{6,7},{7,6},{8,9},{9,8},{10,11... | collective-permute-start | bytes 196616 | tf_op jit(solution)/shard_map/ppermute | solution.py:68
  45.8 1.7 %collective-permute-start.18 = (f32[128,128]{1,0:T(8,128)S(1)}, f32[128,128]{1,0:T(8,128)S(1)}, u32[]{:S(2)}, u32[]{:S(2)}) collective-permute-start(f32[128,128]{1,0:T(8,128)S(1)} %get-tuple-element.50), channel_id=1, source_target_pairs={{0,2},{1,3},{2,0},{3,1},{4,6},{5,7},{6,4},{7,5},{8,10},{9,11},{10,... | collective-permute-start | bytes 196616 | tf_op jit(solution)/shard_map/ppermute | solution.py:68
  47.5 1.9 %collective-permute-start.19 = (f32[128,128]{1,0:T(8,128)S(1)}, f32[128,128]{1,0:T(8,128)S(1)}, u32[]{:S(2)}, u32[]{:S(2)}) collective-permute-start(f32[128,128]{1,0:T(8,128)S(1)} %get-tuple-element.51), channel_id=1, source_target_pairs={{0,3},{1,2},{2,1},{3,0},{4,7},{5,6},{6,5},{7,4},{8,11},{9,10},{10,... | collective-permute-start | bytes 196616 | tf_op jit(solution)/shard_map/ppermute | solution.py:68
  49.4 0.1 collective-permute-done.20.refs_1_
  49.5 0.1 collective-permute-start.24
  49.6 1.9 %shard_map.75 = (f32[8,64,128]{2,1,0:T(8,128)}, f32[8,128]{1,0:T(8,128)S(1)}) custom-call(s32[8,2,3]{2,1,0:T(2,128)S(1)} %shard_map.69.refs_0_, f32[16,64,128]{2,1,0:T(8,128)S(1)} %get-tuple-element.42.refs_1_, f32[128,128]{1,0:T(8,128)S(1)} %get-tuple-element.47.refs_2_.refs_0_), custom_call_target="tpu_custom_call" | custom-call | flops 100000 | tf_op jit(solution)/shard_map/pallas_call | solution.py:30
  51.4 0.0 collective-permute-done.17.refs_1_
  51.4 1.2 %collective-permute-done.18.refs_2_ = f32[128,128]{1,0:T(8,128)S(1)} collective-permute-done((f32[128,128]{1,0:T(8,128)S(1)}, f32[128,128]{1,0:T(8,128)S(1)}, u32[]{:S(2)}, u32[]{:S(2)}) %collective-permute-start.18) | collective-permute-done | bytes 65568 | tf_op jit(solution)/shard_map/ppermute | solution.py:68
  52.6 1.1 %collective-permute-done.19.refs_3_ = f32[128,128]{1,0:T(8,128)S(1)} collective-permute-done((f32[128,128]{1,0:T(8,128)S(1)}, f32[128,128]{1,0:T(8,128)S(1)}, u32[]{:S(2)}, u32[]{:S(2)}) %collective-permute-start.19) | collective-permute-done | bytes 65568 | tf_op jit(solution)/shard_map/ppermute | solution.py:68
  53.7 1.9 %collective-permute-start.23 = (f32[128,128]{1,0:T(8,128)S(1)}, f32[128,128]{1,0:T(8,128)S(1)}, u32[]{:S(2)}, u32[]{:S(2)}) collective-permute-start(f32[128,128]{1,0:T(8,128)S(1)} %shard_map.77.refs_3_.refs_0_), channel_id=1, source_target_pairs={{0,24},{4,28},{8,16},{12,20},{16,8},{20,12},{24,0},{28,4},{1,25},{... | collective-permute-start | bytes 196616 | tf_op jit(solution)/shard_map/ppermute | solution.py:68
  55.6 0.8 %collective-permute-start.22 = (f32[128,128]{1,0:T(8,128)S(1)}, f32[128,128]{1,0:T(8,128)S(1)}, u32[]{:S(2)}, u32[]{:S(2)}) collective-permute-start(f32[128,128]{1,0:T(8,128)S(1)} %shard_map.77.refs_3_.refs_0_), channel_id=1, source_target_pairs={{0,16},{4,20},{8,24},{12,28},{16,0},{20,4},{24,8},{28,12},{1,17},{... | collective-permute-start | bytes 196616 | tf_op jit(solution)/shard_map/ppermute | solution.py:68
  56.4 0.9 %collective-permute-start.21 = (f32[128,128]{1,0:T(8,128)S(1)}, f32[128,128]{1,0:T(8,128)S(1)}, u32[]{:S(2)}, u32[]{:S(2)}) collective-permute-start(f32[128,128]{1,0:T(8,128)S(1)} %shard_map.77.refs_3_.refs_0_), channel_id=1, source_target_pairs={{0,8},{4,12},{8,0},{12,4},{16,24},{20,28},{24,16},{28,20},{1,9},{5... | collective-permute-start | bytes 196616 | tf_op jit(solution)/shard_map/ppermute | solution.py:68
  57.3 0.0 collective-permute-done.24.refs_1_
  57.3 3.4 %shard_map.78.refs_4_ = f32[128,128]{1,0:T(8,128)S(1)} custom-call(f32[128,128]{1,0:T(8,128)S(1)} %shard_map.76.refs_4_.refs_0_, f32[128,128]{1,0:T(8,128)S(1)} %collective-permute-done.24.refs_1_, f32[128,128]{1,0:T(8,128)S(1)} %get-tuple-element.53.refs_2_, f32[128,128]{1,0:T(8,128)S(1)} %shard_map.77.refs_3_.refs_0_), custom_call_target="tpu_custom_call" | custom-call | flops 3500000 | tf_op jit(solution)/shard_map/pallas_call | solution.py:30
  60.7 0.0 collective-permute-done.22.refs_2_
  60.8 0.3 shard_map.79.refs_0_
  61.1 0.1 collective-permute-start.25
  61.2 1.5 %collective-permute-done.25.refs_1_ = f32[4,128,128]{2,1,0:T(8,128)S(1)} collective-permute-done((f32[4,128,128]{2,1,0:T(8,128)S(1)}, f32[4,128,128]{2,1,0:T(8,128)S(1)}, u32[]{:S(2)}, u32[]{:S(2)}) %collective-permute-start.25) | collective-permute-done | bytes 262176 | tf_op jit(solution)/shard_map/ppermute | solution.py:68
  62.7 0.9 %shard_map.80 = f32[16,8,8,128]{3,2,1,0:T(8,128)} custom-call(f32[4,128,128]{2,1,0:T(8,128)S(1)} %shard_map.79.refs_0_, f32[4,128,128]{2,1,0:T(8,128)S(1)} %collective-permute-done.25.refs_1_), custom_call_target="tpu_custom_call" | custom-call | flops 300000 | tf_op jit(solution)/shard_map/pallas_call | solution.py:30
  (17 shorter events, 0.1 us)
Async XLA Ops:
  0.6 1.0 %copy-start = (f32[1024,128]{1,0:T(8,128)S(1)}, f32[1024,128]{1,0:T(8,128)}, u32[]{:S(2)}) copy-start(f32[1024,128]{1,0:T(8,128)} %param.7) | copy-start | bytes 1572868
  0.6 14.1 %copy-start.2 = (s32[1,1,2,3]{3,2,1,0:T(2,128)S(1)}, s32[1,1,2,3]{3,2,1,0:T(2,128)}, u32[]{:S(2)}) copy-start(s32[1,1,2,3]{3,2,1,0:T(2,128)} %param.5) | copy-start | bytes 76
  1.7 12.3 %collective-permute-start = (f32[16,2,8,128]{3,2,1,0:T(8,128)S(1)}, f32[16,2,8,128]{3,2,1,0:T(8,128)S(1)}, u32[]{:S(2)}, u32[]{:S(2)}) collective-permute-start(f32[16,2,8,128]{3,2,1,0:T(8,128)S(1)} %dynamic-slice_bitcast_fusion.refs_0_.refs_1_), channel_id=1, source_target_pairs={{0,1},{1,0},{2,3},{3,2},{4,6},{5,7},{6,4},{7,5},{8,9},{9,8},{10,11... | collective-permute-start | bytes 393224 | tf_op jit(solution)/shard_map/ppermute | solution.py:78
  4.8 9.2 %collective-permute-start.1 = (f32[16,8,128]{2,1,0:T(8,128)S(1)}, f32[16,8,128]{2,1,0:T(8,128)S(1)}, u32[]{:S(2)}, u32[]{:S(2)}) collective-permute-start(f32[16,8,128]{2,1,0:T(8,128)S(1)} %shard_map.59.refs_1_), channel_id=1, source_target_pairs={{0,3},{1,2},{2,1},{3,0},{4,7},{5,6},{6,5},{7,4},{8,11},{9,10},{10,... | collective-permute-start | bytes 196616 | tf_op jit(solution)/shard_map/ppermute | solution.py:68
  7.3 5.2 %collective-permute-start.4 = (s32[2,3]{1,0:T(2,128)}, s32[2,3]{1,0:T(2,128)S(1)}, u32[]{:S(2)}, u32[]{:S(2)}) collective-permute-start(s32[2,3]{1,0:T(2,128)} %bitcast.11), channel_id=1, source_target_pairs={{0,24},{4,28},{8,16},{12,20},{16,8},{20,12},{24,0},{28,4},{1,25},{... | collective-permute-start | bytes 80 | tf_op jit(solution)/shard_map/ppermute | solution.py:68
  9.7 3.8 %collective-permute-start.3 = (s32[2,3]{1,0:T(2,128)}, s32[2,3]{1,0:T(2,128)S(1)}, u32[]{:S(2)}, u32[]{:S(2)}) collective-permute-start(s32[2,3]{1,0:T(2,128)} %bitcast.12), channel_id=1, source_target_pairs={{0,16},{4,20},{8,24},{12,28},{16,0},{20,4},{24,8},{28,12},{1,17},{... | collective-permute-start | bytes 80 | tf_op jit(solution)/shard_map/ppermute | solution.py:68
  10.2 3.8 %collective-permute-start.2 = (s32[2,3]{1,0:T(2,128)}, s32[2,3]{1,0:T(2,128)S(1)}, u32[]{:S(2)}, u32[]{:S(2)}) collective-permute-start(s32[2,3]{1,0:T(2,128)} %bitcast.13), channel_id=1, source_target_pairs={{0,8},{4,12},{8,0},{12,4},{16,24},{20,28},{24,16},{28,20},{1,9},{5... | collective-permute-start | bytes 80 | tf_op jit(solution)/shard_map/ppermute | solution.py:68
  10.8 1.6 %copy-start.1 = (f32[1,1,2,64,4096]{4,3,2,1,0:T(8,128)S(1)}, f32[1,1,2,64,4096]{4,3,2,1,0:T(8,128)}, u32[]{:S(2)}) copy-start(f32[1,1,2,64,4096]{4,3,2,1,0:T(8,128)} %param.4) | copy-start | bytes 6291460
  14.0 1.5 %collective-permute-start.5 = (f32[48,8,128]{2,1,0:T(8,128)S(1)}, f32[48,8,128]{2,1,0:T(8,128)S(1)}, u32[]{:S(2)}, u32[]{:S(2)}) collective-permute-start(f32[48,8,128]{2,1,0:T(8,128)S(1)} %shard_map.61.refs_2_), channel_id=1, source_target_pairs={{0,4},{4,0},{8,12},{12,8},{16,20},{20,16},{24,28},{28,24},{1,5},{5... | collective-permute-start | bytes 589832 | tf_op jit(solution)/shard_map/ppermute | solution.py:68
  16.5 6.7 %collective-permute-start.6 = (f32[192,128]{1,0:T(8,128)S(1)}, f32[192,128]{1,0:T(8,128)S(1)}, u32[]{:S(2)}, u32[]{:S(2)}) collective-permute-start(f32[192,128]{1,0:T(8,128)S(1)} %get-tuple-element.31), channel_id=1, source_target_pairs={{0,8},{4,12},{8,0},{12,4},{16,24},{20,28},{24,16},{28,20},{1,9},{5... | collective-permute-start | bytes 294920 | tf_op jit(solution)/shard_map/ppermute | solution.py:68
  17.1 6.1 %collective-permute-start.7 = (f32[192,128]{1,0:T(8,128)S(1)}, f32[192,128]{1,0:T(8,128)S(1)}, u32[]{:S(2)}, u32[]{:S(2)}) collective-permute-start(f32[192,128]{1,0:T(8,128)S(1)} %get-tuple-element.32), channel_id=1, source_target_pairs={{0,16},{4,20},{8,24},{12,28},{16,0},{20,4},{24,8},{28,12},{1,17},{... | collective-permute-start | bytes 294920 | tf_op jit(solution)/shard_map/ppermute | solution.py:68
  18.6 5.8 %collective-permute-start.8 = (f32[192,128]{1,0:T(8,128)S(1)}, f32[192,128]{1,0:T(8,128)S(1)}, u32[]{:S(2)}, u32[]{:S(2)}) collective-permute-start(f32[192,128]{1,0:T(8,128)S(1)} %get-tuple-element.33), channel_id=1, source_target_pairs={{0,24},{4,28},{8,16},{12,20},{16,8},{20,12},{24,0},{28,4},{1,25},{... | collective-permute-start | bytes 294920 | tf_op jit(solution)/shard_map/ppermute | solution.py:68
  25.8 7.0 %collective-permute-start.11 = (f32[136,128]{1,0:T(8,128)S(1)}, f32[136,128]{1,0:T(8,128)S(1)}, u32[]{:S(2)}, u32[]{:S(2)}) collective-permute-start(f32[136,128]{1,0:T(8,128)S(1)} %get-tuple-element.35.refs_4_.refs_0_), channel_id=1, source_target_pairs={{0,24},{4,28},{8,16},{12,20},{16,8},{20,12},{24,0},{28,4},{1,25},{... | collective-permute-start | bytes 208904 | tf_op jit(solution)/shard_map/ppermute | solution.py:68
  27.6 5.1 %collective-permute-start.10 = (f32[136,128]{1,0:T(8,128)S(1)}, f32[136,128]{1,0:T(8,128)S(1)}, u32[]{:S(2)}, u32[]{:S(2)}) collective-permute-start(f32[136,128]{1,0:T(8,128)S(1)} %get-tuple-element.35.refs_4_.refs_0_), channel_id=1, source_target_pairs={{0,16},{4,20},{8,24},{12,28},{16,0},{20,4},{24,8},{28,12},{1,17},{... | collective-permute-start | bytes 208904 | tf_op jit(solution)/shard_map/ppermute | solution.py:68
  28.5 4.3 %collective-permute-start.9 = (f32[136,128]{1,0:T(8,128)S(1)}, f32[136,128]{1,0:T(8,128)S(1)}, u32[]{:S(2)}, u32[]{:S(2)}) collective-permute-start(f32[136,128]{1,0:T(8,128)S(1)} %get-tuple-element.35.refs_4_.refs_0_), channel_id=1, source_target_pairs={{0,8},{4,12},{8,0},{12,4},{16,24},{20,28},{24,16},{28,20},{1,9},{5... | collective-permute-start | bytes 208904 | tf_op jit(solution)/shard_map/ppermute | solution.py:68
  32.8 1.6 %collective-permute-start.12 = (f32[4,136,128]{2,1,0:T(8,128)S(1)}, f32[4,136,128]{2,1,0:T(8,128)S(1)}, u32[]{:S(2)}, u32[]{:S(2)}) collective-permute-start(f32[4,136,128]{2,1,0:T(8,128)S(1)} %shard_map.68.refs_0_.refs_1_), channel_id=1, source_target_pairs={{0,4},{4,0},{8,12},{12,8},{16,20},{20,16},{24,28},{28,24},{1,5},{5... | collective-permute-start | bytes 835592 | tf_op jit(solution)/shard_map/ppermute | solution.py:68
  36.0 1.3 %collective-permute-start.13 = (f32[4,4,8,128]{3,2,1,0:T(8,128)S(1)}, f32[4,4,8,128]{3,2,1,0:T(8,128)S(1)}, u32[]{:S(2)}, u32[]{:S(2)}) collective-permute-start(f32[4,4,8,128]{3,2,1,0:T(8,128)S(1)} %get-tuple-element.40), channel_id=1, source_target_pairs={{0,4},{4,0},{8,12},{12,8},{16,20},{20,16},{24,28},{28,24},{1,5},{5... | collective-permute-start | bytes 196616 | tf_op jit(solution)/shard_map/ppermute | solution.py:68
  37.3 7.0 %collective-permute-start.14 = (f32[2,4,8,128]{3,2,1,0:T(8,128)S(1)}, f32[2,4,8,128]{3,2,1,0:T(8,128)S(1)}, u32[]{:S(2)}, u32[]{:S(2)}) collective-permute-start(f32[2,4,8,128]{3,2,1,0:T(8,128)S(1)} %get-tuple-element.44), channel_id=1, source_target_pairs={{0,8},{4,12},{8,0},{12,4},{16,24},{20,28},{24,16},{28,20},{1,9},{5... | collective-permute-start | bytes 98312 | tf_op jit(solution)/shard_map/ppermute | solution.py:68
  38.6 5.8 %collective-permute-start.15 = (f32[2,4,8,128]{3,2,1,0:T(8,128)S(1)}, f32[2,4,8,128]{3,2,1,0:T(8,128)S(1)}, u32[]{:S(2)}, u32[]{:S(2)}) collective-permute-start(f32[2,4,8,128]{3,2,1,0:T(8,128)S(1)} %get-tuple-element.45), channel_id=1, source_target_pairs={{0,16},{4,20},{8,24},{12,28},{16,0},{20,4},{24,8},{28,12},{1,17},{... | collective-permute-start | bytes 98312 | tf_op jit(solution)/shard_map/ppermute | solution.py:68
  39.8 4.8 %collective-permute-start.16 = (f32[2,4,8,128]{3,2,1,0:T(8,128)S(1)}, f32[2,4,8,128]{3,2,1,0:T(8,128)S(1)}, u32[]{:S(2)}, u32[]{:S(2)}) collective-permute-start(f32[2,4,8,128]{3,2,1,0:T(8,128)S(1)} %get-tuple-element.46), channel_id=1, source_target_pairs={{0,24},{4,28},{8,16},{12,20},{16,8},{20,12},{24,0},{28,4},{1,25},{... | collective-permute-start | bytes 98312 | tf_op jit(solution)/shard_map/ppermute | solution.py:68
  42.5 7.0 %collective-permute-start.20 = (f32[128,128]{1,0:T(8,128)S(1)}, f32[128,128]{1,0:T(8,128)S(1)}, u32[]{:S(2)}, u32[]{:S(2)}) collective-permute-start(f32[128,128]{1,0:T(8,128)S(1)} %get-tuple-element.43.refs_1_.refs_0_), channel_id=1, source_target_pairs={{0,2},{1,3},{2,0},{3,1},{4,6},{5,7},{6,4},{7,5},{8,10},{9,11},{10,... | collective-permute-start | bytes 196616 | tf_op jit(solution)/shard_map/ppermute | solution.py:68
  44.9 6.5 %collective-permute-start.17 = (f32[128,128]{1,0:T(8,128)S(1)}, f32[128,128]{1,0:T(8,128)S(1)}, u32[]{:S(2)}, u32[]{:S(2)}) collective-permute-start(f32[128,128]{1,0:T(8,128)S(1)} %get-tuple-element.49), channel_id=1, source_target_pairs={{0,1},{1,0},{2,3},{3,2},{4,5},{5,4},{6,7},{7,6},{8,9},{9,8},{10,11... | collective-permute-start | bytes 196616 | tf_op jit(solution)/shard_map/ppermute | solution.py:68
  45.8 6.8 %collective-permute-start.18 = (f32[128,128]{1,0:T(8,128)S(1)}, f32[128,128]{1,0:T(8,128)S(1)}, u32[]{:S(2)}, u32[]{:S(2)}) collective-permute-start(f32[128,128]{1,0:T(8,128)S(1)} %get-tuple-element.50), channel_id=1, source_target_pairs={{0,2},{1,3},{2,0},{3,1},{4,6},{5,7},{6,4},{7,5},{8,10},{9,11},{10,... | collective-permute-start | bytes 196616 | tf_op jit(solution)/shard_map/ppermute | solution.py:68
  47.5 6.2 %collective-permute-start.19 = (f32[128,128]{1,0:T(8,128)S(1)}, f32[128,128]{1,0:T(8,128)S(1)}, u32[]{:S(2)}, u32[]{:S(2)}) collective-permute-start(f32[128,128]{1,0:T(8,128)S(1)} %get-tuple-element.51), channel_id=1, source_target_pairs={{0,3},{1,2},{2,1},{3,0},{4,7},{5,6},{6,5},{7,4},{8,11},{9,10},{10,... | collective-permute-start | bytes 196616 | tf_op jit(solution)/shard_map/ppermute | solution.py:68
  49.5 7.8 %collective-permute-start.24 = (f32[128,128]{1,0:T(8,128)S(1)}, f32[128,128]{1,0:T(8,128)S(1)}, u32[]{:S(2)}, u32[]{:S(2)}) collective-permute-start(f32[128,128]{1,0:T(8,128)S(1)} %shard_map.76.refs_4_.refs_0_), channel_id=1, source_target_pairs={{0,1},{1,0},{2,3},{3,2},{4,5},{5,4},{6,7},{7,6},{8,9},{9,8},{10,11... | collective-permute-start | bytes 196616 | tf_op jit(solution)/shard_map/ppermute | solution.py:68
  53.7 7.0 %collective-permute-start.23 = (f32[128,128]{1,0:T(8,128)S(1)}, f32[128,128]{1,0:T(8,128)S(1)}, u32[]{:S(2)}, u32[]{:S(2)}) collective-permute-start(f32[128,128]{1,0:T(8,128)S(1)} %shard_map.77.refs_3_.refs_0_), channel_id=1, source_target_pairs={{0,24},{4,28},{8,16},{12,20},{16,8},{20,12},{24,0},{28,4},{1,25},{... | collective-permute-start | bytes 196616 | tf_op jit(solution)/shard_map/ppermute | solution.py:68
  55.6 5.1 %collective-permute-start.22 = (f32[128,128]{1,0:T(8,128)S(1)}, f32[128,128]{1,0:T(8,128)S(1)}, u32[]{:S(2)}, u32[]{:S(2)}) collective-permute-start(f32[128,128]{1,0:T(8,128)S(1)} %shard_map.77.refs_3_.refs_0_), channel_id=1, source_target_pairs={{0,16},{4,20},{8,24},{12,28},{16,0},{20,4},{24,8},{28,12},{1,17},{... | collective-permute-start | bytes 196616 | tf_op jit(solution)/shard_map/ppermute | solution.py:68
  56.4 4.3 %collective-permute-start.21 = (f32[128,128]{1,0:T(8,128)S(1)}, f32[128,128]{1,0:T(8,128)S(1)}, u32[]{:S(2)}, u32[]{:S(2)}) collective-permute-start(f32[128,128]{1,0:T(8,128)S(1)} %shard_map.77.refs_3_.refs_0_), channel_id=1, source_target_pairs={{0,8},{4,12},{8,0},{12,4},{16,24},{20,28},{24,16},{28,20},{1,9},{5... | collective-permute-start | bytes 196616 | tf_op jit(solution)/shard_map/ppermute | solution.py:68
  61.1 1.6 %collective-permute-start.25 = (f32[4,128,128]{2,1,0:T(8,128)S(1)}, f32[4,128,128]{2,1,0:T(8,128)S(1)}, u32[]{:S(2)}, u32[]{:S(2)}) collective-permute-start(f32[4,128,128]{2,1,0:T(8,128)S(1)} %shard_map.79.refs_0_), channel_id=1, source_target_pairs={{0,4},{4,0},{8,12},{12,8},{16,20},{20,16},{24,28},{28,24},{1,5},{5... | collective-permute-start | bytes 786440 | tf_op jit(solution)/shard_map/ppermute | solution.py:68

commit v4 on v3

--- a/solution.py
+++ b/solution.py
@@ -83,7 +83,7 @@
     held = {0: value}
     for stride, radix in reversed(digits[skip:]):
         fresh = {}
-        for digit in range(1, radix):
+        for digit in reversed(range(1, radix)):
             for key, item in held.items():
                 fresh[key + digit * stride] = swap_with(item, axis, digit * stride)
         held.update(fresh)
@@ -96,7 +96,7 @@
     items = list(items)
     for stride, radix in digits[skip:]:
         step = stride // unit
-        for digit in range(1, radix):
+        for digit in reversed(range(1, radix)):
             at = [key for key in range(len(items)) if key // step % radix == digit]
             if len(at) == 1:
                 items[at[0]] = swap_with(items[at[0]], axis, digit * stride)
@@ -107,70 +107,105 @@
     return items
 
 
-def inverse_of(grams, other, scale, after=()):
+def eliminate(held, left_ref, right_ref, blocks):
+    step, size = held[0].shape
+    sub = lax.broadcasted_iota(jnp.int32, (step, size), 0)
+    lane = lax.broadcasted_iota(jnp.int32, (step, size), 1)
+
+    def splat_lane(value, index):
+        return jnp.broadcast_to(value[:, index : index + 1], (step, size))
+
+    def splat_row(value, index):
+        return jnp.broadcast_to(value[index : index + 1, :], (step, size))
+
+    for block in blocks:
+        at = slice(step * block, step * block + step)
+        inside = (lane >= step * block) & (lane < step * block + step)
+        upto = lane < step * block + step
+        unit = (lane - step * block == sub).astype(jnp.float32)
+        pivots = [splat_lane(held[block], step * block + t) for t in range(step)]
+        panel = jnp.where(inside, unit, held[block])
+        left_ref[at, :] = jnp.where(upto, panel, 0.0)
+        for p in range(0, step, 2):
+            first, second = sub == p, sub == p + 1
+            corner = splat_row(pivots[p], p)
+            above, below = splat_row(pivots[p + 1], p), splat_row(pivots[p], p + 1)
+            last = splat_row(pivots[p + 1], p + 1)
+            scaled = 1.0 / (corner * last - above * below)
+            i11, i12, i21, i22 = last * scaled, -above * scaled, -below * scaled, corner * scaled
+            one = jnp.where(
+                first, -i11, jnp.where(second, -i21, pivots[p] * i11 + pivots[p + 1] * i21)
+            )
+            two = jnp.where(
+                first, -i12, jnp.where(second, -i22, pivots[p] * i12 + pivots[p + 1] * i22)
+            )
+
+            def clear(value):
+                kept = jnp.where(first | second, 0.0, value)
+                return kept - (one * splat_row(value, p) + two * splat_row(value, p + 1))
+
+            for t in range(p + 2, step):
+                pivots[t] = clear(pivots[t])
+            panel = clear(panel)
+        right_ref[at, :] = jnp.where(upto, panel, 0.0)
+        rows = [splat_row(panel, t) for t in range(step)]
+        for index in range(block + 1, len(held)):
+            pairs = [splat_lane(held[index], step * block + t) * rows[t] for t in range(step)]
+            held[index] = jnp.where(inside, 0.0, held[index]) - add_tree(pairs)
+    return held
+
+
+pivot_rows = 16
+
+
+def start_inverse(grams, other, scale, after):
     size = grams[0].shape[-1]
-    step = 16
+    step = pivot_rows
     count = size // step
     own = other is None
     operands = list(grams) + ([] if own else [other])
-    outputs = [shaped(size, size)] + ([shaped(size, size)] if own else [])
 
     def body(*refs):
-        parts = refs[: len(grams)]
-        out_ref = refs[len(operands)]
-        left_ref, right_ref = refs[-2:]
-        sub = lax.broadcasted_iota(jnp.int32, (step, size), 0)
-        lane = lax.broadcasted_iota(jnp.int32, (step, size), 1)
+        parts, refs = refs[: len(grams)], refs[len(grams) :]
         held = []
         for block in range(count):
             at = slice(step * block, step * block + step)
-            total = add_tree([part[pl.ds(part.shape[0] - size + step * block, step), :] for part in parts])
             if own:
-                refs[len(operands) + 1][at, :] = total
+                half = size // 2
+                here = slice(step * block % half, step * block % half + step)
+                core = lax.axis_index("wide") % 2
+                total = jnp.where(
+                    core == step * block // half, parts[0][here, :], parts[1][here, :]
+                )
+                refs[3][at, :] = total
                 held.append(total * total)
             else:
-                held.append(scale * total * refs[len(grams)][at, :])
-
-        def splat_lane(value, index):
-            return jnp.broadcast_to(value[:, index : index + 1], (step, size))
-
-        def splat_row(value, index):
-            return jnp.broadcast_to(value[index : index + 1, :], (step, size))
-
+                total = add_tree([part[at, :] for part in parts])
+                held.append(scale * total * refs[0][at, :])
+        held_ref, left_ref, right_ref = refs[:3] if own else refs[1:]
+        held = eliminate(held, left_ref, right_ref, range(count // 2))
         for block in range(count):
             at = slice(step * block, step * block + step)
-            inside = (lane >= step * block) & (lane < step * block + step)
-            upto = lane < step * block + step
-            unit = (lane - step * block == sub).astype(jnp.float32)
-            pivots = [splat_lane(held[block], step * block + t) for t in range(step)]
-            panel = jnp.where(inside, unit, held[block])
-            left_ref[at, :] = jnp.where(upto, panel, 0.0)
-            for p in range(0, step, 2):
-                first, second = sub == p, sub == p + 1
-                corner = splat_row(pivots[p], p)
-                above, below = splat_row(pivots[p + 1], p), splat_row(pivots[p], p + 1)
-                last = splat_row(pivots[p + 1], p + 1)
-                scaled = 1.0 / (corner * last - above * below)
-                i11, i12, i21, i22 = last * scaled, -above * scaled, -below * scaled, corner * scaled
-                one = jnp.where(
-                    first, -i11, jnp.where(second, -i21, pivots[p] * i11 + pivots[p + 1] * i21)
-                )
-                two = jnp.where(
-                    first, -i12, jnp.where(second, -i22, pivots[p] * i12 + pivots[p + 1] * i22)
-                )
-
-                def clear(value):
-                    kept = jnp.where(first | second, 0.0, value)
-                    return kept - (one * splat_row(value, p) + two * splat_row(value, p + 1))
-
-                for t in range(p + 2, step):
-                    pivots[t] = clear(pivots[t])
-                panel = clear(panel)
-            right_ref[at, :] = jnp.where(upto, panel, 0.0)
-            rows = [splat_row(panel, t) for t in range(step)]
-            for index in range(block + 1, count):
-                pairs = [splat_lane(held[index], step * block + t) * rows[t] for t in range(step)]
-                held[index] = jnp.where(inside, 0.0, held[index]) - add_tree(pairs)
+            held_ref[at, :] = held[block]
+            if block >= count // 2:
+                left_ref[at, :] = jnp.zeros_like(held[block])
+                right_ref[at, :] = jnp.zeros_like(held[block])
+
+    outputs = [shaped(size, size)] * (4 if own else 3)
+    return kernel_call(body, outputs, operands, about_us=1.8, after=after)
+
+
+def end_inverse(held, left, right, after):
+    size = held.shape[0]
+    step = pivot_rows
+    count = size // step
+
+    def body(held_ref, left_in, right_in, out_ref, left_ref, right_ref):
+        half = size // 2
+        left_ref[:half, :] = left_in[:half, :]
+        right_ref[:half, :] = right_in[:half, :]
+        rows = [held_ref[step * block : step * block + step, :] for block in range(count)]
+        eliminate(rows, left_ref, right_ref, range(count // 2, count))
         out_ref[...] = lax.dot_general(
             left_ref[...],
             right_ref[...],
@@ -181,12 +216,12 @@
 
     return kernel_call(
         body,
-        outputs,
-        operands,
+        [shaped(size, size)],
+        [held, left, right],
         scratch=[pltpu.VMEM((size, size), jnp.float32)] * 2,
-        about_us=3.5,
+        about_us=1.6,
         after=after,
-    )
+    )[0]
 
 
 def own_part(chip_slice):
@@ -255,20 +290,21 @@
     own_blocks, low, rows, rank = own.shape
     partners, slots, _ = coords.shape
     piece_rows = slots * 2 * low * rows
+    share = rank // low
 
     def body(there_ref, own_ref, mine_ref, theirs_ref, *refs):
-        out_refs, coord_ref, sem = refs[:partners], refs[partners], refs[partners + 1]
+        out_refs, (coord_ref, gram_ref, sem) = refs[:partners], refs[partners:]
         narrow_at = lax.axis_index("narrow")
         core = lax.axis_index("wide") % low
         copy = pltpu.make_async_copy(there_ref, coord_ref, sem)
         copy.start()
         here, there = mine_ref[...].reshape(-1, rank), theirs_ref[...].reshape(-1, rank)
         rows_of = [jnp.where(core == j, here, there) for j in range(low)]
-        gram = join_gram(
+        gram_ref[...] = join_gram(
             gram_parts(jnp.concatenate([own_ref[...].reshape(-1, rank)] + rows_of, axis=0))
         )
         for out_ref in out_refs:
-            out_ref[piece_rows:, :] = gram
+            out_ref[piece_rows:, :] = gram_ref[pl.ds(pl.multiple_of(core * share, share), share), :]
         copy.wait()
         for d, out_ref in enumerate(out_refs):
             for pair in range(slots * 2):
@@ -293,14 +329,18 @@
 
     return kernel_call(
         body,
-        [shaped(piece_rows + rank, rank)] * partners,
+        [shaped(piece_rows + share, rank)] * partners,
         [coords, own, mine, theirs],
-        scratch=[pltpu.SMEM(coords.shape, jnp.int32), pltpu.SemaphoreType.DMA],
+        scratch=[
+            pltpu.SMEM(coords.shape, jnp.int32),
+            pltpu.VMEM((rank, rank), jnp.float32),
+            pltpu.SemaphoreType.DMA,
+        ],
         after=after,
     )
 
 
-def first_mode(tags, pieces, spread, wide_size, low):
+def first_mode(tags, pieces, spread, wide_size, low, after):
     rank = pieces[0].shape[1]
     slots, _, width = spread.shape
     edge = width // 4
@@ -344,6 +384,7 @@
         [tags] + list(pieces) + [spread],
         scratch=[pltpu.VMEM((pairs, wide_size, slice_rows, rank), jnp.float32)],
         about_us=3.0,
+        after=after,
     )
 
 
@@ -603,7 +644,7 @@
     return owned.reshape(own_rows, rank), done
 
 
-def pack_pieces(groups):
+def pack_pieces(groups, after):
     low = len(groups)
     partners = groups[0].shape[0]
 
@@ -612,7 +653,9 @@
             for j in range(low):
                 refs[low + d][j] = refs[j][d]
 
-    return kernel_call(body, [shaped(low, *groups[0].shape[1:])] * partners, list(groups))
+    return kernel_call(
+        body, [shaped(low, *groups[0].shape[1:])] * partners, list(groups), after=after
+    )
 
 
 def pack_whole(items, after=(), rows=None):
@@ -679,43 +722,34 @@
     )
 
 
-def add_parts(parts, after=()):
+def add_parts(parts, after=(), rows=None):
+    count, rank = parts[0].shape
+    rows = rows or count
+
     def body(*refs):
-        total = refs[0][...]
-        for ref in refs[1:-1]:
-            total = total + ref[...]
-        refs[-1][...] = total
-
-    return kernel_call(body, [shaped(*parts[0].shape)], list(parts), after=after)[0]
-
-
-def solve_rows(parts, inverse):
-    rows, rank = parts[0].shape
-    count = len(parts)
-
-    def body(*refs):
-        solved = times(
-            jnp.concatenate([ref[...] for ref in refs[:count]], axis=0), refs[count][...]
-        )
-        refs[-1][...] = solved.reshape(count, rows, rank)
-
-    return kernel_call(body, [shaped(count, rows, rank)], list(parts) + [inverse])[0]
-
-
-def lay_rows(parts, own_blocks):
+        refs[-1][...] = add_tree([ref[count - rows :, :] for ref in refs[:-1]])
+
+    return kernel_call(body, [shaped(rows, rank)], list(parts), after=after)[0]
+
+
+def solve_rows(parts, inverse, own_blocks):
     low = len(parts)
     partners, part_rows, rank = parts[0].shape
     rows = part_rows // own_blocks
 
     def body(*refs):
         wide_at = lax.axis_index("wide")
-        for d in range(partners):
-            for j in range(low):
+        for j in range(low):
+            solved = times(refs[j][...].reshape(partners * part_rows, rank), refs[low][...])
+            for d in range(partners):
                 place = wide_at ^ (d * low + j)
                 for block in range(own_blocks):
-                    refs[-1][block, place] = refs[j][d, block * rows : (block + 1) * rows, :]
-
-    return kernel_call(body, [shaped(own_blocks, partners * low, rows, rank)], list(parts))[0]
+                    at = d * part_rows + block * rows
+                    refs[-1][block, place] = solved[at : at + rows]
+
+    return kernel_call(
+        body, [shaped(own_blocks, partners * low, rows, rank)], list(parts) + [inverse]
+    )[0]
 
 
 def on_device(blocks, block_coords, block_count, orbital_factor):
@@ -744,31 +778,37 @@
     pieces = exchange(wanted, "wide", skip=1)
 
     spread, turned = split_blocks(blocks, wanted[:1])
-    rows, terms = first_mode(tags, pieces, spread, wide_size, low)
-    inverse_b, gram_b = inverse_of(pieces, None, 1.0, after=[terms])
-    terms = pack_whole(gather_from(terms, "wide", skip=1), after=[inverse_b])
+    half = add_parts(pieces, [turned], rows=rank // low)
+    rows, terms = first_mode(tags, pieces, spread, wide_size, low, [half])
+    other_half = swap_with(half, "wide", 1)
+    terms = add_parts([terms], [other_half])
+    *started, gram_b = start_inverse([half, other_half], None, 1.0, [terms])
+    terms = pack_whole(gather_from(terms, "wide", skip=1), after=started[:1])
+    inverse_b = end_inverse(*started, [terms])
     column_terms = with_partners(terms, low)
     all_coords = read_coords(column_terms, slots, edge, block_coords.shape[3])
 
     groups = second_mode(column_terms, inverse_b, turned, rows, wide_size)
+    plan = plan_sums(all_coords, slice_rows, narrow_size, own_blocks, groups[:1])
     groups = [groups[0]] + [swap_with(groups[j], "wide", j) for j in range(1, low)]
-    packed = pack_pieces(groups)
+    packed = pack_pieces(groups, [plan])
     pieces = exchange(packed, "wide", skip=1)
 
     gram, aux = column_gram(all_coords, column_terms, inverse_b, edge, packed[:1])
 
-    plan = plan_sums(all_coords, slice_rows, narrow_size, own_blocks, [gram])
-    sums = add_pieces(plan, pieces, narrow_size, [])
+    sums = add_pieces(plan, pieces, narrow_size, [gram])
     parts = exchange(sums, "narrow")
     step = narrow_size // 2
     while step > 1:
         gram = add_parts([gram, swap_with(gram, "narrow", step)], sums[:1])
         step //= 2
-    aux_owned, done = own_aux(all_coords, aux, own_rows, sums[:1])
+    aux_owned, done = own_aux(all_coords, aux, own_rows, [gram])
     total = add_parts(parts, [gram, done])
-    (inverse_a,) = inverse_of([gram, swap_with(gram, "narrow", step)], gram_b, 2.0, [total])
-    solved = solve_rows(gather_from(total, "wide", skip=1), inverse_a)
-    orbital_new = lay_rows(with_partners(solved, low), own_blocks)
+    grams = [gram, swap_with(gram, "narrow", step)]
+    started = start_inverse(grams, gram_b, 2.0, [total])
+    totals = pack_whole(gather_from(total, "wide", skip=1), after=started[:1])
+    inverse_a = end_inverse(*started, [totals])
+    orbital_new = solve_rows(with_partners(totals, low), inverse_a, own_blocks)
     return (aux_owned[None], orbital_new.reshape(own_blocks * edge, rank))
 
 

time: 63.7 us -> 63.4 us (level)
  waiting for transfers between devices: 10.3 us -> 9.5 us
    ppermute x25 -> x26, waiting for transfers between devices: 10.3 us -> 9.5 us  [swap_with(): lax.ppermute(value, axis, [(index, index ^ mask) for index in range(size)])]
    ppermute x25 -> x26, starting transfers between devices: 26.1 us -> 26.3 us  [swap_with(): lax.ppermute(value, axis, [(index, index ^ mask) for index in range(size)])]
    pallas_call x22 -> x26, Pallas kernels: 20 us -> 20.1 us  [kernel_call(): pl.pallas_call(whole, out_shape=outputs, in_specs=[in_smem] * scalars + [...]
  transfers between devices with their start and end apart: 26 -> 27, of which waited for: 11 -> 12; matrix products, arithmetic and copies ran while one was open for 0% -> 0% of each run, Pallas kernels for 24% -> 26%
where the time goes in v4:
time: 63.4 us; the launch traced here: 63.2 us
  starting transfers between devices  29.4 us (46%)
  Pallas kernels  20.1 us (32%)
  waiting for transfers between devices  9.5 us (15%)
  local copies, waits for them, and re-layouts  2.62 us (4%)
  between operations  1.56 us (2%)
    ppermute x26, starting transfers between devices, swap_with(): lax.ppermute(value, axis, [(index, index ^ mask) for index in range(size)])  26.3 us
    pallas_call x26, Pallas kernels, kernel_call(): pl.pallas_call(whole, out_shape=outputs, in_specs=[in_smem] * scalars + [...  20.1 us
    ppermute x26, waiting for transfers between devices, swap_with(): lax.ppermute(value, axis, [(index, index ^ mask) for index in range(size)])  9.5 us
    ppermute x1, starting transfers between devices, send_by_core(): return lax.ppermute(value, ('wide', 'narrow'), pairs)  3.09 us
    unnamed x6, local copies, waits for them, and re-layouts  2.61 us
  transfers between devices with their start and end apart: 27, of which 12 were waited for; matrix products, arithmetic and copies ran while one was open for 0% of the time, Pallas kernels for 26%

profile of v4, /device:TPU:0, one launch (start us, length us, event | category | flops | bytes accessed | tf_op | source)
XLA Modules:
  0.0 63.2 jit_solution(51770623557345580)
XLA Ops:
  0.6 0.0 copy-start
  0.6 0.0 copy-start.2
  0.7 1.0 %copy-done = f32[1024,128]{1,0:T(8,128)S(1)} copy-done((f32[1024,128]{1,0:T(8,128)S(1)}, f32[1024,128]{1,0:T(8,128)}, u32[]{:S(2)}) %copy-start) | copy-done | bytes 524312
  1.7 3.1 %collective-permute-start = (f32[16,2,8,128]{3,2,1,0:T(8,128)S(1)}, f32[16,2,8,128]{3,2,1,0:T(8,128)S(1)}, u32[]{:S(2)}, u32[]{:S(2)}) collective-permute-start(f32[16,2,8,128]{3,2,1,0:T(8,128)S(1)} %dynamic-slice_bitcast_fusion.refs_0_.refs_1_), channel_id=1, source_target_pairs={{0,1},{1,0},{2,3},{3,2},{4,6},{5,7},{6,4},{7,5},{8,9},{9,8},{10,11... | collective-permute-start | bytes 393224 | tf_op jit(solution)/shard_map/ppermute | solution.py:78
  4.8 2.5 %collective-permute-start.1 = (f32[16,8,128]{2,1,0:T(8,128)S(1)}, f32[16,8,128]{2,1,0:T(8,128)S(1)}, u32[]{:S(2)}, u32[]{:S(2)}) collective-permute-start(f32[16,8,128]{2,1,0:T(8,128)S(1)} %shard_map.59.refs_1_), channel_id=1, source_target_pairs={{0,3},{1,2},{2,1},{3,0},{4,7},{5,6},{6,5},{7,4},{8,11},{9,10},{10,... | collective-permute-start | bytes 196616 | tf_op jit(solution)/shard_map/ppermute | solution.py:68
  7.3 2.4 %collective-permute-start.4 = (s32[2,3]{1,0:T(2,128)}, s32[2,3]{1,0:T(2,128)S(1)}, u32[]{:S(2)}, u32[]{:S(2)}) collective-permute-start(s32[2,3]{1,0:T(2,128)} %bitcast.11), channel_id=1, source_target_pairs={{0,24},{4,28},{8,16},{12,20},{16,8},{20,12},{24,0},{28,4},{1,25},{... | collective-permute-start | bytes 80 | tf_op jit(solution)/shard_map/ppermute | solution.py:68
  9.7 0.5 collective-permute-start.3
  10.2 0.5 collective-permute-start.2
  10.8 1.6 %copy-done.1 = f32[1,1,2,64,4096]{4,3,2,1,0:T(8,128)S(1)} copy-done((f32[1,1,2,64,4096]{4,3,2,1,0:T(8,128)S(1)}, f32[1,1,2,64,4096]{4,3,2,1,0:T(8,128)}, u32[]{:S(2)}) %copy-start.1) | copy-done | bytes 2097176
  12.3 0.1 shard_map.60.refs_5_.refs_0_
  12.5 0.0 collective-permute-done.4.refs_4_.refs_3_
  12.5 1.0 %collective-permute-done.3.refs_3_.refs_2_ = s32[2,3]{1,0:T(2,128)S(1)} collective-permute-done((s32[2,3]{1,0:T(2,128)}, s32[2,3]{1,0:T(2,128)S(1)}, u32[]{:S(2)}, u32[]{:S(2)}) %collective-permute-start.3) | collective-permute-done | bytes 56 | tf_op jit(solution)/shard_map/ppermute | solution.py:68
  13.5 0.5 collective-permute-done.2.refs_2_.refs_1_
  14.0 0.0 collective-permute-done.1.refs_1_
  14.0 0.0 collective-permute-done.refs_0_
  14.0 0.1 collective-permute-start.5
  14.8 0.1 shard_map.62
  14.8 0.7 %collective-permute-done.5.refs_3_ = f32[48,8,128]{2,1,0:T(8,128)S(1)} collective-permute-done((f32[48,8,128]{2,1,0:T(8,128)S(1)}, f32[48,8,128]{2,1,0:T(8,128)S(1)}, u32[]{:S(2)}, u32[]{:S(2)}) %collective-permute-start.5) | collective-permute-done | bytes 196640 | tf_op jit(solution)/shard_map/ppermute | solution.py:68
  15.5 1.0 %shard_map.64 = (f32[128,128]{1,0:T(8,128)S(1)}, f32[128,128]{1,0:T(8,128)S(1)}, f32[128,128]{1,0:T(8,128)S(1)}, f32[128,128]{1,0:T(8,128)S(1)}) custom-call(s32[4,2,3]{2,1,0:T(2,128)S(1)} %shard_map.63.refs_0_, f32[16,2,8,128]{3,2,1,0:T(8,128)S(1)} %dynamic-slice_bitcast_fusion.refs_0_.refs_1_, f32[48,8,128]{2,1,0:T(8,128)S(1)} %shard_map.61.refs_2_, ...), custom_call_target="tpu_custom_call" | custom-call | flops 300000 | tf_op jit(solution)/shard_map/pallas_call | solution.py:30
  16.5 0.6 collective-permute-start.6
  17.1 1.5 %collective-permute-start.7 = (f32[128,128]{1,0:T(8,128)S(1)}, f32[128,128]{1,0:T(8,128)S(1)}, u32[]{:S(2)}, u32[]{:S(2)}) collective-permute-start(f32[128,128]{1,0:T(8,128)S(1)} %get-tuple-element.37), channel_id=1, source_target_pairs={{0,16},{4,20},{8,24},{12,28},{16,0},{20,4},{24,8},{28,12},{1,17},{... | collective-permute-start | bytes 196616 | tf_op jit(solution)/shard_map/ppermute | solution.py:68
  18.6 1.4 %collective-permute-start.8 = (f32[128,128]{1,0:T(8,128)S(1)}, f32[128,128]{1,0:T(8,128)S(1)}, u32[]{:S(2)}, u32[]{:S(2)}) collective-permute-start(f32[128,128]{1,0:T(8,128)S(1)} %get-tuple-element.38), channel_id=1, source_target_pairs={{0,24},{4,28},{8,16},{12,20},{16,8},{20,12},{24,0},{28,4},{1,25},{... | collective-permute-start | bytes 196616 | tf_op jit(solution)/shard_map/ppermute | solution.py:68
  20.1 3.1 %shard_map.65 = (bf16[2,4096,256]{2,1,0:T(8,128)(2,1)S(1)}, bf16[2,4096,256]{2,1,0:T(8,128)(2,1)S(1)}) custom-call(f32[2,64,4096]{2,1,0:T(8,128)S(1)} %shard_map.60.refs_5_.refs_0_, f32[128,128]{1,0:T(8,128)S(1)} %get-tuple-element.35.refs_1_.refs_0_), custom_call_target="tpu_custom_call" | custom-call | flops 300000 | tf_op jit(solution)/shard_map/pallas_call | solution.py:30
  23.2 0.0 collective-permute-done.6.refs_1_.refs_2_
  23.2 0.6 collective-permute-done.8.refs_3_.refs_4_
  23.8 0.1 collective-permute-start.9
  23.9 1.3 %shard_map.67 = (f32[4,64,128]{2,1,0:T(8,128)S(1)}, f32[136,128]{1,0:T(8,128)S(1)}) custom-call(f32[8,128]{1,0:T(8,128)S(1)} %get-tuple-element.33.refs_0_, f32[128,128]{1,0:T(8,128)S(1)} %get-tuple-element.35.refs_1_.refs_0_, f32[128,128]{1,0:T(8,128)S(1)} %collective-permute-done.6.refs_1_.refs_2_, f32[128,128]{1,0:T(8,128)S(1)} %collective-permute-done.7.refs_2_.refs_3_, ...), custom_call_target="tpu_custom_call" | custom-call | flops 3000000 | tf_op jit(solution)/shard_map/pallas_call | solution.py:30
  25.2 0.0 collective-permute-done.9.refs_1_
  25.2 1.5 %collective-permute-start.12 = (f32[136,128]{1,0:T(8,128)S(1)}, f32[136,128]{1,0:T(8,128)S(1)}, u32[]{:S(2)}, u32[]{:S(2)}) collective-permute-start(f32[136,128]{1,0:T(8,128)S(1)} %shard_map.68.refs_2_.refs_0_), channel_id=1, source_target_pairs={{0,24},{4,28},{8,16},{12,20},{16,8},{20,12},{24,0},{28,4},{1,25},{... | collective-permute-start | bytes 208904 | tf_op jit(solution)/shard_map/ppermute | solution.py:68
  26.7 1.5 %collective-permute-start.11 = (f32[136,128]{1,0:T(8,128)S(1)}, f32[136,128]{1,0:T(8,128)S(1)}, u32[]{:S(2)}, u32[]{:S(2)}) collective-permute-start(f32[136,128]{1,0:T(8,128)S(1)} %shard_map.68.refs_2_.refs_0_), channel_id=1, source_target_pairs={{0,16},{4,20},{8,24},{12,28},{16,0},{20,4},{24,8},{28,12},{1,17},{... | collective-permute-start | bytes 208904 | tf_op jit(solution)/shard_map/ppermute | solution.py:68
  28.2 0.5 collective-permute-start.10
  28.8 1.7 %shard_map.69 = (f32[128,128]{1,0:T(8,128)S(1)}, f32[128,128]{1,0:T(8,128)S(1)}, f32[128,128]{1,0:T(8,128)S(1)}, f32[128,128]{1,0:T(8,128)S(1)}) custom-call(f32[64,128]{1,0:T(8,128)S(1)} %shard_map.66.refs_6_.refs_0_, f32[64,128]{1,0:T(8,128)S(1)} %collective-permute-done.9.refs_1_, f32[136,128]{1,0:T(8,128)S(1)} %shard_map.68.refs_2_.refs_0_), custom_call_target="tpu_custom_call" | custom-call | flops 1800000 | tf_op jit(solution)/shard_map/pallas_call | solution.py:30
  30.5 0.4 collective-permute-done.12.refs_3_
  30.9 1.4 %collective-permute-done.11.refs_2_ = f32[136,128]{1,0:T(8,128)S(1)} collective-permute-done((f32[136,128]{1,0:T(8,128)S(1)}, f32[136,128]{1,0:T(8,128)S(1)}, u32[]{:S(2)}, u32[]{:S(2)}) %collective-permute-start.11) | collective-permute-done | bytes 69664 | tf_op jit(solution)/shard_map/ppermute | solution.py:68
  32.3 0.3 collective-permute-done.10.refs_1_
  32.6 0.1 collective-permute-start.13
  32.6 1.8 %shard_map.72.refs_2_.refs_3_ = f32[128,128]{1,0:T(8,128)S(1)} custom-call(f32[128,128]{1,0:T(8,128)S(1)} %get-tuple-element.42.refs_4_.refs_0_, f32[128,128]{1,0:T(8,128)S(1)} %get-tuple-element.43.refs_1_, f32[128,128]{1,0:T(8,128)S(1)} %get-tuple-element.44.refs_2_, f32[4,136,128]{2,1,0:T(8,128)S(1)} %shard_map.70.refs_0_.refs_3_.refs_1_), custom_call_target="tpu_custom_call" | custom-call | flops 1600000 | tf_op jit(solution)/shard_map/pallas_call | solution.py:30
  34.4 1.5 %shard_map.73 = (f32[4,4,8,128]{3,2,1,0:T(8,128)S(1)}, f32[4,4,8,128]{3,2,1,0:T(8,128)S(1)}) custom-call(f32[4,136,128]{2,1,0:T(8,128)S(1)} %shard_map.70.refs_0_.refs_3_.refs_1_, f32[4,136,128]{2,1,0:T(8,128)S(1)} %collective-permute-done.13.refs_1_.refs_2_, f32[128,128]{1,0:T(8,128)S(1)} %shard_map.72.refs_2_.refs_3_, ...), custom_call_target="tpu_custom_call" | custom-call | flops 2500000 | tf_op jit(solution)/shard_map/pallas_call | solution.py:30
  36.0 0.6 collective-permute-start.14
  36.5 0.9 %shard_map.74.refs_2_.refs_0_ = bf16[512,256]{1,0:T(8,128)(2,1)S(1)} custom-call(s32[8,2,3]{2,1,0:T(2,128)S(1)} %shard_map.71.refs_0_, f32[4,4,8,128]{3,2,1,0:T(8,128)S(1)} %get-tuple-element.46.refs_1_.refs_0_), custom_call_target="tpu_custom_call" | custom-call | flops 300000 | tf_op jit(solution)/shard_map/pallas_call | solution.py:30
  37.4 0.0 collective-permute-done.14.refs_1_
  37.5 1.0 %collective-permute-start.16 = (f32[2,4,8,128]{3,2,1,0:T(8,128)S(1)}, f32[2,4,8,128]{3,2,1,0:T(8,128)S(1)}, u32[]{:S(2)}, u32[]{:S(2)}) collective-permute-start(f32[2,4,8,128]{3,2,1,0:T(8,128)S(1)} %get-tuple-element.51), channel_id=1, source_target_pairs={{0,8},{4,12},{8,0},{12,4},{16,24},{20,28},{24,16},{28,20},{1,9},{5... | collective-permute-start | bytes 98312 | tf_op jit(solution)/shard_map/ppermute | solution.py:68
  38.5 0.8 %collective-permute-start.17 = (f32[2,4,8,128]{3,2,1,0:T(8,128)S(1)}, f32[2,4,8,128]{3,2,1,0:T(8,128)S(1)}, u32[]{:S(2)}, u32[]{:S(2)}) collective-permute-start(f32[2,4,8,128]{3,2,1,0:T(8,128)S(1)} %get-tuple-element.52), channel_id=1, source_target_pairs={{0,16},{4,20},{8,24},{12,28},{16,0},{20,4},{24,8},{28,12},{1,17},{... | collective-permute-start | bytes 98312 | tf_op jit(solution)/shard_map/ppermute | solution.py:68
  39.4 1.7 %collective-permute-start.18 = (f32[2,4,8,128]{3,2,1,0:T(8,128)S(1)}, f32[2,4,8,128]{3,2,1,0:T(8,128)S(1)}, u32[]{:S(2)}, u32[]{:S(2)}) collective-permute-start(f32[2,4,8,128]{3,2,1,0:T(8,128)S(1)} %get-tuple-element.53), channel_id=1, source_target_pairs={{0,24},{4,28},{8,16},{12,20},{16,8},{20,12},{24,0},{28,4},{1,25},{... | collective-permute-start | bytes 98312 | tf_op jit(solution)/shard_map/ppermute | solution.py:68
  41.0 1.6 %shard_map.76 = (f32[128,128]{1,0:T(8,128)S(1)}, f32[16,64,128]{2,1,0:T(8,128)S(1)}) custom-call(s32[8,2,3]{2,1,0:T(2,128)S(1)} %shard_map.71.refs_0_, f32[4,136,128]{2,1,0:T(8,128)S(1)} %shard_map.70.refs_0_.refs_3_.refs_1_, f32[4,136,128]{2,1,0:T(8,128)S(1)} %collective-permute-done.13.refs_1_.refs_2_, f32[128,128]{1,0:T(8,128)S(1)} %shard_map.72.refs_2_.refs_3_, ...), custom_call_target="tpu_custom_call" | custom-call | flops 100000 | tf_op jit(solution)/shard_map/pallas_call | solution.py:30
  42.6 0.7 %collective-permute-start.15 = (f32[128,128]{1,0:T(8,128)S(1)}, f32[128,128]{1,0:T(8,128)S(1)}, u32[]{:S(2)}, u32[]{:S(2)}) collective-permute-start(f32[128,128]{1,0:T(8,128)S(1)} %get-tuple-element.50.refs_5_.refs_0_), channel_id=1, source_target_pairs={{0,2},{1,3},{2,0},{3,1},{4,6},{5,7},{6,4},{7,5},{8,10},{9,11},{10,... | collective-permute-start | bytes 196616 | tf_op jit(solution)/shard_map/ppermute | solution.py:68
  43.4 0.8 %collective-permute-done.18.refs_4_ = f32[2,4,8,128]{3,2,1,0:T(8,128)S(1)} collective-permute-done((f32[2,4,8,128]{3,2,1,0:T(8,128)S(1)}, f32[2,4,8,128]{3,2,1,0:T(8,128)S(1)}, u32[]{:S(2)}, u32[]{:S(2)}) %collective-permute-start.18) | collective-permute-done | bytes 32800 | tf_op jit(solution)/shard_map/ppermute | solution.py:68
  44.2 0.3 shard_map.77
  44.5 0.7 %collective-permute-start.19 = (f32[128,128]{1,0:T(8,128)S(1)}, f32[128,128]{1,0:T(8,128)S(1)}, u32[]{:S(2)}, u32[]{:S(2)}) collective-permute-start(f32[128,128]{1,0:T(8,128)S(1)} %get-tuple-element.56), channel_id=1, source_target_pairs={{0,1},{1,0},{2,3},{3,2},{4,5},{5,4},{6,7},{7,6},{8,9},{9,8},{10,11... | collective-permute-start | bytes 196616 | tf_op jit(solution)/shard_map/ppermute | solution.py:68
  45.2 1.5 %collective-permute-start.20 = (f32[128,128]{1,0:T(8,128)S(1)}, f32[128,128]{1,0:T(8,128)S(1)}, u32[]{:S(2)}, u32[]{:S(2)}) collective-permute-start(f32[128,128]{1,0:T(8,128)S(1)} %get-tuple-element.57), channel_id=1, source_target_pairs={{0,2},{1,3},{2,0},{3,1},{4,6},{5,7},{6,4},{7,5},{8,10},{9,11},{10,... | collective-permute-start | bytes 196616 | tf_op jit(solution)/shard_map/ppermute | solution.py:68
  46.7 2.3 %collective-permute-start.21 = (f32[128,128]{1,0:T(8,128)S(1)}, f32[128,128]{1,0:T(8,128)S(1)}, u32[]{:S(2)}, u32[]{:S(2)}) collective-permute-start(f32[128,128]{1,0:T(8,128)S(1)} %get-tuple-element.58), channel_id=1, source_target_pairs={{0,3},{1,2},{2,1},{3,0},{4,7},{5,6},{6,5},{7,4},{8,11},{9,10},{10,... | collective-permute-start | bytes 196616 | tf_op jit(solution)/shard_map/ppermute | solution.py:68
  48.9 1.0 %collective-permute-done.15.refs_1_ = f32[128,128]{1,0:T(8,128)S(1)} collective-permute-done((f32[128,128]{1,0:T(8,128)S(1)}, f32[128,128]{1,0:T(8,128)S(1)}, u32[]{:S(2)}, u32[]{:S(2)}) %collective-permute-start.15) | collective-permute-done | bytes 65568 | tf_op jit(solution)/shard_map/ppermute | solution.py:68
  50.0 0.1 collective-permute-start.25
  50.1 1.9 %shard_map.79 = (f32[8,64,128]{2,1,0:T(8,128)}, f32[8,128]{1,0:T(8,128)S(1)}) custom-call(s32[8,2,3]{2,1,0:T(2,128)S(1)} %shard_map.71.refs_0_, f32[16,64,128]{2,1,0:T(8,128)S(1)} %get-tuple-element.49.refs_1_, f32[128,128]{1,0:T(8,128)S(1)} %shard_map.78.refs_2_.refs_4_.refs_0_), custom_call_target="tpu_custom_call" | custom-call | flops 100000 | tf_op jit(solution)/shard_map/pallas_call | solution.py:30
  51.9 1.3 %collective-permute-done.20.refs_2_ = f32[128,128]{1,0:T(8,128)S(1)} collective-permute-done((f32[128,128]{1,0:T(8,128)S(1)}, f32[128,128]{1,0:T(8,128)S(1)}, u32[]{:S(2)}, u32[]{:S(2)}) %collective-permute-start.20) | collective-permute-done | bytes 65568 | tf_op jit(solution)/shard_map/ppermute | solution.py:68
  53.3 1.5 %collective-permute-start.24 = (f32[128,128]{1,0:T(8,128)S(1)}, f32[128,128]{1,0:T(8,128)S(1)}, u32[]{:S(2)}, u32[]{:S(2)}) collective-permute-start(f32[128,128]{1,0:T(8,128)S(1)} %shard_map.80.refs_3_.refs_0_), channel_id=1, source_target_pairs={{0,24},{4,28},{8,16},{12,20},{16,8},{20,12},{24,0},{28,4},{1,25},{... | collective-permute-start | bytes 196616 | tf_op jit(solution)/shard_map/ppermute | solution.py:68
  54.8 1.0 %collective-permute-start.23 = (f32[128,128]{1,0:T(8,128)S(1)}, f32[128,128]{1,0:T(8,128)S(1)}, u32[]{:S(2)}, u32[]{:S(2)}) collective-permute-start(f32[128,128]{1,0:T(8,128)S(1)} %shard_map.80.refs_3_.refs_0_), channel_id=1, source_target_pairs={{0,16},{4,20},{8,24},{12,28},{16,0},{20,4},{24,8},{28,12},{1,17},{... | collective-permute-start | bytes 196616 | tf_op jit(solution)/shard_map/ppermute | solution.py:68
  55.8 1.1 %collective-permute-start.22 = (f32[128,128]{1,0:T(8,128)S(1)}, f32[128,128]{1,0:T(8,128)S(1)}, u32[]{:S(2)}, u32[]{:S(2)}) collective-permute-start(f32[128,128]{1,0:T(8,128)S(1)} %shard_map.80.refs_3_.refs_0_), channel_id=1, source_target_pairs={{0,8},{4,12},{8,0},{12,4},{16,24},{20,28},{24,16},{28,20},{1,9},{5... | collective-permute-start | bytes 196616 | tf_op jit(solution)/shard_map/ppermute | solution.py:68
  56.8 1.7 %shard_map.81 = (f32[128,128]{1,0:T(8,128)S(1)}, f32[128,128]{1,0:T(8,128)S(1)}, f32[128,128]{1,0:T(8,128)S(1)}) custom-call(f32[128,128]{1,0:T(8,128)S(1)} %shard_map.78.refs_2_.refs_4_.refs_0_, f32[128,128]{1,0:T(8,128)S(1)} %collective-permute-done.25.refs_1_, f32[128,128]{1,0:T(8,128)S(1)} %get-tuple-element.60.refs_2_, ...), custom_call_target="tpu_custom_call" | custom-call | flops 1800000 | tf_op jit(solution)/shard_map/pallas_call | solution.py:30
  58.6 0.6 %collective-permute-done.23.refs_2_ = f32[128,128]{1,0:T(8,128)S(1)} collective-permute-done((f32[128,128]{1,0:T(8,128)S(1)}, f32[128,128]{1,0:T(8,128)S(1)}, u32[]{:S(2)}, u32[]{:S(2)}) %collective-permute-start.23) | collective-permute-done | bytes 65568 | tf_op jit(solution)/shard_map/ppermute | solution.py:68
  59.2 0.8 %collective-permute-done.22.refs_1_ = f32[128,128]{1,0:T(8,128)S(1)} collective-permute-done((f32[128,128]{1,0:T(8,128)S(1)}, f32[128,128]{1,0:T(8,128)S(1)}, u32[]{:S(2)}, u32[]{:S(2)}) %collective-permute-start.22) | collective-permute-done | bytes 65568 | tf_op jit(solution)/shard_map/ppermute | solution.py:68
  60.1 0.1 collective-permute-start.26
  60.2 1.8 %shard_map.83.refs_2_ = f32[128,128]{1,0:T(8,128)S(1)} custom-call(f32[128,128]{1,0:T(8,128)S(1)} %get-tuple-element.61.refs_4_.refs_0_, f32[128,128]{1,0:T(8,128)S(1)} %get-tuple-element.62.refs_1_, f32[128,128]{1,0:T(8,128)S(1)} %get-tuple-element.63.refs_2_, f32[4,128,128]{2,1,0:T(8,128)S(1)} %shard_map.82.refs_3_.refs_0_), custom_call_target="tpu_custom_call" | custom-call | flops 1600000 | tf_op jit(solution)/shard_map/pallas_call | solution.py:30
  61.9 1.2 %shard_map.84 = f32[16,8,8,128]{3,2,1,0:T(8,128)} custom-call(f32[4,128,128]{2,1,0:T(8,128)S(1)} %shard_map.82.refs_3_.refs_0_, f32[4,128,128]{2,1,0:T(8,128)S(1)} %collective-permute-done.26.refs_1_, f32[128,128]{1,0:T(8,128)S(1)} %shard_map.83.refs_2_), custom_call_target="tpu_custom_call" | custom-call | flops 300000 | tf_op jit(solution)/shard_map/pallas_call | solution.py:30
  (23 shorter events, 0.2 us)
Async XLA Ops:
  0.6 1.0 %copy-start = (f32[1024,128]{1,0:T(8,128)S(1)}, f32[1024,128]{1,0:T(8,128)}, u32[]{:S(2)}) copy-start(f32[1024,128]{1,0:T(8,128)} %param.7) | copy-start | bytes 1572868
  0.6 14.1 %copy-start.2 = (s32[1,1,2,3]{3,2,1,0:T(2,128)S(1)}, s32[1,1,2,3]{3,2,1,0:T(2,128)}, u32[]{:S(2)}) copy-start(s32[1,1,2,3]{3,2,1,0:T(2,128)} %param.5) | copy-start | bytes 76
  1.7 12.3 %collective-permute-start = (f32[16,2,8,128]{3,2,1,0:T(8,128)S(1)}, f32[16,2,8,128]{3,2,1,0:T(8,128)S(1)}, u32[]{:S(2)}, u32[]{:S(2)}) collective-permute-start(f32[16,2,8,128]{3,2,1,0:T(8,128)S(1)} %dynamic-slice_bitcast_fusion.refs_0_.refs_1_), channel_id=1, source_target_pairs={{0,1},{1,0},{2,3},{3,2},{4,6},{5,7},{6,4},{7,5},{8,9},{9,8},{10,11... | collective-permute-start | bytes 393224 | tf_op jit(solution)/shard_map/ppermute | solution.py:78
  4.8 9.2 %collective-permute-start.1 = (f32[16,8,128]{2,1,0:T(8,128)S(1)}, f32[16,8,128]{2,1,0:T(8,128)S(1)}, u32[]{:S(2)}, u32[]{:S(2)}) collective-permute-start(f32[16,8,128]{2,1,0:T(8,128)S(1)} %shard_map.59.refs_1_), channel_id=1, source_target_pairs={{0,3},{1,2},{2,1},{3,0},{4,7},{5,6},{6,5},{7,4},{8,11},{9,10},{10,... | collective-permute-start | bytes 196616 | tf_op jit(solution)/shard_map/ppermute | solution.py:68
  7.3 5.2 %collective-permute-start.4 = (s32[2,3]{1,0:T(2,128)}, s32[2,3]{1,0:T(2,128)S(1)}, u32[]{:S(2)}, u32[]{:S(2)}) collective-permute-start(s32[2,3]{1,0:T(2,128)} %bitcast.11), channel_id=1, source_target_pairs={{0,24},{4,28},{8,16},{12,20},{16,8},{20,12},{24,0},{28,4},{1,25},{... | collective-permute-start | bytes 80 | tf_op jit(solution)/shard_map/ppermute | solution.py:68
  9.7 3.8 %collective-permute-start.3 = (s32[2,3]{1,0:T(2,128)}, s32[2,3]{1,0:T(2,128)S(1)}, u32[]{:S(2)}, u32[]{:S(2)}) collective-permute-start(s32[2,3]{1,0:T(2,128)} %bitcast.12), channel_id=1, source_target_pairs={{0,16},{4,20},{8,24},{12,28},{16,0},{20,4},{24,8},{28,12},{1,17},{... | collective-permute-start | bytes 80 | tf_op jit(solution)/shard_map/ppermute | solution.py:68
  10.2 3.8 %collective-permute-start.2 = (s32[2,3]{1,0:T(2,128)}, s32[2,3]{1,0:T(2,128)S(1)}, u32[]{:S(2)}, u32[]{:S(2)}) collective-permute-start(s32[2,3]{1,0:T(2,128)} %bitcast.13), channel_id=1, source_target_pairs={{0,8},{4,12},{8,0},{12,4},{16,24},{20,28},{24,16},{28,20},{1,9},{5... | collective-permute-start | bytes 80 | tf_op jit(solution)/shard_map/ppermute | solution.py:68
  10.8 1.6 %copy-start.1 = (f32[1,1,2,64,4096]{4,3,2,1,0:T(8,128)S(1)}, f32[1,1,2,64,4096]{4,3,2,1,0:T(8,128)}, u32[]{:S(2)}) copy-start(f32[1,1,2,64,4096]{4,3,2,1,0:T(8,128)} %param.4) | copy-start | bytes 6291460
  14.0 1.5 %collective-permute-start.5 = (f32[48,8,128]{2,1,0:T(8,128)S(1)}, f32[48,8,128]{2,1,0:T(8,128)S(1)}, u32[]{:S(2)}, u32[]{:S(2)}) collective-permute-start(f32[48,8,128]{2,1,0:T(8,128)S(1)} %shard_map.61.refs_2_), channel_id=1, source_target_pairs={{0,4},{4,0},{8,12},{12,8},{16,20},{20,16},{24,28},{28,24},{1,5},{5... | collective-permute-start | bytes 589832 | tf_op jit(solution)/shard_map/ppermute | solution.py:68
  16.5 6.7 %collective-permute-start.6 = (f32[128,128]{1,0:T(8,128)S(1)}, f32[128,128]{1,0:T(8,128)S(1)}, u32[]{:S(2)}, u32[]{:S(2)}) collective-permute-start(f32[128,128]{1,0:T(8,128)S(1)} %get-tuple-element.36), channel_id=1, source_target_pairs={{0,8},{4,12},{8,0},{12,4},{16,24},{20,28},{24,16},{28,20},{1,9},{5... | collective-permute-start | bytes 196616 | tf_op jit(solution)/shard_map/ppermute | solution.py:68
  17.1 6.1 %collective-permute-start.7 = (f32[128,128]{1,0:T(8,128)S(1)}, f32[128,128]{1,0:T(8,128)S(1)}, u32[]{:S(2)}, u32[]{:S(2)}) collective-permute-start(f32[128,128]{1,0:T(8,128)S(1)} %get-tuple-element.37), channel_id=1, source_target_pairs={{0,16},{4,20},{8,24},{12,28},{16,0},{20,4},{24,8},{28,12},{1,17},{... | collective-permute-start | bytes 196616 | tf_op jit(solution)/shard_map/ppermute | solution.py:68
  18.6 5.2 %collective-permute-start.8 = (f32[128,128]{1,0:T(8,128)S(1)}, f32[128,128]{1,0:T(8,128)S(1)}, u32[]{:S(2)}, u32[]{:S(2)}) collective-permute-start(f32[128,128]{1,0:T(8,128)S(1)} %get-tuple-element.38), channel_id=1, source_target_pairs={{0,24},{4,28},{8,16},{12,20},{16,8},{20,12},{24,0},{28,4},{1,25},{... | collective-permute-start | bytes 196616 | tf_op jit(solution)/shard_map/ppermute | solution.py:68
  23.8 1.4 %collective-permute-start.9 = (f32[64,128]{1,0:T(8,128)S(1)}, f32[64,128]{1,0:T(8,128)S(1)}, u32[]{:S(2)}, u32[]{:S(2)}) collective-permute-start(f32[64,128]{1,0:T(8,128)S(1)} %shard_map.66.refs_6_.refs_0_), channel_id=1, source_target_pairs={{0,4},{4,0},{8,12},{12,8},{16,20},{20,16},{24,28},{28,24},{1,5},{5... | collective-permute-start | bytes 98312 | tf_op jit(solution)/shard_map/ppermute | solution.py:68
  25.2 5.7 %collective-permute-start.12 = (f32[136,128]{1,0:T(8,128)S(1)}, f32[136,128]{1,0:T(8,128)S(1)}, u32[]{:S(2)}, u32[]{:S(2)}) collective-permute-start(f32[136,128]{1,0:T(8,128)S(1)} %shard_map.68.refs_2_.refs_0_), channel_id=1, source_target_pairs={{0,24},{4,28},{8,16},{12,20},{16,8},{20,12},{24,0},{28,4},{1,25},{... | collective-permute-start | bytes 208904 | tf_op jit(solution)/shard_map/ppermute | solution.py:68
  26.7 5.5 %collective-permute-start.11 = (f32[136,128]{1,0:T(8,128)S(1)}, f32[136,128]{1,0:T(8,128)S(1)}, u32[]{:S(2)}, u32[]{:S(2)}) collective-permute-start(f32[136,128]{1,0:T(8,128)S(1)} %shard_map.68.refs_2_.refs_0_), channel_id=1, source_target_pairs={{0,16},{4,20},{8,24},{12,28},{16,0},{20,4},{24,8},{28,12},{1,17},{... | collective-permute-start | bytes 208904 | tf_op jit(solution)/shard_map/ppermute | solution.py:68
  28.2 4.3 %collective-permute-start.10 = (f32[136,128]{1,0:T(8,128)S(1)}, f32[136,128]{1,0:T(8,128)S(1)}, u32[]{:S(2)}, u32[]{:S(2)}) collective-permute-start(f32[136,128]{1,0:T(8,128)S(1)} %shard_map.68.refs_2_.refs_0_), channel_id=1, source_target_pairs={{0,8},{4,12},{8,0},{12,4},{16,24},{20,28},{24,16},{28,20},{1,9},{5... | collective-permute-start | bytes 208904 | tf_op jit(solution)/shard_map/ppermute | solution.py:68
  32.6 1.8 %collective-permute-start.13 = (f32[4,136,128]{2,1,0:T(8,128)S(1)}, f32[4,136,128]{2,1,0:T(8,128)S(1)}, u32[]{:S(2)}, u32[]{:S(2)}) collective-permute-start(f32[4,136,128]{2,1,0:T(8,128)S(1)} %shard_map.70.refs_0_.refs_3_.refs_1_), channel_id=1, source_target_pairs={{0,4},{4,0},{8,12},{12,8},{16,20},{20,16},{24,28},{28,24},{1,5},{5... | collective-permute-start | bytes 835592 | tf_op jit(solution)/shard_map/ppermute | solution.py:68
  36.0 1.5 %collective-permute-start.14 = (f32[4,4,8,128]{3,2,1,0:T(8,128)S(1)}, f32[4,4,8,128]{3,2,1,0:T(8,128)S(1)}, u32[]{:S(2)}, u32[]{:S(2)}) collective-permute-start(f32[4,4,8,128]{3,2,1,0:T(8,128)S(1)} %get-tuple-element.47), channel_id=1, source_target_pairs={{0,4},{4,0},{8,12},{12,8},{16,20},{20,16},{24,28},{28,24},{1,5},{5... | collective-permute-start | bytes 196616 | tf_op jit(solution)/shard_map/ppermute | solution.py:68
  37.5 5.9 %collective-permute-start.16 = (f32[2,4,8,128]{3,2,1,0:T(8,128)S(1)}, f32[2,4,8,128]{3,2,1,0:T(8,128)S(1)}, u32[]{:S(2)}, u32[]{:S(2)}) collective-permute-start(f32[2,4,8,128]{3,2,1,0:T(8,128)S(1)} %get-tuple-element.51), channel_id=1, source_target_pairs={{0,8},{4,12},{8,0},{12,4},{16,24},{20,28},{24,16},{28,20},{1,9},{5... | collective-permute-start | bytes 98312 | tf_op jit(solution)/shard_map/ppermute | solution.py:68
  38.5 4.8 %collective-permute-start.17 = (f32[2,4,8,128]{3,2,1,0:T(8,128)S(1)}, f32[2,4,8,128]{3,2,1,0:T(8,128)S(1)}, u32[]{:S(2)}, u32[]{:S(2)}) collective-permute-start(f32[2,4,8,128]{3,2,1,0:T(8,128)S(1)} %get-tuple-element.52), channel_id=1, source_target_pairs={{0,16},{4,20},{8,24},{12,28},{16,0},{20,4},{24,8},{28,12},{1,17},{... | collective-permute-start | bytes 98312 | tf_op jit(solution)/shard_map/ppermute | solution.py:68
  39.4 4.8 %collective-permute-start.18 = (f32[2,4,8,128]{3,2,1,0:T(8,128)S(1)}, f32[2,4,8,128]{3,2,1,0:T(8,128)S(1)}, u32[]{:S(2)}, u32[]{:S(2)}) collective-permute-start(f32[2,4,8,128]{3,2,1,0:T(8,128)S(1)} %get-tuple-element.53), channel_id=1, source_target_pairs={{0,24},{4,28},{8,16},{12,20},{16,8},{20,12},{24,0},{28,4},{1,25},{... | collective-permute-start | bytes 98312 | tf_op jit(solution)/shard_map/ppermute | solution.py:68
  42.6 7.4 %collective-permute-start.15 = (f32[128,128]{1,0:T(8,128)S(1)}, f32[128,128]{1,0:T(8,128)S(1)}, u32[]{:S(2)}, u32[]{:S(2)}) collective-permute-start(f32[128,128]{1,0:T(8,128)S(1)} %get-tuple-element.50.refs_5_.refs_0_), channel_id=1, source_target_pairs={{0,2},{1,3},{2,0},{3,1},{4,6},{5,7},{6,4},{7,5},{8,10},{9,11},{10,... | collective-permute-start | bytes 196616 | tf_op jit(solution)/shard_map/ppermute | solution.py:68
  44.5 7.5 %collective-permute-start.19 = (f32[128,128]{1,0:T(8,128)S(1)}, f32[128,128]{1,0:T(8,128)S(1)}, u32[]{:S(2)}, u32[]{:S(2)}) collective-permute-start(f32[128,128]{1,0:T(8,128)S(1)} %get-tuple-element.56), channel_id=1, source_target_pairs={{0,1},{1,0},{2,3},{3,2},{4,5},{5,4},{6,7},{7,6},{8,9},{9,8},{10,11... | collective-permute-start | bytes 196616 | tf_op jit(solution)/shard_map/ppermute | solution.py:68
  45.2 8.1 %collective-permute-start.20 = (f32[128,128]{1,0:T(8,128)S(1)}, f32[128,128]{1,0:T(8,128)S(1)}, u32[]{:S(2)}, u32[]{:S(2)}) collective-permute-start(f32[128,128]{1,0:T(8,128)S(1)} %get-tuple-element.57), channel_id=1, source_target_pairs={{0,2},{1,3},{2,0},{3,1},{4,6},{5,7},{6,4},{7,5},{8,10},{9,11},{10,... | collective-permute-start | bytes 196616 | tf_op jit(solution)/shard_map/ppermute | solution.py:68
  46.7 6.6 %collective-permute-start.21 = (f32[128,128]{1,0:T(8,128)S(1)}, f32[128,128]{1,0:T(8,128)S(1)}, u32[]{:S(2)}, u32[]{:S(2)}) collective-permute-start(f32[128,128]{1,0:T(8,128)S(1)} %get-tuple-element.58), channel_id=1, source_target_pairs={{0,3},{1,2},{2,1},{3,0},{4,7},{5,6},{6,5},{7,4},{8,11},{9,10},{10,... | collective-permute-start | bytes 196616 | tf_op jit(solution)/shard_map/ppermute | solution.py:68
  50.0 6.9 %collective-permute-start.25 = (f32[128,128]{1,0:T(8,128)S(1)}, f32[128,128]{1,0:T(8,128)S(1)}, u32[]{:S(2)}, u32[]{:S(2)}) collective-permute-start(f32[128,128]{1,0:T(8,128)S(1)} %shard_map.78.refs_2_.refs_4_.refs_0_), channel_id=1, source_target_pairs={{0,1},{1,0},{2,3},{3,2},{4,5},{5,4},{6,7},{7,6},{8,9},{9,8},{10,11... | collective-permute-start | bytes 196616 | tf_op jit(solution)/shard_map/ppermute | solution.py:68
  53.3 5.3 %collective-permute-start.24 = (f32[128,128]{1,0:T(8,128)S(1)}, f32[128,128]{1,0:T(8,128)S(1)}, u32[]{:S(2)}, u32[]{:S(2)}) collective-permute-start(f32[128,128]{1,0:T(8,128)S(1)} %shard_map.80.refs_3_.refs_0_), channel_id=1, source_target_pairs={{0,24},{4,28},{8,16},{12,20},{16,8},{20,12},{24,0},{28,4},{1,25},{... | collective-permute-start | bytes 196616 | tf_op jit(solution)/shard_map/ppermute | solution.py:68
  54.8 4.4 %collective-permute-start.23 = (f32[128,128]{1,0:T(8,128)S(1)}, f32[128,128]{1,0:T(8,128)S(1)}, u32[]{:S(2)}, u32[]{:S(2)}) collective-permute-start(f32[128,128]{1,0:T(8,128)S(1)} %shard_map.80.refs_3_.refs_0_), channel_id=1, source_target_pairs={{0,16},{4,20},{8,24},{12,28},{16,0},{20,4},{24,8},{28,12},{1,17},{... | collective-permute-start | bytes 196616 | tf_op jit(solution)/shard_map/ppermute | solution.py:68
  55.8 4.3 %collective-permute-start.22 = (f32[128,128]{1,0:T(8,128)S(1)}, f32[128,128]{1,0:T(8,128)S(1)}, u32[]{:S(2)}, u32[]{:S(2)}) collective-permute-start(f32[128,128]{1,0:T(8,128)S(1)} %shard_map.80.refs_3_.refs_0_), channel_id=1, source_target_pairs={{0,8},{4,12},{8,0},{12,4},{16,24},{20,28},{24,16},{28,20},{1,9},{5... | collective-permute-start | bytes 196616 | tf_op jit(solution)/shard_map/ppermute | solution.py:68
  60.1 1.8 %collective-permute-start.26 = (f32[4,128,128]{2,1,0:T(8,128)S(1)}, f32[4,128,128]{2,1,0:T(8,128)S(1)}, u32[]{:S(2)}, u32[]{:S(2)}) collective-permute-start(f32[4,128,128]{2,1,0:T(8,128)S(1)} %shard_map.82.refs_3_.refs_0_), channel_id=1, source_target_pairs={{0,4},{4,0},{8,12},{12,8},{16,20},{20,16},{24,28},{28,24},{1,5},{5... | collective-permute-start | bytes 786440 | tf_op jit(solution)/shard_map/ppermute | solution.py:68

commit v5 on v4

--- a/solution.py
+++ b/solution.py
@@ -158,6 +158,10 @@
 pivot_rows = 16
 
 
+def first_steps(count):
+    return count * 3 // 4
+
+
 def start_inverse(grams, other, scale, after):
     size = grams[0].shape[-1]
     step = pivot_rows
@@ -183,11 +187,11 @@
                 total = add_tree([part[at, :] for part in parts])
                 held.append(scale * total * refs[0][at, :])
         held_ref, left_ref, right_ref = refs[:3] if own else refs[1:]
-        held = eliminate(held, left_ref, right_ref, range(count // 2))
+        held = eliminate(held, left_ref, right_ref, range(first_steps(count)))
         for block in range(count):
             at = slice(step * block, step * block + step)
             held_ref[at, :] = held[block]
-            if block >= count // 2:
+            if block >= first_steps(count):
                 left_ref[at, :] = jnp.zeros_like(held[block])
                 right_ref[at, :] = jnp.zeros_like(held[block])
 
@@ -201,11 +205,11 @@
     count = size // step
 
     def body(held_ref, left_in, right_in, out_ref, left_ref, right_ref):
-        half = size // 2
-        left_ref[:half, :] = left_in[:half, :]
-        right_ref[:half, :] = right_in[:half, :]
+        done = first_steps(count) * step
+        left_ref[:done, :] = left_in[:done, :]
+        right_ref[:done, :] = right_in[:done, :]
         rows = [held_ref[step * block : step * block + step, :] for block in range(count)]
-        eliminate(rows, left_ref, right_ref, range(count // 2, count))
+        eliminate(rows, left_ref, right_ref, range(first_steps(count), count))
         out_ref[...] = lax.dot_general(
             left_ref[...],
             right_ref[...],
@@ -286,57 +290,63 @@
     )[0]
 
 
-def pick_pieces(coords, own, mine, theirs, narrow_size, after):
+def gram_of(items):
+    rank = items[0].shape[-1]
+
+    def body(*refs):
+        rows = jnp.concatenate([ref[...].reshape(-1, rank) for ref in refs[:-1]], axis=0)
+        refs[-1][...] = join_gram(gram_parts(rows))
+
+    return kernel_call(body, [shaped(rank, rank)], list(items))[0]
+
+
+def pick_pieces(coords, own, mine, theirs, gram, narrow_size):
     own_blocks, low, rows, rank = own.shape
     partners, slots, _ = coords.shape
     piece_rows = slots * 2 * low * rows
     share = rank // low
 
-    def body(there_ref, own_ref, mine_ref, theirs_ref, *refs):
-        out_refs, (coord_ref, gram_ref, sem) = refs[:partners], refs[partners:]
+    def body(there_ref, own_ref, mine_ref, theirs_ref, gram_here, *refs):
+        out_refs, (coord_ref, gram_ref, all_ref, sem) = refs[:partners], refs[partners:]
         narrow_at = lax.axis_index("narrow")
         core = lax.axis_index("wide") % low
         copy = pltpu.make_async_copy(there_ref, coord_ref, sem)
         copy.start()
-        here, there = mine_ref[...].reshape(-1, rank), theirs_ref[...].reshape(-1, rank)
-        rows_of = [jnp.where(core == j, here, there) for j in range(low)]
-        gram_ref[...] = join_gram(
-            gram_parts(jnp.concatenate([own_ref[...].reshape(-1, rank)] + rows_of, axis=0))
-        )
+        gram_ref[...] = gram_here[...] + join_gram(gram_parts(theirs_ref[...].reshape(-1, rank)))
         for out_ref in out_refs:
             out_ref[piece_rows:, :] = gram_ref[pl.ds(pl.multiple_of(core * share, share), share), :]
+        for j in range(low):
+            for local in range(own_blocks):
+                all_ref[j * own_blocks + local] = own_ref[local, j]
+                for m in range(1, narrow_size):
+                    last = m == narrow_size - 1
+                    holder = j if last else (m - 1) % low
+                    at = (m - 1) // low * own_blocks * low + local * low + j
+                    if last:
+                        at = (narrow_size - 2) * own_blocks + local
+                    all_ref[(m * low + j) * own_blocks + local] = jnp.where(
+                        core == holder, mine_ref[at], theirs_ref[at]
+                    )
         copy.wait()
         for d, out_ref in enumerate(out_refs):
             for pair in range(slots * 2):
                 block = coord_ref[d, pair // 2, 1 + pair % 2]
                 owner = (block // own_blocks) ^ narrow_at
-                local = block % own_blocks
-                before = jnp.maximum(owner, 1) - 1
-                last = before == narrow_size - 2
                 for j in range(low):
-                    slice_at = core ^ j
-                    holder = jnp.where(last, slice_at, before % low)
-                    at = jnp.where(
-                        last,
-                        (narrow_size - 2) * own_blocks + local,
-                        (before // low * own_blocks + local) * low + slice_at,
-                    )
-                    away = jnp.where(holder == core, mine_ref[at], theirs_ref[at])
+                    at = (owner * low + (core ^ j)) * own_blocks + block % own_blocks
                     to = (pair * low + j) * rows
-                    out_ref[to : to + rows, :] = jnp.where(
-                        owner == 0, own_ref[local, slice_at], away
-                    )
+                    out_ref[to : to + rows, :] = all_ref[at]
 
     return kernel_call(
         body,
         [shaped(piece_rows + share, rank)] * partners,
-        [coords, own, mine, theirs],
+        [coords, own, mine, theirs, gram],
         scratch=[
             pltpu.SMEM(coords.shape, jnp.int32),
             pltpu.VMEM((rank, rank), jnp.float32),
+            pltpu.VMEM((narrow_size * low * own_blocks, rows, rank), jnp.float32),
             pltpu.SemaphoreType.DMA,
         ],
-        after=after,
     )
 
 
@@ -411,10 +421,11 @@
                     rest = value - high
                     middle = rest.astype(jnp.bfloat16).astype(jnp.float32)
                     low = rest - middle
-                    other_high, other_middle, other_low = roll(high), roll(middle), roll(low)
+                    first = roll(jnp.where(left, middle, high))
+                    second = roll(jnp.where(left, high, low))
                     rows = [
-                        [jnp.where(left, high, other_middle), jnp.where(left, low, other_high)],
-                        [jnp.where(left, other_high, middle), jnp.where(left, other_low, high)],
+                        [jnp.where(left, high, first), jnp.where(left, low, second)],
+                        [jnp.where(left, first, middle), jnp.where(left, second, high)],
                     ]
                     row_at = pl.multiple_of((at // lanes + inner) * lanes, lanes)
                     for half in range(2):
@@ -484,35 +495,55 @@
     return high, middle, low
 
 
-def second_mode(terms, inverse, spread_blocks, rows, wide_size):
+def tag_of(ref, d, slots, edge, slot, at):
+    return ref[d, slots * edge + slot : slots * edge + slot + 1, at : at + 1]
+
+
+def sum_terms(terms, own, slots, edge, after):
+    partners, _, rank = terms.shape
+
+    def body(term_ref, own_ref, out_ref):
+        for slot in range(slots):
+            here = tag_of(own_ref, 0, slots, edge, slot, 0)
+            total = None
+            for d in range(partners):
+                for other in range(slots):
+                    same = (tag_of(term_ref, d, slots, edge, other, 0) == here).astype(jnp.float32)
+                    part = term_ref[d, other * edge : (other + 1) * edge, :] * same
+                    total = part if total is None else total + part
+            out_ref[slot * edge : (slot + 1) * edge, :] = total
+
+    return kernel_call(body, [shaped(slots * edge, rank)], [terms, own], after=after)[0]
+
+
+def second_mode(partial, terms, inverse, spread_blocks, rows, wide_size):
     low = len(terms)
     pairs, edge, rank = rows.shape
     slots = pairs // 2
     slice_rows = edge // wide_size
     chunk = 4
 
-    def tag_of(ref, d, slot, at):
-        return ref[d, slots * edge + slot : slots * edge + slot + 1, at : at + 1]
-
-    def body(*refs):
+    def body(partial_ref, *refs):
         term_refs = refs[: len(terms)]
         inverse_ref, spread_ref, rows_ref = refs[len(terms) : len(terms) + 3]
         out_refs = refs[len(terms) + 3 : len(terms) + 3 + low]
         held_ref = refs[-1]
         sums = []
         for slot in range(slots):
-            total = None
+            total = partial_ref[slot * edge : (slot + 1) * edge, :]
+            here = tag_of(term_refs[0], 0, slots, edge, slot, 0)
             for m in range(wide_size):
+                if m % low == 0:
+                    continue
                 for other in range(slots):
-                    there = tag_of(term_refs[m % low], m // low, other, 0)
-                    same = (there == tag_of(term_refs[0], 0, slot, 0)).astype(jnp.float32)
-                    here = slice(other * edge, (other + 1) * edge)
-                    part = term_refs[m % low][m // low, here, :] * same
-                    total = part if total is None else total + part
+                    there = tag_of(term_refs[m % low], m // low, slots, edge, other, 0)
+                    same = (there == here).astype(jnp.float32)
+                    part = term_refs[m % low][m // low, other * edge : (other + 1) * edge, :]
+                    total = total + part * same
             sums.append(total)
         aux = times(jnp.concatenate(sums, axis=0), inverse_ref[...])
         for slot in range(slots):
-            weight = tag_of(term_refs[0], 0, slot, live_at)
+            weight = tag_of(term_refs[0], 0, slots, edge, slot, live_at)
             stacked = stack_parts(aux[slot * edge : (slot + 1) * edge] * weight)
             rows_i, rows_j = rows_ref[2 * slot], rows_ref[2 * slot + 1]
 
@@ -547,7 +578,7 @@
     return kernel_call(
         body,
         [shaped(wide_size // low, 2 * slots, slice_rows, rank)] * low,
-        list(terms) + [inverse, spread_blocks, rows],
+        [partial] + list(terms) + [inverse, spread_blocks, rows],
         scratch=[pltpu.VMEM((2 * slots, edge, rank), jnp.float32)],
         about_us=2.5,
     )
@@ -732,23 +763,41 @@
     return kernel_call(body, [shaped(rows, rank)], list(parts), after=after)[0]
 
 
-def solve_rows(parts, inverse, own_blocks):
-    low = len(parts)
-    partners, part_rows, rank = parts[0].shape
+def solve_rows(rows, inverse, after):
+    shape = rows.shape
+
+    def body(rows_ref, inverse_ref, out_ref):
+        solved = times(rows_ref[...].reshape(-1, shape[-1]), inverse_ref[...])
+        out_ref[...] = solved.reshape(shape)
+
+    return kernel_call(body, [shaped(*shape)], [rows, inverse], after=after)[0]
+
+
+def lay_rows(solved, others, inverse, own_blocks):
+    low = 1 + len(others)
+    partners, part_rows, rank = solved.shape
     rows = part_rows // own_blocks
 
-    def body(*refs):
+    def body(solved_ref, *refs):
         wide_at = lax.axis_index("wide")
+        inverse_ref, out_ref = refs[len(others) :]
         for j in range(low):
-            solved = times(refs[j][...].reshape(partners * part_rows, rank), refs[low][...])
+            if j == 0:
+                value = solved_ref[...].reshape(partners * part_rows, rank)
+            else:
+                value = times(
+                    refs[j - 1][...].reshape(partners * part_rows, rank), inverse_ref[...]
+                )
             for d in range(partners):
                 place = wide_at ^ (d * low + j)
                 for block in range(own_blocks):
                     at = d * part_rows + block * rows
-                    refs[-1][block, place] = solved[at : at + rows]
-
-    return kernel_call(
-        body, [shaped(own_blocks, partners * low, rows, rank)], list(parts) + [inverse]
+                    out_ref[block, place] = value[at : at + rows]
+
+    return kernel_call(
+        body,
+        [shaped(own_blocks, partners * low, rows, rank)],
+        [solved] + list(others) + [inverse],
     )[0]
 
 
@@ -774,7 +823,8 @@
     theirs = swap_with(mine, "wide", 1)
     tags, coords = open_tags(block_coords[0, 0], block_count, rank, [mine])
     coords = pack_whole([coords] + arrived)
-    wanted = pick_pieces(coords, chip_slice, mine, theirs, narrow_size, [])
+    gram = gram_of([chip_slice, mine])
+    wanted = pick_pieces(coords, chip_slice, mine, theirs, gram, narrow_size)
     pieces = exchange(wanted, "wide", skip=1)
 
     spread, turned = split_blocks(blocks, wanted[:1])
@@ -788,7 +838,8 @@
     column_terms = with_partners(terms, low)
     all_coords = read_coords(column_terms, slots, edge, block_coords.shape[3])
 
-    groups = second_mode(column_terms, inverse_b, turned, rows, wide_size)
+    partial = sum_terms(terms, terms, slots, edge, [inverse_b])
+    groups = second_mode(partial, column_terms, inverse_b, turned, rows, wide_size)
     plan = plan_sums(all_coords, slice_rows, narrow_size, own_blocks, groups[:1])
     groups = [groups[0]] + [swap_with(groups[j], "wide", j) for j in range(1, low)]
     packed = pack_pieces(groups, [plan])
@@ -808,7 +859,8 @@
     started = start_inverse(grams, gram_b, 2.0, [total])
     totals = pack_whole(gather_from(total, "wide", skip=1), after=started[:1])
     inverse_a = end_inverse(*started, [totals])
-    orbital_new = solve_rows(with_partners(totals, low), inverse_a, own_blocks)
+    solved = solve_rows(totals, inverse_a, [])
+    orbital_new = lay_rows(solved, with_partners(totals, low)[1:], inverse_a, own_blocks)
     return (aux_owned[None], orbital_new.reshape(own_blocks * edge, rank))
 
 

time: 63.4 us -> 62.3 us (0.983)
    pallas_call x26 -> x29, Pallas kernels: 20.1 us -> 19.8 us  [kernel_call(): pl.pallas_call(whole, out_shape=outputs, in_specs=[in_smem] * scalars + [...]
  transfers between devices with their start and end apart: 27 -> 27, of which waited for: 12 -> 13; matrix products, arithmetic and copies ran while one was open for 0% -> 0% of each run, Pallas kernels for 26% -> 26%
where the time goes in v5:
time: 62.3 us; the launch traced here: 62.1 us
  starting transfers between devices  28.9 us (46%)
  Pallas kernels  19.8 us (32%)
  waiting for transfers between devices  9.12 us (15%)
  local copies, waits for them, and re-layouts  2.62 us (4%)
  between operations  1.58 us (3%)
    ppermute x26, starting transfers between devices, swap_with(): lax.ppermute(value, axis, [(index, index ^ mask) for index in range(size)])  25.8 us
    pallas_call x29, Pallas kernels, kernel_call(): pl.pallas_call(whole, out_shape=outputs, in_specs=[in_smem] * scalars + [...  19.8 us
    ppermute x26, waiting for transfers between devices, swap_with(): lax.ppermute(value, axis, [(index, index ^ mask) for index in range(size)])  9.11 us
    ppermute x1, starting transfers between devices, send_by_core(): return lax.ppermute(value, ('wide', 'narrow'), pairs)  3.09 us
    unnamed x6, local copies, waits for them, and re-layouts  2.61 us
  transfers between devices with their start and end apart: 27, of which 13 were waited for; matrix products, arithmetic and copies ran while one was open for 0% of the time, Pallas kernels for 26%

profile of v5, /device:TPU:0, one launch (start us, length us, event | category | flops | bytes accessed | tf_op | source)
XLA Modules:
  0.0 62.1 jit_solution(16112716133947823653)
XLA Ops:
  0.6 0.0 copy-start
  0.6 0.0 copy-start.2
  0.7 1.0 %copy-done = f32[1024,128]{1,0:T(8,128)S(1)} copy-done((f32[1024,128]{1,0:T(8,128)S(1)}, f32[1024,128]{1,0:T(8,128)}, u32[]{:S(2)}) %copy-start) | copy-done | bytes 524312
  1.7 3.1 %collective-permute-start = (f32[16,2,8,128]{3,2,1,0:T(8,128)S(1)}, f32[16,2,8,128]{3,2,1,0:T(8,128)S(1)}, u32[]{:S(2)}, u32[]{:S(2)}) collective-permute-start(f32[16,2,8,128]{3,2,1,0:T(8,128)S(1)} %dynamic-slice_bitcast_fusion.refs_0_.refs_1_), channel_id=1, source_target_pairs={{0,1},{1,0},{2,3},{3,2},{4,6},{5,7},{6,4},{7,5},{8,9},{9,8},{10,11... | collective-permute-start | bytes 393224 | tf_op jit(solution)/shard_map/ppermute | solution.py:78
  4.8 2.5 %collective-permute-start.1 = (f32[16,8,128]{2,1,0:T(8,128)S(1)}, f32[16,8,128]{2,1,0:T(8,128)S(1)}, u32[]{:S(2)}, u32[]{:S(2)}) collective-permute-start(f32[16,8,128]{2,1,0:T(8,128)S(1)} %shard_map.59.refs_1_), channel_id=1, source_target_pairs={{0,3},{1,2},{2,1},{3,0},{4,7},{5,6},{6,5},{7,4},{8,11},{9,10},{10,... | collective-permute-start | bytes 196616 | tf_op jit(solution)/shard_map/ppermute | solution.py:68
  7.3 2.4 %collective-permute-start.4 = (s32[2,3]{1,0:T(2,128)}, s32[2,3]{1,0:T(2,128)S(1)}, u32[]{:S(2)}, u32[]{:S(2)}) collective-permute-start(s32[2,3]{1,0:T(2,128)} %bitcast.11), channel_id=1, source_target_pairs={{0,24},{4,28},{8,16},{12,20},{16,8},{20,12},{24,0},{28,4},{1,25},{... | collective-permute-start | bytes 80 | tf_op jit(solution)/shard_map/ppermute | solution.py:68
  9.7 0.5 collective-permute-start.3
  10.2 0.5 collective-permute-start.2
  10.8 1.6 %copy-done.1 = f32[1,1,2,64,4096]{4,3,2,1,0:T(8,128)S(1)} copy-done((f32[1,1,2,64,4096]{4,3,2,1,0:T(8,128)S(1)}, f32[1,1,2,64,4096]{4,3,2,1,0:T(8,128)}, u32[]{:S(2)}) %copy-start.1) | copy-done | bytes 2097176
  12.3 0.1 shard_map.60.refs_5_.refs_0_
  12.5 0.0 collective-permute-done.4.refs_4_.refs_3_
  12.5 1.0 %collective-permute-done.3.refs_3_.refs_2_ = s32[2,3]{1,0:T(2,128)S(1)} collective-permute-done((s32[2,3]{1,0:T(2,128)}, s32[2,3]{1,0:T(2,128)S(1)}, u32[]{:S(2)}, u32[]{:S(2)}) %collective-permute-start.3) | collective-permute-done | bytes 56 | tf_op jit(solution)/shard_map/ppermute | solution.py:68
  13.5 0.5 collective-permute-done.2.refs_2_.refs_1_
  14.0 0.1 collective-permute-start.5
  14.7 0.4 shard_map.64.refs_4_
  15.2 0.1 shard_map.62
  15.3 0.3 collective-permute-done.5.refs_3_
  15.5 0.8 %shard_map.65 = (f32[128,128]{1,0:T(8,128)S(1)}, f32[128,128]{1,0:T(8,128)S(1)}, f32[128,128]{1,0:T(8,128)S(1)}, f32[128,128]{1,0:T(8,128)S(1)}) custom-call(s32[4,2,3]{2,1,0:T(2,128)S(1)} %shard_map.63.refs_0_, f32[16,2,8,128]{3,2,1,0:T(8,128)S(1)} %dynamic-slice_bitcast_fusion.refs_0_.refs_1_, f32[48,8,128]{2,1,0:T(8,128)S(1)} %shard_map.61.refs_2_.refs_1_, ...), custom_call_target="tpu_custom_call" | custom-call | flops 300000 | tf_op jit(solution)/shard_map/pallas_call | solution.py:30
  16.3 0.6 collective-permute-start.6
  16.9 1.5 %collective-permute-start.7 = (f32[128,128]{1,0:T(8,128)S(1)}, f32[128,128]{1,0:T(8,128)S(1)}, u32[]{:S(2)}, u32[]{:S(2)}) collective-permute-start(f32[128,128]{1,0:T(8,128)S(1)} %get-tuple-element.37), channel_id=1, source_target_pairs={{0,16},{4,20},{8,24},{12,28},{16,0},{20,4},{24,8},{28,12},{1,17},{... | collective-permute-start | bytes 196616 | tf_op jit(solution)/shard_map/ppermute | solution.py:68
  18.4 1.4 %collective-permute-start.8 = (f32[128,128]{1,0:T(8,128)S(1)}, f32[128,128]{1,0:T(8,128)S(1)}, u32[]{:S(2)}, u32[]{:S(2)}) collective-permute-start(f32[128,128]{1,0:T(8,128)S(1)} %get-tuple-element.38), channel_id=1, source_target_pairs={{0,24},{4,28},{8,16},{12,20},{16,8},{20,12},{24,0},{28,4},{1,25},{... | collective-permute-start | bytes 196616 | tf_op jit(solution)/shard_map/ppermute | solution.py:68
  19.9 3.0 %shard_map.66 = (bf16[2,4096,256]{2,1,0:T(8,128)(2,1)S(1)}, bf16[2,4096,256]{2,1,0:T(8,128)(2,1)S(1)}) custom-call(f32[2,64,4096]{2,1,0:T(8,128)S(1)} %shard_map.60.refs_5_.refs_0_, f32[128,128]{1,0:T(8,128)S(1)} %get-tuple-element.35.refs_1_.refs_0_), custom_call_target="tpu_custom_call" | custom-call | flops 300000 | tf_op jit(solution)/shard_map/pallas_call | solution.py:30
  22.9 0.7 %collective-permute-done.8.refs_3_.refs_4_ = f32[128,128]{1,0:T(8,128)S(1)} collective-permute-done((f32[128,128]{1,0:T(8,128)S(1)}, f32[128,128]{1,0:T(8,128)S(1)}, u32[]{:S(2)}, u32[]{:S(2)}) %collective-permute-start.8) | collective-permute-done | bytes 65568 | tf_op jit(solution)/shard_map/ppermute | solution.py:68
  23.6 0.1 collective-permute-start.9
  23.7 1.3 %shard_map.68 = (f32[4,64,128]{2,1,0:T(8,128)S(1)}, f32[136,128]{1,0:T(8,128)S(1)}) custom-call(f32[8,128]{1,0:T(8,128)S(1)} %get-tuple-element.33.refs_0_, f32[128,128]{1,0:T(8,128)S(1)} %get-tuple-element.35.refs_1_.refs_0_, f32[128,128]{1,0:T(8,128)S(1)} %collective-permute-done.6.refs_1_.refs_2_, f32[128,128]{1,0:T(8,128)S(1)} %collective-permute-done.7.refs_2_.refs_3_, ...), custom_call_target="tpu_custom_call" | custom-call | flops 3000000 | tf_op jit(solution)/shard_map/pallas_call | solution.py:30
  25.0 1.5 %collective-permute-start.12 = (f32[136,128]{1,0:T(8,128)S(1)}, f32[136,128]{1,0:T(8,128)S(1)}, u32[]{:S(2)}, u32[]{:S(2)}) collective-permute-start(f32[136,128]{1,0:T(8,128)S(1)} %shard_map.69.refs_2_.refs_0_), channel_id=1, source_target_pairs={{0,24},{4,28},{8,16},{12,20},{16,8},{20,12},{24,0},{28,4},{1,25},{... | collective-permute-start | bytes 208904 | tf_op jit(solution)/shard_map/ppermute | solution.py:68
  26.5 1.5 %collective-permute-start.11 = (f32[136,128]{1,0:T(8,128)S(1)}, f32[136,128]{1,0:T(8,128)S(1)}, u32[]{:S(2)}, u32[]{:S(2)}) collective-permute-start(f32[136,128]{1,0:T(8,128)S(1)} %shard_map.69.refs_2_.refs_0_), channel_id=1, source_target_pairs={{0,16},{4,20},{8,24},{12,28},{16,0},{20,4},{24,8},{28,12},{1,17},{... | collective-permute-start | bytes 208904 | tf_op jit(solution)/shard_map/ppermute | solution.py:68
  28.0 0.5 collective-permute-start.10
  28.6 2.4 %shard_map.70 = (f32[128,128]{1,0:T(8,128)S(1)}, f32[128,128]{1,0:T(8,128)S(1)}, f32[128,128]{1,0:T(8,128)S(1)}, f32[128,128]{1,0:T(8,128)S(1)}) custom-call(f32[64,128]{1,0:T(8,128)S(1)} %shard_map.67.refs_6_.refs_0_, f32[64,128]{1,0:T(8,128)S(1)} %collective-permute-done.9.refs_1_, f32[136,128]{1,0:T(8,128)S(1)} %shard_map.69.refs_2_.refs_0_), custom_call_target="tpu_custom_call" | custom-call | flops 1800000 | tf_op jit(solution)/shard_map/pallas_call | solution.py:30
  30.9 1.1 %collective-permute-done.11.refs_2_ = f32[136,128]{1,0:T(8,128)S(1)} collective-permute-done((f32[136,128]{1,0:T(8,128)S(1)}, f32[136,128]{1,0:T(8,128)S(1)}, u32[]{:S(2)}, u32[]{:S(2)}) %collective-permute-start.11) | collective-permute-done | bytes 69664 | tf_op jit(solution)/shard_map/ppermute | solution.py:68
  32.1 0.3 collective-permute-done.10.refs_1_
  32.4 0.1 collective-permute-start.13
  32.4 0.8 %shard_map.73.refs_2_.refs_3_ = f32[128,128]{1,0:T(8,128)S(1)} custom-call(f32[128,128]{1,0:T(8,128)S(1)} %get-tuple-element.42.refs_4_.refs_0_, f32[128,128]{1,0:T(8,128)S(1)} %get-tuple-element.43.refs_1_, f32[128,128]{1,0:T(8,128)S(1)} %get-tuple-element.44.refs_2_, f32[4,136,128]{2,1,0:T(8,128)S(1)} %shard_map.71.refs_0_.refs_3_.refs_1_), custom_call_target="tpu_custom_call" | custom-call | flops 1600000 | tf_op jit(solution)/shard_map/pallas_call | solution.py:30
  33.3 0.1 shard_map.74.refs_0_
  33.4 0.6 %collective-permute-done.13.refs_1_.refs_2_ = f32[4,136,128]{2,1,0:T(8,128)S(1)} collective-permute-done((f32[4,136,128]{2,1,0:T(8,128)S(1)}, f32[4,136,128]{2,1,0:T(8,128)S(1)}, u32[]{:S(2)}, u32[]{:S(2)}) %collective-permute-start.13) | collective-permute-done | bytes 278560 | tf_op jit(solution)/shard_map/ppermute | solution.py:68
  34.0 1.5 %shard_map.75 = (f32[4,4,8,128]{3,2,1,0:T(8,128)S(1)}, f32[4,4,8,128]{3,2,1,0:T(8,128)S(1)}) custom-call(f32[128,128]{1,0:T(8,128)S(1)} %shard_map.74.refs_0_, f32[4,136,128]{2,1,0:T(8,128)S(1)} %shard_map.71.refs_0_.refs_3_.refs_1_, f32[4,136,128]{2,1,0:T(8,128)S(1)} %collective-permute-done.13.refs_1_.refs_2_, f32[128,128]{1,0:T(8,128)S(1)} %shard_map.73.refs_2_.refs_3_, ...), custom_call_target="tpu_custom_call" | custom-call | flops 2500000 | tf_op jit(solution)/shard_map/pallas_call | solution.py:30
  35.5 0.2 collective-permute-start.14
  35.7 0.9 %shard_map.76.refs_2_.refs_0_ = bf16[512,256]{1,0:T(8,128)(2,1)S(1)} custom-call(s32[8,2,3]{2,1,0:T(2,128)S(1)} %shard_map.72.refs_0_, f32[4,4,8,128]{3,2,1,0:T(8,128)S(1)} %get-tuple-element.46.refs_1_.refs_0_), custom_call_target="tpu_custom_call" | custom-call | flops 300000 | tf_op jit(solution)/shard_map/pallas_call | solution.py:30
  36.6 0.2 collective-permute-done.14.refs_1_
  36.8 0.9 %collective-permute-start.16 = (f32[2,4,8,128]{3,2,1,0:T(8,128)S(1)}, f32[2,4,8,128]{3,2,1,0:T(8,128)S(1)}, u32[]{:S(2)}, u32[]{:S(2)}) collective-permute-start(f32[2,4,8,128]{3,2,1,0:T(8,128)S(1)} %get-tuple-element.51), channel_id=1, source_target_pairs={{0,8},{4,12},{8,0},{12,4},{16,24},{20,28},{24,16},{28,20},{1,9},{5... | collective-permute-start | bytes 98312 | tf_op jit(solution)/shard_map/ppermute | solution.py:68
  37.7 1.0 %collective-permute-start.17 = (f32[2,4,8,128]{3,2,1,0:T(8,128)S(1)}, f32[2,4,8,128]{3,2,1,0:T(8,128)S(1)}, u32[]{:S(2)}, u32[]{:S(2)}) collective-permute-start(f32[2,4,8,128]{3,2,1,0:T(8,128)S(1)} %get-tuple-element.52), channel_id=1, source_target_pairs={{0,16},{4,20},{8,24},{12,28},{16,0},{20,4},{24,8},{28,12},{1,17},{... | collective-permute-start | bytes 98312 | tf_op jit(solution)/shard_map/ppermute | solution.py:68
  38.7 1.7 %collective-permute-start.18 = (f32[2,4,8,128]{3,2,1,0:T(8,128)S(1)}, f32[2,4,8,128]{3,2,1,0:T(8,128)S(1)}, u32[]{:S(2)}, u32[]{:S(2)}) collective-permute-start(f32[2,4,8,128]{3,2,1,0:T(8,128)S(1)} %get-tuple-element.53), channel_id=1, source_target_pairs={{0,24},{4,28},{8,16},{12,20},{16,8},{20,12},{24,0},{28,4},{1,25},{... | collective-permute-start | bytes 98312 | tf_op jit(solution)/shard_map/ppermute | solution.py:68
  40.4 1.6 %shard_map.78 = (f32[128,128]{1,0:T(8,128)S(1)}, f32[16,64,128]{2,1,0:T(8,128)S(1)}) custom-call(s32[8,2,3]{2,1,0:T(2,128)S(1)} %shard_map.72.refs_0_, f32[4,136,128]{2,1,0:T(8,128)S(1)} %shard_map.71.refs_0_.refs_3_.refs_1_, f32[4,136,128]{2,1,0:T(8,128)S(1)} %collective-permute-done.13.refs_1_.refs_2_, f32[128,128]{1,0:T(8,128)S(1)} %shard_map.73.refs_2_.refs_3_, ...), custom_call_target="tpu_custom_call" | custom-call | flops 100000 | tf_op jit(solution)/shard_map/pallas_call | solution.py:30
  42.0 0.6 %collective-permute-start.15 = (f32[128,128]{1,0:T(8,128)S(1)}, f32[128,128]{1,0:T(8,128)S(1)}, u32[]{:S(2)}, u32[]{:S(2)}) collective-permute-start(f32[128,128]{1,0:T(8,128)S(1)} %get-tuple-element.50.refs_5_.refs_0_), channel_id=1, source_target_pairs={{0,2},{1,3},{2,0},{3,1},{4,6},{5,7},{6,4},{7,5},{8,10},{9,11},{10,... | collective-permute-start | bytes 196616 | tf_op jit(solution)/shard_map/ppermute | solution.py:68
  42.6 0.9 %collective-permute-done.18.refs_4_ = f32[2,4,8,128]{3,2,1,0:T(8,128)S(1)} collective-permute-done((f32[2,4,8,128]{3,2,1,0:T(8,128)S(1)}, f32[2,4,8,128]{3,2,1,0:T(8,128)S(1)}, u32[]{:S(2)}, u32[]{:S(2)}) %collective-permute-start.18) | collective-permute-done | bytes 32800 | tf_op jit(solution)/shard_map/ppermute | solution.py:68
  43.5 0.3 shard_map.79
  43.8 0.7 %collective-permute-start.19 = (f32[128,128]{1,0:T(8,128)S(1)}, f32[128,128]{1,0:T(8,128)S(1)}, u32[]{:S(2)}, u32[]{:S(2)}) collective-permute-start(f32[128,128]{1,0:T(8,128)S(1)} %get-tuple-element.56), channel_id=1, source_target_pairs={{0,1},{1,0},{2,3},{3,2},{4,5},{5,4},{6,7},{7,6},{8,9},{9,8},{10,11... | collective-permute-start | bytes 196616 | tf_op jit(solution)/shard_map/ppermute | solution.py:68
  44.6 1.4 %collective-permute-start.20 = (f32[128,128]{1,0:T(8,128)S(1)}, f32[128,128]{1,0:T(8,128)S(1)}, u32[]{:S(2)}, u32[]{:S(2)}) collective-permute-start(f32[128,128]{1,0:T(8,128)S(1)} %get-tuple-element.57), channel_id=1, source_target_pairs={{0,2},{1,3},{2,0},{3,1},{4,6},{5,7},{6,4},{7,5},{8,10},{9,11},{10,... | collective-permute-start | bytes 196616 | tf_op jit(solution)/shard_map/ppermute | solution.py:68
  46.0 2.3 %collective-permute-start.21 = (f32[128,128]{1,0:T(8,128)S(1)}, f32[128,128]{1,0:T(8,128)S(1)}, u32[]{:S(2)}, u32[]{:S(2)}) collective-permute-start(f32[128,128]{1,0:T(8,128)S(1)} %get-tuple-element.58), channel_id=1, source_target_pairs={{0,3},{1,2},{2,1},{3,0},{4,7},{5,6},{6,5},{7,4},{8,11},{9,10},{10,... | collective-permute-start | bytes 196616 | tf_op jit(solution)/shard_map/ppermute | solution.py:68
  48.3 1.3 %collective-permute-done.15.refs_1_ = f32[128,128]{1,0:T(8,128)S(1)} collective-permute-done((f32[128,128]{1,0:T(8,128)S(1)}, f32[128,128]{1,0:T(8,128)S(1)}, u32[]{:S(2)}, u32[]{:S(2)}) %collective-permute-start.15) | collective-permute-done | bytes 65568 | tf_op jit(solution)/shard_map/ppermute | solution.py:68
  49.6 0.1 collective-permute-start.25
  49.7 1.9 %shard_map.81 = (f32[8,64,128]{2,1,0:T(8,128)}, f32[8,128]{1,0:T(8,128)S(1)}) custom-call(s32[8,2,3]{2,1,0:T(2,128)S(1)} %shard_map.72.refs_0_, f32[16,64,128]{2,1,0:T(8,128)S(1)} %get-tuple-element.49.refs_1_, f32[128,128]{1,0:T(8,128)S(1)} %shard_map.80.refs_2_.refs_4_.refs_0_), custom_call_target="tpu_custom_call" | custom-call | flops 100000 | tf_op jit(solution)/shard_map/pallas_call | solution.py:30
  51.5 1.2 %collective-permute-done.20.refs_2_ = f32[128,128]{1,0:T(8,128)S(1)} collective-permute-done((f32[128,128]{1,0:T(8,128)S(1)}, f32[128,128]{1,0:T(8,128)S(1)}, u32[]{:S(2)}, u32[]{:S(2)}) %collective-permute-start.20) | collective-permute-done | bytes 65568 | tf_op jit(solution)/shard_map/ppermute | solution.py:68
  52.7 1.4 %collective-permute-start.24 = (f32[128,128]{1,0:T(8,128)S(1)}, f32[128,128]{1,0:T(8,128)S(1)}, u32[]{:S(2)}, u32[]{:S(2)}) collective-permute-start(f32[128,128]{1,0:T(8,128)S(1)} %shard_map.82.refs_3_.refs_0_), channel_id=1, source_target_pairs={{0,24},{4,28},{8,16},{12,20},{16,8},{20,12},{24,0},{28,4},{1,25},{... | collective-permute-start | bytes 196616 | tf_op jit(solution)/shard_map/ppermute | solution.py:68
  54.1 1.0 %collective-permute-start.23 = (f32[128,128]{1,0:T(8,128)S(1)}, f32[128,128]{1,0:T(8,128)S(1)}, u32[]{:S(2)}, u32[]{:S(2)}) collective-permute-start(f32[128,128]{1,0:T(8,128)S(1)} %shard_map.82.refs_3_.refs_0_), channel_id=1, source_target_pairs={{0,16},{4,20},{8,24},{12,28},{16,0},{20,4},{24,8},{28,12},{1,17},{... | collective-permute-start | bytes 196616 | tf_op jit(solution)/shard_map/ppermute | solution.py:68
  55.1 1.2 %collective-permute-start.22 = (f32[128,128]{1,0:T(8,128)S(1)}, f32[128,128]{1,0:T(8,128)S(1)}, u32[]{:S(2)}, u32[]{:S(2)}) collective-permute-start(f32[128,128]{1,0:T(8,128)S(1)} %shard_map.82.refs_3_.refs_0_), channel_id=1, source_target_pairs={{0,8},{4,12},{8,0},{12,4},{16,24},{20,28},{24,16},{28,20},{1,9},{5... | collective-permute-start | bytes 196616 | tf_op jit(solution)/shard_map/ppermute | solution.py:68
  56.3 2.4 %shard_map.83 = (f32[128,128]{1,0:T(8,128)S(1)}, f32[128,128]{1,0:T(8,128)S(1)}, f32[128,128]{1,0:T(8,128)S(1)}) custom-call(f32[128,128]{1,0:T(8,128)S(1)} %shard_map.80.refs_2_.refs_4_.refs_0_, f32[128,128]{1,0:T(8,128)S(1)} %collective-permute-done.25.refs_1_, f32[128,128]{1,0:T(8,128)S(1)} %get-tuple-element.60.refs_2_, ...), custom_call_target="tpu_custom_call" | custom-call | flops 1800000 | tf_op jit(solution)/shard_map/pallas_call | solution.py:30
  58.7 0.0 collective-permute-done.23.refs_2_
  58.7 0.7 %collective-permute-done.22.refs_1_ = f32[128,128]{1,0:T(8,128)S(1)} collective-permute-done((f32[128,128]{1,0:T(8,128)S(1)}, f32[128,128]{1,0:T(8,128)S(1)}, u32[]{:S(2)}, u32[]{:S(2)}) %collective-permute-start.22) | collective-permute-done | bytes 65568 | tf_op jit(solution)/shard_map/ppermute | solution.py:68
  59.4 0.1 collective-permute-start.26
  59.5 0.8 %shard_map.85.refs_1_.refs_2_ = f32[128,128]{1,0:T(8,128)S(1)} custom-call(f32[128,128]{1,0:T(8,128)S(1)} %get-tuple-element.61.refs_4_.refs_0_, f32[128,128]{1,0:T(8,128)S(1)} %get-tuple-element.62.refs_1_, f32[128,128]{1,0:T(8,128)S(1)} %get-tuple-element.63.refs_2_, f32[4,128,128]{2,1,0:T(8,128)S(1)} %shard_map.84.refs_3_.refs_0_), custom_call_target="tpu_custom_call" | custom-call | flops 1600000 | tf_op jit(solution)/shard_map/pallas_call | solution.py:30
  60.3 0.3 shard_map.86.refs_0_
  60.6 0.4 collective-permute-done.26.refs_1_
  61.0 1.1 %shard_map.87 = f32[16,8,8,128]{3,2,1,0:T(8,128)} custom-call(f32[4,128,128]{2,1,0:T(8,128)S(1)} %shard_map.86.refs_0_, f32[4,128,128]{2,1,0:T(8,128)S(1)} %collective-permute-done.26.refs_1_, f32[128,128]{1,0:T(8,128)S(1)} %shard_map.85.refs_1_.refs_2_), custom_call_target="tpu_custom_call" | custom-call | flops 300000 | tf_op jit(solution)/shard_map/pallas_call | solution.py:30
  (26 shorter events, 0.2 us)
Async XLA Ops:
  0.6 1.0 %copy-start = (f32[1024,128]{1,0:T(8,128)S(1)}, f32[1024,128]{1,0:T(8,128)}, u32[]{:S(2)}) copy-start(f32[1024,128]{1,0:T(8,128)} %param.7) | copy-start | bytes 1572868
  0.6 14.5 %copy-start.2 = (s32[1,1,2,3]{3,2,1,0:T(2,128)S(1)}, s32[1,1,2,3]{3,2,1,0:T(2,128)}, u32[]{:S(2)}) copy-start(s32[1,1,2,3]{3,2,1,0:T(2,128)} %param.5) | copy-start | bytes 76
  1.7 12.3 %collective-permute-start = (f32[16,2,8,128]{3,2,1,0:T(8,128)S(1)}, f32[16,2,8,128]{3,2,1,0:T(8,128)S(1)}, u32[]{:S(2)}, u32[]{:S(2)}) collective-permute-start(f32[16,2,8,128]{3,2,1,0:T(8,128)S(1)} %dynamic-slice_bitcast_fusion.refs_0_.refs_1_), channel_id=1, source_target_pairs={{0,1},{1,0},{2,3},{3,2},{4,6},{5,7},{6,4},{7,5},{8,9},{9,8},{10,11... | collective-permute-start | bytes 393224 | tf_op jit(solution)/shard_map/ppermute | solution.py:78
  4.8 9.2 %collective-permute-start.1 = (f32[16,8,128]{2,1,0:T(8,128)S(1)}, f32[16,8,128]{2,1,0:T(8,128)S(1)}, u32[]{:S(2)}, u32[]{:S(2)}) collective-permute-start(f32[16,8,128]{2,1,0:T(8,128)S(1)} %shard_map.59.refs_1_), channel_id=1, source_target_pairs={{0,3},{1,2},{2,1},{3,0},{4,7},{5,6},{6,5},{7,4},{8,11},{9,10},{10,... | collective-permute-start | bytes 196616 | tf_op jit(solution)/shard_map/ppermute | solution.py:68
  7.3 5.2 %collective-permute-start.4 = (s32[2,3]{1,0:T(2,128)}, s32[2,3]{1,0:T(2,128)S(1)}, u32[]{:S(2)}, u32[]{:S(2)}) collective-permute-start(s32[2,3]{1,0:T(2,128)} %bitcast.11), channel_id=1, source_target_pairs={{0,24},{4,28},{8,16},{12,20},{16,8},{20,12},{24,0},{28,4},{1,25},{... | collective-permute-start | bytes 80 | tf_op jit(solution)/shard_map/ppermute | solution.py:68
  9.7 3.8 %collective-permute-start.3 = (s32[2,3]{1,0:T(2,128)}, s32[2,3]{1,0:T(2,128)S(1)}, u32[]{:S(2)}, u32[]{:S(2)}) collective-permute-start(s32[2,3]{1,0:T(2,128)} %bitcast.12), channel_id=1, source_target_pairs={{0,16},{4,20},{8,24},{12,28},{16,0},{20,4},{24,8},{28,12},{1,17},{... | collective-permute-start | bytes 80 | tf_op jit(solution)/shard_map/ppermute | solution.py:68
  10.2 3.8 %collective-permute-start.2 = (s32[2,3]{1,0:T(2,128)}, s32[2,3]{1,0:T(2,128)S(1)}, u32[]{:S(2)}, u32[]{:S(2)}) collective-permute-start(s32[2,3]{1,0:T(2,128)} %bitcast.13), channel_id=1, source_target_pairs={{0,8},{4,12},{8,0},{12,4},{16,24},{20,28},{24,16},{28,20},{1,9},{5... | collective-permute-start | bytes 80 | tf_op jit(solution)/shard_map/ppermute | solution.py:68
  10.8 1.6 %copy-start.1 = (f32[1,1,2,64,4096]{4,3,2,1,0:T(8,128)S(1)}, f32[1,1,2,64,4096]{4,3,2,1,0:T(8,128)}, u32[]{:S(2)}) copy-start(f32[1,1,2,64,4096]{4,3,2,1,0:T(8,128)} %param.4) | copy-start | bytes 6291460
  14.0 1.5 %collective-permute-start.5 = (f32[48,8,128]{2,1,0:T(8,128)S(1)}, f32[48,8,128]{2,1,0:T(8,128)S(1)}, u32[]{:S(2)}, u32[]{:S(2)}) collective-permute-start(f32[48,8,128]{2,1,0:T(8,128)S(1)} %shard_map.61.refs_2_.refs_1_), channel_id=1, source_target_pairs={{0,4},{4,0},{8,12},{12,8},{16,20},{20,16},{24,28},{28,24},{1,5},{5... | collective-permute-start | bytes 589832 | tf_op jit(solution)/shard_map/ppermute | solution.py:68
  16.3 6.6 %collective-permute-start.6 = (f32[128,128]{1,0:T(8,128)S(1)}, f32[128,128]{1,0:T(8,128)S(1)}, u32[]{:S(2)}, u32[]{:S(2)}) collective-permute-start(f32[128,128]{1,0:T(8,128)S(1)} %get-tuple-element.36), channel_id=1, source_target_pairs={{0,8},{4,12},{8,0},{12,4},{16,24},{20,28},{24,16},{28,20},{1,9},{5... | collective-permute-start | bytes 196616 | tf_op jit(solution)/shard_map/ppermute | solution.py:68
  16.9 6.0 %collective-permute-start.7 = (f32[128,128]{1,0:T(8,128)S(1)}, f32[128,128]{1,0:T(8,128)S(1)}, u32[]{:S(2)}, u32[]{:S(2)}) collective-permute-start(f32[128,128]{1,0:T(8,128)S(1)} %get-tuple-element.37), channel_id=1, source_target_pairs={{0,16},{4,20},{8,24},{12,28},{16,0},{20,4},{24,8},{28,12},{1,17},{... | collective-permute-start | bytes 196616 | tf_op jit(solution)/shard_map/ppermute | solution.py:68
  18.4 5.2 %collective-permute-start.8 = (f32[128,128]{1,0:T(8,128)S(1)}, f32[128,128]{1,0:T(8,128)S(1)}, u32[]{:S(2)}, u32[]{:S(2)}) collective-permute-start(f32[128,128]{1,0:T(8,128)S(1)} %get-tuple-element.38), channel_id=1, source_target_pairs={{0,24},{4,28},{8,16},{12,20},{16,8},{20,12},{24,0},{28,4},{1,25},{... | collective-permute-start | bytes 196616 | tf_op jit(solution)/shard_map/ppermute | solution.py:68
  23.6 1.4 %collective-permute-start.9 = (f32[64,128]{1,0:T(8,128)S(1)}, f32[64,128]{1,0:T(8,128)S(1)}, u32[]{:S(2)}, u32[]{:S(2)}) collective-permute-start(f32[64,128]{1,0:T(8,128)S(1)} %shard_map.67.refs_6_.refs_0_), channel_id=1, source_target_pairs={{0,4},{4,0},{8,12},{12,8},{16,20},{20,16},{24,28},{28,24},{1,5},{5... | collective-permute-start | bytes 98312 | tf_op jit(solution)/shard_map/ppermute | solution.py:68
  25.0 5.9 %collective-permute-start.12 = (f32[136,128]{1,0:T(8,128)S(1)}, f32[136,128]{1,0:T(8,128)S(1)}, u32[]{:S(2)}, u32[]{:S(2)}) collective-permute-start(f32[136,128]{1,0:T(8,128)S(1)} %shard_map.69.refs_2_.refs_0_), channel_id=1, source_target_pairs={{0,24},{4,28},{8,16},{12,20},{16,8},{20,12},{24,0},{28,4},{1,25},{... | collective-permute-start | bytes 208904 | tf_op jit(solution)/shard_map/ppermute | solution.py:68
  26.5 5.5 %collective-permute-start.11 = (f32[136,128]{1,0:T(8,128)S(1)}, f32[136,128]{1,0:T(8,128)S(1)}, u32[]{:S(2)}, u32[]{:S(2)}) collective-permute-start(f32[136,128]{1,0:T(8,128)S(1)} %shard_map.69.refs_2_.refs_0_), channel_id=1, source_target_pairs={{0,16},{4,20},{8,24},{12,28},{16,0},{20,4},{24,8},{28,12},{1,17},{... | collective-permute-start | bytes 208904 | tf_op jit(solution)/shard_map/ppermute | solution.py:68
  28.0 4.3 %collective-permute-start.10 = (f32[136,128]{1,0:T(8,128)S(1)}, f32[136,128]{1,0:T(8,128)S(1)}, u32[]{:S(2)}, u32[]{:S(2)}) collective-permute-start(f32[136,128]{1,0:T(8,128)S(1)} %shard_map.69.refs_2_.refs_0_), channel_id=1, source_target_pairs={{0,8},{4,12},{8,0},{12,4},{16,24},{20,28},{24,16},{28,20},{1,9},{5... | collective-permute-start | bytes 208904 | tf_op jit(solution)/shard_map/ppermute | solution.py:68
  32.4 1.6 %collective-permute-start.13 = (f32[4,136,128]{2,1,0:T(8,128)S(1)}, f32[4,136,128]{2,1,0:T(8,128)S(1)}, u32[]{:S(2)}, u32[]{:S(2)}) collective-permute-start(f32[4,136,128]{2,1,0:T(8,128)S(1)} %shard_map.71.refs_0_.refs_3_.refs_1_), channel_id=1, source_target_pairs={{0,4},{4,0},{8,12},{12,8},{16,20},{20,16},{24,28},{28,24},{1,5},{5... | collective-permute-start | bytes 835592 | tf_op jit(solution)/shard_map/ppermute | solution.py:68
  35.5 1.3 %collective-permute-start.14 = (f32[4,4,8,128]{3,2,1,0:T(8,128)S(1)}, f32[4,4,8,128]{3,2,1,0:T(8,128)S(1)}, u32[]{:S(2)}, u32[]{:S(2)}) collective-permute-start(f32[4,4,8,128]{3,2,1,0:T(8,128)S(1)} %get-tuple-element.47), channel_id=1, source_target_pairs={{0,4},{4,0},{8,12},{12,8},{16,20},{20,16},{24,28},{28,24},{1,5},{5... | collective-permute-start | bytes 196616 | tf_op jit(solution)/shard_map/ppermute | solution.py:68
  36.8 5.8 %collective-permute-start.16 = (f32[2,4,8,128]{3,2,1,0:T(8,128)S(1)}, f32[2,4,8,128]{3,2,1,0:T(8,128)S(1)}, u32[]{:S(2)}, u32[]{:S(2)}) collective-permute-start(f32[2,4,8,128]{3,2,1,0:T(8,128)S(1)} %get-tuple-element.51), channel_id=1, source_target_pairs={{0,8},{4,12},{8,0},{12,4},{16,24},{20,28},{24,16},{28,20},{1,9},{5... | collective-permute-start | bytes 98312 | tf_op jit(solution)/shard_map/ppermute | solution.py:68
  37.7 4.9 %collective-permute-start.17 = (f32[2,4,8,128]{3,2,1,0:T(8,128)S(1)}, f32[2,4,8,128]{3,2,1,0:T(8,128)S(1)}, u32[]{:S(2)}, u32[]{:S(2)}) collective-permute-start(f32[2,4,8,128]{3,2,1,0:T(8,128)S(1)} %get-tuple-element.52), channel_id=1, source_target_pairs={{0,16},{4,20},{8,24},{12,28},{16,0},{20,4},{24,8},{28,12},{1,17},{... | collective-permute-start | bytes 98312 | tf_op jit(solution)/shard_map/ppermute | solution.py:68
  38.7 4.8 %collective-permute-start.18 = (f32[2,4,8,128]{3,2,1,0:T(8,128)S(1)}, f32[2,4,8,128]{3,2,1,0:T(8,128)S(1)}, u32[]{:S(2)}, u32[]{:S(2)}) collective-permute-start(f32[2,4,8,128]{3,2,1,0:T(8,128)S(1)} %get-tuple-element.53), channel_id=1, source_target_pairs={{0,24},{4,28},{8,16},{12,20},{16,8},{20,12},{24,0},{28,4},{1,25},{... | collective-permute-start | bytes 98312 | tf_op jit(solution)/shard_map/ppermute | solution.py:68
  42.0 7.6 %collective-permute-start.15 = (f32[128,128]{1,0:T(8,128)S(1)}, f32[128,128]{1,0:T(8,128)S(1)}, u32[]{:S(2)}, u32[]{:S(2)}) collective-permute-start(f32[128,128]{1,0:T(8,128)S(1)} %get-tuple-element.50.refs_5_.refs_0_), channel_id=1, source_target_pairs={{0,2},{1,3},{2,0},{3,1},{4,6},{5,7},{6,4},{7,5},{8,10},{9,11},{10,... | collective-permute-start | bytes 196616 | tf_op jit(solution)/shard_map/ppermute | solution.py:68
  43.8 7.7 %collective-permute-start.19 = (f32[128,128]{1,0:T(8,128)S(1)}, f32[128,128]{1,0:T(8,128)S(1)}, u32[]{:S(2)}, u32[]{:S(2)}) collective-permute-start(f32[128,128]{1,0:T(8,128)S(1)} %get-tuple-element.56), channel_id=1, source_target_pairs={{0,1},{1,0},{2,3},{3,2},{4,5},{5,4},{6,7},{7,6},{8,9},{9,8},{10,11... | collective-permute-start | bytes 196616 | tf_op jit(solution)/shard_map/ppermute | solution.py:68
  44.6 8.1 %collective-permute-start.20 = (f32[128,128]{1,0:T(8,128)S(1)}, f32[128,128]{1,0:T(8,128)S(1)}, u32[]{:S(2)}, u32[]{:S(2)}) collective-permute-start(f32[128,128]{1,0:T(8,128)S(1)} %get-tuple-element.57), channel_id=1, source_target_pairs={{0,2},{1,3},{2,0},{3,1},{4,6},{5,7},{6,4},{7,5},{8,10},{9,11},{10,... | collective-permute-start | bytes 196616 | tf_op jit(solution)/shard_map/ppermute | solution.py:68
  46.0 6.7 %collective-permute-start.21 = (f32[128,128]{1,0:T(8,128)S(1)}, f32[128,128]{1,0:T(8,128)S(1)}, u32[]{:S(2)}, u32[]{:S(2)}) collective-permute-start(f32[128,128]{1,0:T(8,128)S(1)} %get-tuple-element.58), channel_id=1, source_target_pairs={{0,3},{1,2},{2,1},{3,0},{4,7},{5,6},{6,5},{7,4},{8,11},{9,10},{10,... | collective-permute-start | bytes 196616 | tf_op jit(solution)/shard_map/ppermute | solution.py:68
  49.6 6.7 %collective-permute-start.25 = (f32[128,128]{1,0:T(8,128)S(1)}, f32[128,128]{1,0:T(8,128)S(1)}, u32[]{:S(2)}, u32[]{:S(2)}) collective-permute-start(f32[128,128]{1,0:T(8,128)S(1)} %shard_map.80.refs_2_.refs_4_.refs_0_), channel_id=1, source_target_pairs={{0,1},{1,0},{2,3},{3,2},{4,5},{5,4},{6,7},{7,6},{8,9},{9,8},{10,11... | collective-permute-start | bytes 196616 | tf_op jit(solution)/shard_map/ppermute | solution.py:68
  52.7 5.9 %collective-permute-start.24 = (f32[128,128]{1,0:T(8,128)S(1)}, f32[128,128]{1,0:T(8,128)S(1)}, u32[]{:S(2)}, u32[]{:S(2)}) collective-permute-start(f32[128,128]{1,0:T(8,128)S(1)} %shard_map.82.refs_3_.refs_0_), channel_id=1, source_target_pairs={{0,24},{4,28},{8,16},{12,20},{16,8},{20,12},{24,0},{28,4},{1,25},{... | collective-permute-start | bytes 196616 | tf_op jit(solution)/shard_map/ppermute | solution.py:68
  54.1 4.6 %collective-permute-start.23 = (f32[128,128]{1,0:T(8,128)S(1)}, f32[128,128]{1,0:T(8,128)S(1)}, u32[]{:S(2)}, u32[]{:S(2)}) collective-permute-start(f32[128,128]{1,0:T(8,128)S(1)} %shard_map.82.refs_3_.refs_0_), channel_id=1, source_target_pairs={{0,16},{4,20},{8,24},{12,28},{16,0},{20,4},{24,8},{28,12},{1,17},{... | collective-permute-start | bytes 196616 | tf_op jit(solution)/shard_map/ppermute | solution.py:68
  55.1 4.3 %collective-permute-start.22 = (f32[128,128]{1,0:T(8,128)S(1)}, f32[128,128]{1,0:T(8,128)S(1)}, u32[]{:S(2)}, u32[]{:S(2)}) collective-permute-start(f32[128,128]{1,0:T(8,128)S(1)} %shard_map.82.refs_3_.refs_0_), channel_id=1, source_target_pairs={{0,8},{4,12},{8,0},{12,4},{16,24},{20,28},{24,16},{28,20},{1,9},{5... | collective-permute-start | bytes 196616 | tf_op jit(solution)/shard_map/ppermute | solution.py:68
  59.4 1.6 %collective-permute-start.26 = (f32[4,128,128]{2,1,0:T(8,128)S(1)}, f32[4,128,128]{2,1,0:T(8,128)S(1)}, u32[]{:S(2)}, u32[]{:S(2)}) collective-permute-start(f32[4,128,128]{2,1,0:T(8,128)S(1)} %shard_map.84.refs_3_.refs_0_), channel_id=1, source_target_pairs={{0,4},{4,0},{8,12},{12,8},{16,20},{20,16},{24,28},{28,24},{1,5},{5... | collective-permute-start | bytes 786440 | tf_op jit(solution)/shard_map/ppermute | solution.py:68

commit v6 on v5

--- a/solution.py
+++ b/solution.py
@@ -186,7 +186,18 @@
             else:
                 total = add_tree([part[at, :] for part in parts])
                 held.append(scale * total * refs[0][at, :])
-        held_ref, left_ref, right_ref = refs[:3] if own else refs[1:]
+        held_ref, left_ref, right_ref, scale_ref = refs[:3] + refs[4:] if own else refs[1:]
+        sub = lax.broadcasted_iota(jnp.int32, (step, size), 0)
+        lane = lax.broadcasted_iota(jnp.int32, (step, size), 1)
+        diagonals = [
+            jnp.where(lane - step * block == sub, held[block], 0.0) for block in range(count)
+        ]
+        along = lax.rsqrt(jnp.sum(add_tree(diagonals), axis=0, keepdims=True))
+        for block in range(count):
+            at = slice(step * block, step * block + step)
+            down = lax.rsqrt(jnp.sum(diagonals[block], axis=1, keepdims=True))
+            held[block] = (held[block] * down) * along
+            scale_ref[at, :] = jnp.broadcast_to(down, (step, size)) * along
         held = eliminate(held, left_ref, right_ref, range(first_steps(count)))
         for block in range(count):
             at = slice(step * block, step * block + step)
@@ -195,33 +206,34 @@
                 left_ref[at, :] = jnp.zeros_like(held[block])
                 right_ref[at, :] = jnp.zeros_like(held[block])
 
-    outputs = [shaped(size, size)] * (4 if own else 3)
+    outputs = [shaped(size, size)] * (5 if own else 4)
     return kernel_call(body, outputs, operands, about_us=1.8, after=after)
 
 
-def end_inverse(held, left, right, after):
+def end_inverse(held, left, right, scaling, after):
     size = held.shape[0]
     step = pivot_rows
     count = size // step
 
-    def body(held_ref, left_in, right_in, out_ref, left_ref, right_ref):
+    def body(held_ref, left_in, right_in, scale_ref, out_ref, left_ref, right_ref):
         done = first_steps(count) * step
         left_ref[:done, :] = left_in[:done, :]
         right_ref[:done, :] = right_in[:done, :]
         rows = [held_ref[step * block : step * block + step, :] for block in range(count)]
         eliminate(rows, left_ref, right_ref, range(first_steps(count), count))
-        out_ref[...] = lax.dot_general(
+        inverse = lax.dot_general(
             left_ref[...],
             right_ref[...],
             (((0,), (0,)), ((), ())),
             precision=precise_level,
             preferred_element_type=jnp.float32,
         )
+        out_ref[...] = inverse * scale_ref[...]
 
     return kernel_call(
         body,
         [shaped(size, size)],
-        [held, left, right],
+        [held, left, right, scaling],
         scratch=[pltpu.VMEM((size, size), jnp.float32)] * 2,
         about_us=1.6,
         after=after,
@@ -832,7 +844,8 @@
     rows, terms = first_mode(tags, pieces, spread, wide_size, low, [half])
     other_half = swap_with(half, "wide", 1)
     terms = add_parts([terms], [other_half])
-    *started, gram_b = start_inverse([half, other_half], None, 1.0, [terms])
+    held, left, right, gram_b, scaling = start_inverse([half, other_half], None, 1.0, [terms])
+    started = [held, left, right, scaling]
     terms = pack_whole(gather_from(terms, "wide", skip=1), after=started[:1])
     inverse_b = end_inverse(*started, [terms])
     column_terms = with_partners(terms, low)

time: 62.3 us -> 62.3 us (level)
  transfers between devices with their start and end apart: 27 -> 27, of which waited for: 13 -> 13; matrix products, arithmetic and copies ran while one was open for 0% -> 0% of each run, Pallas kernels for 26% -> 27%
where the time goes in v6:
time: 62.3 us; the launch traced here: 62.1 us
  starting transfers between devices  28.9 us (46%)
  Pallas kernels  20.1 us (32%)
  waiting for transfers between devices  8.84 us (14%)
  local copies, waits for them, and re-layouts  2.62 us (4%)
  between operations  1.58 us (3%)
    ppermute x26, starting transfers between devices, swap_with(): lax.ppermute(value, axis, [(index, index ^ mask) for index in range(size)])  25.8 us
    pallas_call x29, Pallas kernels, kernel_call(): pl.pallas_call(whole, out_shape=outputs, in_specs=[in_smem] * scalars + [...  20.1 us
    ppermute x26, waiting for transfers between devices, swap_with(): lax.ppermute(value, axis, [(index, index ^ mask) for index in range(size)])  8.84 us
    ppermute x1, starting transfers between devices, send_by_core(): return lax.ppermute(value, ('wide', 'narrow'), pairs)  3.09 us
    unnamed x6, local copies, waits for them, and re-layouts  2.61 us
  transfers between devices with their start and end apart: 27, of which 13 were waited for; matrix products, arithmetic and copies ran while one was open for 0% of the time, Pallas kernels for 27%

profile of v6, /device:TPU:0, one launch (start us, length us, event | category | flops | bytes accessed | tf_op | source)
XLA Modules:
  0.0 62.1 jit_solution(2645046772184464925)
XLA Ops:
  0.6 0.0 copy-start
  0.6 0.0 copy-start.2
  0.7 1.0 %copy-done = f32[1024,128]{1,0:T(8,128)S(1)} copy-done((f32[1024,128]{1,0:T(8,128)S(1)}, f32[1024,128]{1,0:T(8,128)}, u32[]{:S(2)}) %copy-start) | copy-done | bytes 524312
  1.7 3.1 %collective-permute-start = (f32[16,2,8,128]{3,2,1,0:T(8,128)S(1)}, f32[16,2,8,128]{3,2,1,0:T(8,128)S(1)}, u32[]{:S(2)}, u32[]{:S(2)}) collective-permute-start(f32[16,2,8,128]{3,2,1,0:T(8,128)S(1)} %dynamic-slice_bitcast_fusion.refs_0_.refs_1_), channel_id=1, source_target_pairs={{0,1},{1,0},{2,3},{3,2},{4,6},{5,7},{6,4},{7,5},{8,9},{9,8},{10,11... | collective-permute-start | bytes 393224 | tf_op jit(solution)/shard_map/ppermute | solution.py:78
  4.8 2.5 %collective-permute-start.1 = (f32[16,8,128]{2,1,0:T(8,128)S(1)}, f32[16,8,128]{2,1,0:T(8,128)S(1)}, u32[]{:S(2)}, u32[]{:S(2)}) collective-permute-start(f32[16,8,128]{2,1,0:T(8,128)S(1)} %shard_map.59.refs_1_), channel_id=1, source_target_pairs={{0,3},{1,2},{2,1},{3,0},{4,7},{5,6},{6,5},{7,4},{8,11},{9,10},{10,... | collective-permute-start | bytes 196616 | tf_op jit(solution)/shard_map/ppermute | solution.py:68
  7.3 2.4 %collective-permute-start.4 = (s32[2,3]{1,0:T(2,128)}, s32[2,3]{1,0:T(2,128)S(1)}, u32[]{:S(2)}, u32[]{:S(2)}) collective-permute-start(s32[2,3]{1,0:T(2,128)} %bitcast.11), channel_id=1, source_target_pairs={{0,24},{4,28},{8,16},{12,20},{16,8},{20,12},{24,0},{28,4},{1,25},{... | collective-permute-start | bytes 80 | tf_op jit(solution)/shard_map/ppermute | solution.py:68
  9.7 0.5 collective-permute-start.3
  10.2 0.5 collective-permute-start.2
  10.8 1.6 %copy-done.1 = f32[1,1,2,64,4096]{4,3,2,1,0:T(8,128)S(1)} copy-done((f32[1,1,2,64,4096]{4,3,2,1,0:T(8,128)S(1)}, f32[1,1,2,64,4096]{4,3,2,1,0:T(8,128)}, u32[]{:S(2)}) %copy-start.1) | copy-done | bytes 2097176
  12.3 0.1 shard_map.60.refs_5_.refs_0_
  12.5 0.0 collective-permute-done.4.refs_4_.refs_3_
  12.5 1.0 %collective-permute-done.3.refs_3_.refs_2_ = s32[2,3]{1,0:T(2,128)S(1)} collective-permute-done((s32[2,3]{1,0:T(2,128)}, s32[2,3]{1,0:T(2,128)S(1)}, u32[]{:S(2)}, u32[]{:S(2)}) %collective-permute-start.3) | collective-permute-done | bytes 56 | tf_op jit(solution)/shard_map/ppermute | solution.py:68
  13.5 0.5 collective-permute-done.2.refs_2_.refs_1_
  14.0 0.0 collective-permute-done.1.refs_1_
  14.0 0.1 collective-permute-start.5
  14.7 0.4 shard_map.64.refs_4_
  15.2 0.1 shard_map.62
  15.3 0.3 collective-permute-done.5.refs_3_
  15.5 0.8 %shard_map.65 = (f32[128,128]{1,0:T(8,128)S(1)}, f32[128,128]{1,0:T(8,128)S(1)}, f32[128,128]{1,0:T(8,128)S(1)}, f32[128,128]{1,0:T(8,128)S(1)}) custom-call(s32[4,2,3]{2,1,0:T(2,128)S(1)} %shard_map.63.refs_0_, f32[16,2,8,128]{3,2,1,0:T(8,128)S(1)} %dynamic-slice_bitcast_fusion.refs_0_.refs_1_, f32[48,8,128]{2,1,0:T(8,128)S(1)} %shard_map.61.refs_2_.refs_1_, ...), custom_call_target="tpu_custom_call" | custom-call | flops 300000 | tf_op jit(solution)/shard_map/pallas_call | solution.py:30
  16.3 0.6 collective-permute-start.6
  16.9 1.5 %collective-permute-start.7 = (f32[128,128]{1,0:T(8,128)S(1)}, f32[128,128]{1,0:T(8,128)S(1)}, u32[]{:S(2)}, u32[]{:S(2)}) collective-permute-start(f32[128,128]{1,0:T(8,128)S(1)} %get-tuple-element.39), channel_id=1, source_target_pairs={{0,16},{4,20},{8,24},{12,28},{16,0},{20,4},{24,8},{28,12},{1,17},{... | collective-permute-start | bytes 196616 | tf_op jit(solution)/shard_map/ppermute | solution.py:68
  18.4 1.4 %collective-permute-start.8 = (f32[128,128]{1,0:T(8,128)S(1)}, f32[128,128]{1,0:T(8,128)S(1)}, u32[]{:S(2)}, u32[]{:S(2)}) collective-permute-start(f32[128,128]{1,0:T(8,128)S(1)} %get-tuple-element.40), channel_id=1, source_target_pairs={{0,24},{4,28},{8,16},{12,20},{16,8},{20,12},{24,0},{28,4},{1,25},{... | collective-permute-start | bytes 196616 | tf_op jit(solution)/shard_map/ppermute | solution.py:68
  19.9 3.0 %shard_map.66 = (bf16[2,4096,256]{2,1,0:T(8,128)(2,1)S(1)}, bf16[2,4096,256]{2,1,0:T(8,128)(2,1)S(1)}) custom-call(f32[2,64,4096]{2,1,0:T(8,128)S(1)} %shard_map.60.refs_5_.refs_0_, f32[128,128]{1,0:T(8,128)S(1)} %get-tuple-element.37.refs_1_.refs_0_), custom_call_target="tpu_custom_call" | custom-call | flops 300000 | tf_op jit(solution)/shard_map/pallas_call | solution.py:30
  22.9 0.7 %collective-permute-done.8.refs_3_.refs_4_ = f32[128,128]{1,0:T(8,128)S(1)} collective-permute-done((f32[128,128]{1,0:T(8,128)S(1)}, f32[128,128]{1,0:T(8,128)S(1)}, u32[]{:S(2)}, u32[]{:S(2)}) %collective-permute-start.8) | collective-permute-done | bytes 65568 | tf_op jit(solution)/shard_map/ppermute | solution.py:68
  23.6 0.1 collective-permute-start.9
  23.7 1.3 %shard_map.68 = (f32[4,64,128]{2,1,0:T(8,128)S(1)}, f32[136,128]{1,0:T(8,128)S(1)}) custom-call(f32[8,128]{1,0:T(8,128)S(1)} %get-tuple-element.35.refs_0_, f32[128,128]{1,0:T(8,128)S(1)} %get-tuple-element.37.refs_1_.refs_0_, f32[128,128]{1,0:T(8,128)S(1)} %collective-permute-done.6.refs_1_.refs_2_, f32[128,128]{1,0:T(8,128)S(1)} %collective-permute-done.7.refs_2_.refs_3_, ...), custom_call_target="tpu_custom_call" | custom-call | flops 3000000 | tf_op jit(solution)/shard_map/pallas_call | solution.py:30
  25.0 1.5 %collective-permute-start.12 = (f32[136,128]{1,0:T(8,128)S(1)}, f32[136,128]{1,0:T(8,128)S(1)}, u32[]{:S(2)}, u32[]{:S(2)}) collective-permute-start(f32[136,128]{1,0:T(8,128)S(1)} %shard_map.69.refs_2_.refs_0_), channel_id=1, source_target_pairs={{0,24},{4,28},{8,16},{12,20},{16,8},{20,12},{24,0},{28,4},{1,25},{... | collective-permute-start | bytes 208904 | tf_op jit(solution)/shard_map/ppermute | solution.py:68
  26.5 1.5 %collective-permute-start.11 = (f32[136,128]{1,0:T(8,128)S(1)}, f32[136,128]{1,0:T(8,128)S(1)}, u32[]{:S(2)}, u32[]{:S(2)}) collective-permute-start(f32[136,128]{1,0:T(8,128)S(1)} %shard_map.69.refs_2_.refs_0_), channel_id=1, source_target_pairs={{0,16},{4,20},{8,24},{12,28},{16,0},{20,4},{24,8},{28,12},{1,17},{... | collective-permute-start | bytes 208904 | tf_op jit(solution)/shard_map/ppermute | solution.py:68
  28.0 0.5 collective-permute-start.10
  28.6 2.5 %shard_map.70 = (f32[128,128]{1,0:T(8,128)S(1)}, f32[128,128]{1,0:T(8,128)S(1)}, f32[128,128]{1,0:T(8,128)S(1)}, f32[128,128]{1,0:T(8,128)S(1)}, f32[128,128]{1,0:T(8,128)S(1)}) custom-call(f32[64,128]{1,0:T(8,128)S(1)} %shard_map.67.refs_6_.refs_0_, f32[64,128]{1,0:T(8,128)S(1)} %collective-permute-done.9.refs_1_, f32[136,128]{1,0:T(8,128)S(1)} %shard_map.69.refs_2_.refs_0_), custom_call_target="tpu_custom_call" | custom-call | flops 1800000 | tf_op jit(solution)/shard_map/pallas_call | solution.py:30
  31.1 1.0 %collective-permute-done.11.refs_2_ = f32[136,128]{1,0:T(8,128)S(1)} collective-permute-done((f32[136,128]{1,0:T(8,128)S(1)}, f32[136,128]{1,0:T(8,128)S(1)}, u32[]{:S(2)}, u32[]{:S(2)}) %collective-permute-start.11) | collective-permute-done | bytes 69664 | tf_op jit(solution)/shard_map/ppermute | solution.py:68
  32.1 0.3 collective-permute-done.10.refs_1_
  32.4 0.1 collective-permute-start.13
  32.4 0.8 %shard_map.73.refs_2_.refs_3_ = f32[128,128]{1,0:T(8,128)S(1)} custom-call(f32[128,128]{1,0:T(8,128)S(1)} %get-tuple-element.44.refs_4_.refs_0_, f32[128,128]{1,0:T(8,128)S(1)} %get-tuple-element.45.refs_1_, f32[128,128]{1,0:T(8,128)S(1)} %get-tuple-element.46.refs_2_, f32[128,128]{1,0:T(8,128)S(1)} %get-tuple-element.47.refs_3_, ...), custom_call_target="tpu_custom_call" | custom-call | flops 1600000 | tf_op jit(solution)/shard_map/pallas_call | solution.py:30
  33.3 0.1 shard_map.74.refs_0_
  33.4 0.6 %collective-permute-done.13.refs_1_.refs_2_ = f32[4,136,128]{2,1,0:T(8,128)S(1)} collective-permute-done((f32[4,136,128]{2,1,0:T(8,128)S(1)}, f32[4,136,128]{2,1,0:T(8,128)S(1)}, u32[]{:S(2)}, u32[]{:S(2)}) %collective-permute-start.13) | collective-permute-done | bytes 278560 | tf_op jit(solution)/shard_map/ppermute | solution.py:68
  34.0 1.5 %shard_map.75 = (f32[4,4,8,128]{3,2,1,0:T(8,128)S(1)}, f32[4,4,8,128]{3,2,1,0:T(8,128)S(1)}) custom-call(f32[128,128]{1,0:T(8,128)S(1)} %shard_map.74.refs_0_, f32[4,136,128]{2,1,0:T(8,128)S(1)} %shard_map.71.refs_0_.refs_4_.refs_1_, f32[4,136,128]{2,1,0:T(8,128)S(1)} %collective-permute-done.13.refs_1_.refs_2_, f32[128,128]{1,0:T(8,128)S(1)} %shard_map.73.refs_2_.refs_3_, ...), custom_call_target="tpu_custom_call" | custom-call | flops 2500000 | tf_op jit(solution)/shard_map/pallas_call | solution.py:30
  35.5 0.2 collective-permute-start.14
  35.7 0.9 %shard_map.76.refs_2_.refs_0_ = bf16[512,256]{1,0:T(8,128)(2,1)S(1)} custom-call(s32[8,2,3]{2,1,0:T(2,128)S(1)} %shard_map.72.refs_0_, f32[4,4,8,128]{3,2,1,0:T(8,128)S(1)} %get-tuple-element.49.refs_1_.refs_0_), custom_call_target="tpu_custom_call" | custom-call | flops 300000 | tf_op jit(solution)/shard_map/pallas_call | solution.py:30
  36.6 0.2 collective-permute-done.14.refs_1_
  36.8 0.9 %collective-permute-start.16 = (f32[2,4,8,128]{3,2,1,0:T(8,128)S(1)}, f32[2,4,8,128]{3,2,1,0:T(8,128)S(1)}, u32[]{:S(2)}, u32[]{:S(2)}) collective-permute-start(f32[2,4,8,128]{3,2,1,0:T(8,128)S(1)} %get-tuple-element.54), channel_id=1, source_target_pairs={{0,8},{4,12},{8,0},{12,4},{16,24},{20,28},{24,16},{28,20},{1,9},{5... | collective-permute-start | bytes 98312 | tf_op jit(solution)/shard_map/ppermute | solution.py:68
  37.7 1.0 %collective-permute-start.17 = (f32[2,4,8,128]{3,2,1,0:T(8,128)S(1)}, f32[2,4,8,128]{3,2,1,0:T(8,128)S(1)}, u32[]{:S(2)}, u32[]{:S(2)}) collective-permute-start(f32[2,4,8,128]{3,2,1,0:T(8,128)S(1)} %get-tuple-element.55), channel_id=1, source_target_pairs={{0,16},{4,20},{8,24},{12,28},{16,0},{20,4},{24,8},{28,12},{1,17},{... | collective-permute-start | bytes 98312 | tf_op jit(solution)/shard_map/ppermute | solution.py:68
  38.7 1.7 %collective-permute-start.18 = (f32[2,4,8,128]{3,2,1,0:T(8,128)S(1)}, f32[2,4,8,128]{3,2,1,0:T(8,128)S(1)}, u32[]{:S(2)}, u32[]{:S(2)}) collective-permute-start(f32[2,4,8,128]{3,2,1,0:T(8,128)S(1)} %get-tuple-element.56), channel_id=1, source_target_pairs={{0,24},{4,28},{8,16},{12,20},{16,8},{20,12},{24,0},{28,4},{1,25},{... | collective-permute-start | bytes 98312 | tf_op jit(solution)/shard_map/ppermute | solution.py:68
  40.4 1.6 %shard_map.78 = (f32[128,128]{1,0:T(8,128)S(1)}, f32[16,64,128]{2,1,0:T(8,128)S(1)}) custom-call(s32[8,2,3]{2,1,0:T(2,128)S(1)} %shard_map.72.refs_0_, f32[4,136,128]{2,1,0:T(8,128)S(1)} %shard_map.71.refs_0_.refs_4_.refs_1_, f32[4,136,128]{2,1,0:T(8,128)S(1)} %collective-permute-done.13.refs_1_.refs_2_, f32[128,128]{1,0:T(8,128)S(1)} %shard_map.73.refs_2_.refs_3_, ...), custom_call_target="tpu_custom_call" | custom-call | flops 100000 | tf_op jit(solution)/shard_map/pallas_call | solution.py:30
  42.0 0.6 %collective-permute-start.15 = (f32[128,128]{1,0:T(8,128)S(1)}, f32[128,128]{1,0:T(8,128)S(1)}, u32[]{:S(2)}, u32[]{:S(2)}) collective-permute-start(f32[128,128]{1,0:T(8,128)S(1)} %get-tuple-element.53.refs_5_.refs_0_), channel_id=1, source_target_pairs={{0,2},{1,3},{2,0},{3,1},{4,6},{5,7},{6,4},{7,5},{8,10},{9,11},{10,... | collective-permute-start | bytes 196616 | tf_op jit(solution)/shard_map/ppermute | solution.py:68
  42.6 0.9 %collective-permute-done.18.refs_4_ = f32[2,4,8,128]{3,2,1,0:T(8,128)S(1)} collective-permute-done((f32[2,4,8,128]{3,2,1,0:T(8,128)S(1)}, f32[2,4,8,128]{3,2,1,0:T(8,128)S(1)}, u32[]{:S(2)}, u32[]{:S(2)}) %collective-permute-start.18) | collective-permute-done | bytes 32800 | tf_op jit(solution)/shard_map/ppermute | solution.py:68
  43.5 0.3 shard_map.79
  43.8 0.7 %collective-permute-start.19 = (f32[128,128]{1,0:T(8,128)S(1)}, f32[128,128]{1,0:T(8,128)S(1)}, u32[]{:S(2)}, u32[]{:S(2)}) collective-permute-start(f32[128,128]{1,0:T(8,128)S(1)} %get-tuple-element.59), channel_id=1, source_target_pairs={{0,1},{1,0},{2,3},{3,2},{4,5},{5,4},{6,7},{7,6},{8,9},{9,8},{10,11... | collective-permute-start | bytes 196616 | tf_op jit(solution)/shard_map/ppermute | solution.py:68
  44.6 1.4 %collective-permute-start.20 = (f32[128,128]{1,0:T(8,128)S(1)}, f32[128,128]{1,0:T(8,128)S(1)}, u32[]{:S(2)}, u32[]{:S(2)}) collective-permute-start(f32[128,128]{1,0:T(8,128)S(1)} %get-tuple-element.60), channel_id=1, source_target_pairs={{0,2},{1,3},{2,0},{3,1},{4,6},{5,7},{6,4},{7,5},{8,10},{9,11},{10,... | collective-permute-start | bytes 196616 | tf_op jit(solution)/shard_map/ppermute | solution.py:68
  46.0 2.3 %collective-permute-start.21 = (f32[128,128]{1,0:T(8,128)S(1)}, f32[128,128]{1,0:T(8,128)S(1)}, u32[]{:S(2)}, u32[]{:S(2)}) collective-permute-start(f32[128,128]{1,0:T(8,128)S(1)} %get-tuple-element.61), channel_id=1, source_target_pairs={{0,3},{1,2},{2,1},{3,0},{4,7},{5,6},{6,5},{7,4},{8,11},{9,10},{10,... | collective-permute-start | bytes 196616 | tf_op jit(solution)/shard_map/ppermute | solution.py:68
  48.3 1.3 %collective-permute-done.15.refs_1_ = f32[128,128]{1,0:T(8,128)S(1)} collective-permute-done((f32[128,128]{1,0:T(8,128)S(1)}, f32[128,128]{1,0:T(8,128)S(1)}, u32[]{:S(2)}, u32[]{:S(2)}) %collective-permute-start.15) | collective-permute-done | bytes 65568 | tf_op jit(solution)/shard_map/ppermute | solution.py:68
  49.6 0.1 collective-permute-start.25
  49.7 1.9 %shard_map.81 = (f32[8,64,128]{2,1,0:T(8,128)}, f32[8,128]{1,0:T(8,128)S(1)}) custom-call(s32[8,2,3]{2,1,0:T(2,128)S(1)} %shard_map.72.refs_0_, f32[16,64,128]{2,1,0:T(8,128)S(1)} %get-tuple-element.52.refs_1_, f32[128,128]{1,0:T(8,128)S(1)} %shard_map.80.refs_2_.refs_4_.refs_0_), custom_call_target="tpu_custom_call" | custom-call | flops 100000 | tf_op jit(solution)/shard_map/pallas_call | solution.py:30
  51.5 1.2 %collective-permute-done.20.refs_2_ = f32[128,128]{1,0:T(8,128)S(1)} collective-permute-done((f32[128,128]{1,0:T(8,128)S(1)}, f32[128,128]{1,0:T(8,128)S(1)}, u32[]{:S(2)}, u32[]{:S(2)}) %collective-permute-start.20) | collective-permute-done | bytes 65568 | tf_op jit(solution)/shard_map/ppermute | solution.py:68
  52.7 1.4 %collective-permute-start.24 = (f32[128,128]{1,0:T(8,128)S(1)}, f32[128,128]{1,0:T(8,128)S(1)}, u32[]{:S(2)}, u32[]{:S(2)}) collective-permute-start(f32[128,128]{1,0:T(8,128)S(1)} %shard_map.82.refs_3_.refs_0_), channel_id=1, source_target_pairs={{0,24},{4,28},{8,16},{12,20},{16,8},{20,12},{24,0},{28,4},{1,25},{... | collective-permute-start | bytes 196616 | tf_op jit(solution)/shard_map/ppermute | solution.py:68
  54.1 1.0 %collective-permute-start.23 = (f32[128,128]{1,0:T(8,128)S(1)}, f32[128,128]{1,0:T(8,128)S(1)}, u32[]{:S(2)}, u32[]{:S(2)}) collective-permute-start(f32[128,128]{1,0:T(8,128)S(1)} %shard_map.82.refs_3_.refs_0_), channel_id=1, source_target_pairs={{0,16},{4,20},{8,24},{12,28},{16,0},{20,4},{24,8},{28,12},{1,17},{... | collective-permute-start | bytes 196616 | tf_op jit(solution)/shard_map/ppermute | solution.py:68
  55.1 1.2 %collective-permute-start.22 = (f32[128,128]{1,0:T(8,128)S(1)}, f32[128,128]{1,0:T(8,128)S(1)}, u32[]{:S(2)}, u32[]{:S(2)}) collective-permute-start(f32[128,128]{1,0:T(8,128)S(1)} %shard_map.82.refs_3_.refs_0_), channel_id=1, source_target_pairs={{0,8},{4,12},{8,0},{12,4},{16,24},{20,28},{24,16},{28,20},{1,9},{5... | collective-permute-start | bytes 196616 | tf_op jit(solution)/shard_map/ppermute | solution.py:68
  56.3 2.5 %shard_map.83 = (f32[128,128]{1,0:T(8,128)S(1)}, f32[128,128]{1,0:T(8,128)S(1)}, f32[128,128]{1,0:T(8,128)S(1)}, f32[128,128]{1,0:T(8,128)S(1)}) custom-call(f32[128,128]{1,0:T(8,128)S(1)} %shard_map.80.refs_2_.refs_4_.refs_0_, f32[128,128]{1,0:T(8,128)S(1)} %collective-permute-done.25.refs_1_, f32[128,128]{1,0:T(8,128)S(1)} %get-tuple-element.63.refs_2_, ...), custom_call_target="tpu_custom_call" | custom-call | flops 1800000 | tf_op jit(solution)/shard_map/pallas_call | solution.py:30
  58.8 0.6 collective-permute-done.22.refs_1_
  59.4 0.1 collective-permute-start.26
  59.4 0.8 %shard_map.85.refs_1_.refs_2_ = f32[128,128]{1,0:T(8,128)S(1)} custom-call(f32[128,128]{1,0:T(8,128)S(1)} %get-tuple-element.64.refs_4_.refs_0_, f32[128,128]{1,0:T(8,128)S(1)} %get-tuple-element.65.refs_1_, f32[128,128]{1,0:T(8,128)S(1)} %get-tuple-element.66.refs_2_, f32[128,128]{1,0:T(8,128)S(1)} %get-tuple-element.67.refs_3_, ...), custom_call_target="tpu_custom_call" | custom-call | flops 1600000 | tf_op jit(solution)/shard_map/pallas_call | solution.py:30
  60.3 0.3 shard_map.86.refs_0_
  60.6 0.4 collective-permute-done.26.refs_1_
  61.0 1.1 %shard_map.87 = f32[16,8,8,128]{3,2,1,0:T(8,128)} custom-call(f32[4,128,128]{2,1,0:T(8,128)S(1)} %shard_map.86.refs_0_, f32[4,128,128]{2,1,0:T(8,128)S(1)} %collective-permute-done.26.refs_1_, f32[128,128]{1,0:T(8,128)S(1)} %shard_map.85.refs_1_.refs_2_), custom_call_target="tpu_custom_call" | custom-call | flops 300000 | tf_op jit(solution)/shard_map/pallas_call | solution.py:30
  (26 shorter events, 0.2 us)
Async XLA Ops:
  0.6 1.0 %copy-start = (f32[1024,128]{1,0:T(8,128)S(1)}, f32[1024,128]{1,0:T(8,128)}, u32[]{:S(2)}) copy-start(f32[1024,128]{1,0:T(8,128)} %param.7) | copy-start | bytes 1572868
  0.6 14.5 %copy-start.2 = (s32[1,1,2,3]{3,2,1,0:T(2,128)S(1)}, s32[1,1,2,3]{3,2,1,0:T(2,128)}, u32[]{:S(2)}) copy-start(s32[1,1,2,3]{3,2,1,0:T(2,128)} %param.5) | copy-start | bytes 76
  1.7 12.3 %collective-permute-start = (f32[16,2,8,128]{3,2,1,0:T(8,128)S(1)}, f32[16,2,8,128]{3,2,1,0:T(8,128)S(1)}, u32[]{:S(2)}, u32[]{:S(2)}) collective-permute-start(f32[16,2,8,128]{3,2,1,0:T(8,128)S(1)} %dynamic-slice_bitcast_fusion.refs_0_.refs_1_), channel_id=1, source_target_pairs={{0,1},{1,0},{2,3},{3,2},{4,6},{5,7},{6,4},{7,5},{8,9},{9,8},{10,11... | collective-permute-start | bytes 393224 | tf_op jit(solution)/shard_map/ppermute | solution.py:78
  4.8 9.2 %collective-permute-start.1 = (f32[16,8,128]{2,1,0:T(8,128)S(1)}, f32[16,8,128]{2,1,0:T(8,128)S(1)}, u32[]{:S(2)}, u32[]{:S(2)}) collective-permute-start(f32[16,8,128]{2,1,0:T(8,128)S(1)} %shard_map.59.refs_1_), channel_id=1, source_target_pairs={{0,3},{1,2},{2,1},{3,0},{4,7},{5,6},{6,5},{7,4},{8,11},{9,10},{10,... | collective-permute-start | bytes 196616 | tf_op jit(solution)/shard_map/ppermute | solution.py:68
  7.3 5.2 %collective-permute-start.4 = (s32[2,3]{1,0:T(2,128)}, s32[2,3]{1,0:T(2,128)S(1)}, u32[]{:S(2)}, u32[]{:S(2)}) collective-permute-start(s32[2,3]{1,0:T(2,128)} %bitcast.11), channel_id=1, source_target_pairs={{0,24},{4,28},{8,16},{12,20},{16,8},{20,12},{24,0},{28,4},{1,25},{... | collective-permute-start | bytes 80 | tf_op jit(solution)/shard_map/ppermute | solution.py:68
  9.7 3.8 %collective-permute-start.3 = (s32[2,3]{1,0:T(2,128)}, s32[2,3]{1,0:T(2,128)S(1)}, u32[]{:S(2)}, u32[]{:S(2)}) collective-permute-start(s32[2,3]{1,0:T(2,128)} %bitcast.12), channel_id=1, source_target_pairs={{0,16},{4,20},{8,24},{12,28},{16,0},{20,4},{24,8},{28,12},{1,17},{... | collective-permute-start | bytes 80 | tf_op jit(solution)/shard_map/ppermute | solution.py:68
  10.2 3.8 %collective-permute-start.2 = (s32[2,3]{1,0:T(2,128)}, s32[2,3]{1,0:T(2,128)S(1)}, u32[]{:S(2)}, u32[]{:S(2)}) collective-permute-start(s32[2,3]{1,0:T(2,128)} %bitcast.13), channel_id=1, source_target_pairs={{0,8},{4,12},{8,0},{12,4},{16,24},{20,28},{24,16},{28,20},{1,9},{5... | collective-permute-start | bytes 80 | tf_op jit(solution)/shard_map/ppermute | solution.py:68
  10.8 1.6 %copy-start.1 = (f32[1,1,2,64,4096]{4,3,2,1,0:T(8,128)S(1)}, f32[1,1,2,64,4096]{4,3,2,1,0:T(8,128)}, u32[]{:S(2)}) copy-start(f32[1,1,2,64,4096]{4,3,2,1,0:T(8,128)} %param.4) | copy-start | bytes 6291460
  14.0 1.5 %collective-permute-start.5 = (f32[48,8,128]{2,1,0:T(8,128)S(1)}, f32[48,8,128]{2,1,0:T(8,128)S(1)}, u32[]{:S(2)}, u32[]{:S(2)}) collective-permute-start(f32[48,8,128]{2,1,0:T(8,128)S(1)} %shard_map.61.refs_2_.refs_1_), channel_id=1, source_target_pairs={{0,4},{4,0},{8,12},{12,8},{16,20},{20,16},{24,28},{28,24},{1,5},{5... | collective-permute-start | bytes 589832 | tf_op jit(solution)/shard_map/ppermute | solution.py:68
  16.3 6.6 %collective-permute-start.6 = (f32[128,128]{1,0:T(8,128)S(1)}, f32[128,128]{1,0:T(8,128)S(1)}, u32[]{:S(2)}, u32[]{:S(2)}) collective-permute-start(f32[128,128]{1,0:T(8,128)S(1)} %get-tuple-element.38), channel_id=1, source_target_pairs={{0,8},{4,12},{8,0},{12,4},{16,24},{20,28},{24,16},{28,20},{1,9},{5... | collective-permute-start | bytes 196616 | tf_op jit(solution)/shard_map/ppermute | solution.py:68
  16.9 6.0 %collective-permute-start.7 = (f32[128,128]{1,0:T(8,128)S(1)}, f32[128,128]{1,0:T(8,128)S(1)}, u32[]{:S(2)}, u32[]{:S(2)}) collective-permute-start(f32[128,128]{1,0:T(8,128)S(1)} %get-tuple-element.39), channel_id=1, source_target_pairs={{0,16},{4,20},{8,24},{12,28},{16,0},{20,4},{24,8},{28,12},{1,17},{... | collective-permute-start | bytes 196616 | tf_op jit(solution)/shard_map/ppermute | solution.py:68
  18.4 5.2 %collective-permute-start.8 = (f32[128,128]{1,0:T(8,128)S(1)}, f32[128,128]{1,0:T(8,128)S(1)}, u32[]{:S(2)}, u32[]{:S(2)}) collective-permute-start(f32[128,128]{1,0:T(8,128)S(1)} %get-tuple-element.40), channel_id=1, source_target_pairs={{0,24},{4,28},{8,16},{12,20},{16,8},{20,12},{24,0},{28,4},{1,25},{... | collective-permute-start | bytes 196616 | tf_op jit(solution)/shard_map/ppermute | solution.py:68
  23.6 1.4 %collective-permute-start.9 = (f32[64,128]{1,0:T(8,128)S(1)}, f32[64,128]{1,0:T(8,128)S(1)}, u32[]{:S(2)}, u32[]{:S(2)}) collective-permute-start(f32[64,128]{1,0:T(8,128)S(1)} %shard_map.67.refs_6_.refs_0_), channel_id=1, source_target_pairs={{0,4},{4,0},{8,12},{12,8},{16,20},{20,16},{24,28},{28,24},{1,5},{5... | collective-permute-start | bytes 98312 | tf_op jit(solution)/shard_map/ppermute | solution.py:68
  25.0 6.1 %collective-permute-start.12 = (f32[136,128]{1,0:T(8,128)S(1)}, f32[136,128]{1,0:T(8,128)S(1)}, u32[]{:S(2)}, u32[]{:S(2)}) collective-permute-start(f32[136,128]{1,0:T(8,128)S(1)} %shard_map.69.refs_2_.refs_0_), channel_id=1, source_target_pairs={{0,24},{4,28},{8,16},{12,20},{16,8},{20,12},{24,0},{28,4},{1,25},{... | collective-permute-start | bytes 208904 | tf_op jit(solution)/shard_map/ppermute | solution.py:68
  26.5 5.5 %collective-permute-start.11 = (f32[136,128]{1,0:T(8,128)S(1)}, f32[136,128]{1,0:T(8,128)S(1)}, u32[]{:S(2)}, u32[]{:S(2)}) collective-permute-start(f32[136,128]{1,0:T(8,128)S(1)} %shard_map.69.refs_2_.refs_0_), channel_id=1, source_target_pairs={{0,16},{4,20},{8,24},{12,28},{16,0},{20,4},{24,8},{28,12},{1,17},{... | collective-permute-start | bytes 208904 | tf_op jit(solution)/shard_map/ppermute | solution.py:68
  28.0 4.3 %collective-permute-start.10 = (f32[136,128]{1,0:T(8,128)S(1)}, f32[136,128]{1,0:T(8,128)S(1)}, u32[]{:S(2)}, u32[]{:S(2)}) collective-permute-start(f32[136,128]{1,0:T(8,128)S(1)} %shard_map.69.refs_2_.refs_0_), channel_id=1, source_target_pairs={{0,8},{4,12},{8,0},{12,4},{16,24},{20,28},{24,16},{28,20},{1,9},{5... | collective-permute-start | bytes 208904 | tf_op jit(solution)/shard_map/ppermute | solution.py:68
  32.4 1.6 %collective-permute-start.13 = (f32[4,136,128]{2,1,0:T(8,128)S(1)}, f32[4,136,128]{2,1,0:T(8,128)S(1)}, u32[]{:S(2)}, u32[]{:S(2)}) collective-permute-start(f32[4,136,128]{2,1,0:T(8,128)S(1)} %shard_map.71.refs_0_.refs_4_.refs_1_), channel_id=1, source_target_pairs={{0,4},{4,0},{8,12},{12,8},{16,20},{20,16},{24,28},{28,24},{1,5},{5... | collective-permute-start | bytes 835592 | tf_op jit(solution)/shard_map/ppermute | solution.py:68
  35.5 1.3 %collective-permute-start.14 = (f32[4,4,8,128]{3,2,1,0:T(8,128)S(1)}, f32[4,4,8,128]{3,2,1,0:T(8,128)S(1)}, u32[]{:S(2)}, u32[]{:S(2)}) collective-permute-start(f32[4,4,8,128]{3,2,1,0:T(8,128)S(1)} %get-tuple-element.50), channel_id=1, source_target_pairs={{0,4},{4,0},{8,12},{12,8},{16,20},{20,16},{24,28},{28,24},{1,5},{5... | collective-permute-start | bytes 196616 | tf_op jit(solution)/shard_map/ppermute | solution.py:68
  36.8 5.8 %collective-permute-start.16 = (f32[2,4,8,128]{3,2,1,0:T(8,128)S(1)}, f32[2,4,8,128]{3,2,1,0:T(8,128)S(1)}, u32[]{:S(2)}, u32[]{:S(2)}) collective-permute-start(f32[2,4,8,128]{3,2,1,0:T(8,128)S(1)} %get-tuple-element.54), channel_id=1, source_target_pairs={{0,8},{4,12},{8,0},{12,4},{16,24},{20,28},{24,16},{28,20},{1,9},{5... | collective-permute-start | bytes 98312 | tf_op jit(solution)/shard_map/ppermute | solution.py:68
  37.7 4.9 %collective-permute-start.17 = (f32[2,4,8,128]{3,2,1,0:T(8,128)S(1)}, f32[2,4,8,128]{3,2,1,0:T(8,128)S(1)}, u32[]{:S(2)}, u32[]{:S(2)}) collective-permute-start(f32[2,4,8,128]{3,2,1,0:T(8,128)S(1)} %get-tuple-element.55), channel_id=1, source_target_pairs={{0,16},{4,20},{8,24},{12,28},{16,0},{20,4},{24,8},{28,12},{1,17},{... | collective-permute-start | bytes 98312 | tf_op jit(solution)/shard_map/ppermute | solution.py:68
  38.7 4.8 %collective-permute-start.18 = (f32[2,4,8,128]{3,2,1,0:T(8,128)S(1)}, f32[2,4,8,128]{3,2,1,0:T(8,128)S(1)}, u32[]{:S(2)}, u32[]{:S(2)}) collective-permute-start(f32[2,4,8,128]{3,2,1,0:T(8,128)S(1)} %get-tuple-element.56), channel_id=1, source_target_pairs={{0,24},{4,28},{8,16},{12,20},{16,8},{20,12},{24,0},{28,4},{1,25},{... | collective-permute-start | bytes 98312 | tf_op jit(solution)/shard_map/ppermute | solution.py:68
  42.0 7.6 %collective-permute-start.15 = (f32[128,128]{1,0:T(8,128)S(1)}, f32[128,128]{1,0:T(8,128)S(1)}, u32[]{:S(2)}, u32[]{:S(2)}) collective-permute-start(f32[128,128]{1,0:T(8,128)S(1)} %get-tuple-element.53.refs_5_.refs_0_), channel_id=1, source_target_pairs={{0,2},{1,3},{2,0},{3,1},{4,6},{5,7},{6,4},{7,5},{8,10},{9,11},{10,... | collective-permute-start | bytes 196616 | tf_op jit(solution)/shard_map/ppermute | solution.py:68
  43.8 7.7 %collective-permute-start.19 = (f32[128,128]{1,0:T(8,128)S(1)}, f32[128,128]{1,0:T(8,128)S(1)}, u32[]{:S(2)}, u32[]{:S(2)}) collective-permute-start(f32[128,128]{1,0:T(8,128)S(1)} %get-tuple-element.59), channel_id=1, source_target_pairs={{0,1},{1,0},{2,3},{3,2},{4,5},{5,4},{6,7},{7,6},{8,9},{9,8},{10,11... | collective-permute-start | bytes 196616 | tf_op jit(solution)/shard_map/ppermute | solution.py:68
  44.6 8.1 %collective-permute-start.20 = (f32[128,128]{1,0:T(8,128)S(1)}, f32[128,128]{1,0:T(8,128)S(1)}, u32[]{:S(2)}, u32[]{:S(2)}) collective-permute-start(f32[128,128]{1,0:T(8,128)S(1)} %get-tuple-element.60), channel_id=1, source_target_pairs={{0,2},{1,3},{2,0},{3,1},{4,6},{5,7},{6,4},{7,5},{8,10},{9,11},{10,... | collective-permute-start | bytes 196616 | tf_op jit(solution)/shard_map/ppermute | solution.py:68
  46.0 6.7 %collective-permute-start.21 = (f32[128,128]{1,0:T(8,128)S(1)}, f32[128,128]{1,0:T(8,128)S(1)}, u32[]{:S(2)}, u32[]{:S(2)}) collective-permute-start(f32[128,128]{1,0:T(8,128)S(1)} %get-tuple-element.61), channel_id=1, source_target_pairs={{0,3},{1,2},{2,1},{3,0},{4,7},{5,6},{6,5},{7,4},{8,11},{9,10},{10,... | collective-permute-start | bytes 196616 | tf_op jit(solution)/shard_map/ppermute | solution.py:68
  49.6 6.7 %collective-permute-start.25 = (f32[128,128]{1,0:T(8,128)S(1)}, f32[128,128]{1,0:T(8,128)S(1)}, u32[]{:S(2)}, u32[]{:S(2)}) collective-permute-start(f32[128,128]{1,0:T(8,128)S(1)} %shard_map.80.refs_2_.refs_4_.refs_0_), channel_id=1, source_target_pairs={{0,1},{1,0},{2,3},{3,2},{4,5},{5,4},{6,7},{7,6},{8,9},{9,8},{10,11... | collective-permute-start | bytes 196616 | tf_op jit(solution)/shard_map/ppermute | solution.py:68
  52.7 6.0 %collective-permute-start.24 = (f32[128,128]{1,0:T(8,128)S(1)}, f32[128,128]{1,0:T(8,128)S(1)}, u32[]{:S(2)}, u32[]{:S(2)}) collective-permute-start(f32[128,128]{1,0:T(8,128)S(1)} %shard_map.82.refs_3_.refs_0_), channel_id=1, source_target_pairs={{0,24},{4,28},{8,16},{12,20},{16,8},{20,12},{24,0},{28,4},{1,25},{... | collective-permute-start | bytes 196616 | tf_op jit(solution)/shard_map/ppermute | solution.py:68
  54.1 4.7 %collective-permute-start.23 = (f32[128,128]{1,0:T(8,128)S(1)}, f32[128,128]{1,0:T(8,128)S(1)}, u32[]{:S(2)}, u32[]{:S(2)}) collective-permute-start(f32[128,128]{1,0:T(8,128)S(1)} %shard_map.82.refs_3_.refs_0_), channel_id=1, source_target_pairs={{0,16},{4,20},{8,24},{12,28},{16,0},{20,4},{24,8},{28,12},{1,17},{... | collective-permute-start | bytes 196616 | tf_op jit(solution)/shard_map/ppermute | solution.py:68
  55.1 4.3 %collective-permute-start.22 = (f32[128,128]{1,0:T(8,128)S(1)}, f32[128,128]{1,0:T(8,128)S(1)}, u32[]{:S(2)}, u32[]{:S(2)}) collective-permute-start(f32[128,128]{1,0:T(8,128)S(1)} %shard_map.82.refs_3_.refs_0_), channel_id=1, source_target_pairs={{0,8},{4,12},{8,0},{12,4},{16,24},{20,28},{24,16},{28,20},{1,9},{5... | collective-permute-start | bytes 196616 | tf_op jit(solution)/shard_map/ppermute | solution.py:68
  59.4 1.6 %collective-permute-start.26 = (f32[4,128,128]{2,1,0:T(8,128)S(1)}, f32[4,128,128]{2,1,0:T(8,128)S(1)}, u32[]{:S(2)}, u32[]{:S(2)}) collective-permute-start(f32[4,128,128]{2,1,0:T(8,128)S(1)} %shard_map.84.refs_4_.refs_0_), channel_id=1, source_target_pairs={{0,4},{4,0},{8,12},{12,8},{16,20},{20,16},{24,28},{28,24},{1,5},{5... | collective-permute-start | bytes 786440 | tf_op jit(solution)/shard_map/ppermute | solution.py:68
